TPU v7x, 32 devices: a whole 2x2x4 slice. The times are simulated.
32 devices in a mesh: dp: 8 (over z, x), tensor: 4 (over y, core).
Axes of the slice: x: 2, y: 2, z: 4, core: 2. Of those that a mesh axis runs over, the one named last changes fastest.
Arguments:
- tokens: bfloat16 [4096, 768], P(('dp', 'tensor')), may hold values from -6 to 6
- cotangent: bfloat16 [4096, 768], P(('dp', 'tensor')), may hold values from -6 to 6
- w_qkv: bfloat16 [768, 3, 768], P('dp', None, 'tensor'), may hold values from -0.21875 to 0.21875
- w_out_attn: bfloat16 [768, 768], P('dp', 'tensor'), may hold values from -3 to 3
- w_router: bfloat16 [768, 4], P('dp'), may hold values from -0.109375 to 0.109375
- w_in: bfloat16 [768, 4, 3072], P('dp', None, 'tensor'), may hold values from -0.21875 to 0.21875
- w_out: bfloat16 [768, 4, 3072], P('dp', None, 'tensor'), may hold values from -0.875 to 0.875
- norm1_gain: bfloat16 [768], P('dp'), may hold values from 0.099609375 to 1.8984375
- norm2_gain: bfloat16 [768], P('dp'), may hold values from 0.099609375 to 1.8984375
- bias_table: bfloat16 [384], P('dp'), may hold values from -4 to 4
- seq_length: int32 [8], P('dp'), may hold values from 385 to 512, as said below
- expert_ids: int32 [4096], P('dp'), may hold values from 0 to 3
- expert_slots: int32 [4096], P('dp'), may hold values from -1 to 127, as said below
- buckets: int32 [1023], replicated, may hold values from 0 to 31
Outputs:
- layer_out: bfloat16 [4096, 768], P(('dp', 'tensor'))
- grad_tokens: float32 [4096, 768], P(('dp', 'tensor'))
- grad_w_qkv: float32 [768, 3, 768], P('dp', None, 'tensor')
- grad_w_out_attn: float32 [768, 768], P('dp', 'tensor')
- grad_w_router: float32 [768, 4], P('dp')
- grad_w_in: float32 [768, 4, 3072], P('dp', None, 'tensor')
- grad_w_out: float32 [768, 4, 3072], P('dp', None, 'tensor')
- grad_norm1_gain: float32 [768], P('dp')
- grad_norm2_gain: float32 [768], P('dp')
- grad_bias_table: float32 [384], P('dp')
Inputs may be any that keep to these rules, and one draw needn't show every extreme that they name: Positions at or past a group's seq_length are padding; some group is full. `expert_slots`: within one group no two tokens share an expert and a slot; -1 marks a token that is not sent (padding, or over the capacity of 128); in every group some expert's 128 slots are all used.
All inputs are finite; a program needn't handle non-finite values.
Results may differ from a plain program's by a relative error of at most 0.017.
Values may be sent and summed in bfloat16 or wider, within the bound.
No kernel may reach another device: no remote copies, remote signals or barrier semaphores. Data moves between devices by JAX's collectives and lax.ppermute only.
A program may use at most 192 MiB of HBM per device.

v0:
```python
import functools

import jax
import jax.numpy as jnp
from jax import lax
from jax.experimental import pallas as pl
from jax.experimental.pallas import tpu as pltpu
from jax.sharding import PartitionSpec as P

D = 768
H = 12
HD = 64
NB = 32
E = 4
SEQ = 512
CAP = 128
T = 4
LH = H // T
LW = LH * HD
ROWS = SEQ // T
SUB = CAP // T
SPAN = 2 * SEQ
TILE = 128
TILES = SEQ // TILE

EPSILON = 1e-06
HIGHEST_PRECISION = lax.Precision.HIGHEST
BF = jnp.bfloat16
F32 = jnp.float32


def mm(a, b, ca, cb):
    return lax.dot_general(a, b, (((ca,), (cb,)), ((), ())), preferred_element_type=F32)


def over_t(x, k):
    return lax.ppermute(x, "tensor", [(i, i ^ k) for i in range(T)])


def over_z(x, d):
    n = lax.axis_size("dp")
    r = n // E
    return lax.ppermute(x, "dp", [(i, ((i // r) ^ d) * r + i % r) for i in range(n)])


def over_r(x, c):
    n = lax.axis_size("dp")
    r = n // E
    return lax.ppermute(x, "dp", [(i, (i // r) * r + ((i % r) ^ c)) for i in range(n)])


def natural(parts, index):
    bit = 1
    while bit < len(parts):
        flip = (index & bit) != 0
        parts = [jnp.where(flip, parts[j ^ bit], parts[j]) for j in range(len(parts))]
        bit *= 2
    return parts


def gather_t(x):
    far = over_t(x, 2)
    return x, far, over_t(jnp.stack([x, far]), 1)


def in_order(gathered):
    own, far, near = gathered
    return [own, near[0], far, near[1]]


def scatter_t(kept, sent, *earlier):
    first = over_t(sent, 1).astype(F32)
    away = after((kept[1].astype(F32) + first[1]).astype(BF), *earlier)
    return kept[0].astype(F32) + first[0] + over_t(away, 2).astype(F32)


def pick(x, index, axis):
    return lax.dynamic_index_in_dim(x, index, axis, keepdims=False)


def after(x, *others):
    return lax.optimization_barrier((x, others))[0]


def swap_r(x):
    total = x[0].astype(F32)
    for c in range(1, x.shape[0]):
        total = total + over_r(x[c], c).astype(F32)
    return total


def deliver_z(x):
    return [x[0]] + [over_z(x[d], d) for d in range(1, E)]


def sum_everywhere(x, *earlier):
    R = lax.axis_size("dp") // E
    for k in (1, 2):
        x = x + over_t(x, k)
    x = after(x, *earlier)
    c = 1
    while c < R:
        x = x + over_r(x, c)
        c *= 2
    for d in (1, 2):
        x = x + over_z(x, d)
    return x


VMEM = pl.BlockSpec(memory_space=pltpu.VMEM)
SMEM = pl.BlockSpec(memory_space=pltpu.SMEM)
PARAMS = pltpu.CompilerParams(vmem_limit_bytes=48 * 2**20)


def call(kernel, name, micros, outs, scratch, at, *operands):
    moved = sum(a.size * a.dtype.itemsize for a in operands)
    return pl.pallas_call(
        kernel,
        out_shape=[jax.ShapeDtypeStruct(shape, kind) for shape, kind in outs],
        in_specs=[SMEM] + [VMEM] * len(operands),
        out_specs=[VMEM] * len(outs),
        scratch_shapes=[pltpu.VMEM(shape, kind) for shape, kind in scratch],
        compiler_params=PARAMS,
        cost_estimate=pl.CostEstimate(
            flops=micros * 10**9, bytes_accessed=moved, transcendentals=0
        ),
        name=name,
    )(at, *operands)


def block(index, length):
    return pl.ds(pl.multiple_of(index * length, length), length)


def place_rows(target, own_ref, far_ref, near_ref, t):
    for k, rows in ((0, own_ref[...]), (1, near_ref[0]), (2, far_ref[...]), (3, near_ref[1])):
        at = k if t is None else t ^ k
        target[block(at, ROWS), :] = rows


def place_weight(target, refs, at_ref, local):
    z, r, R = at_ref[0], at_ref[1], len(refs)
    for c in range(R):
        for d in range(E):
            target[block((z ^ d) * R + (r ^ c), local), :] = refs[c][d, :local, :]


def send_rows(source, out_ref, at_ref):
    R, _, local, _ = out_ref.shape
    for c in range(R):
        for d in range(E):
            at = block((at_ref[0] ^ d) * R + (at_ref[1] ^ c), local)
            out_ref[c, d] = source[at, :].astype(BF)


def attention_forward(
    at_ref,
    own_ref,
    far_ref,
    near_ref,
    gain_ref,
    rel_ref,
    slots_ref,
    *rest,
    pieces,
):
    refs, rest = rest[:pieces], rest[pieces:]
    normed_ref, qkv_ref, probs_ref, heads_ref, kept_ref, sent_ref, tokens_ref, weight_ref = rest
    t, length = at_ref[2], at_ref[3]
    if pieces == 1:
        weight_ref[...] = refs[0][...]
    else:
        place_weight(weight_ref, refs, at_ref, D // (pieces * E))
    place_rows(tokens_ref, own_ref, far_ref, near_ref, t)
    inputs = tokens_ref[...].astype(F32)
    normed_ref[...] = (inputs * norm_scale(inputs) * gain_ref[...]).astype(BF)
    qkv_ref[...] = mm(normed_ref[...], weight_ref[:, : 3 * LW], 1, 0).astype(BF)
    live = lax.broadcasted_iota(jnp.int32, (TILE, SEQ), 1) < length
    for h in range(LH):
        key = qkv_ref[:, LW + h * HD : LW + (h + 1) * HD]
        value = qkv_ref[:, 2 * LW + h * HD : 2 * LW + (h + 1) * HD]
        bias = jnp.broadcast_to(rel_ref[h : h + 1, :], (TILE, SPAN))
        for i in range(TILES):
            rows = slice(i * TILE, (i + 1) * TILE)
            query = qkv_ref[rows, h * HD : (h + 1) * HD]
            rolled = pltpu.roll(bias, SEQ + 1 + i * TILE, 1, stride=1, stride_axis=0)[:, :SEQ]
            scores = mm(query, key, 1, 1) * 0.125 + rolled
            scores = jnp.where(live, scores, -1e30)
            exponent = jnp.exp(scores - jnp.max(scores, axis=1, keepdims=True))
            probs = exponent / jnp.sum(exponent, axis=1, keepdims=True)
            probs_ref[h, rows, :] = probs
            heads_ref[rows, h * HD : (h + 1) * HD] = mm(probs.astype(BF), value, 1, 0).astype(BF)
    in_slots = mm(slots_ref[...], heads_ref[...], 1, 0).astype(BF)
    part = mm(in_slots, weight_ref[:, 3 * LW :], 1, 1).astype(BF)
    for k, out in ((0, kept_ref.at[0]), (1, sent_ref.at[0]), (2, kept_ref.at[1]), (3, sent_ref.at[1])):
        out[...] = part[k * ROWS : (k + 1) * ROWS]


def attention_backward(
    at_ref,
    own_ref,
    far_ref,
    near_ref,
    slots_ref,
    weight_ref,
    tokens_ref,
    normed_ref,
    qkv_ref,
    probs_ref,
    heads_ref,
    grads_ref,
    kept_ref,
    sent_ref,
    gain_ref,
    rel_ref,
    slot_scratch,
    heads_scratch,
    qkv_scratch,
    wide_scratch,
    weight_scratch,
):
    t = at_ref[2]
    place_rows(slot_scratch, own_ref, far_ref, near_ref, None)
    attended = mm(slots_ref[...], slot_scratch[...], 0, 0).astype(BF)
    heads_scratch[...] = mm(attended, weight_ref[:, 3 * LW :], 1, 0).astype(BF)
    weight_scratch[:, 3 * LW :] = mm(attended, heads_ref[...], 0, 0)
    flip = (
        lax.broadcasted_iota(jnp.int32, (TILE, TILE), 0)
        + lax.broadcasted_iota(jnp.int32, (TILE, TILE), 1)
        == TILE - 1
    ).astype(BF)
    rel_ref[...] = jnp.zeros_like(rel_ref)
    for h in range(LH):
        key = qkv_ref[:, LW + h * HD : LW + (h + 1) * HD]
        value = qkv_ref[:, 2 * LW + h * HD : 2 * LW + (h + 1) * HD]
        grad_key = jnp.zeros((SEQ, HD), F32)
        grad_value = jnp.zeros((SEQ, HD), F32)
        diagonal = [None] * (2 * TILES - 1)
        for i in range(TILES):
            rows = slice(i * TILE, (i + 1) * TILE)
            query = qkv_ref[rows, h * HD : (h + 1) * HD]
            grad = heads_scratch[rows, h * HD : (h + 1) * HD]
            probs = probs_ref[h, rows, :]
            grad_probs = mm(grad, value, 1, 1)
            inner = jnp.sum(probs * grad_probs, axis=1, keepdims=True)
            low = (probs * (grad_probs - inner)).astype(BF)
            qkv_scratch[rows, h * HD : (h + 1) * HD] = (mm(low, key, 1, 0) * 0.125).astype(BF)
            grad_key = grad_key + mm(low, query, 0, 0)
            grad_value = grad_value + mm(probs.astype(BF), grad, 0, 0)
            for j in range(TILES):
                turned = mm(low[:, j * TILE : (j + 1) * TILE], flip, 1, 0)
                at = i - j + TILES - 1
                diagonal[at] = turned if diagonal[at] is None else diagonal[at] + turned
        qkv_scratch[:, LW + h * HD : LW + (h + 1) * HD] = (grad_key * 0.125).astype(BF)
        qkv_scratch[:, 2 * LW + h * HD : 2 * LW + (h + 1) * HD] = grad_value.astype(BF)
        for at, part in enumerate(diagonal):
            wide = jnp.concatenate([part, jnp.zeros((TILE, TILE), F32)], axis=1)
            line = jnp.sum(pltpu.roll(wide, 0, 1, stride=1, stride_axis=0), axis=0, keepdims=True)
            rel_ref[h : h + 1, at * TILE : (at + 2) * TILE] += line
    weight_scratch[:, : 3 * LW] = mm(normed_ref[...], qkv_scratch[...], 0, 0)
    if len(grads_ref.shape) == 4:
        send_rows(weight_scratch, grads_ref, at_ref)
    else:
        grads_ref[...] = weight_scratch[...].astype(BF)
    wide_scratch[...] = mm(qkv_scratch[...], weight_ref[:, : 3 * LW], 1, 1)
    inputs = tokens_ref[...].astype(F32)
    gain_ref[...] = jnp.sum(
        wide_scratch[...] * inputs * norm_scale(inputs), axis=0, keepdims=True
    )
    for k, out in ((0, kept_ref.at[0]), (1, sent_ref.at[0]), (2, kept_ref.at[1]), (3, sent_ref.at[1])):
        out[...] = wide_scratch[block(t ^ k, ROWS), :].astype(BF)


def expert_layer(
    at_ref,
    own_ref,
    far_ref,
    near_ref,
    own_grad_ref,
    far_grad_ref,
    near_grad_ref,
    router_ref,
    *rest,
    pieces,
):
    in_refs, out_refs, rest = rest[:pieces], rest[pieces : 2 * pieces], rest[2 * pieces :]
    buffer_ref, grad_ref, activation_ref, grad_pre_ref, kept_ref, sent_ref, in_ref, out_ref = rest
    if pieces == 1:
        in_ref[...] = in_refs[0][...]
        out_ref[...] = out_refs[0][...]
    else:
        place_weight(in_ref, in_refs, at_ref, D // (pieces * E))
        place_weight(out_ref, out_refs, at_ref, D // (pieces * E))
    place_rows(buffer_ref, own_ref, far_ref, near_ref, None)
    place_rows(grad_ref, own_grad_ref, far_grad_ref, near_grad_ref, None)
    logits = mm(buffer_ref[...], router_ref[...], 1, 0)
    lane = lax.broadcasted_iota(jnp.int32, logits.shape, 1)
    logits = jnp.where(lane < E, logits, -1e30)
    exponent = jnp.exp(logits - jnp.max(logits, axis=1, keepdims=True))
    mine = jnp.sum(jnp.where(lane == at_ref[0], exponent, 0.0), axis=1, keepdims=True)
    gate = mine / jnp.sum(exponent, axis=1, keepdims=True)
    grad_ref[...] = (gate * grad_ref[...].astype(F32)).astype(BF)
    pre = mm(buffer_ref[...], in_ref[...], 1, 0)
    square = pre * pre
    tanh = jnp.tanh(0.7978845608028654 * (pre + 0.044715 * pre * square))
    half = 0.5 * (1.0 + tanh)
    activation_ref[...] = (pre * half).astype(BF)
    slope = half + 0.5 * pre * (1.0 - tanh * tanh) * (
        0.7978845608028654 * (1.0 + 3.0 * 0.044715 * square)
    )
    grad_act = mm(grad_ref[...], out_ref[...], 1, 0)
    grad_pre_ref[...] = (grad_act * slope).astype(BF)
    for k, out in ((0, kept_ref.at[0]), (1, sent_ref.at[0]), (2, kept_ref.at[1]), (3, sent_ref.at[1])):
        rows = slice(k * ROWS, (k + 1) * ROWS)
        out[:, :D] = mm(activation_ref[rows, :], out_ref[...], 1, 1).astype(BF)
        out[:, D:] = mm(grad_pre_ref[rows, :], in_ref[...], 1, 1).astype(BF)


def weight_gradient(at_ref, left_ref, right_ref, out_ref, scratch):
    scratch[...] = mm(left_ref[...], right_ref[...], 0, 0)
    if len(out_ref.shape) == 4:
        send_rows(scratch, out_ref, at_ref)
    else:
        out_ref[...] = scratch[...].astype(BF)


def norm_scale(values):
    return lax.rsqrt(jnp.mean(values * values, axis=-1, keepdims=True) + EPSILON)


def norm_back(grad, values, scale, gain):
    u = grad * gain
    inner = jnp.mean(u * values, axis=-1, keepdims=True)
    return scale * u - scale * scale * scale * values * inner


def body(
    tokens,
    cotangent,
    w_qkv,
    w_out_attn,
    w_router,
    w_in,
    w_out,
    norm1_gain,
    norm2_gain,
    bias_table,
    seq_length,
    expert_ids,
    expert_slots,
    buckets,
):
    n = lax.axis_size("dp")
    R = n // E
    at_dp = lax.axis_index("dp")
    z, r = at_dp // R, at_dp % R
    t = lax.axis_index("tensor")
    local = D // n
    width = w_in.shape[2]
    aligned = local % 16 == 0
    place_at = jnp.stack([z, r, t, seq_length[0]]).astype(jnp.int32)

    def whole(parts):
        if aligned:
            return [jnp.stack(part) if isinstance(part, list) else part for part in parts]
        rows = [jnp.stack(natural(list(part), z)) for part in parts]
        return [jnp.stack(natural(rows, r), axis=1).reshape(D, -1)]

    def blocks_to_send(grad):
        if aligned:
            return grad
        x = grad.reshape(E, R, local, -1)
        x = jnp.stack([pick(x, r ^ c, 1) for c in range(R)])
        return jnp.stack([pick(x, z ^ d, 1) for d in range(E)], axis=1)

    grads_shape = (R, E, local) if aligned else (D,)

    line = jnp.concatenate([w_router.T.reshape(-1), norm1_gain, norm2_gain, bias_table])
    line = jnp.pad(line, (0, -line.shape[0] % 128))[None]
    lines = lax.all_gather(line, "dp", axis=0, tiled=True)
    router_rows = lines[:, : local * E].reshape(n, E, local).transpose(1, 0, 2).reshape(E, D)
    gain_one = lines[:, local * E : local * (E + 1)].reshape(1, D).astype(F32)
    gain_two = lines[:, local * (E + 1) : local * (E + 2)].reshape(1, D).astype(F32)
    table_flat = lines[:, local * (E + 2) : local * (E + 2) + H * NB // n].reshape(-1)

    packed = jnp.concatenate([w_qkv.reshape(local, 3 * LW), w_out_attn], axis=1)
    packed_z = [packed] + [over_z(packed, d) for d in range(1, E)]
    packed_all = [packed_z] + [[over_r(part, c) for part in packed_z] for c in range(1, R)]

    both_parts = gather_t(jnp.concatenate([tokens, cotangent], axis=1))
    token_parts = [part[..., :D] for part in both_parts]
    cotangent_all = jnp.concatenate(natural([p[:, D:] for p in in_order(both_parts)], t), axis=0)

    sent = expert_slots >= 0
    absolute = jnp.where(sent, expert_ids * CAP + expert_slots, -1)
    position = jnp.arange(SEQ, dtype=jnp.int32)
    empty = ~jnp.any(absolute[None, :] == position[:, None], axis=1)
    before = position[None, :] <= position[:, None]
    empty_rank = jnp.sum((before & empty[None, :]).astype(jnp.int32), axis=1)
    unsent_rank = jnp.sum((before & ~sent[None, :]).astype(jnp.int32), axis=1)
    match = empty[None, :] & (empty_rank[None, :] == unsent_rank[:, None])
    spare = jnp.sum(jnp.where(match, position[None, :], 0), axis=1)
    slot = jnp.where(sent, absolute, spare)
    in_expert = slot % CAP
    place = ((in_expert // SUB) ^ t) * ROWS + ((slot // CAP) ^ z) * SUB + in_expert % SUB
    to_slots_mask = place[None, :] == position[:, None]
    to_slots = to_slots_mask.astype(BF)
    own_mask = to_slots_mask[:ROWS]
    sent_own = jnp.any(own_mask & sent[None, :], axis=1)
    chosen_own = jnp.sum(jnp.where(own_mask, expert_ids[None, :], 0), axis=1)
    own_tokens = lax.dynamic_slice_in_dim(place, t * ROWS, ROWS, 0)
    from_slots_own = (own_tokens[:, None] == position[None, :]).astype(BF)

    def dispatch_z(rows):
        rows = jnp.where(sent_own[:, None], rows, 0).astype(BF)
        return jnp.concatenate(deliver_z(rows.reshape(E, SUB, D)), axis=0)

    grad_output = mm(to_slots[:ROWS], cotangent_all, 1, 0)
    cotangent_z = dispatch_z(grad_output)
    in_parts = deliver_z(jnp.stack([pick(after(w_in, cotangent_z), z ^ d, 1) for d in range(E)]))
    out_parts = deliver_z(jnp.stack([pick(after(w_out, in_parts), z ^ d, 1) for d in range(E)]))
    in_columns, out_columns = jnp.stack(in_parts), jnp.stack(out_parts)
    in_weight = whole([in_columns] + [over_r(in_columns, c) for c in range(1, R)])
    out_weight = whole([out_columns] + [over_r(out_columns, c) for c in range(1, R)])
    cotangent_parts = gather_t(cotangent_z)

    table_rows = lax.dynamic_slice_in_dim(table_flat.astype(F32).reshape(H, NB), t * LH, LH, 0)
    bucket_table = (buckets[None, :] == jnp.arange(NB, dtype=jnp.int32)[:, None]).astype(F32)
    reversed_rel = jnp.dot(
        table_rows,
        jnp.pad(bucket_table[:, ::-1], ((0, 0), (0, 1))),
        precision=HIGHEST_PRECISION,
    )
    packed_refs = whole(packed_all)
    normed_all, qkv, probs, heads_all, kept, given, tokens_all, attention_weight = call(
        functools.partial(attention_forward, pieces=len(packed_refs)),
        "attention_forward",
        12,
        [
            ((SEQ, D), BF),
            ((SEQ, 3 * LW), BF),
            ((LH, SEQ, SEQ), F32),
            ((SEQ, LW), BF),
            ((2, ROWS, D), BF),
            ((2, ROWS, D), BF),
            ((SEQ, D), BF),
            ((D, 4 * LW), BF),
        ],
        [],
        place_at,
        *token_parts,
        gain_one,
        reversed_rel,
        after(to_slots, cotangent_z),
        *packed_refs,
    )
    attended = scatter_t(kept, after(given, in_columns, cotangent_parts[1]))
    inputs = mm(to_slots[:ROWS], tokens_all, 1, 0)
    middle = inputs + attended
    scale_two = norm_scale(middle)
    normed_two = (middle * scale_two * gain_two).astype(BF)

    buffer_parts = gather_t(dispatch_z(after(normed_two, out_columns, in_weight)))
    router = jnp.pad(router_rows.T, ((0, 0), (0, 128 - E)))
    buffer, grad_expert, activation, grad_pre, kept, given = call(
        functools.partial(expert_layer, pieces=len(in_weight)),
        "expert_layer",
        8,
        [
            ((SEQ, D), BF),
            ((SEQ, D), BF),
            ((SEQ, width), BF),
            ((SEQ, width), BF),
            ((2, ROWS, 2 * D), BF),
            ((2, ROWS, 2 * D), BF),
        ],
        [((D, width), BF), ((D, width), BF)],
        place_at,
        *buffer_parts,
        *cotangent_parts,
        router,
        *in_weight,
        *out_weight,
    )

    def expert_gradient(name, left, right):
        (out,) = call(
            weight_gradient,
            name,
            2,
            [((*grads_shape, width), BF)],
            [((D, width), F32)],
            place_at,
            left,
            right,
        )
        return blocks_to_send(out)

    out_terms = expert_gradient("grad_w_out", grad_expert, activation)
    in_terms = expert_gradient("grad_w_in", buffer, grad_pre)
    mine = scatter_t(kept, given).astype(BF)
    out_sums = swap_r(out_terms).astype(BF)
    returned = jnp.concatenate(deliver_z(mine.reshape(E, SUB, 2 * D)), axis=0).astype(F32)
    combined, grad_normed_two = returned[:, :D], returned[:, D:]
    in_sums = swap_r(after(in_terms, out_sums)).astype(BF)
    out_delivered = deliver_z(after(out_sums, returned))

    experts = jnp.arange(E, dtype=jnp.int32)[None, :]
    route = jax.nn.softmax(mm(normed_two, router_rows, 1, 1), axis=-1)
    chosen = experts == chosen_own[:, None]
    gate = jnp.sum(jnp.where(chosen, route, 0.0), axis=-1)
    layer_rows = (middle + gate[:, None] * combined).astype(BF)
    grad_gate = jnp.sum(grad_output * combined, axis=-1)
    grad_logits = gate[:, None] * (chosen.astype(F32) - route) * grad_gate[:, None]
    grad_router = lax.dot_general(
        grad_logits,
        normed_two.astype(F32),
        (((0,), (0,)), ((), ())),
        precision=HIGHEST_PRECISION,
    )
    grad_normed_two = grad_normed_two + jnp.dot(
        grad_logits, router_rows.astype(F32), precision=HIGHEST_PRECISION
    )
    grad_gain_two = jnp.sum(grad_normed_two * middle * scale_two, axis=0, keepdims=True)
    grad_middle = (grad_output + norm_back(grad_normed_two, middle, scale_two, gain_two)).astype(BF)
    grad_parts = gather_t(after(grad_middle, out_sums))
    layer_parts = gather_t(after(layer_rows, grad_parts))

    late_terms, kept, given, grad_gain_one, grad_rel = call(
        attention_backward,
        "attention_backward",
        12,
        [
            ((*grads_shape, 4 * LW), BF),
            ((2, ROWS, D), BF),
            ((2, ROWS, D), BF),
            ((1, D), F32),
            ((LH, SPAN), F32),
        ],
        [
            ((SEQ, D), BF),
            ((SEQ, LW), BF),
            ((SEQ, 3 * LW), BF),
            ((SEQ, D), F32),
            ((D, 4 * LW), F32),
        ],
        place_at,
        *grad_parts,
        after(to_slots, in_sums),
        attention_weight,
        tokens_all,
        normed_all,
        qkv,
        probs,
        heads_all,
    )
    in_delivered = deliver_z(after(in_sums, out_delivered, grad_parts))
    late_terms, kept, given, grad_gain_one, grad_rel = after(
        (late_terms, kept, given, grad_gain_one, grad_rel), in_delivered, layer_parts[1]
    )
    late_sums = swap_r(blocks_to_send(late_terms)).astype(BF)
    grad_normed_one = scatter_t(kept, given)
    own_inputs = tokens.astype(F32)
    grad_slots = jnp.concatenate(in_order(grad_parts), axis=0)
    grad_tokens = mm(from_slots_own, grad_slots, 1, 0) + norm_back(
        grad_normed_one, own_inputs, norm_scale(own_inputs), gain_one
    )
    layer_slots = jnp.concatenate(in_order(layer_parts), axis=0)
    layer_out = mm(from_slots_own, layer_slots, 1, 0).astype(BF)
    grad_table_rows = lax.dot_general(
        grad_rel[:, : 2 * SEQ - 1],
        bucket_table,
        (((1,), (1,)), ((), ())),
        precision=HIGHEST_PRECISION,
    )
    grad_table = lax.dynamic_update_slice_in_dim(
        jnp.zeros((H, NB), F32), grad_table_rows, t * LH, 0
    ).reshape(1, -1)
    small = sum_everywhere(
        jnp.concatenate(
            [
                grad_router,
                grad_gain_two,
                grad_gain_one,
                jnp.pad(grad_table, ((0, 0), (0, D - H * NB))),
                jnp.zeros((1, D), F32),
            ],
            axis=0,
        ),
        late_sums,
    )
    late_parts = deliver_z(late_sums)
    late = sum(part.astype(F32) for part in late_parts)
    small_own = lax.dynamic_slice_in_dim(small[: E + 2], at_dp * local, local, 1)
    table_own = lax.dynamic_slice_in_dim(small[E + 2], at_dp * (H * NB // n), H * NB // n, 0)
    return (
        layer_out,
        grad_tokens,
        late[:, : 3 * LW].reshape(local, 3, LW),
        late[:, 3 * LW :],
        small_own[:E].T,
        jnp.stack(natural(in_delivered, z), axis=1).astype(F32),
        jnp.stack(natural(out_delivered, z), axis=1).astype(F32),
        small_own[E + 1],
        small_own[E],
        table_own,
    )


def solution(mesh):
    in_specs = (
        P(("dp", "tensor"), None),
        P(("dp", "tensor"), None),
        P("dp", None, "tensor"),
        P("dp", "tensor"),
        P("dp", None),
        P("dp", None, "tensor"),
        P("dp", None, "tensor"),
        P("dp"),
        P("dp"),
        P("dp"),
        P("dp"),
        P("dp"),
        P("dp"),
        P(),
    )
    out_specs = (
        P(("dp", "tensor"), None),
        P(("dp", "tensor"), None),
        P("dp", None, "tensor"),
        P("dp", "tensor"),
        P("dp", None),
        P("dp", None, "tensor"),
        P("dp", None, "tensor"),
        P("dp"),
        P("dp"),
        P("dp"),
    )
    return jax.shard_map(body, mesh=mesh, in_specs=in_specs, out_specs=out_specs, check_vma=False)
```

profile of v0, /device:TPU:0, one launch (start us, length us, event | category | flops | bytes accessed | tf_op | source)
XLA Modules:
  0.0 246.9 jit_solution(5286063326539119702)
XLA Ops:
  2.0 1.5 pad_maximum_fusion.11
  3.6 5.0 %collective-permute-start.7 = (bf16[96,768]{1,0:T(8,128)(2,1)}, bf16[96,768]{1,0:T(8,128)(2,1)}, u32[]{:S(2)}, u32[]{:S(2)}) collective-permute-start(bf16[96,768]{1,0:T(8,128)(2,1)} %pad_maximum_fusion.11), channel_id=1, source_target_pairs={{0,24},{4,28},{8,16},{12,20},{16,8},{20,12},{24,0},{28,4},{1,25},{... | collective-permute-start | bytes 442376 | tf_op jit(solution)/shard_map/ppermute | solution.py:43
  9.2 1.7 collective-permute-start.8
  12.8 1.6 collective-permute-start
  14.9 30.6 %all-gather.1 = bf16[8,1,640]{2,1,0:T(2,128)(2,1)S(1)} all-gather(bf16[1,1,640]{2,1,0:T(2,128)(2,1)S(1)} %reshape.194), channel_id=2, replica_groups=mesh['dp'=8,'tensor'=4] {'dp'}, dimensions={0}, use_global_device_ids=true | all-gather | bytes 11520 | tf_op jit(solution)/shard_map/all_gather | solution.py:380
  49.3 1.4 collective-permute-start.10
  53.7 3.1 %collective-permute-start.4 = (bf16[32,768]{1,0:T(8,128)(2,1)S(1)}, bf16[32,768]{1,0:T(8,128)(2,1)S(1)}, u32[]{:S(2)}, u32[]{:S(2)}) collective-permute-start(bf16[32,768]{1,0:T(8,128)(2,1)S(1)} %get-tuple-element.191), channel_id=1, source_target_pairs={{0,24},{4,28},{8,16},{12,20},{16,8},{20,12},{24,0},{28,4},{1,25},{... | collective-permute-start | bytes 147464 | tf_op jit(solution)/shard_map/ppermute | solution.py:43
  58.7 2.8 %collective-permute-done.9 = bf16[96,768]{1,0:T(8,128)(2,1)S(1)} collective-permute-done((bf16[96,768]{1,0:T(8,128)(2,1)}, bf16[96,768]{1,0:T(8,128)(2,1)S(1)}, u32[]{:S(2)}, u32[]{:S(2)}) %collective-permute-start.9) | collective-permute-done | bytes 147488 | tf_op jit(solution)/shard_map/ppermute | solution.py:49
  63.2 1.9 collective-permute-start.14
  65.4 2.3 collective-permute-start.12
  67.6 8.0 %attention_forward.1 = (bf16[512,768]{1,0:T(8,128)(2,1)S(1)}, bf16[512,576]{1,0:T(8,128)(2,1)S(1)}, f32[3,512,512]{2,1,0:T(8,128)}, bf16[512,192]{1,0:T(8,128)(2...) custom-call(s32[4]{0:T(128)S(1)} %pad_add_fusion.at_ref, ...), custom_call_target="tpu_custom_call" | custom-call | flops 12000000000 | bytes 2505728 | tf_op jit(solution)/shard_map/attention_forward/pallas_call | solution.py:117
  76.4 1.5 collective-permute-done.13
  79.0 2.3 collective-permute-start.20
  81.3 2.1 collective-permute-start.18
  85.0 1.5 collective-permute-start.17
  87.9 6.0 %collective-permute-done.19 = bf16[96,768]{1,0:T(8,128)(2,1)} collective-permute-done((bf16[96,768]{1,0:T(8,128)(2,1)}, bf16[96,768]{1,0:T(8,128)(2,1)}, u32[]{:S(2)}, u32[]{:S(2)}) %collective-permute-start.19) | collective-permute-done | bytes 147488 | tf_op jit(solution)/shard_map/ppermute | solution.py:43
  95.1 1.6 multiply_reduce_fusion.3
  96.8 4.4 %collective-permute-done.21.rest_1_ = bf16[4,96,768]{2,1,0:T(8,128)(2,1)S(1)} collective-permute-done((bf16[4,96,768]{2,1,0:T(8,128)(2,1)S(1)}, bf16[4,96,768]{2,1,0:T(8,128)(2,1)S(1)}, u32[]{:S(2)}, u32[]{:S(2)}) %collective-permute-start.21) | collective-permute-done | bytes 589856 | tf_op jit(solution)/shard_map/ppermute | solution.py:49
  101.4 2.3 collective-permute-start.24
  103.7 2.1 collective-permute-start.22
  105.8 1.9 collective-permute-done.24
  110.8 3.6 %collective-permute-done.25.far_ref = bf16[128,768]{1,0:T(8,128)(2,1)S(1)} collective-permute-done((bf16[128,768]{1,0:T(8,128)(2,1)S(1)}, bf16[128,768]{1,0:T(8,128)(2,1)S(1)}, u32[]{:S(2)}, u32[]{:S(2)}) %collective-permute-start.25) | collective-permute-done | bytes 196640 | tf_op jit(solution)/shard_map/ppermute | solution.py:37
  120.1 5.9 %collective-permute-done.28.rest_3_ = bf16[4,96,768]{2,1,0:T(8,128)(2,1)} collective-permute-done((bf16[4,96,768]{2,1,0:T(8,128)(2,1)S(1)}, bf16[4,96,768]{2,1,0:T(8,128)(2,1)}, u32[]{:S(2)}, u32[]{:S(2)}) %collective-permute-start.28) | collective-permute-done | bytes 589856 | tf_op jit(solution)/shard_map/ppermute | solution.py:49
  128.0 6.7 %expert_layer.1 = (bf16[512,768]{1,0:T(8,128)(2,1)S(1)}, bf16[512,768]{1,0:T(8,128)(2,1)S(1)}, bf16[512,768]{1,0:T(8,128)(2,1)}, bf16[512,768]{1,0:T(8,128)(2,1)...) custom-call(s32[4]{0:T(128)S(1)} %pad_add_fusion.at_ref, ...), custom_call_target="tpu_custom_call" | custom-call | flops 8000000000 | bytes 4128768 | tf_op jit(solution)/shard_map/expert_layer/pallas_call | solution.py:117
  135.9 1.5 grad_w_out.1
  138.2 1.5 grad_w_in.1
  140.9 1.6 collective-permute-start.30
  142.4 10.7 %collective-permute-done.34 = bf16[4,96,768]{2,1,0:T(8,128)(2,1)S(1)} collective-permute-done((bf16[4,96,768]{2,1,0:T(8,128)(2,1)S(1)}, bf16[4,96,768]{2,1,0:T(8,128)(2,1)S(1)}, u32[]{:S(2)}, u32[]{:S(2)}) %collective-permute-start.34) | collective-permute-done | bytes 589856 | tf_op jit(solution)/shard_map/ppermute | solution.py:49
  154.3 2.1 collective-permute-start.33
  157.2 1.6 collective-permute-start.31
  158.8 9.6 %collective-permute-done.39 = bf16[4,96,768]{2,1,0:T(8,128)(2,1)S(1)} collective-permute-done((bf16[4,96,768]{2,1,0:T(8,128)(2,1)S(1)}, bf16[4,96,768]{2,1,0:T(8,128)(2,1)S(1)}, u32[]{:S(2)}, u32[]{:S(2)}) %collective-permute-start.39) | collective-permute-done | bytes 589856 | tf_op jit(solution)/shard_map/ppermute | solution.py:49
  170.2 1.6 collective-permute-start.35
  171.8 2.0 collective-permute-start.42
  174.5 1.7 collective-permute-start.40
  176.6 3.9 %collective-permute-done.42 = bf16[96,768]{1,0:T(8,128)(2,1)S(1)} collective-permute-done((bf16[96,768]{1,0:T(8,128)(2,1)S(1)}, bf16[96,768]{1,0:T(8,128)(2,1)S(1)}, u32[]{:S(2)}, u32[]{:S(2)}) %collective-permute-start.42) | collective-permute-done | bytes 147488 | tf_op jit(solution)/shard_map/ppermute | solution.py:43
  180.5 5.8 %collective-permute-done.41 = bf16[96,768]{1,0:T(8,128)(2,1)S(1)} collective-permute-done((bf16[96,768]{1,0:T(8,128)(2,1)S(1)}, bf16[96,768]{1,0:T(8,128)(2,1)S(1)}, u32[]{:S(2)}, u32[]{:S(2)}) %collective-permute-start.41) | collective-permute-done | bytes 147488 | tf_op jit(solution)/shard_map/ppermute | solution.py:43
  186.5 1.8 copy.87
  188.8 2.3 collective-permute-start.45
  191.2 2.1 collective-permute-start.43
  193.3 10.9 %attention_backward.1 = (bf16[2,4,96,768]{3,2,1,0:T(8,128)(2,1)S(1)}, bf16[2,128,768]{2,1,0:T(8,128)(2,1)S(1)}, bf16[2,128,768]{2,1,0:T(8,128)(2,1)}, f32[1,768]{1,0:T(1,128)S(1)}, f32[3,1024]{1,0:T(4,128)S(1)}) custom-call(s32[4]{0:T(128)S(1)} %pad_add_fusion.at_ref, bf16[128,768]{1,0:T(8,128)(2,1)S(1)} %add_convert_fusion.own_ref, ...), custom_call_target="tpu_custom_call" | custom-call | flops 12000000000 | bytes 7995392 | tf_op jit(solution)/shard_map/attention_backward/pallas_call | solution.py:117
  205.2 1.8 copy.86
  209.6 1.6 collective-permute-start.53
  214.6 1.6 collective-permute-start.47
  217.2 9.1 %collective-permute-done.48 = bf16[4,96,768]{2,1,0:T(8,128)(2,1)S(1)} collective-permute-done((bf16[4,96,768]{2,1,0:T(8,128)(2,1)S(1)}, bf16[4,96,768]{2,1,0:T(8,128)(2,1)S(1)}, u32[]{:S(2)}, u32[]{:S(2)}) %collective-permute-start.48) | collective-permute-done | bytes 589856 | tf_op jit(solution)/shard_map/ppermute | solution.py:49
  227.5 2.2 collective-permute-start.51
  232.2 4.6 %collective-permute-done.55 = f32[8,768]{1,0:T(8,128)S(1)} collective-permute-done((f32[8,768]{1,0:T(8,128)S(1)}, f32[8,768]{1,0:T(8,128)S(1)}, u32[]{:S(2)}, u32[]{:S(2)}) %collective-permute-start.55) | collective-permute-done | bytes 24608 | tf_op jit(solution)/shard_map/ppermute | solution.py:43
  236.9 2.8 %collective-permute-start.56 = (f32[8,768]{1,0:T(8,128)S(1)}, f32[8,768]{1,0:T(8,128)S(1)}, u32[]{:S(2)}, u32[]{:S(2)}) collective-permute-start(f32[8,768]{1,0:T(8,128)S(1)} %add.213), channel_id=1, source_target_pairs={{0,16},{4,20},{8,24},{12,28},{16,0},{20,4},{24,8},{28,12},{1,17},{... | collective-permute-start | bytes 73736 | tf_op jit(solution)/shard_map/ppermute | solution.py:43
  240.7 2.6 %collective-permute-done.56 = f32[8,768]{1,0:T(8,128)S(1)} collective-permute-done((f32[8,768]{1,0:T(8,128)S(1)}, f32[8,768]{1,0:T(8,128)S(1)}, u32[]{:S(2)}, u32[]{:S(2)}) %collective-permute-start.56) | collective-permute-done | bytes 24608 | tf_op jit(solution)/shard_map/ppermute | solution.py:43
  (277 shorter events, 55.7 us)
Async XLA Ops:
  3.6 45.1 %collective-permute-start.7 = (bf16[96,768]{1,0:T(8,128)(2,1)}, bf16[96,768]{1,0:T(8,128)(2,1)}, u32[]{:S(2)}, u32[]{:S(2)}) collective-permute-start(bf16[96,768]{1,0:T(8,128)(2,1)} %pad_maximum_fusion.11), channel_id=1, source_target_pairs={{0,24},{4,28},{8,16},{12,20},{16,8},{20,12},{24,0},{28,4},{1,25},{... | collective-permute-start | bytes 442376 | tf_op jit(solution)/shard_map/ppermute | solution.py:43
  8.6 40.7 %collective-permute-start.6 = (bf16[96,768]{1,0:T(8,128)(2,1)}, bf16[96,768]{1,0:T(8,128)(2,1)S(1)}, u32[]{:S(2)}, u32[]{:S(2)}) collective-permute-start(bf16[96,768]{1,0:T(8,128)(2,1)} %pad_maximum_fusion.11), channel_id=1, source_target_pairs={{0,16},{4,20},{8,24},{12,28},{16,0},{20,4},{24,8},{28,12},{1,17},{... | collective-permute-start | bytes 442376 | tf_op jit(solution)/shard_map/ppermute | solution.py:43
  8.6 42.1 %collective-permute-start.5 = (bf16[96,768]{1,0:T(8,128)(2,1)}, bf16[96,768]{1,0:T(8,128)(2,1)}, u32[]{:S(2)}, u32[]{:S(2)}) collective-permute-start(bf16[96,768]{1,0:T(8,128)(2,1)} %pad_maximum_fusion.11), channel_id=1, source_target_pairs={{0,8},{4,12},{8,0},{12,4},{16,24},{20,28},{24,16},{28,20},{1,9},{5... | collective-permute-start | bytes 442376 | tf_op jit(solution)/shard_map/ppermute | solution.py:43
  9.2 47.6 %collective-permute-start.8 = (bf16[96,768]{1,0:T(8,128)(2,1)}, bf16[96,768]{1,0:T(8,128)(2,1)S(1)}, u32[]{:S(2)}, u32[]{:S(2)}) collective-permute-start(bf16[96,768]{1,0:T(8,128)(2,1)} %pad_maximum_fusion.11), channel_id=1, source_target_pairs={{0,4},{4,0},{8,12},{12,8},{16,20},{20,16},{24,28},{28,24},{1,5},{5... | collective-permute-start | bytes 442376 | tf_op jit(solution)/shard_map/ppermute | solution.py:49
  12.8 35.1 %collective-permute-start = (bf16[128,1536]{1,0:T(8,128)(2,1)S(1)}, bf16[128,1536]{1,0:T(8,128)(2,1)S(1)}, u32[]{:S(2)}, u32[]{:S(2)}) collective-permute-start(bf16[128,1536]{1,0:T(8,128)(2,1)S(1)} %constant_dynamic-update-slice_fusion), channel_id=1, source_target_pairs={{0,2},{1,3},{2,0},{3,1},{4,6},{5,7},{6,4},{7,5},{8,10},{9,11},{10,... | collective-permute-start | bytes 1179656 | tf_op jit(solution)/shard_map/ppermute | solution.py:37
  48.7 8.2 %collective-permute-start.11 = (bf16[96,768]{1,0:T(8,128)(2,1)}, bf16[96,768]{1,0:T(8,128)(2,1)S(1)}, u32[]{:S(2)}, u32[]{:S(2)}) collective-permute-start(bf16[96,768]{1,0:T(8,128)(2,1)} %collective-permute-done.7), channel_id=1, source_target_pairs={{0,4},{4,0},{8,12},{12,8},{16,20},{20,16},{24,28},{28,24},{1,5},{5... | collective-permute-start | bytes 442376 | tf_op jit(solution)/shard_map/ppermute | solution.py:49
  49.3 9.4 %collective-permute-start.10 = (bf16[96,768]{1,0:T(8,128)(2,1)S(1)}, bf16[96,768]{1,0:T(8,128)(2,1)S(1)}, u32[]{:S(2)}, u32[]{:S(2)}) collective-permute-start(bf16[96,768]{1,0:T(8,128)(2,1)S(1)} %collective-permute-done.6), channel_id=1, source_target_pairs={{0,4},{4,0},{8,12},{12,8},{16,20},{20,16},{24,28},{28,24},{1,5},{5... | collective-permute-start | bytes 442376 | tf_op jit(solution)/shard_map/ppermute | solution.py:49
  50.8 10.7 %collective-permute-start.9 = (bf16[96,768]{1,0:T(8,128)(2,1)}, bf16[96,768]{1,0:T(8,128)(2,1)S(1)}, u32[]{:S(2)}, u32[]{:S(2)}) collective-permute-start(bf16[96,768]{1,0:T(8,128)(2,1)} %collective-permute-done.5), channel_id=1, source_target_pairs={{0,4},{4,0},{8,12},{12,8},{16,20},{20,16},{24,28},{28,24},{1,5},{5... | collective-permute-start | bytes 442376 | tf_op jit(solution)/shard_map/ppermute | solution.py:49
  53.7 8.0 %collective-permute-start.4 = (bf16[32,768]{1,0:T(8,128)(2,1)S(1)}, bf16[32,768]{1,0:T(8,128)(2,1)S(1)}, u32[]{:S(2)}, u32[]{:S(2)}) collective-permute-start(bf16[32,768]{1,0:T(8,128)(2,1)S(1)} %get-tuple-element.191), channel_id=1, source_target_pairs={{0,24},{4,28},{8,16},{12,20},{16,8},{20,12},{24,0},{28,4},{1,25},{... | collective-permute-start | bytes 147464 | tf_op jit(solution)/shard_map/ppermute | solution.py:43
  62.5 15.4 %collective-permute-start.15 = (bf16[128,768]{1,0:T(8,128)(2,1)S(1)}, bf16[128,768]{1,0:T(8,128)(2,1)S(1)}, u32[]{:S(2)}, u32[]{:S(2)}) collective-permute-start(bf16[128,768]{1,0:T(8,128)(2,1)S(1)} %get-tuple-element.183.own_grad_ref), channel_id=1, source_target_pairs={{0,2},{1,3},{2,0},{3,1},{4,6},{5,7},{6,4},{7,5},{8,10},{9,11},{10,... | collective-permute-start | bytes 589832 | tf_op jit(solution)/shard_map/ppermute | solution.py:37
  63.2 13.2 %collective-permute-start.14 = (bf16[96,768]{1,0:T(8,128)(2,1)S(1)}, bf16[96,768]{1,0:T(8,128)(2,1)S(1)}, u32[]{:S(2)}, u32[]{:S(2)}) collective-permute-start(bf16[96,768]{1,0:T(8,128)(2,1)S(1)} %get-tuple-element.170), channel_id=1, source_target_pairs={{0,24},{4,28},{8,16},{12,20},{16,8},{20,12},{24,0},{28,4},{1,25},{... | collective-permute-start | bytes 442376 | tf_op jit(solution)/shard_map/ppermute | solution.py:43
  65.1 12.8 %collective-permute-start.13 = (bf16[96,768]{1,0:T(8,128)(2,1)S(1)}, bf16[96,768]{1,0:T(8,128)(2,1)S(1)}, u32[]{:S(2)}, u32[]{:S(2)}) collective-permute-start(bf16[96,768]{1,0:T(8,128)(2,1)S(1)} %get-tuple-element.171), channel_id=1, source_target_pairs={{0,16},{4,20},{8,24},{12,28},{16,0},{20,4},{24,8},{28,12},{1,17},{... | collective-permute-start | bytes 442376 | tf_op jit(solution)/shard_map/ppermute | solution.py:43
  65.4 12.5 %collective-permute-start.12 = (bf16[96,768]{1,0:T(8,128)(2,1)S(1)}, bf16[96,768]{1,0:T(8,128)(2,1)S(1)}, u32[]{:S(2)}, u32[]{:S(2)}) collective-permute-start(bf16[96,768]{1,0:T(8,128)(2,1)S(1)} %get-tuple-element.172), channel_id=1, source_target_pairs={{0,8},{4,12},{8,0},{12,4},{16,24},{20,28},{24,16},{28,20},{1,9},{5... | collective-permute-start | bytes 442376 | tf_op jit(solution)/shard_map/ppermute | solution.py:43
  78.0 5.4 %collective-permute-start.16 = (bf16[2,128,768]{2,1,0:T(8,128)(2,1)S(1)}, bf16[2,128,768]{2,1,0:T(8,128)(2,1)S(1)}, u32[]{:S(2)}, u32[]{:S(2)}) collective-permute-start(bf16[2,128,768]{2,1,0:T(8,128)(2,1)S(1)} %get-tuple-element.51), channel_id=1, source_target_pairs={{0,1},{1,0},{2,3},{3,2},{4,5},{5,4},{6,7},{7,6},{8,9},{9,8},{10,11... | collective-permute-start | bytes 1179656 | tf_op jit(solution)/shard_map/ppermute | solution.py:37
  79.0 8.9 %collective-permute-start.20 = (bf16[96,768]{1,0:T(8,128)(2,1)}, bf16[96,768]{1,0:T(8,128)(2,1)}, u32[]{:S(2)}, u32[]{:S(2)}) collective-permute-start(bf16[96,768]{1,0:T(8,128)(2,1)} %get-tuple-element.166), channel_id=1, source_target_pairs={{0,24},{4,28},{8,16},{12,20},{16,8},{20,12},{24,0},{28,4},{1,25},{... | collective-permute-start | bytes 442376 | tf_op jit(solution)/shard_map/ppermute | solution.py:43
  81.3 12.7 %collective-permute-start.19 = (bf16[96,768]{1,0:T(8,128)(2,1)}, bf16[96,768]{1,0:T(8,128)(2,1)}, u32[]{:S(2)}, u32[]{:S(2)}) collective-permute-start(bf16[96,768]{1,0:T(8,128)(2,1)} %get-tuple-element.167), channel_id=1, source_target_pairs={{0,16},{4,20},{8,24},{12,28},{16,0},{20,4},{24,8},{28,12},{1,17},{... | collective-permute-start | bytes 442376 | tf_op jit(solution)/shard_map/ppermute | solution.py:43
  81.3 12.7 %collective-permute-start.18 = (bf16[96,768]{1,0:T(8,128)(2,1)}, bf16[96,768]{1,0:T(8,128)(2,1)}, u32[]{:S(2)}, u32[]{:S(2)}) collective-permute-start(bf16[96,768]{1,0:T(8,128)(2,1)} %get-tuple-element.168), channel_id=1, source_target_pairs={{0,8},{4,12},{8,0},{12,4},{16,24},{20,28},{24,16},{28,20},{1,9},{5... | collective-permute-start | bytes 442376 | tf_op jit(solution)/shard_map/ppermute | solution.py:43
  85.0 10.0 %collective-permute-start.17 = (bf16[128,768]{1,0:T(8,128)(2,1)}, bf16[128,768]{1,0:T(8,128)(2,1)}, u32[]{:S(2)}, u32[]{:S(2)}) collective-permute-start(bf16[128,768]{1,0:T(8,128)(2,1)} %fusion.46), channel_id=1, source_target_pairs={{0,2},{1,3},{2,0},{3,1},{4,6},{5,7},{6,4},{7,5},{8,10},{9,11},{10,... | collective-permute-start | bytes 589832 | tf_op jit(solution)/shard_map/ppermute | solution.py:37
  86.6 14.6 %collective-permute-start.21 = (bf16[4,96,768]{2,1,0:T(8,128)(2,1)S(1)}, bf16[4,96,768]{2,1,0:T(8,128)(2,1)S(1)}, u32[]{:S(2)}, u32[]{:S(2)}) collective-permute-start(bf16[4,96,768]{2,1,0:T(8,128)(2,1)S(1)} %pad_maximum_fusion.3.rest_0_), channel_id=1, source_target_pairs={{0,4},{4,0},{8,12},{12,8},{16,20},{20,16},{24,28},{28,24},{1,5},{5... | collective-permute-start | bytes 1769480 | tf_op jit(solution)/shard_map/ppermute | solution.py:49
  101.4 6.3 %collective-permute-start.24 = (bf16[32,768]{1,0:T(8,128)(2,1)S(1)}, bf16[32,768]{1,0:T(8,128)(2,1)S(1)}, u32[]{:S(2)}, u32[]{:S(2)}) collective-permute-start(bf16[32,768]{1,0:T(8,128)(2,1)S(1)} %get-tuple-element.187), channel_id=1, source_target_pairs={{0,24},{4,28},{8,16},{12,20},{16,8},{20,12},{24,0},{28,4},{1,25},{... | collective-permute-start | bytes 147464 | tf_op jit(solution)/shard_map/ppermute | solution.py:43
  108.7 5.7 %collective-permute-start.25 = (bf16[128,768]{1,0:T(8,128)(2,1)S(1)}, bf16[128,768]{1,0:T(8,128)(2,1)S(1)}, u32[]{:S(2)}, u32[]{:S(2)}) collective-permute-start(bf16[128,768]{1,0:T(8,128)(2,1)S(1)} %get-tuple-element.185.own_ref), channel_id=1, source_target_pairs={{0,2},{1,3},{2,0},{3,1},{4,6},{5,7},{6,4},{7,5},{8,10},{9,11},{10,... | collective-permute-start | bytes 589832 | tf_op jit(solution)/shard_map/ppermute | solution.py:37
  110.1 9.9 %collective-permute-start.27 = (bf16[2,128,768]{2,1,0:T(8,128)(2,1)}, bf16[2,128,768]{2,1,0:T(8,128)(2,1)}, u32[]{:S(2)}, u32[]{:S(2)}) collective-permute-start(bf16[2,128,768]{2,1,0:T(8,128)(2,1)} %pad_maximum_fusion.6), channel_id=1, source_target_pairs={{0,1},{1,0},{2,3},{3,2},{4,5},{5,4},{6,7},{7,6},{8,9},{9,8},{10,11... | collective-permute-start | bytes 1179656 | tf_op jit(solution)/shard_map/ppermute | solution.py:37
  110.1 15.8 %collective-permute-start.28 = (bf16[4,96,768]{2,1,0:T(8,128)(2,1)S(1)}, bf16[4,96,768]{2,1,0:T(8,128)(2,1)}, u32[]{:S(2)}, u32[]{:S(2)}) collective-permute-start(bf16[4,96,768]{2,1,0:T(8,128)(2,1)S(1)} %pad_maximum_fusion.4.rest_2_), channel_id=1, source_target_pairs={{0,4},{4,0},{8,12},{12,8},{16,20},{20,16},{24,28},{28,24},{1,5},{5... | collective-permute-start | bytes 1769480 | tf_op jit(solution)/shard_map/ppermute | solution.py:49
  115.9 10.0 %collective-permute-start.26 = (bf16[2,128,768]{2,1,0:T(8,128)(2,1)}, bf16[2,128,768]{2,1,0:T(8,128)(2,1)}, u32[]{:S(2)}, u32[]{:S(2)}) collective-permute-start(bf16[2,128,768]{2,1,0:T(8,128)(2,1)} %pad_maximum_fusion.5), channel_id=1, source_target_pairs={{0,1},{1,0},{2,3},{3,2},{4,5},{5,4},{6,7},{7,6},{8,9},{9,8},{10,11... | collective-permute-start | bytes 1179656 | tf_op jit(solution)/shard_map/ppermute | solution.py:37
  137.4 15.8 %collective-permute-start.34 = (bf16[4,96,768]{2,1,0:T(8,128)(2,1)S(1)}, bf16[4,96,768]{2,1,0:T(8,128)(2,1)S(1)}, u32[]{:S(2)}, u32[]{:S(2)}) collective-permute-start(bf16[4,96,768]{2,1,0:T(8,128)(2,1)S(1)} %slice_bitcast_fusion), channel_id=1, source_target_pairs={{0,4},{4,0},{8,12},{12,8},{16,20},{20,16},{24,28},{28,24},{1,5},{5... | collective-permute-start | bytes 1769480 | tf_op jit(solution)/shard_map/ppermute | solution.py:49
  140.9 13.3 %collective-permute-start.30 = (bf16[128,1536]{1,0:T(8,128)(2,1)S(1)}, bf16[128,1536]{1,0:T(8,128)(2,1)S(1)}, u32[]{:S(2)}, u32[]{:S(2)}) collective-permute-start(bf16[128,1536]{1,0:T(8,128)(2,1)S(1)} %fusion.36), channel_id=1, source_target_pairs={{0,2},{1,3},{2,0},{3,1},{4,6},{5,7},{6,4},{7,5},{8,10},{9,11},{10,... | collective-permute-start | bytes 1179656 | tf_op jit(solution)/shard_map/ppermute | solution.py:37
  153.4 15.0 %collective-permute-start.39 = (bf16[4,96,768]{2,1,0:T(8,128)(2,1)S(1)}, bf16[4,96,768]{2,1,0:T(8,128)(2,1)S(1)}, u32[]{:S(2)}, u32[]{:S(2)}) collective-permute-start(bf16[4,96,768]{2,1,0:T(8,128)(2,1)S(1)} %slice_bitcast_fusion.3), channel_id=1, source_target_pairs={{0,4},{4,0},{8,12},{12,8},{16,20},{20,16},{24,28},{28,24},{1,5},{5... | collective-permute-start | bytes 1769480 | tf_op jit(solution)/shard_map/ppermute | solution.py:49
  154.3 14.2 %collective-permute-start.33 = (bf16[32,1536]{1,0:T(8,128)(2,1)S(1)}, bf16[32,1536]{1,0:T(8,128)(2,1)S(1)}, u32[]{:S(2)}, u32[]{:S(2)}) collective-permute-start(bf16[32,1536]{1,0:T(8,128)(2,1)S(1)} %get-tuple-element.178), channel_id=1, source_target_pairs={{0,24},{4,28},{8,16},{12,20},{16,8},{20,12},{24,0},{28,4},{1,25},{... | collective-permute-start | bytes 294920 | tf_op jit(solution)/shard_map/ppermute | solution.py:43
  156.4 12.2 %collective-permute-start.32 = (bf16[32,1536]{1,0:T(8,128)(2,1)S(1)}, bf16[32,1536]{1,0:T(8,128)(2,1)S(1)}, u32[]{:S(2)}, u32[]{:S(2)}) collective-permute-start(bf16[32,1536]{1,0:T(8,128)(2,1)S(1)} %get-tuple-element.179), channel_id=1, source_target_pairs={{0,16},{4,20},{8,24},{12,28},{16,0},{20,4},{24,8},{28,12},{1,17},{... | collective-permute-start | bytes 294920 | tf_op jit(solution)/shard_map/ppermute | solution.py:43
  157.2 11.4 %collective-permute-start.31 = (bf16[32,1536]{1,0:T(8,128)(2,1)S(1)}, bf16[32,1536]{1,0:T(8,128)(2,1)S(1)}, u32[]{:S(2)}, u32[]{:S(2)}) collective-permute-start(bf16[32,1536]{1,0:T(8,128)(2,1)S(1)} %get-tuple-element.180), channel_id=1, source_target_pairs={{0,8},{4,12},{8,0},{12,4},{16,24},{20,28},{24,16},{28,20},{1,9},{5... | collective-permute-start | bytes 294920 | tf_op jit(solution)/shard_map/ppermute | solution.py:43
  170.2 6.3 %collective-permute-start.35 = (bf16[128,768]{1,0:T(8,128)(2,1)S(1)}, bf16[128,768]{1,0:T(8,128)(2,1)S(1)}, u32[]{:S(2)}, u32[]{:S(2)}) collective-permute-start(bf16[128,768]{1,0:T(8,128)(2,1)S(1)} %add_convert_fusion.own_ref), channel_id=1, source_target_pairs={{0,2},{1,3},{2,0},{3,1},{4,6},{5,7},{6,4},{7,5},{8,10},{9,11},{10,... | collective-permute-start | bytes 589832 | tf_op jit(solution)/shard_map/ppermute | solution.py:37
  171.8 8.7 %collective-permute-start.42 = (bf16[96,768]{1,0:T(8,128)(2,1)S(1)}, bf16[96,768]{1,0:T(8,128)(2,1)S(1)}, u32[]{:S(2)}, u32[]{:S(2)}) collective-permute-start(bf16[96,768]{1,0:T(8,128)(2,1)S(1)} %get-tuple-element.162), channel_id=1, source_target_pairs={{0,24},{4,28},{8,16},{12,20},{16,8},{20,12},{24,0},{28,4},{1,25},{... | collective-permute-start | bytes 442376 | tf_op jit(solution)/shard_map/ppermute | solution.py:43
  173.8 12.4 %collective-permute-start.41 = (bf16[96,768]{1,0:T(8,128)(2,1)S(1)}, bf16[96,768]{1,0:T(8,128)(2,1)S(1)}, u32[]{:S(2)}, u32[]{:S(2)}) collective-permute-start(bf16[96,768]{1,0:T(8,128)(2,1)S(1)} %get-tuple-element.163), channel_id=1, source_target_pairs={{0,16},{4,20},{8,24},{12,28},{16,0},{20,4},{24,8},{28,12},{1,17},{... | collective-permute-start | bytes 442376 | tf_op jit(solution)/shard_map/ppermute | solution.py:43
  174.5 11.8 %collective-permute-start.40 = (bf16[96,768]{1,0:T(8,128)(2,1)S(1)}, bf16[96,768]{1,0:T(8,128)(2,1)S(1)}, u32[]{:S(2)}, u32[]{:S(2)}) collective-permute-start(bf16[96,768]{1,0:T(8,128)(2,1)S(1)} %get-tuple-element.164), channel_id=1, source_target_pairs={{0,8},{4,12},{8,0},{12,4},{16,24},{20,28},{24,16},{28,20},{1,9},{5... | collective-permute-start | bytes 442376 | tf_op jit(solution)/shard_map/ppermute | solution.py:43
  176.5 11.8 %collective-permute-start.36 = (bf16[2,128,768]{2,1,0:T(8,128)(2,1)S(1)}, bf16[2,128,768]{2,1,0:T(8,128)(2,1)S(1)}, u32[]{:S(2)}, u32[]{:S(2)}) collective-permute-start(bf16[2,128,768]{2,1,0:T(8,128)(2,1)S(1)} %pad_maximum_fusion.7), channel_id=1, source_target_pairs={{0,1},{1,0},{2,3},{3,2},{4,5},{5,4},{6,7},{7,6},{8,9},{9,8},{10,11... | collective-permute-start | bytes 1179656 | tf_op jit(solution)/shard_map/ppermute | solution.py:37
  188.3 18.7 %collective-permute-start.37 = (bf16[128,768]{1,0:T(8,128)(2,1)S(1)}, bf16[128,768]{1,0:T(8,128)(2,1)S(1)}, u32[]{:S(2)}, u32[]{:S(2)}) collective-permute-start(bf16[128,768]{1,0:T(8,128)(2,1)S(1)} %get-tuple-element.59), channel_id=1, source_target_pairs={{0,2},{1,3},{2,0},{3,1},{4,6},{5,7},{6,4},{7,5},{8,10},{9,11},{10,... | collective-permute-start | bytes 589832 | tf_op jit(solution)/shard_map/ppermute | solution.py:37
  188.8 16.2 %collective-permute-start.45 = (bf16[96,768]{1,0:T(8,128)(2,1)S(1)}, bf16[96,768]{1,0:T(8,128)(2,1)S(1)}, u32[]{:S(2)}, u32[]{:S(2)}) collective-permute-start(bf16[96,768]{1,0:T(8,128)(2,1)S(1)} %get-tuple-element.159), channel_id=1, source_target_pairs={{0,24},{4,28},{8,16},{12,20},{16,8},{20,12},{24,0},{28,4},{1,25},{... | collective-permute-start | bytes 442376 | tf_op jit(solution)/shard_map/ppermute | solution.py:43
  191.2 13.8 %collective-permute-start.44 = (bf16[96,768]{1,0:T(8,128)(2,1)S(1)}, bf16[96,768]{1,0:T(8,128)(2,1)S(1)}, u32[]{:S(2)}, u32[]{:S(2)}) collective-permute-start(bf16[96,768]{1,0:T(8,128)(2,1)S(1)} %get-tuple-element.160), channel_id=1, source_target_pairs={{0,16},{4,20},{8,24},{12,28},{16,0},{20,4},{24,8},{28,12},{1,17},{... | collective-permute-start | bytes 442376 | tf_op jit(solution)/shard_map/ppermute | solution.py:43
  191.2 13.8 %collective-permute-start.43 = (bf16[96,768]{1,0:T(8,128)(2,1)S(1)}, bf16[96,768]{1,0:T(8,128)(2,1)S(1)}, u32[]{:S(2)}, u32[]{:S(2)}) collective-permute-start(bf16[96,768]{1,0:T(8,128)(2,1)S(1)} %get-tuple-element.161), channel_id=1, source_target_pairs={{0,8},{4,12},{8,0},{12,4},{16,24},{20,28},{24,16},{28,20},{1,9},{5... | collective-permute-start | bytes 442376 | tf_op jit(solution)/shard_map/ppermute | solution.py:43
  207.0 6.5 %collective-permute-start.46 = (bf16[2,128,768]{2,1,0:T(8,128)(2,1)}, bf16[2,128,768]{2,1,0:T(8,128)(2,1)}, u32[]{:S(2)}, u32[]{:S(2)}) collective-permute-start(bf16[2,128,768]{2,1,0:T(8,128)(2,1)} %get-tuple-element.77), channel_id=1, source_target_pairs={{0,1},{1,0},{2,3},{3,2},{4,5},{5,4},{6,7},{7,6},{8,9},{9,8},{10,11... | collective-permute-start | bytes 1179656 | tf_op jit(solution)/shard_map/ppermute | solution.py:37
  209.0 7.1 %collective-permute-start.38 = (bf16[2,128,768]{2,1,0:T(8,128)(2,1)S(1)}, bf16[2,128,768]{2,1,0:T(8,128)(2,1)S(1)}, u32[]{:S(2)}, u32[]{:S(2)}) collective-permute-start(bf16[2,128,768]{2,1,0:T(8,128)(2,1)S(1)} %pad_maximum_fusion.8), channel_id=1, source_target_pairs={{0,1},{1,0},{2,3},{3,2},{4,5},{5,4},{6,7},{7,6},{8,9},{9,8},{10,11... | collective-permute-start | bytes 1179656 | tf_op jit(solution)/shard_map/ppermute | solution.py:37
  211.2 15.1 %collective-permute-start.48 = (bf16[4,96,768]{2,1,0:T(8,128)(2,1)S(1)}, bf16[4,96,768]{2,1,0:T(8,128)(2,1)S(1)}, u32[]{:S(2)}, u32[]{:S(2)}) collective-permute-start(bf16[4,96,768]{2,1,0:T(8,128)(2,1)S(1)} %slice_bitcast_fusion.2), channel_id=1, source_target_pairs={{0,4},{4,0},{8,12},{12,8},{16,20},{20,16},{24,28},{28,24},{1,5},{5... | collective-permute-start | bytes 1769480 | tf_op jit(solution)/shard_map/ppermute | solution.py:49
  214.6 16.4 %collective-permute-start.47 = (bf16[128,768]{1,0:T(8,128)(2,1)S(1)}, bf16[128,768]{1,0:T(8,128)(2,1)S(1)}, u32[]{:S(2)}, u32[]{:S(2)}) collective-permute-start(bf16[128,768]{1,0:T(8,128)(2,1)S(1)} %fusion.47), channel_id=1, source_target_pairs={{0,2},{1,3},{2,0},{3,1},{4,6},{5,7},{6,4},{7,5},{8,10},{9,11},{10,... | collective-permute-start | bytes 589832 | tf_op jit(solution)/shard_map/ppermute | solution.py:37
  227.4 17.7 %collective-permute-start.49 = (bf16[96,768]{1,0:T(8,128)(2,1)S(1)}, bf16[96,768]{1,0:T(8,128)(2,1)S(1)}, u32[]{:S(2)}, u32[]{:S(2)}) collective-permute-start(bf16[96,768]{1,0:T(8,128)(2,1)S(1)} %get-tuple-element.156), channel_id=1, source_target_pairs={{0,8},{4,12},{8,0},{12,4},{16,24},{20,28},{24,16},{28,20},{1,9},{5... | collective-permute-start | bytes 442376 | tf_op jit(solution)/shard_map/ppermute | solution.py:43
  227.5 17.6 %collective-permute-start.51 = (bf16[96,768]{1,0:T(8,128)(2,1)S(1)}, bf16[96,768]{1,0:T(8,128)(2,1)S(1)}, u32[]{:S(2)}, u32[]{:S(2)}) collective-permute-start(bf16[96,768]{1,0:T(8,128)(2,1)S(1)} %get-tuple-element.157), channel_id=1, source_target_pairs={{0,24},{4,28},{8,16},{12,20},{16,8},{20,12},{24,0},{28,4},{1,25},{... | collective-permute-start | bytes 442376 | tf_op jit(solution)/shard_map/ppermute | solution.py:43
  229.7 15.4 %collective-permute-start.50 = (bf16[96,768]{1,0:T(8,128)(2,1)S(1)}, bf16[96,768]{1,0:T(8,128)(2,1)S(1)}, u32[]{:S(2)}, u32[]{:S(2)}) collective-permute-start(bf16[96,768]{1,0:T(8,128)(2,1)S(1)} %get-tuple-element.158), channel_id=1, source_target_pairs={{0,16},{4,20},{8,24},{12,28},{16,0},{20,4},{24,8},{28,12},{1,17},{... | collective-permute-start | bytes 442376 | tf_op jit(solution)/shard_map/ppermute | solution.py:43
  231.2 5.7 %collective-permute-start.55 = (f32[8,768]{1,0:T(8,128)S(1)}, f32[8,768]{1,0:T(8,128)S(1)}, u32[]{:S(2)}, u32[]{:S(2)}) collective-permute-start(f32[8,768]{1,0:T(8,128)S(1)} %add.212), channel_id=1, source_target_pairs={{0,8},{4,12},{8,0},{12,4},{16,24},{20,28},{24,16},{28,20},{1,9},{5... | collective-permute-start | bytes 73736 | tf_op jit(solution)/shard_map/ppermute | solution.py:43
  236.9 6.4 %collective-permute-start.56 = (f32[8,768]{1,0:T(8,128)S(1)}, f32[8,768]{1,0:T(8,128)S(1)}, u32[]{:S(2)}, u32[]{:S(2)}) collective-permute-start(f32[8,768]{1,0:T(8,128)S(1)} %add.213), channel_id=1, source_target_pairs={{0,16},{4,20},{8,24},{12,28},{16,0},{20,4},{24,8},{28,12},{1,17},{... | collective-permute-start | bytes 73736 | tf_op jit(solution)/shard_map/ppermute | solution.py:43
  (50 other events, 432.8 us)
where the time goes:
time: 248 us; the launch traced here: 247 us
  waiting for transfers between devices  76.1 us (31%)
  starting transfers between devices  65.4 us (26%)
  blocking collectives  30.6 us (12%)
  Pallas kernels  28.6 us (12%)
  local copies, waits for them, and re-layouts  23.4 us (9%)
  other arithmetic  13.8 us (6%)
  matrix products  6.82 us (3%)
    ppermute x29, starting transfers between devices, over_z(): lax.ppermute(x, 'dp', [(i, (i // r ^ d) * r + i % r) for i in range(n)])  44.1 us
    ppermute x10, waiting for transfers between devices, over_r(): lax.ppermute(x, 'dp', [(i, i // r * r + (i % r ^ c)) for i in range(n)])  43.2 us
    all_gather x1, blocking collectives, body(): lines = lax.all_gather(line, 'dp', axis=0, tiled=True)  30.6 us
    pallas_call x5, Pallas kernels, call(): pl.pallas_call(kernel, out_shape=[jax.ShapeDtypeStruct(shape, kind) for s...  28.6 us
    ppermute x29, waiting for transfers between devices, over_z(): lax.ppermute(x, 'dp', [(i, (i // r ^ d) * r + i % r) for i in range(n)])  27.9 us
    unnamed x91, local copies, waits for them, and re-layouts  14.8 us
    ppermute x18, starting transfers between devices, over_t(): return lax.ppermute(x, 'tensor', [(i, i ^ k) for i in range(T)])  11.9 us
    ppermute x10, starting transfers between devices, over_r(): lax.ppermute(x, 'dp', [(i, i // r * r + (i % r ^ c)) for i in range(n)])  9.4 us
  transfers between devices with their start and end apart: 57, of which 19 were waited for; matrix products, arithmetic and copies ran while one was open for 12% of the time, Pallas kernels for 9%

commit v1 on v0

--- a/solution.py
+++ b/solution.py
@@ -97,13 +97,24 @@
     R = lax.axis_size("dp") // E
     for k in (1, 2):
         x = x + over_t(x, k)
+    for d in (1, 2):
+        x = x + over_z(x, d)
     x = after(x, *earlier)
     c = 1
     while c < R:
         x = x + over_r(x, c)
         c *= 2
-    for d in (1, 2):
-        x = x + over_z(x, d)
+    return x
+
+
+def gather_lines(x, at_dp):
+    R = lax.axis_size("dp") // E
+    bit = 1
+    while bit < E * R:
+        other = over_r(x, bit) if bit < R else over_z(x, bit // R)
+        upper = (at_dp & bit) != 0
+        x = jnp.concatenate([jnp.where(upper, other, x), jnp.where(upper, x, other)], axis=0)
+        bit *= 2
     return x
 
 
@@ -377,7 +388,7 @@
 
     line = jnp.concatenate([w_router.T.reshape(-1), norm1_gain, norm2_gain, bias_table])
     line = jnp.pad(line, (0, -line.shape[0] % 128))[None]
-    lines = lax.all_gather(line, "dp", axis=0, tiled=True)
+    lines = gather_lines(line, at_dp)
     router_rows = lines[:, : local * E].reshape(n, E, local).transpose(1, 0, 2).reshape(E, D)
     gain_one = lines[:, local * E : local * (E + 1)].reshape(1, D).astype(F32)
     gain_two = lines[:, local * (E + 1) : local * (E + 2)].reshape(1, D).astype(F32)
@@ -385,7 +396,11 @@
 
     packed = jnp.concatenate([w_qkv.reshape(local, 3 * LW), w_out_attn], axis=1)
     packed_z = [packed] + [over_z(packed, d) for d in range(1, E)]
-    packed_all = [packed_z] + [[over_r(part, c) for part in packed_z] for c in range(1, R)]
+    packed_r = [over_r(packed, c) for c in range(1, R)]
+    packed_rest = [over_r(jnp.stack(packed_z[1:]), c) for c in range(1, R)]
+    packed_all = [packed_z] + [
+        [first, *(rest[d] for d in range(E - 1))] for first, rest in zip(packed_r, packed_rest)
+    ]
 
     both_parts = gather_t(jnp.concatenate([tokens, cotangent], axis=1))
     token_parts = [part[..., :D] for part in both_parts]
@@ -416,10 +431,13 @@
         return jnp.concatenate(deliver_z(rows.reshape(E, SUB, D)), axis=0)
 
     grad_output = mm(to_slots[:ROWS], cotangent_all, 1, 0)
-    cotangent_z = dispatch_z(grad_output)
-    in_parts = deliver_z(jnp.stack([pick(after(w_in, cotangent_z), z ^ d, 1) for d in range(E)]))
-    out_parts = deliver_z(jnp.stack([pick(after(w_out, in_parts), z ^ d, 1) for d in range(E)]))
-    in_columns, out_columns = jnp.stack(in_parts), jnp.stack(out_parts)
+    masked = jnp.where(sent_own[:, None], grad_output, 0).astype(BF).reshape(E, SUB, D)
+    in_rows = after(w_in, packed_z, packed_r, both_parts)
+    in_columns = jnp.stack(deliver_z(jnp.stack([pick(in_rows, z ^ d, 1) for d in range(E)])))
+    out_rows = after(w_out, in_columns)
+    out_rows = jnp.stack([pick(out_rows, z ^ d, 1) for d in range(E)])
+    out_z = jnp.stack(deliver_z(jnp.concatenate([out_rows, masked], axis=1)))
+    out_columns, cotangent_z = out_z[:, :local], out_z[:, local:].reshape(E * SUB, D)
     in_weight = whole([in_columns] + [over_r(in_columns, c) for c in range(1, R)])
     out_weight = whole([out_columns] + [over_r(out_columns, c) for c in range(1, R)])
     cotangent_parts = gather_t(cotangent_z)
@@ -432,7 +450,7 @@
         precision=HIGHEST_PRECISION,
     )
     packed_refs = whole(packed_all)
-    normed_all, qkv, probs, heads_all, kept, given, tokens_all, attention_weight = call(
+    forward = call(
         functools.partial(attention_forward, pieces=len(packed_refs)),
         "attention_forward",
         12,
@@ -451,16 +469,19 @@
         *token_parts,
         gain_one,
         reversed_rel,
-        after(to_slots, cotangent_z),
+        to_slots,
         *packed_refs,
     )
-    attended = scatter_t(kept, after(given, in_columns, cotangent_parts[1]))
+    normed_all, qkv, probs, heads_all, kept, given, tokens_all, attention_weight = after(
+        forward, in_columns
+    )
+    attended = scatter_t(kept, given)
     inputs = mm(to_slots[:ROWS], tokens_all, 1, 0)
     middle = inputs + attended
     scale_two = norm_scale(middle)
     normed_two = (middle * scale_two * gain_two).astype(BF)
 
-    buffer_parts = gather_t(dispatch_z(after(normed_two, out_columns, in_weight)))
+    buffer_parts = gather_t(dispatch_z(after(normed_two, out_z, in_weight)))
     router = jnp.pad(router_rows.T, ((0, 0), (0, 128 - E)))
     buffer, grad_expert, activation, grad_pre, kept, given = call(
         functools.partial(expert_layer, pieces=len(in_weight)),
@@ -483,6 +504,7 @@
         *out_weight,
     )
 
+
     def expert_gradient(name, left, right):
         (out,) = call(
             weight_gradient,
@@ -500,10 +522,10 @@
     in_terms = expert_gradient("grad_w_in", buffer, grad_pre)
     mine = scatter_t(kept, given).astype(BF)
     out_sums = swap_r(out_terms).astype(BF)
-    returned = jnp.concatenate(deliver_z(mine.reshape(E, SUB, 2 * D)), axis=0).astype(F32)
+    in_sums = swap_r(after(in_terms, out_sums, mine)).astype(BF)
+    returned = deliver_z(after(mine, out_sums).reshape(E, SUB, 2 * D))
+    returned = jnp.concatenate(returned, axis=0).astype(F32)
     combined, grad_normed_two = returned[:, :D], returned[:, D:]
-    in_sums = swap_r(after(in_terms, out_sums)).astype(BF)
-    out_delivered = deliver_z(after(out_sums, returned))
 
     experts = jnp.arange(E, dtype=jnp.int32)[None, :]
     route = jax.nn.softmax(mm(normed_two, router_rows, 1, 1), axis=-1)
@@ -523,7 +545,7 @@
     )
     grad_gain_two = jnp.sum(grad_normed_two * middle * scale_two, axis=0, keepdims=True)
     grad_middle = (grad_output + norm_back(grad_normed_two, middle, scale_two, gain_two)).astype(BF)
-    grad_parts = gather_t(after(grad_middle, out_sums))
+    grad_parts = gather_t(after(grad_middle, in_sums))
     layer_parts = gather_t(after(layer_rows, grad_parts))
 
     late_terms, kept, given, grad_gain_one, grad_rel = call(
@@ -546,7 +568,7 @@
         ],
         place_at,
         *grad_parts,
-        after(to_slots, in_sums),
+        to_slots,
         attention_weight,
         tokens_all,
         normed_all,
@@ -554,11 +576,14 @@
         probs,
         heads_all,
     )
-    in_delivered = deliver_z(after(in_sums, out_delivered, grad_parts))
-    late_terms, kept, given, grad_gain_one, grad_rel = after(
-        (late_terms, kept, given, grad_gain_one, grad_rel), in_delivered, layer_parts[1]
-    )
-    late_sums = swap_r(blocks_to_send(late_terms)).astype(BF)
+    expert_sums = jnp.stack([in_sums, out_sums], axis=1)
+    delivered = deliver_z(after(expert_sums, grad_middle))
+    late_terms, kept, given, grad_gain_one, grad_rel, delivered = after(
+        (late_terms, kept, given, grad_gain_one, grad_rel, delivered), layer_parts[1]
+    )
+    late_terms = blocks_to_send(late_terms)
+    far_sums = swap_r(late_terms[:, 2:]).astype(BF)
+    near_sums = swap_r(after(late_terms[:, :2], far_sums)).astype(BF)
     grad_normed_one = scatter_t(kept, given)
     own_inputs = tokens.astype(F32)
     grad_slots = jnp.concatenate(in_order(grad_parts), axis=0)
@@ -587,10 +612,11 @@
             ],
             axis=0,
         ),
-        late_sums,
-    )
-    late_parts = deliver_z(late_sums)
-    late = sum(part.astype(F32) for part in late_parts)
+        far_sums,
+    )
+    late = near_sums[0].astype(F32)
+    for d, part in ((2, far_sums[0]), (3, far_sums[1]), (1, near_sums[1])):
+        late = late + over_z(part, d).astype(F32)
     small_own = lax.dynamic_slice_in_dim(small[: E + 2], at_dp * local, local, 1)
     table_own = lax.dynamic_slice_in_dim(small[E + 2], at_dp * (H * NB // n), H * NB // n, 0)
     return (
@@ -599,8 +625,8 @@
         late[:, : 3 * LW].reshape(local, 3, LW),
         late[:, 3 * LW :],
         small_own[:E].T,
-        jnp.stack(natural(in_delivered, z), axis=1).astype(F32),
-        jnp.stack(natural(out_delivered, z), axis=1).astype(F32),
+        jnp.stack(natural([part[0] for part in delivered], z), axis=1).astype(F32),
+        jnp.stack(natural([part[1] for part in delivered], z), axis=1).astype(F32),
         small_own[E + 1],
         small_own[E],
         table_own,

time: 248 us -> 220 us (0.89)
  blocking collectives: 30.6 us -> 0 us
  waiting for transfers between devices: 76.1 us -> 84.1 us
    all_gather x1 -> x0, blocking collectives: 30.6 us -> none  [body(): lines = lax.all_gather(line, 'dp', axis=0, tiled=True)]
    ppermute x18, waiting for transfers between devices: 4.99 us -> 14 us  [over_t(): return lax.ppermute(x, 'tensor', [(i, i ^ k) for i in range(T)])]
    ppermute x10, waiting for transfers between devices: 43.2 us -> 34.8 us  [over_r(): lax.ppermute(x, 'dp', [(i, i // r * r + (i % r ^ c)) for i in range(n)])]
    ppermute x29 -> x25, waiting for transfers between devices: 27.9 us -> 35.3 us  [over_z(): lax.ppermute(x, 'dp', [(i, (i // r ^ d) * r + i % r) for i in range(n)])]
    unnamed x91 -> x93, local copies, waits for them, and re-layouts: 14.8 us -> 12.3 us
    ppermute x29 -> x25, starting transfers between devices: 44.1 us -> 42.8 us  [over_z(): lax.ppermute(x, 'dp', [(i, (i // r ^ d) * r + i % r) for i in range(n)])]
  transfers between devices with their start and end apart: 57 -> 53, of which waited for: 19 -> 26; matrix products, arithmetic and copies ran while one was open for 12% -> 14% of each run, Pallas kernels for 9% -> 10%
where the time goes in v1:
time: 220 us; the launch traced here: 219 us
  waiting for transfers between devices  84.1 us (38%)
  starting transfers between devices  63.8 us (29%)
  Pallas kernels  27.8 us (13%)
  local copies, waits for them, and re-layouts  23 us (10%)
  other arithmetic  12.4 us (6%)
  matrix products  5.51 us (3%)
  between operations  2.34 us (1%)
    ppermute x25, starting transfers between devices, over_z(): lax.ppermute(x, 'dp', [(i, (i // r ^ d) * r + i % r) for i in range(n)])  42.8 us
    ppermute x25, waiting for transfers between devices, over_z(): lax.ppermute(x, 'dp', [(i, (i // r ^ d) * r + i % r) for i in range(n)])  35.3 us
    ppermute x10, waiting for transfers between devices, over_r(): lax.ppermute(x, 'dp', [(i, i // r * r + (i % r ^ c)) for i in range(n)])  34.8 us
    pallas_call x5, Pallas kernels, call(): pl.pallas_call(kernel, out_shape=[jax.ShapeDtypeStruct(shape, kind) for s...  27.8 us
    ppermute x18, waiting for transfers between devices, over_t(): return lax.ppermute(x, 'tensor', [(i, i ^ k) for i in range(T)])  14 us
    unnamed x93, local copies, waits for them, and re-layouts  12.3 us
    ppermute x10, starting transfers between devices, over_r(): lax.ppermute(x, 'dp', [(i, i // r * r + (i % r ^ c)) for i in range(n)])  11.2 us
    ppermute x18, starting transfers between devices, over_t(): return lax.ppermute(x, 'tensor', [(i, i ^ k) for i in range(T)])  9.86 us
  transfers between devices with their start and end apart: 53, of which 26 were waited for; matrix products, arithmetic and copies ran while one was open for 14% of the time, Pallas kernels for 10%

profile of v1, /device:TPU:0, one launch (start us, length us, event | category | flops | bytes accessed | tf_op | source)
XLA Modules:
  0.0 218.9 jit_solution(14301259730169642440)
XLA Ops:
  1.9 1.5 pad_maximum_fusion.13
  3.5 2.9 %collective-permute-start.8 = (bf16[96,768]{1,0:T(8,128)(2,1)}, bf16[96,768]{1,0:T(8,128)(2,1)}, u32[]{:S(2)}, u32[]{:S(2)}) collective-permute-start(bf16[96,768]{1,0:T(8,128)(2,1)} %pad_maximum_fusion.13), channel_id=1, source_target_pairs={{0,4},{4,0},{8,12},{12,8},{16,20},{20,16},{24,28},{28,24},{1,5},{5... | collective-permute-start | bytes 442376 | tf_op jit(solution)/shard_map/ppermute | solution.py:49
  6.4 3.6 %collective-permute-start.7 = (bf16[96,768]{1,0:T(8,128)(2,1)}, bf16[96,768]{1,0:T(8,128)(2,1)S(1)}, u32[]{:S(2)}, u32[]{:S(2)}) collective-permute-start(bf16[96,768]{1,0:T(8,128)(2,1)} %pad_maximum_fusion.13), channel_id=1, source_target_pairs={{0,24},{4,28},{8,16},{12,20},{16,8},{20,12},{24,0},{28,4},{1,25},{... | collective-permute-start | bytes 442376 | tf_op jit(solution)/shard_map/ppermute | solution.py:43
  14.1 1.6 collective-permute-start
  20.4 1.6 collective-permute-done.3
  22.6 1.6 collective-permute-done
  24.1 2.6 %collective-permute-start.4 = (bf16[4,640]{1,0:T(4,128)(2,1)S(1)}, bf16[4,640]{1,0:T(4,128)(2,1)S(1)}, u32[]{:S(2)}, u32[]{:S(2)}) collective-permute-start(bf16[4,640]{1,0:T(4,128)(2,1)S(1)} %pad_maximum_fusion.15), channel_id=1, source_target_pairs={{0,16},{4,20},{8,24},{12,28},{16,0},{20,4},{24,8},{28,12},{1,17},{... | collective-permute-start | bytes 15368 | tf_op jit(solution)/shard_map/ppermute | solution.py:43
  26.9 1.8 collective-permute-done.4
  29.5 1.5 collective-permute-start.9
  32.6 9.8 %collective-permute-done.9 = bf16[3,96,768]{2,1,0:T(8,128)(2,1)} collective-permute-done((bf16[3,96,768]{2,1,0:T(8,128)(2,1)}, bf16[3,96,768]{2,1,0:T(8,128)(2,1)}, u32[]{:S(2)}, u32[]{:S(2)}) %collective-permute-start.9) | collective-permute-done | bytes 442400 | tf_op jit(solution)/shard_map/ppermute | solution.py:49
  43.7 2.2 collective-permute-start.12
  46.6 1.5 collective-permute-start.10
  49.1 8.0 %attention_forward.1 = (bf16[512,768]{1,0:T(8,128)(2,1)S(1)}, bf16[512,576]{1,0:T(8,128)(2,1)S(1)}, f32[3,512,512]{2,1,0:T(8,128)}, bf16[512,192]{1,0:T(8,128)(2...) custom-call(s32[4]{0:T(128)S(1)} %pad_add_fusion.at_ref, ...), custom_call_target="tpu_custom_call" | custom-call | flops 12000000000 | bytes 2505728 | tf_op jit(solution)/shard_map/attention_forward/pallas_call | solution.py:128
  59.7 1.6 collective-permute-start.18
  61.6 2.7 %collective-permute-start.17 = (bf16[128,768]{1,0:T(8,128)(2,1)S(1)}, bf16[128,768]{1,0:T(8,128)(2,1)S(1)}, u32[]{:S(2)}, u32[]{:S(2)}) collective-permute-start(bf16[128,768]{1,0:T(8,128)(2,1)S(1)} %get-tuple-element.160), channel_id=1, source_target_pairs={{0,24},{4,28},{8,16},{12,20},{16,8},{20,12},{24,0},{28,4},{1,25},{... | collective-permute-start | bytes 589832 | tf_op jit(solution)/shard_map/ppermute | solution.py:43
  64.3 1.7 collective-permute-start.15
  66.2 1.6 collective-permute-start.14
  68.0 3.3 %collective-permute-done.17 = bf16[128,768]{1,0:T(8,128)(2,1)S(1)} collective-permute-done((bf16[128,768]{1,0:T(8,128)(2,1)S(1)}, bf16[128,768]{1,0:T(8,128)(2,1)S(1)}, u32[]{:S(2)}, u32[]{:S(2)}) %collective-permute-start.17) | collective-permute-done | bytes 196640 | tf_op jit(solution)/shard_map/ppermute | solution.py:43
  71.3 9.5 %collective-permute-done.16 = bf16[128,768]{1,0:T(8,128)(2,1)S(1)} collective-permute-done((bf16[128,768]{1,0:T(8,128)(2,1)S(1)}, bf16[128,768]{1,0:T(8,128)(2,1)S(1)}, u32[]{:S(2)}, u32[]{:S(2)}) %collective-permute-start.16) | collective-permute-done | bytes 196640 | tf_op jit(solution)/shard_map/ppermute | solution.py:43
  81.4 2.3 %collective-permute-start.21 = (bf16[32,768]{1,0:T(8,128)(2,1)S(1)}, bf16[32,768]{1,0:T(8,128)(2,1)S(1)}, u32[]{:S(2)}, u32[]{:S(2)}) collective-permute-start(bf16[32,768]{1,0:T(8,128)(2,1)S(1)} %get-tuple-element.187), channel_id=1, source_target_pairs={{0,24},{4,28},{8,16},{12,20},{16,8},{20,12},{24,0},{28,4},{1,25},{... | collective-permute-start | bytes 147464 | tf_op jit(solution)/shard_map/ppermute | solution.py:43
  83.7 2.2 collective-permute-start.19
  85.9 1.5 collective-permute-start.24
  88.8 1.6 collective-permute-start.22
  93.3 2.6 %collective-permute-done.22.far_ref = bf16[128,768]{1,0:T(8,128)(2,1)S(1)} collective-permute-done((bf16[128,768]{1,0:T(8,128)(2,1)S(1)}, bf16[128,768]{1,0:T(8,128)(2,1)S(1)}, u32[]{:S(2)}, u32[]{:S(2)}) %collective-permute-start.22) | collective-permute-done | bytes 196640 | tf_op jit(solution)/shard_map/ppermute | solution.py:37
  101.5 3.4 %collective-permute-done.26.rest_3_ = bf16[4,96,768]{2,1,0:T(8,128)(2,1)} collective-permute-done((bf16[4,96,768]{2,1,0:T(8,128)(2,1)S(1)}, bf16[4,96,768]{2,1,0:T(8,128)(2,1)}, u32[]{:S(2)}, u32[]{:S(2)}) %collective-permute-start.26) | collective-permute-done | bytes 589856 | tf_op jit(solution)/shard_map/ppermute | solution.py:49
  105.9 6.7 %expert_layer.1 = (bf16[512,768]{1,0:T(8,128)(2,1)S(1)}, bf16[512,768]{1,0:T(8,128)(2,1)S(1)}, bf16[512,768]{1,0:T(8,128)(2,1)}, bf16[512,768]{1,0:T(8,128)(2,1)...) custom-call(s32[4]{0:T(128)S(1)} %pad_add_fusion.at_ref, ...), custom_call_target="tpu_custom_call" | custom-call | flops 8000000000 | bytes 4128768 | tf_op jit(solution)/shard_map/expert_layer/pallas_call | solution.py:128
  114.1 1.5 grad_w_out.1
  117.4 1.5 grad_w_in.1
  118.9 12.6 %collective-permute-done.29 = bf16[4,96,768]{2,1,0:T(8,128)(2,1)S(1)} collective-permute-done((bf16[4,96,768]{2,1,0:T(8,128)(2,1)S(1)}, bf16[4,96,768]{2,1,0:T(8,128)(2,1)S(1)}, u32[]{:S(2)}, u32[]{:S(2)}) %collective-permute-start.29) | collective-permute-done | bytes 589856 | tf_op jit(solution)/shard_map/ppermute | solution.py:49
  131.8 2.1 collective-permute-start.32
  133.9 2.3 %collective-permute-start.30 = (bf16[32,1536]{1,0:T(8,128)(2,1)S(1)}, bf16[32,1536]{1,0:T(8,128)(2,1)S(1)}, u32[]{:S(2)}, u32[]{:S(2)}) collective-permute-start(bf16[32,1536]{1,0:T(8,128)(2,1)S(1)} %get-tuple-element.180), channel_id=1, source_target_pairs={{0,8},{4,12},{8,0},{12,4},{16,24},{20,28},{24,16},{28,20},{1,9},{5... | collective-permute-start | bytes 294920 | tf_op jit(solution)/shard_map/ppermute | solution.py:43
  136.9 2.5 %collective-permute-done.32 = bf16[32,1536]{1,0:T(8,128)(2,1)S(1)} collective-permute-done((bf16[32,1536]{1,0:T(8,128)(2,1)S(1)}, bf16[32,1536]{1,0:T(8,128)(2,1)S(1)}, u32[]{:S(2)}, u32[]{:S(2)}) %collective-permute-start.32) | collective-permute-done | bytes 98336 | tf_op jit(solution)/shard_map/ppermute | solution.py:43
  139.4 3.4 %collective-permute-done.31 = bf16[32,1536]{1,0:T(8,128)(2,1)S(1)} collective-permute-done((bf16[32,1536]{1,0:T(8,128)(2,1)S(1)}, bf16[32,1536]{1,0:T(8,128)(2,1)S(1)}, u32[]{:S(2)}, u32[]{:S(2)}) %collective-permute-start.31) | collective-permute-done | bytes 98336 | tf_op jit(solution)/shard_map/ppermute | solution.py:43
  143.7 6.8 %collective-permute-done.33 = bf16[4,96,768]{2,1,0:T(8,128)(2,1)S(1)} collective-permute-done((bf16[4,96,768]{2,1,0:T(8,128)(2,1)S(1)}, bf16[4,96,768]{2,1,0:T(8,128)(2,1)S(1)}, u32[]{:S(2)}, u32[]{:S(2)}) %collective-permute-start.33) | collective-permute-done | bytes 589856 | tf_op jit(solution)/shard_map/ppermute | solution.py:49
  151.5 4.8 %collective-permute-done.34.far_ref = bf16[128,768]{1,0:T(8,128)(2,1)S(1)} collective-permute-done((bf16[128,768]{1,0:T(8,128)(2,1)S(1)}, bf16[128,768]{1,0:T(8,128)(2,1)S(1)}, u32[]{:S(2)}, u32[]{:S(2)}) %collective-permute-start.34) | collective-permute-done | bytes 196640 | tf_op jit(solution)/shard_map/ppermute | solution.py:37
  157.5 1.7 collective-permute-start.38
  159.3 1.8 collective-permute-start.40
  161.6 10.1 %attention_backward.1 = (bf16[2,4,96,768]{3,2,1,0:T(8,128)(2,1)S(1)}, bf16[2,128,768]{2,1,0:T(8,128)(2,1)S(1)}, bf16[2,128,768]{2,1,0:T(8,128)(2,1)S(1)}, f32[1,768]{1,0:T(1,128)S(1)}, f32[3,1024]{1,0:T(4,128)S(1)}) custom-call(s32[4]{0:T(128)S(1)} %pad_add_fusion.at_ref, bf16[128,768]{1,0:T(8,128)(2,1)S(1)} %add_convert_fusion.own_ref, ...), custom_call_target="tpu_custom_call" | custom-call | flops 12000000000 | bytes 7995392 | tf_op jit(solution)/shard_map/attention_backward/pallas_call | solution.py:128
  173.4 6.0 %collective-permute-done.40 = bf16[2,96,768]{2,1,0:T(8,128)(2,1)S(1)} collective-permute-done((bf16[2,96,768]{2,1,0:T(8,128)(2,1)S(1)}, bf16[2,96,768]{2,1,0:T(8,128)(2,1)S(1)}, u32[]{:S(2)}, u32[]{:S(2)}) %collective-permute-start.40) | collective-permute-done | bytes 294944 | tf_op jit(solution)/shard_map/ppermute | solution.py:43
  184.1 1.8 collective-permute-done.49
  185.9 6.7 %collective-permute-start.50 = (f32[8,768]{1,0:T(8,128)S(1)}, f32[8,768]{1,0:T(8,128)S(1)}, u32[]{:S(2)}, u32[]{:S(2)}) collective-permute-start(f32[8,768]{1,0:T(8,128)S(1)} %add.215), channel_id=1, source_target_pairs={{0,8},{4,12},{8,0},{12,4},{16,24},{20,28},{24,16},{28,20},{1,9},{5... | collective-permute-start | bytes 73736 | tf_op jit(solution)/shard_map/ppermute | solution.py:43
  192.7 1.7 collective-permute-done.50
  194.4 2.6 %collective-permute-start.51 = (f32[8,768]{1,0:T(8,128)S(1)}, f32[8,768]{1,0:T(8,128)S(1)}, u32[]{:S(2)}, u32[]{:S(2)}) collective-permute-start(f32[8,768]{1,0:T(8,128)S(1)} %add.216), channel_id=1, source_target_pairs={{0,16},{4,20},{8,24},{12,28},{16,0},{20,4},{24,8},{28,12},{1,17},{... | collective-permute-start | bytes 73736 | tf_op jit(solution)/shard_map/ppermute | solution.py:43
  197.2 1.8 copy.66
  199.0 1.8 copy.65
  203.2 1.7 collective-permute-start.46
  209.7 2.0 collective-permute-done.44
  215.1 2.0 collective-permute-done.47
  (285 shorter events, 56.3 us)
Async XLA Ops:
  3.5 29.1 %collective-permute-start.8 = (bf16[96,768]{1,0:T(8,128)(2,1)}, bf16[96,768]{1,0:T(8,128)(2,1)}, u32[]{:S(2)}, u32[]{:S(2)}) collective-permute-start(bf16[96,768]{1,0:T(8,128)(2,1)} %pad_maximum_fusion.13), channel_id=1, source_target_pairs={{0,4},{4,0},{8,12},{12,8},{16,20},{20,16},{24,28},{28,24},{1,5},{5... | collective-permute-start | bytes 442376 | tf_op jit(solution)/shard_map/ppermute | solution.py:49
  6.4 22.3 %collective-permute-start.7 = (bf16[96,768]{1,0:T(8,128)(2,1)}, bf16[96,768]{1,0:T(8,128)(2,1)S(1)}, u32[]{:S(2)}, u32[]{:S(2)}) collective-permute-start(bf16[96,768]{1,0:T(8,128)(2,1)} %pad_maximum_fusion.13), channel_id=1, source_target_pairs={{0,24},{4,28},{8,16},{12,20},{16,8},{20,12},{24,0},{28,4},{1,25},{... | collective-permute-start | bytes 442376 | tf_op jit(solution)/shard_map/ppermute | solution.py:43
  10.0 18.7 %collective-permute-start.6 = (bf16[96,768]{1,0:T(8,128)(2,1)}, bf16[96,768]{1,0:T(8,128)(2,1)S(1)}, u32[]{:S(2)}, u32[]{:S(2)}) collective-permute-start(bf16[96,768]{1,0:T(8,128)(2,1)} %pad_maximum_fusion.13), channel_id=1, source_target_pairs={{0,16},{4,20},{8,24},{12,28},{16,0},{20,4},{24,8},{28,12},{1,17},{... | collective-permute-start | bytes 442376 | tf_op jit(solution)/shard_map/ppermute | solution.py:43
  11.6 6.5 %collective-permute-start.2 = (bf16[1,640]{1,0:T(2,128)(2,1)S(1)}, bf16[1,640]{1,0:T(2,128)(2,1)S(1)}, u32[]{:S(2)}, u32[]{:S(2)}) collective-permute-start(bf16[1,640]{1,0:T(2,128)(2,1)S(1)} %broadcast_in_dim.61), channel_id=1, source_target_pairs={{0,4},{4,0},{8,12},{12,8},{16,20},{20,16},{24,28},{28,24},{1,5},{5... | collective-permute-start | bytes 3848 | tf_op jit(solution)/shard_map/ppermute | solution.py:49
  14.1 10.1 %collective-permute-start = (bf16[128,1536]{1,0:T(8,128)(2,1)S(1)}, bf16[128,1536]{1,0:T(8,128)(2,1)S(1)}, u32[]{:S(2)}, u32[]{:S(2)}) collective-permute-start(bf16[128,1536]{1,0:T(8,128)(2,1)S(1)} %constant_dynamic-update-slice_fusion), channel_id=1, source_target_pairs={{0,2},{1,3},{2,0},{3,1},{4,6},{5,7},{6,4},{7,5},{8,10},{9,11},{10,... | collective-permute-start | bytes 1179656 | tf_op jit(solution)/shard_map/ppermute | solution.py:37
  22.0 6.7 %collective-permute-start.5 = (bf16[96,768]{1,0:T(8,128)(2,1)}, bf16[96,768]{1,0:T(8,128)(2,1)S(1)}, u32[]{:S(2)}, u32[]{:S(2)}) collective-permute-start(bf16[96,768]{1,0:T(8,128)(2,1)} %pad_maximum_fusion.13), channel_id=1, source_target_pairs={{0,8},{4,12},{8,0},{12,4},{16,24},{20,28},{24,16},{28,20},{1,9},{5... | collective-permute-start | bytes 442376 | tf_op jit(solution)/shard_map/ppermute | solution.py:43
  24.1 4.5 %collective-permute-start.4 = (bf16[4,640]{1,0:T(4,128)(2,1)S(1)}, bf16[4,640]{1,0:T(4,128)(2,1)S(1)}, u32[]{:S(2)}, u32[]{:S(2)}) collective-permute-start(bf16[4,640]{1,0:T(4,128)(2,1)S(1)} %pad_maximum_fusion.15), channel_id=1, source_target_pairs={{0,16},{4,20},{8,24},{12,28},{16,0},{20,4},{24,8},{28,12},{1,17},{... | collective-permute-start | bytes 15368 | tf_op jit(solution)/shard_map/ppermute | solution.py:43
  28.7 14.9 %collective-permute-start.1 = (bf16[2,128,1536]{2,1,0:T(8,128)(2,1)S(1)}, bf16[2,128,1536]{2,1,0:T(8,128)(2,1)S(1)}, u32[]{:S(2)}, u32[]{:S(2)}) collective-permute-start(bf16[2,128,1536]{2,1,0:T(8,128)(2,1)S(1)} %pad_maximum_fusion.1), channel_id=1, source_target_pairs={{0,1},{1,0},{2,3},{3,2},{4,5},{5,4},{6,7},{7,6},{8,9},{9,8},{10,11... | collective-permute-start | bytes 2359304 | tf_op jit(solution)/shard_map/ppermute | solution.py:37
  29.5 12.9 %collective-permute-start.9 = (bf16[3,96,768]{2,1,0:T(8,128)(2,1)}, bf16[3,96,768]{2,1,0:T(8,128)(2,1)}, u32[]{:S(2)}, u32[]{:S(2)}) collective-permute-start(bf16[3,96,768]{2,1,0:T(8,128)(2,1)} %pad_maximum_fusion.7), channel_id=1, source_target_pairs={{0,4},{4,0},{8,12},{12,8},{16,20},{20,16},{24,28},{28,24},{1,5},{5... | collective-permute-start | bytes 1327112 | tf_op jit(solution)/shard_map/ppermute | solution.py:49
  43.7 14.8 %collective-permute-start.12 = (bf16[96,768]{1,0:T(8,128)(2,1)S(1)}, bf16[96,768]{1,0:T(8,128)(2,1)S(1)}, u32[]{:S(2)}, u32[]{:S(2)}) collective-permute-start(bf16[96,768]{1,0:T(8,128)(2,1)S(1)} %get-tuple-element.170), channel_id=1, source_target_pairs={{0,24},{4,28},{8,16},{12,20},{16,8},{20,12},{24,0},{28,4},{1,25},{... | collective-permute-start | bytes 442376 | tf_op jit(solution)/shard_map/ppermute | solution.py:43
  45.9 13.8 %collective-permute-start.11 = (bf16[96,768]{1,0:T(8,128)(2,1)S(1)}, bf16[96,768]{1,0:T(8,128)(2,1)S(1)}, u32[]{:S(2)}, u32[]{:S(2)}) collective-permute-start(bf16[96,768]{1,0:T(8,128)(2,1)S(1)} %get-tuple-element.171), channel_id=1, source_target_pairs={{0,16},{4,20},{8,24},{12,28},{16,0},{20,4},{24,8},{28,12},{1,17},{... | collective-permute-start | bytes 442376 | tf_op jit(solution)/shard_map/ppermute | solution.py:43
  46.6 13.0 %collective-permute-start.10 = (bf16[96,768]{1,0:T(8,128)(2,1)S(1)}, bf16[96,768]{1,0:T(8,128)(2,1)S(1)}, u32[]{:S(2)}, u32[]{:S(2)}) collective-permute-start(bf16[96,768]{1,0:T(8,128)(2,1)S(1)} %get-tuple-element.172), channel_id=1, source_target_pairs={{0,8},{4,12},{8,0},{12,4},{16,24},{20,28},{24,16},{28,20},{1,9},{5... | collective-permute-start | bytes 442376 | tf_op jit(solution)/shard_map/ppermute | solution.py:43
  59.7 21.6 %collective-permute-start.18 = (bf16[4,96,768]{2,1,0:T(8,128)(2,1)S(1)}, bf16[4,96,768]{2,1,0:T(8,128)(2,1)S(1)}, u32[]{:S(2)}, u32[]{:S(2)}) collective-permute-start(bf16[4,96,768]{2,1,0:T(8,128)(2,1)S(1)} %pad_maximum_fusion.6.rest_0_), channel_id=1, source_target_pairs={{0,4},{4,0},{8,12},{12,8},{16,20},{20,16},{24,28},{28,24},{1,5},{5... | collective-permute-start | bytes 1769480 | tf_op jit(solution)/shard_map/ppermute | solution.py:49
  61.3 4.7 %collective-permute-start.13 = (bf16[2,128,768]{2,1,0:T(8,128)(2,1)S(1)}, bf16[2,128,768]{2,1,0:T(8,128)(2,1)S(1)}, u32[]{:S(2)}, u32[]{:S(2)}) collective-permute-start(bf16[2,128,768]{2,1,0:T(8,128)(2,1)S(1)} %get-tuple-element.67), channel_id=1, source_target_pairs={{0,1},{1,0},{2,3},{3,2},{4,5},{5,4},{6,7},{7,6},{8,9},{9,8},{10,11... | collective-permute-start | bytes 1179656 | tf_op jit(solution)/shard_map/ppermute | solution.py:37
  61.6 9.7 %collective-permute-start.17 = (bf16[128,768]{1,0:T(8,128)(2,1)S(1)}, bf16[128,768]{1,0:T(8,128)(2,1)S(1)}, u32[]{:S(2)}, u32[]{:S(2)}) collective-permute-start(bf16[128,768]{1,0:T(8,128)(2,1)S(1)} %get-tuple-element.160), channel_id=1, source_target_pairs={{0,24},{4,28},{8,16},{12,20},{16,8},{20,12},{24,0},{28,4},{1,25},{... | collective-permute-start | bytes 589832 | tf_op jit(solution)/shard_map/ppermute | solution.py:43
  64.3 16.5 %collective-permute-start.16 = (bf16[128,768]{1,0:T(8,128)(2,1)S(1)}, bf16[128,768]{1,0:T(8,128)(2,1)S(1)}, u32[]{:S(2)}, u32[]{:S(2)}) collective-permute-start(bf16[128,768]{1,0:T(8,128)(2,1)S(1)} %get-tuple-element.161), channel_id=1, source_target_pairs={{0,16},{4,20},{8,24},{12,28},{16,0},{20,4},{24,8},{28,12},{1,17},{... | collective-permute-start | bytes 589832 | tf_op jit(solution)/shard_map/ppermute | solution.py:43
  64.3 16.5 %collective-permute-start.15 = (bf16[128,768]{1,0:T(8,128)(2,1)S(1)}, bf16[128,768]{1,0:T(8,128)(2,1)S(1)}, u32[]{:S(2)}, u32[]{:S(2)}) collective-permute-start(bf16[128,768]{1,0:T(8,128)(2,1)S(1)} %get-tuple-element.162), channel_id=1, source_target_pairs={{0,8},{4,12},{8,0},{12,4},{16,24},{20,28},{24,16},{28,20},{1,9},{5... | collective-permute-start | bytes 589832 | tf_op jit(solution)/shard_map/ppermute | solution.py:43
  66.2 14.8 %collective-permute-start.14 = (bf16[128,768]{1,0:T(8,128)(2,1)S(1)}, bf16[128,768]{1,0:T(8,128)(2,1)S(1)}, u32[]{:S(2)}, u32[]{:S(2)}) collective-permute-start(bf16[128,768]{1,0:T(8,128)(2,1)S(1)} %fusion.48), channel_id=1, source_target_pairs={{0,2},{1,3},{2,0},{3,1},{4,6},{5,7},{6,4},{7,5},{8,10},{9,11},{10,... | collective-permute-start | bytes 589832 | tf_op jit(solution)/shard_map/ppermute | solution.py:37
  81.4 6.1 %collective-permute-start.21 = (bf16[32,768]{1,0:T(8,128)(2,1)S(1)}, bf16[32,768]{1,0:T(8,128)(2,1)S(1)}, u32[]{:S(2)}, u32[]{:S(2)}) collective-permute-start(bf16[32,768]{1,0:T(8,128)(2,1)S(1)} %get-tuple-element.187), channel_id=1, source_target_pairs={{0,24},{4,28},{8,16},{12,20},{16,8},{20,12},{24,0},{28,4},{1,25},{... | collective-permute-start | bytes 147464 | tf_op jit(solution)/shard_map/ppermute | solution.py:43
  83.7 5.0 %collective-permute-start.20 = (bf16[32,768]{1,0:T(8,128)(2,1)S(1)}, bf16[32,768]{1,0:T(8,128)(2,1)S(1)}, u32[]{:S(2)}, u32[]{:S(2)}) collective-permute-start(bf16[32,768]{1,0:T(8,128)(2,1)S(1)} %get-tuple-element.188), channel_id=1, source_target_pairs={{0,16},{4,20},{8,24},{12,28},{16,0},{20,4},{24,8},{28,12},{1,17},{... | collective-permute-start | bytes 147464 | tf_op jit(solution)/shard_map/ppermute | solution.py:43
  83.7 5.0 %collective-permute-start.19 = (bf16[32,768]{1,0:T(8,128)(2,1)S(1)}, bf16[32,768]{1,0:T(8,128)(2,1)S(1)}, u32[]{:S(2)}, u32[]{:S(2)}) collective-permute-start(bf16[32,768]{1,0:T(8,128)(2,1)S(1)} %get-tuple-element.189), channel_id=1, source_target_pairs={{0,8},{4,12},{8,0},{12,4},{16,24},{20,28},{24,16},{28,20},{1,9},{5... | collective-permute-start | bytes 147464 | tf_op jit(solution)/shard_map/ppermute | solution.py:43
  85.9 6.6 %collective-permute-start.24 = (bf16[128,768]{1,0:T(8,128)(2,1)S(1)}, bf16[128,768]{1,0:T(8,128)(2,1)S(1)}, u32[]{:S(2)}, u32[]{:S(2)}) collective-permute-start(bf16[128,768]{1,0:T(8,128)(2,1)S(1)} %bitcast.172), channel_id=1, source_target_pairs={{0,2},{1,3},{2,0},{3,1},{4,6},{5,7},{6,4},{7,5},{8,10},{9,11},{10,... | collective-permute-start | bytes 589832 | tf_op jit(solution)/shard_map/ppermute | solution.py:37
  88.8 7.0 %collective-permute-start.22 = (bf16[128,768]{1,0:T(8,128)(2,1)S(1)}, bf16[128,768]{1,0:T(8,128)(2,1)S(1)}, u32[]{:S(2)}, u32[]{:S(2)}) collective-permute-start(bf16[128,768]{1,0:T(8,128)(2,1)S(1)} %get-tuple-element.185.own_ref), channel_id=1, source_target_pairs={{0,2},{1,3},{2,0},{3,1},{4,6},{5,7},{6,4},{7,5},{8,10},{9,11},{10,... | collective-permute-start | bytes 589832 | tf_op jit(solution)/shard_map/ppermute | solution.py:37
  90.4 14.4 %collective-permute-start.26 = (bf16[4,96,768]{2,1,0:T(8,128)(2,1)S(1)}, bf16[4,96,768]{2,1,0:T(8,128)(2,1)}, u32[]{:S(2)}, u32[]{:S(2)}) collective-permute-start(bf16[4,96,768]{2,1,0:T(8,128)(2,1)S(1)} %slice.344.rest_2_), channel_id=1, source_target_pairs={{0,4},{4,0},{8,12},{12,8},{16,20},{20,16},{24,28},{28,24},{1,5},{5... | collective-permute-start | bytes 1769480 | tf_op jit(solution)/shard_map/ppermute | solution.py:49
  93.3 8.2 %collective-permute-start.25 = (bf16[2,128,768]{2,1,0:T(8,128)(2,1)}, bf16[2,128,768]{2,1,0:T(8,128)(2,1)}, u32[]{:S(2)}, u32[]{:S(2)}) collective-permute-start(bf16[2,128,768]{2,1,0:T(8,128)(2,1)} %pad_maximum_fusion.9), channel_id=1, source_target_pairs={{0,1},{1,0},{2,3},{3,2},{4,5},{5,4},{6,7},{7,6},{8,9},{9,8},{10,11... | collective-permute-start | bytes 1179656 | tf_op jit(solution)/shard_map/ppermute | solution.py:37
  96.6 8.2 %collective-permute-start.23 = (bf16[2,128,768]{2,1,0:T(8,128)(2,1)}, bf16[2,128,768]{2,1,0:T(8,128)(2,1)}, u32[]{:S(2)}, u32[]{:S(2)}) collective-permute-start(bf16[2,128,768]{2,1,0:T(8,128)(2,1)} %pad_maximum_fusion.8), channel_id=1, source_target_pairs={{0,1},{1,0},{2,3},{3,2},{4,5},{5,4},{6,7},{7,6},{8,9},{9,8},{10,11... | collective-permute-start | bytes 1179656 | tf_op jit(solution)/shard_map/ppermute | solution.py:37
  115.7 15.8 %collective-permute-start.29 = (bf16[4,96,768]{2,1,0:T(8,128)(2,1)S(1)}, bf16[4,96,768]{2,1,0:T(8,128)(2,1)S(1)}, u32[]{:S(2)}, u32[]{:S(2)}) collective-permute-start(bf16[4,96,768]{2,1,0:T(8,128)(2,1)S(1)} %slice_bitcast_fusion), channel_id=1, source_target_pairs={{0,4},{4,0},{8,12},{12,8},{16,20},{20,16},{24,28},{28,24},{1,5},{5... | collective-permute-start | bytes 1769480 | tf_op jit(solution)/shard_map/ppermute | solution.py:49
  116.8 14.8 %collective-permute-start.28 = (bf16[128,1536]{1,0:T(8,128)(2,1)S(1)}, bf16[128,1536]{1,0:T(8,128)(2,1)S(1)}, u32[]{:S(2)}, u32[]{:S(2)}) collective-permute-start(bf16[128,1536]{1,0:T(8,128)(2,1)S(1)} %fusion.37), channel_id=1, source_target_pairs={{0,2},{1,3},{2,0},{3,1},{4,6},{5,7},{6,4},{7,5},{8,10},{9,11},{10,... | collective-permute-start | bytes 1179656 | tf_op jit(solution)/shard_map/ppermute | solution.py:37
  131.8 7.6 %collective-permute-start.32 = (bf16[32,1536]{1,0:T(8,128)(2,1)S(1)}, bf16[32,1536]{1,0:T(8,128)(2,1)S(1)}, u32[]{:S(2)}, u32[]{:S(2)}) collective-permute-start(bf16[32,1536]{1,0:T(8,128)(2,1)S(1)} %get-tuple-element.178), channel_id=1, source_target_pairs={{0,24},{4,28},{8,16},{12,20},{16,8},{20,12},{24,0},{28,4},{1,25},{... | collective-permute-start | bytes 294920 | tf_op jit(solution)/shard_map/ppermute | solution.py:43
  133.9 8.8 %collective-permute-start.31 = (bf16[32,1536]{1,0:T(8,128)(2,1)S(1)}, bf16[32,1536]{1,0:T(8,128)(2,1)S(1)}, u32[]{:S(2)}, u32[]{:S(2)}) collective-permute-start(bf16[32,1536]{1,0:T(8,128)(2,1)S(1)} %get-tuple-element.179), channel_id=1, source_target_pairs={{0,16},{4,20},{8,24},{12,28},{16,0},{20,4},{24,8},{28,12},{1,17},{... | collective-permute-start | bytes 294920 | tf_op jit(solution)/shard_map/ppermute | solution.py:43
  133.9 8.8 %collective-permute-start.30 = (bf16[32,1536]{1,0:T(8,128)(2,1)S(1)}, bf16[32,1536]{1,0:T(8,128)(2,1)S(1)}, u32[]{:S(2)}, u32[]{:S(2)}) collective-permute-start(bf16[32,1536]{1,0:T(8,128)(2,1)S(1)} %get-tuple-element.180), channel_id=1, source_target_pairs={{0,8},{4,12},{8,0},{12,4},{16,24},{20,28},{24,16},{28,20},{1,9},{5... | collective-permute-start | bytes 294920 | tf_op jit(solution)/shard_map/ppermute | solution.py:43
  136.3 14.2 %collective-permute-start.33 = (bf16[4,96,768]{2,1,0:T(8,128)(2,1)S(1)}, bf16[4,96,768]{2,1,0:T(8,128)(2,1)S(1)}, u32[]{:S(2)}, u32[]{:S(2)}) collective-permute-start(bf16[4,96,768]{2,1,0:T(8,128)(2,1)S(1)} %slice_bitcast_fusion.2), channel_id=1, source_target_pairs={{0,4},{4,0},{8,12},{12,8},{16,20},{20,16},{24,28},{28,24},{1,5},{5... | collective-permute-start | bytes 1769480 | tf_op jit(solution)/shard_map/ppermute | solution.py:49
  150.6 5.7 %collective-permute-start.34 = (bf16[128,768]{1,0:T(8,128)(2,1)S(1)}, bf16[128,768]{1,0:T(8,128)(2,1)S(1)}, u32[]{:S(2)}, u32[]{:S(2)}) collective-permute-start(bf16[128,768]{1,0:T(8,128)(2,1)S(1)} %add_convert_fusion.own_ref), channel_id=1, source_target_pairs={{0,2},{1,3},{2,0},{3,1},{4,6},{5,7},{6,4},{7,5},{8,10},{9,11},{10,... | collective-permute-start | bytes 589832 | tf_op jit(solution)/shard_map/ppermute | solution.py:37
  156.4 4.7 %collective-permute-start.35 = (bf16[2,128,768]{2,1,0:T(8,128)(2,1)S(1)}, bf16[2,128,768]{2,1,0:T(8,128)(2,1)S(1)}, u32[]{:S(2)}, u32[]{:S(2)}) collective-permute-start(bf16[2,128,768]{2,1,0:T(8,128)(2,1)S(1)} %pad_maximum_fusion.10), channel_id=1, source_target_pairs={{0,1},{1,0},{2,3},{3,2},{4,5},{5,4},{6,7},{7,6},{8,9},{9,8},{10,11... | collective-permute-start | bytes 1179656 | tf_op jit(solution)/shard_map/ppermute | solution.py:37
  156.5 16.8 %collective-permute-start.39 = (bf16[2,96,768]{2,1,0:T(8,128)(2,1)S(1)}, bf16[2,96,768]{2,1,0:T(8,128)(2,1)S(1)}, u32[]{:S(2)}, u32[]{:S(2)}) collective-permute-start(bf16[2,96,768]{2,1,0:T(8,128)(2,1)S(1)} %get-tuple-element.154), channel_id=1, source_target_pairs={{0,16},{4,20},{8,24},{12,28},{16,0},{20,4},{24,8},{28,12},{1,17},{... | collective-permute-start | bytes 884744 | tf_op jit(solution)/shard_map/ppermute | solution.py:43
  157.5 15.9 %collective-permute-start.38 = (bf16[2,96,768]{2,1,0:T(8,128)(2,1)S(1)}, bf16[2,96,768]{2,1,0:T(8,128)(2,1)S(1)}, u32[]{:S(2)}, u32[]{:S(2)}) collective-permute-start(bf16[2,96,768]{2,1,0:T(8,128)(2,1)S(1)} %get-tuple-element.155), channel_id=1, source_target_pairs={{0,8},{4,12},{8,0},{12,4},{16,24},{20,28},{24,16},{28,20},{1,9},{5... | collective-permute-start | bytes 884744 | tf_op jit(solution)/shard_map/ppermute | solution.py:43
  159.3 20.1 %collective-permute-start.40 = (bf16[2,96,768]{2,1,0:T(8,128)(2,1)S(1)}, bf16[2,96,768]{2,1,0:T(8,128)(2,1)S(1)}, u32[]{:S(2)}, u32[]{:S(2)}) collective-permute-start(bf16[2,96,768]{2,1,0:T(8,128)(2,1)S(1)} %slice_bitcast_fusion.10), channel_id=1, source_target_pairs={{0,24},{4,28},{8,16},{12,20},{16,8},{20,12},{24,0},{28,4},{1,25},{... | collective-permute-start | bytes 884744 | tf_op jit(solution)/shard_map/ppermute | solution.py:43
  161.1 18.3 %collective-permute-start.36 = (bf16[128,768]{1,0:T(8,128)(2,1)S(1)}, bf16[128,768]{1,0:T(8,128)(2,1)S(1)}, u32[]{:S(2)}, u32[]{:S(2)}) collective-permute-start(bf16[128,768]{1,0:T(8,128)(2,1)S(1)} %get-tuple-element.79), channel_id=1, source_target_pairs={{0,2},{1,3},{2,0},{3,1},{4,6},{5,7},{6,4},{7,5},{8,10},{9,11},{10,... | collective-permute-start | bytes 589832 | tf_op jit(solution)/shard_map/ppermute | solution.py:37
  180.9 19.9 %collective-permute-start.43 = (bf16[2,96,768]{2,1,0:T(8,128)(2,1)S(1)}, bf16[2,96,768]{2,1,0:T(8,128)(2,1)S(1)}, u32[]{:S(2)}, u32[]{:S(2)}) collective-permute-start(bf16[2,96,768]{2,1,0:T(8,128)(2,1)S(1)} %slice_bitcast_fusion.9), channel_id=1, source_target_pairs={{0,4},{4,0},{8,12},{12,8},{16,20},{20,16},{24,28},{28,24},{1,5},{5... | collective-permute-start | bytes 884744 | tf_op jit(solution)/shard_map/ppermute | solution.py:49
  183.5 25.1 %collective-permute-start.37 = (bf16[2,128,768]{2,1,0:T(8,128)(2,1)S(1)}, bf16[2,128,768]{2,1,0:T(8,128)(2,1)S(1)}, u32[]{:S(2)}, u32[]{:S(2)}) collective-permute-start(bf16[2,128,768]{2,1,0:T(8,128)(2,1)S(1)} %pad_maximum_fusion.11), channel_id=1, source_target_pairs={{0,1},{1,0},{2,3},{3,2},{4,5},{5,4},{6,7},{7,6},{8,9},{9,8},{10,11... | collective-permute-start | bytes 1179656 | tf_op jit(solution)/shard_map/ppermute | solution.py:37
  183.6 24.3 %collective-permute-start.41 = (bf16[2,128,768]{2,1,0:T(8,128)(2,1)}, bf16[2,128,768]{2,1,0:T(8,128)(2,1)S(1)}, u32[]{:S(2)}, u32[]{:S(2)}) collective-permute-start(bf16[2,128,768]{2,1,0:T(8,128)(2,1)} %copy-done.5), channel_id=1, source_target_pairs={{0,1},{1,0},{2,3},{3,2},{4,5},{5,4},{6,7},{7,6},{8,9},{9,8},{10,11... | collective-permute-start | bytes 1179656 | tf_op jit(solution)/shard_map/ppermute | solution.py:37
  185.9 8.5 %collective-permute-start.50 = (f32[8,768]{1,0:T(8,128)S(1)}, f32[8,768]{1,0:T(8,128)S(1)}, u32[]{:S(2)}, u32[]{:S(2)}) collective-permute-start(f32[8,768]{1,0:T(8,128)S(1)} %add.215), channel_id=1, source_target_pairs={{0,8},{4,12},{8,0},{12,4},{16,24},{20,28},{24,16},{28,20},{1,9},{5... | collective-permute-start | bytes 73736 | tf_op jit(solution)/shard_map/ppermute | solution.py:43
  194.4 6.3 %collective-permute-start.51 = (f32[8,768]{1,0:T(8,128)S(1)}, f32[8,768]{1,0:T(8,128)S(1)}, u32[]{:S(2)}, u32[]{:S(2)}) collective-permute-start(f32[8,768]{1,0:T(8,128)S(1)} %add.216), channel_id=1, source_target_pairs={{0,16},{4,20},{8,24},{12,28},{16,0},{20,4},{24,8},{28,12},{1,17},{... | collective-permute-start | bytes 73736 | tf_op jit(solution)/shard_map/ppermute | solution.py:43
  202.1 13.0 %collective-permute-start.45 = (bf16[96,768]{1,0:T(8,128)(2,1)S(1)}, bf16[96,768]{1,0:T(8,128)(2,1)S(1)}, u32[]{:S(2)}, u32[]{:S(2)}) collective-permute-start(bf16[96,768]{1,0:T(8,128)(2,1)S(1)} %get-tuple-element.182), channel_id=1, source_target_pairs={{0,16},{4,20},{8,24},{12,28},{16,0},{20,4},{24,8},{28,12},{1,17},{... | collective-permute-start | bytes 442376 | tf_op jit(solution)/shard_map/ppermute | solution.py:43
  203.2 11.9 %collective-permute-start.46 = (bf16[96,768]{1,0:T(8,128)(2,1)S(1)}, bf16[96,768]{1,0:T(8,128)(2,1)S(1)}, u32[]{:S(2)}, u32[]{:S(2)}) collective-permute-start(bf16[96,768]{1,0:T(8,128)(2,1)S(1)} %get-tuple-element.183), channel_id=1, source_target_pairs={{0,24},{4,28},{8,16},{12,20},{16,8},{20,12},{24,0},{28,4},{1,25},{... | collective-permute-start | bytes 442376 | tf_op jit(solution)/shard_map/ppermute | solution.py:43
  205.0 6.7 %collective-permute-start.44 = (bf16[2,96,768]{2,1,0:T(8,128)(2,1)S(1)}, bf16[2,96,768]{2,1,0:T(8,128)(2,1)S(1)}, u32[]{:S(2)}, u32[]{:S(2)}) collective-permute-start(bf16[2,96,768]{2,1,0:T(8,128)(2,1)S(1)} %slice_bitcast_fusion.8), channel_id=1, source_target_pairs={{0,4},{4,0},{8,12},{12,8},{16,20},{20,16},{24,28},{28,24},{1,5},{5... | collective-permute-start | bytes 884744 | tf_op jit(solution)/shard_map/ppermute | solution.py:49
  208.0 5.7 %collective-permute-start.42 = (bf16[128,768]{1,0:T(8,128)(2,1)S(1)}, bf16[128,768]{1,0:T(8,128)(2,1)S(1)}, u32[]{:S(2)}, u32[]{:S(2)}) collective-permute-start(bf16[128,768]{1,0:T(8,128)(2,1)S(1)} %fusion.49), channel_id=1, source_target_pairs={{0,2},{1,3},{2,0},{3,1},{4,6},{5,7},{6,4},{7,5},{8,10},{9,11},{10,... | collective-permute-start | bytes 589832 | tf_op jit(solution)/shard_map/ppermute | solution.py:37
  211.8 5.2 %collective-permute-start.47 = (bf16[96,768]{1,0:T(8,128)(2,1)S(1)}, bf16[96,768]{1,0:T(8,128)(2,1)S(1)}, u32[]{:S(2)}, u32[]{:S(2)}) collective-permute-start(bf16[96,768]{1,0:T(8,128)(2,1)S(1)} %slice_bitcast_fusion.18), channel_id=1, source_target_pairs={{0,8},{4,12},{8,0},{12,4},{16,24},{20,28},{24,16},{28,20},{1,9},{5... | collective-permute-start | bytes 442376 | tf_op jit(solution)/shard_map/ppermute | solution.py:43
  (48 other events, 385.4 us)

commit v2 on v1

--- a/solution.py
+++ b/solution.py
@@ -58,9 +58,9 @@
     return parts
 
 
-def gather_t(x):
+def gather_t(x, *earlier):
     far = over_t(x, 2)
-    return x, far, over_t(jnp.stack([x, far]), 1)
+    return x, far, over_t(after(jnp.stack([x, far]), *earlier), 1)
 
 
 def in_order(gathered):
@@ -83,38 +83,25 @@
 
 
 def swap_r(x):
-    total = x[0].astype(F32)
-    for c in range(1, x.shape[0]):
-        total = total + over_r(x[c], c).astype(F32)
-    return total
+    return [x[0]] + [over_r(x[c], c) for c in range(1, x.shape[0])]
+
+
+def add(terms):
+    return sum(term.astype(F32) for term in terms)
 
 
 def deliver_z(x):
     return [x[0]] + [over_z(x[d], d) for d in range(1, E)]
 
 
-def sum_everywhere(x, *earlier):
+def sum_but_z(x):
     R = lax.axis_size("dp") // E
-    for k in (1, 2):
-        x = x + over_t(x, k)
-    for d in (1, 2):
-        x = x + over_z(x, d)
-    x = after(x, *earlier)
     c = 1
     while c < R:
         x = x + over_r(x, c)
         c *= 2
-    return x
-
-
-def gather_lines(x, at_dp):
-    R = lax.axis_size("dp") // E
-    bit = 1
-    while bit < E * R:
-        other = over_r(x, bit) if bit < R else over_z(x, bit // R)
-        upper = (at_dp & bit) != 0
-        x = jnp.concatenate([jnp.where(upper, other, x), jnp.where(upper, x, other)], axis=0)
-        bit *= 2
+    for k in (1, 2):
+        x = x + over_t(x, k)
     return x
 
 
@@ -387,20 +374,23 @@
     grads_shape = (R, E, local) if aligned else (D,)
 
     line = jnp.concatenate([w_router.T.reshape(-1), norm1_gain, norm2_gain, bias_table])
-    line = jnp.pad(line, (0, -line.shape[0] % 128))[None]
-    lines = gather_lines(line, at_dp)
+    line = jnp.pad(line, (0, 4 * LW - line.shape[0]))[None]
+    packed = jnp.concatenate(
+        [jnp.concatenate([w_qkv.reshape(local, 3 * LW), w_out_attn], axis=1), line], axis=0
+    )
+    packed_z = [packed] + [over_z(packed, d) for d in range(1, E)]
+    packed_r = [
+        [over_r(packed, c), *over_r(jnp.stack([part[:local] for part in packed_z[1:]]), c)]
+        for c in range(1, R)
+    ]
+    packed_all = [[part[:local] for part in parts] for parts in [packed_z] + packed_r]
+    lines = jnp.stack(natural([part[local] for part in packed_z], z))
+    lines = [lines] + [over_r(lines, c) for c in range(1, R)]
+    lines = jnp.stack(natural(lines, r), axis=1).reshape(n, -1)
     router_rows = lines[:, : local * E].reshape(n, E, local).transpose(1, 0, 2).reshape(E, D)
     gain_one = lines[:, local * E : local * (E + 1)].reshape(1, D).astype(F32)
     gain_two = lines[:, local * (E + 1) : local * (E + 2)].reshape(1, D).astype(F32)
     table_flat = lines[:, local * (E + 2) : local * (E + 2) + H * NB // n].reshape(-1)
-
-    packed = jnp.concatenate([w_qkv.reshape(local, 3 * LW), w_out_attn], axis=1)
-    packed_z = [packed] + [over_z(packed, d) for d in range(1, E)]
-    packed_r = [over_r(packed, c) for c in range(1, R)]
-    packed_rest = [over_r(jnp.stack(packed_z[1:]), c) for c in range(1, R)]
-    packed_all = [packed_z] + [
-        [first, *(rest[d] for d in range(E - 1))] for first, rest in zip(packed_r, packed_rest)
-    ]
 
     both_parts = gather_t(jnp.concatenate([tokens, cotangent], axis=1))
     token_parts = [part[..., :D] for part in both_parts]
@@ -432,7 +422,7 @@
 
     grad_output = mm(to_slots[:ROWS], cotangent_all, 1, 0)
     masked = jnp.where(sent_own[:, None], grad_output, 0).astype(BF).reshape(E, SUB, D)
-    in_rows = after(w_in, packed_z, packed_r, both_parts)
+    in_rows = after(w_in, packed_z)
     in_columns = jnp.stack(deliver_z(jnp.stack([pick(in_rows, z ^ d, 1) for d in range(E)])))
     out_rows = after(w_out, in_columns)
     out_rows = jnp.stack([pick(out_rows, z ^ d, 1) for d in range(E)])
@@ -469,19 +459,17 @@
         *token_parts,
         gain_one,
         reversed_rel,
-        to_slots,
+        after(to_slots, in_columns),
         *packed_refs,
     )
-    normed_all, qkv, probs, heads_all, kept, given, tokens_all, attention_weight = after(
-        forward, in_columns
-    )
+    normed_all, qkv, probs, heads_all, kept, given, tokens_all, attention_weight = forward
     attended = scatter_t(kept, given)
     inputs = mm(to_slots[:ROWS], tokens_all, 1, 0)
     middle = inputs + attended
     scale_two = norm_scale(middle)
     normed_two = (middle * scale_two * gain_two).astype(BF)
 
-    buffer_parts = gather_t(dispatch_z(after(normed_two, out_z, in_weight)))
+    buffer_parts = gather_t(dispatch_z(after(normed_two, out_z, in_weight)), out_weight)
     router = jnp.pad(router_rows.T, ((0, 0), (0, 128 - E)))
     buffer, grad_expert, activation, grad_pre, kept, given = call(
         functools.partial(expert_layer, pieces=len(in_weight)),
@@ -521,8 +509,8 @@
     out_terms = expert_gradient("grad_w_out", grad_expert, activation)
     in_terms = expert_gradient("grad_w_in", buffer, grad_pre)
     mine = scatter_t(kept, given).astype(BF)
-    out_sums = swap_r(out_terms).astype(BF)
-    in_sums = swap_r(after(in_terms, out_sums, mine)).astype(BF)
+    out_sums = add(swap_r(out_terms)).astype(BF)
+    in_sums = add(swap_r(after(in_terms, out_sums, mine))).astype(BF)
     returned = deliver_z(after(mine, out_sums).reshape(E, SUB, 2 * D))
     returned = jnp.concatenate(returned, axis=0).astype(F32)
     combined, grad_normed_two = returned[:, :D], returned[:, D:]
@@ -545,7 +533,7 @@
     )
     grad_gain_two = jnp.sum(grad_normed_two * middle * scale_two, axis=0, keepdims=True)
     grad_middle = (grad_output + norm_back(grad_normed_two, middle, scale_two, gain_two)).astype(BF)
-    grad_parts = gather_t(after(grad_middle, in_sums))
+    grad_parts = gather_t(grad_middle, in_sums)
     layer_parts = gather_t(after(layer_rows, grad_parts))
 
     late_terms, kept, given, grad_gain_one, grad_rel = call(
@@ -582,8 +570,8 @@
         (late_terms, kept, given, grad_gain_one, grad_rel, delivered), layer_parts[1]
     )
     late_terms = blocks_to_send(late_terms)
-    far_sums = swap_r(late_terms[:, 2:]).astype(BF)
-    near_sums = swap_r(after(late_terms[:, :2], far_sums)).astype(BF)
+    far_sums = add(swap_r(late_terms[:, 2:])).astype(BF)
+    near_terms = swap_r(after(late_terms[:, :2], far_sums))
     grad_normed_one = scatter_t(kept, given)
     own_inputs = tokens.astype(F32)
     grad_slots = jnp.concatenate(in_order(grad_parts), axis=0)
@@ -601,7 +589,7 @@
     grad_table = lax.dynamic_update_slice_in_dim(
         jnp.zeros((H, NB), F32), grad_table_rows, t * LH, 0
     ).reshape(1, -1)
-    small = sum_everywhere(
+    small = sum_but_z(
         jnp.concatenate(
             [
                 grad_router,
@@ -611,12 +599,15 @@
                 jnp.zeros((1, D), F32),
             ],
             axis=0,
-        ),
-        far_sums,
-    )
-    late = near_sums[0].astype(F32)
-    for d, part in ((2, far_sums[0]), (3, far_sums[1]), (1, near_sums[1])):
-        late = late + over_z(part, d).astype(F32)
+        )
+    )
+    low = small.astype(BF)
+    far = [over_z(jnp.concatenate([far_sums[d - 2], low], axis=0), d) for d in (2, 3)]
+    near_sums = add(after(near_terms, far))
+    near = over_z(jnp.concatenate([near_sums[1].astype(BF), low], axis=0), 1)
+    late = jnp.concatenate([near_sums[0], small], axis=0)
+    late = late + far[0].astype(F32) + far[1].astype(F32) + near.astype(F32)
+    late, small = late[:local], late[local:]
     small_own = lax.dynamic_slice_in_dim(small[: E + 2], at_dp * local, local, 1)
     table_own = lax.dynamic_slice_in_dim(small[E + 2], at_dp * (H * NB // n), H * NB // n, 0)
     return (

time: 220 us -> 209 us (0.950)
  waiting for transfers between devices: 84.1 us -> 69.3 us
  local copies, waits for them, and re-layouts: 23 us -> 26.9 us
  starting transfers between devices: 63.8 us -> 60.6 us
  other arithmetic: 12.4 us -> 15 us
    ppermute x10, waiting for transfers between devices: 34.8 us -> 13 us  [over_r(): lax.ppermute(x, 'dp', [(i, i // r * r + (i % r ^ c)) for i in range(n)])]
    ppermute x25 -> x21, waiting for transfers between devices: 35.3 us -> 45.8 us  [over_z(): lax.ppermute(x, 'dp', [(i, (i // r ^ d) * r + i % r) for i in range(n)])]
    ppermute x25 -> x21, starting transfers between devices: 42.8 us -> 35 us  [over_z(): lax.ppermute(x, 'dp', [(i, (i // r ^ d) * r + i % r) for i in range(n)])]
    ppermute x18, waiting for transfers between devices: 14 us -> 10.5 us  [over_t(): return lax.ppermute(x, 'tensor', [(i, i ^ k) for i in range(T)])]
    ppermute x18, starting transfers between devices: 9.86 us -> 13.2 us  [over_t(): return lax.ppermute(x, 'tensor', [(i, i ^ k) for i in range(T)])]
    unnamed x93 -> x81, local copies, waits for them, and re-layouts: 12.3 us -> 14.2 us
  transfers between devices with their start and end apart: 53 -> 49, of which waited for: 26 -> 21; matrix products, arithmetic and copies ran while one was open for 14% -> 16% of each run, Pallas kernels for 10% -> 6%
where the time goes in v2:
time: 209 us; the launch traced here: 208 us
  waiting for transfers between devices  69.3 us (33%)
  starting transfers between devices  60.6 us (29%)
  Pallas kernels  27.6 us (13%)
  local copies, waits for them, and re-layouts  26.9 us (13%)
  other arithmetic  15 us (7%)
  matrix products  6.6 us (3%)
  between operations  2.36 us (1%)
    ppermute x21, waiting for transfers between devices, over_z(): lax.ppermute(x, 'dp', [(i, (i // r ^ d) * r + i % r) for i in range(n)])  45.8 us
    ppermute x21, starting transfers between devices, over_z(): lax.ppermute(x, 'dp', [(i, (i // r ^ d) * r + i % r) for i in range(n)])  35 us
    pallas_call x5, Pallas kernels, call(): pl.pallas_call(kernel, out_shape=[jax.ShapeDtypeStruct(shape, kind) for s...  27.6 us
    unnamed x81, local copies, waits for them, and re-layouts  14.2 us
    ppermute x18, starting transfers between devices, over_t(): return lax.ppermute(x, 'tensor', [(i, i ^ k) for i in range(T)])  13.2 us
    ppermute x10, waiting for transfers between devices, over_r(): lax.ppermute(x, 'dp', [(i, i // r * r + (i % r ^ c)) for i in range(n)])  13 us
    ppermute x10, starting transfers between devices, over_r(): lax.ppermute(x, 'dp', [(i, i // r * r + (i % r ^ c)) for i in range(n)])  12.4 us
    ppermute x18, waiting for transfers between devices, over_t(): return lax.ppermute(x, 'tensor', [(i, i ^ k) for i in range(T)])  10.5 us
  transfers between devices with their start and end apart: 49, of which 21 were waited for; matrix products, arithmetic and copies ran while one was open for 16% of the time, Pallas kernels for 6%

profile of v2, /device:TPU:0, one launch (start us, length us, event | category | flops | bytes accessed | tf_op | source)
XLA Modules:
  0.0 208.4 jit_solution(4944328303324635668)
XLA Ops:
  4.4 3.0 %collective-permute-start.9 = (bf16[97,768]{1,0:T(8,128)(2,1)S(1)}, bf16[97,768]{1,0:T(8,128)(2,1)S(1)}, u32[]{:S(2)}, u32[]{:S(2)}) collective-permute-start(bf16[97,768]{1,0:T(8,128)(2,1)S(1)} %pad_maximum_fusion.16), channel_id=1, source_target_pairs={{0,4},{4,0},{8,12},{12,8},{16,20},{20,16},{24,28},{28,24},{1,5},{5... | collective-permute-start | bytes 446984 | tf_op jit(solution)/shard_map/ppermute | solution.py:49
  7.4 1.6 collective-permute-start.4
  9.0 2.6 %collective-permute-start.3 = (bf16[97,768]{1,0:T(8,128)(2,1)S(1)}, bf16[97,768]{1,0:T(8,128)(2,1)S(1)}, u32[]{:S(2)}, u32[]{:S(2)}) collective-permute-start(bf16[97,768]{1,0:T(8,128)(2,1)S(1)} %pad_maximum_fusion.16), channel_id=1, source_target_pairs={{0,16},{4,20},{8,24},{12,28},{16,0},{20,4},{24,8},{28,12},{1,17},{... | collective-permute-start | bytes 446984 | tf_op jit(solution)/shard_map/ppermute | solution.py:43
  13.7 1.6 collective-permute-start
  18.8 5.0 %collective-permute-done.3 = bf16[97,768]{1,0:T(8,128)(2,1)S(1)} collective-permute-done((bf16[97,768]{1,0:T(8,128)(2,1)S(1)}, bf16[97,768]{1,0:T(8,128)(2,1)S(1)}, u32[]{:S(2)}, u32[]{:S(2)}) %collective-permute-start.3) | collective-permute-done | bytes 149024 | tf_op jit(solution)/shard_map/ppermute | solution.py:43
  25.4 1.5 collective-permute-start.10
  27.7 2.1 %collective-permute-start.8 = (bf16[96,768]{1,0:T(8,128)(2,1)}, bf16[96,768]{1,0:T(8,128)(2,1)S(1)}, u32[]{:S(2)}, u32[]{:S(2)}) collective-permute-start(bf16[96,768]{1,0:T(8,128)(2,1)} %get-tuple-element.174), channel_id=1, source_target_pairs={{0,24},{4,28},{8,16},{12,20},{16,8},{20,12},{24,0},{28,4},{1,25},{... | collective-permute-start | bytes 442376 | tf_op jit(solution)/shard_map/ppermute | solution.py:43
  29.9 1.7 collective-permute-start.7
  33.9 2.6 %collective-permute-done.8 = bf16[96,768]{1,0:T(8,128)(2,1)S(1)} collective-permute-done((bf16[96,768]{1,0:T(8,128)(2,1)}, bf16[96,768]{1,0:T(8,128)(2,1)S(1)}, u32[]{:S(2)}, u32[]{:S(2)}) %collective-permute-start.8) | collective-permute-done | bytes 147488 | tf_op jit(solution)/shard_map/ppermute | solution.py:43
  36.4 5.0 %collective-permute-done.7 = bf16[96,768]{1,0:T(8,128)(2,1)} collective-permute-done((bf16[96,768]{1,0:T(8,128)(2,1)S(1)}, bf16[96,768]{1,0:T(8,128)(2,1)}, u32[]{:S(2)}, u32[]{:S(2)}) %collective-permute-start.7) | collective-permute-done | bytes 147488 | tf_op jit(solution)/shard_map/ppermute | solution.py:43
  45.9 8.0 %attention_forward.1 = (bf16[512,768]{1,0:T(8,128)(2,1)S(1)}, bf16[512,576]{1,0:T(8,128)(2,1)S(1)}, f32[3,512,512]{2,1,0:T(8,128)}, bf16[512,192]{1,0:T(8,128)(2...) custom-call(s32[4]{0:T(128)S(1)} %pad_add_fusion.at_ref, ...), custom_call_target="tpu_custom_call" | custom-call | flops 12000000000 | bytes 2505728 | tf_op jit(solution)/shard_map/attention_forward/pallas_call | solution.py:115
  54.0 1.9 select_convert_fusion
  56.9 2.6 %collective-permute-start.15 = (bf16[128,768]{1,0:T(8,128)(2,1)}, bf16[128,768]{1,0:T(8,128)(2,1)S(1)}, u32[]{:S(2)}, u32[]{:S(2)}) collective-permute-start(bf16[128,768]{1,0:T(8,128)(2,1)} %get-tuple-element.162), channel_id=1, source_target_pairs={{0,24},{4,28},{8,16},{12,20},{16,8},{20,12},{24,0},{28,4},{1,25},{... | collective-permute-start | bytes 589832 | tf_op jit(solution)/shard_map/ppermute | solution.py:43
  59.5 1.7 collective-permute-start.13
  62.9 1.5 collective-permute-start.12
  65.1 1.7 collective-permute-done.15
  66.8 9.4 %collective-permute-done.14 = bf16[128,768]{1,0:T(8,128)(2,1)} collective-permute-done((bf16[128,768]{1,0:T(8,128)(2,1)}, bf16[128,768]{1,0:T(8,128)(2,1)}, u32[]{:S(2)}, u32[]{:S(2)}) %collective-permute-start.14) | collective-permute-done | bytes 196640 | tf_op jit(solution)/shard_map/ppermute | solution.py:43
  77.9 1.3 multiply_reduce_fusion.3
  79.5 2.3 %collective-permute-start.19 = (bf16[32,768]{1,0:T(8,128)(2,1)S(1)}, bf16[32,768]{1,0:T(8,128)(2,1)S(1)}, u32[]{:S(2)}, u32[]{:S(2)}) collective-permute-start(bf16[32,768]{1,0:T(8,128)(2,1)S(1)} %get-tuple-element.191), channel_id=1, source_target_pairs={{0,24},{4,28},{8,16},{12,20},{16,8},{20,12},{24,0},{28,4},{1,25},{... | collective-permute-start | bytes 147464 | tf_op jit(solution)/shard_map/ppermute | solution.py:43
  82.0 2.0 collective-permute-start.17
  84.0 1.6 collective-permute-start.23
  85.8 1.6 collective-permute-done.18
  88.6 2.3 %collective-permute-done.23.far_grad_ref = bf16[128,768]{1,0:T(8,128)(2,1)S(1)} collective-permute-done((bf16[128,768]{1,0:T(8,128)(2,1)S(1)}, bf16[128,768]{1,0:T(8,128)(2,1)S(1)}, u32[]{:S(2)}, u32[]{:S(2)}) %collective-permute-start.23) | collective-permute-done | bytes 196640 | tf_op jit(solution)/shard_map/ppermute | solution.py:37
  91.7 2.2 %collective-permute-done.20.far_ref = bf16[128,768]{1,0:T(8,128)(2,1)S(1)} collective-permute-done((bf16[128,768]{1,0:T(8,128)(2,1)S(1)}, bf16[128,768]{1,0:T(8,128)(2,1)S(1)}, u32[]{:S(2)}, u32[]{:S(2)}) %collective-permute-start.20) | collective-permute-done | bytes 196640 | tf_op jit(solution)/shard_map/ppermute | solution.py:37
  100.8 6.6 %expert_layer.1 = (bf16[512,768]{1,0:T(8,128)(2,1)S(1)}, bf16[512,768]{1,0:T(8,128)(2,1)S(1)}, bf16[512,768]{1,0:T(8,128)(2,1)}, bf16[512,768]{1,0:T(8,128)(2,1)...) custom-call(s32[4]{0:T(128)S(1)} %pad_add_fusion.at_ref, ...), custom_call_target="tpu_custom_call" | custom-call | flops 8000000000 | bytes 4128768 | tf_op jit(solution)/shard_map/expert_layer/pallas_call | solution.py:115
  109.3 1.5 grad_w_out.1
  112.4 1.6 collective-permute-start.26
  114.0 1.5 grad_w_in.1
  115.5 10.7 %collective-permute-done.27 = bf16[4,96,768]{2,1,0:T(8,128)(2,1)S(1)} collective-permute-done((bf16[4,96,768]{2,1,0:T(8,128)(2,1)S(1)}, bf16[4,96,768]{2,1,0:T(8,128)(2,1)S(1)}, u32[]{:S(2)}, u32[]{:S(2)}) %collective-permute-start.27) | collective-permute-done | bytes 589856 | tf_op jit(solution)/shard_map/ppermute | solution.py:49
  126.5 2.3 %collective-permute-start.30 = (bf16[32,1536]{1,0:T(8,128)(2,1)S(1)}, bf16[32,1536]{1,0:T(8,128)(2,1)S(1)}, u32[]{:S(2)}, u32[]{:S(2)}) collective-permute-start(bf16[32,1536]{1,0:T(8,128)(2,1)S(1)} %get-tuple-element.182), channel_id=1, source_target_pairs={{0,24},{4,28},{8,16},{12,20},{16,8},{20,12},{24,0},{28,4},{1,25},{... | collective-permute-start | bytes 294920 | tf_op jit(solution)/shard_map/ppermute | solution.py:43
  128.8 2.2 %collective-permute-start.28 = (bf16[32,1536]{1,0:T(8,128)(2,1)S(1)}, bf16[32,1536]{1,0:T(8,128)(2,1)S(1)}, u32[]{:S(2)}, u32[]{:S(2)}) collective-permute-start(bf16[32,1536]{1,0:T(8,128)(2,1)S(1)} %get-tuple-element.184), channel_id=1, source_target_pairs={{0,8},{4,12},{8,0},{12,4},{16,24},{20,28},{24,16},{28,20},{1,9},{5... | collective-permute-start | bytes 294920 | tf_op jit(solution)/shard_map/ppermute | solution.py:43
  132.3 1.8 collective-permute-done.30
  134.1 2.9 %collective-permute-done.29 = bf16[32,1536]{1,0:T(8,128)(2,1)S(1)} collective-permute-done((bf16[32,1536]{1,0:T(8,128)(2,1)S(1)}, bf16[32,1536]{1,0:T(8,128)(2,1)S(1)}, u32[]{:S(2)}, u32[]{:S(2)}) %collective-permute-start.29) | collective-permute-done | bytes 98336 | tf_op jit(solution)/shard_map/ppermute | solution.py:43
  137.9 1.5 collective-permute-start.31
  139.7 4.9 %collective-permute-done.31.far_ref = bf16[128,768]{1,0:T(8,128)(2,1)S(1)} collective-permute-done((bf16[128,768]{1,0:T(8,128)(2,1)S(1)}, bf16[128,768]{1,0:T(8,128)(2,1)S(1)}, u32[]{:S(2)}, u32[]{:S(2)}) %collective-permute-start.31) | collective-permute-done | bytes 196640 | tf_op jit(solution)/shard_map/ppermute | solution.py:37
  146.1 1.7 collective-permute-start.36
  147.9 1.7 collective-permute-start.38
  150.8 10.1 %attention_backward.1 = (bf16[2,4,96,768]{3,2,1,0:T(8,128)(2,1)S(1)}, bf16[2,128,768]{2,1,0:T(8,128)(2,1)S(1)}, bf16[2,128,768]{2,1,0:T(8,128)(2,1)S(1)}, f32[1,768]{1,0:T(1,128)S(1)}, f32[3,1024]{1,0:T(4,128)S(1)}) custom-call(s32[4]{0:T(128)S(1)} %pad_add_fusion.at_ref, bf16[128,768]{1,0:T(8,128)(2,1)S(1)} %add_convert_fusion.own_ref, ...), custom_call_target="tpu_custom_call" | custom-call | flops 12000000000 | bytes 7995392 | tf_op jit(solution)/shard_map/attention_backward/pallas_call | solution.py:115
  162.1 5.9 %collective-permute-done.38 = bf16[2,96,768]{2,1,0:T(8,128)(2,1)S(1)} collective-permute-done((bf16[2,96,768]{2,1,0:T(8,128)(2,1)S(1)}, bf16[2,96,768]{2,1,0:T(8,128)(2,1)S(1)}, u32[]{:S(2)}, u32[]{:S(2)}) %collective-permute-start.38) | collective-permute-done | bytes 294944 | tf_op jit(solution)/shard_map/ppermute | solution.py:43
  170.0 1.4 collective-permute-start.43
  172.2 1.7 collective-permute-done.43
  176.5 1.8 copy.87
  178.3 1.8 copy.86
  180.8 2.3 %collective-permute-start.47 = (bf16[104,768]{1,0:T(8,128)(2,1)S(1)}, bf16[104,768]{1,0:T(8,128)(2,1)S(1)}, u32[]{:S(2)}, u32[]{:S(2)}) collective-permute-start(bf16[104,768]{1,0:T(8,128)(2,1)S(1)} %get-tuple-element.194), channel_id=1, source_target_pairs={{0,24},{4,28},{8,16},{12,20},{16,8},{20,12},{24,0},{28,4},{1,25},{... | collective-permute-start | bytes 479240 | tf_op jit(solution)/shard_map/ppermute | solution.py:43
  183.1 5.9 %collective-permute-start.46 = (bf16[104,768]{1,0:T(8,128)(2,1)S(1)}, bf16[104,768]{1,0:T(8,128)(2,1)S(1)}, u32[]{:S(2)}, u32[]{:S(2)}) collective-permute-start(bf16[104,768]{1,0:T(8,128)(2,1)S(1)} %get-tuple-element.195), channel_id=1, source_target_pairs={{0,16},{4,20},{8,24},{12,28},{16,0},{20,4},{24,8},{28,12},{1,17},{... | collective-permute-start | bytes 479240 | tf_op jit(solution)/shard_map/ppermute | solution.py:43
  189.1 1.4 collective-permute-start.42
  193.6 5.7 %collective-permute-done.46 = bf16[104,768]{1,0:T(8,128)(2,1)S(1)} collective-permute-done((bf16[104,768]{1,0:T(8,128)(2,1)S(1)}, bf16[104,768]{1,0:T(8,128)(2,1)S(1)}, u32[]{:S(2)}, u32[]{:S(2)}) %collective-permute-start.46) | collective-permute-done | bytes 159776 | tf_op jit(solution)/shard_map/ppermute | solution.py:43
  200.9 3.9 %collective-permute-done.48 = bf16[104,768]{1,0:T(8,128)(2,1)S(1)} collective-permute-done((bf16[104,768]{1,0:T(8,128)(2,1)S(1)}, bf16[104,768]{1,0:T(8,128)(2,1)S(1)}, u32[]{:S(2)}, u32[]{:S(2)}) %collective-permute-start.48) | collective-permute-done | bytes 159776 | tf_op jit(solution)/shard_map/ppermute | solution.py:43
  (277 shorter events, 56.7 us)
Async XLA Ops:
  4.4 25.5 %collective-permute-start.9 = (bf16[97,768]{1,0:T(8,128)(2,1)S(1)}, bf16[97,768]{1,0:T(8,128)(2,1)S(1)}, u32[]{:S(2)}, u32[]{:S(2)}) collective-permute-start(bf16[97,768]{1,0:T(8,128)(2,1)S(1)} %pad_maximum_fusion.16), channel_id=1, source_target_pairs={{0,4},{4,0},{8,12},{12,8},{16,20},{20,16},{24,28},{28,24},{1,5},{5... | collective-permute-start | bytes 446984 | tf_op jit(solution)/shard_map/ppermute | solution.py:49
  7.4 11.4 %collective-permute-start.4 = (bf16[97,768]{1,0:T(8,128)(2,1)S(1)}, bf16[97,768]{1,0:T(8,128)(2,1)S(1)}, u32[]{:S(2)}, u32[]{:S(2)}) collective-permute-start(bf16[97,768]{1,0:T(8,128)(2,1)S(1)} %pad_maximum_fusion.16), channel_id=1, source_target_pairs={{0,8},{4,12},{8,0},{12,4},{16,24},{20,28},{24,16},{28,20},{1,9},{5... | collective-permute-start | bytes 446984 | tf_op jit(solution)/shard_map/ppermute | solution.py:43
  9.0 14.8 %collective-permute-start.3 = (bf16[97,768]{1,0:T(8,128)(2,1)S(1)}, bf16[97,768]{1,0:T(8,128)(2,1)S(1)}, u32[]{:S(2)}, u32[]{:S(2)}) collective-permute-start(bf16[97,768]{1,0:T(8,128)(2,1)S(1)} %pad_maximum_fusion.16), channel_id=1, source_target_pairs={{0,16},{4,20},{8,24},{12,28},{16,0},{20,4},{24,8},{28,12},{1,17},{... | collective-permute-start | bytes 446984 | tf_op jit(solution)/shard_map/ppermute | solution.py:43
  11.6 12.2 %collective-permute-start.2 = (bf16[97,768]{1,0:T(8,128)(2,1)S(1)}, bf16[97,768]{1,0:T(8,128)(2,1)S(1)}, u32[]{:S(2)}, u32[]{:S(2)}) collective-permute-start(bf16[97,768]{1,0:T(8,128)(2,1)S(1)} %pad_maximum_fusion.16), channel_id=1, source_target_pairs={{0,24},{4,28},{8,16},{12,20},{16,8},{20,12},{24,0},{28,4},{1,25},{... | collective-permute-start | bytes 446984 | tf_op jit(solution)/shard_map/ppermute | solution.py:43
  13.7 18.7 %collective-permute-start = (bf16[128,1536]{1,0:T(8,128)(2,1)S(1)}, bf16[128,1536]{1,0:T(8,128)(2,1)S(1)}, u32[]{:S(2)}, u32[]{:S(2)}) collective-permute-start(bf16[128,1536]{1,0:T(8,128)(2,1)S(1)} %constant_dynamic-update-slice_fusion), channel_id=1, source_target_pairs={{0,2},{1,3},{2,0},{3,1},{4,6},{5,7},{6,4},{7,5},{8,10},{9,11},{10,... | collective-permute-start | bytes 1179656 | tf_op jit(solution)/shard_map/ppermute | solution.py:37
  23.9 7.7 %collective-permute-start.5 = (bf16[4,768]{1,0:T(4,128)(2,1)S(1)}, bf16[4,768]{1,0:T(4,128)(2,1)S(1)}, u32[]{:S(2)}, u32[]{:S(2)}) collective-permute-start(bf16[4,768]{1,0:T(4,128)(2,1)S(1)} %pad_maximum_fusion.18), channel_id=1, source_target_pairs={{0,4},{4,0},{8,12},{12,8},{16,20},{20,16},{24,28},{28,24},{1,5},{5... | collective-permute-start | bytes 18440 | tf_op jit(solution)/shard_map/ppermute | solution.py:49
  25.4 18.4 %collective-permute-start.10 = (bf16[3,96,768]{2,1,0:T(8,128)(2,1)}, bf16[3,96,768]{2,1,0:T(8,128)(2,1)}, u32[]{:S(2)}, u32[]{:S(2)}) collective-permute-start(bf16[3,96,768]{2,1,0:T(8,128)(2,1)} %pad_maximum_fusion.7), channel_id=1, source_target_pairs={{0,4},{4,0},{8,12},{12,8},{16,20},{20,16},{24,28},{28,24},{1,5},{5... | collective-permute-start | bytes 1327112 | tf_op jit(solution)/shard_map/ppermute | solution.py:49
  27.7 8.7 %collective-permute-start.8 = (bf16[96,768]{1,0:T(8,128)(2,1)}, bf16[96,768]{1,0:T(8,128)(2,1)S(1)}, u32[]{:S(2)}, u32[]{:S(2)}) collective-permute-start(bf16[96,768]{1,0:T(8,128)(2,1)} %get-tuple-element.174), channel_id=1, source_target_pairs={{0,24},{4,28},{8,16},{12,20},{16,8},{20,12},{24,0},{28,4},{1,25},{... | collective-permute-start | bytes 442376 | tf_op jit(solution)/shard_map/ppermute | solution.py:43
  29.9 11.5 %collective-permute-start.7 = (bf16[96,768]{1,0:T(8,128)(2,1)S(1)}, bf16[96,768]{1,0:T(8,128)(2,1)}, u32[]{:S(2)}, u32[]{:S(2)}) collective-permute-start(bf16[96,768]{1,0:T(8,128)(2,1)S(1)} %get-tuple-element.175), channel_id=1, source_target_pairs={{0,16},{4,20},{8,24},{12,28},{16,0},{20,4},{24,8},{28,12},{1,17},{... | collective-permute-start | bytes 442376 | tf_op jit(solution)/shard_map/ppermute | solution.py:43
  31.6 9.8 %collective-permute-start.6 = (bf16[96,768]{1,0:T(8,128)(2,1)S(1)}, bf16[96,768]{1,0:T(8,128)(2,1)}, u32[]{:S(2)}, u32[]{:S(2)}) collective-permute-start(bf16[96,768]{1,0:T(8,128)(2,1)S(1)} %get-tuple-element.176), channel_id=1, source_target_pairs={{0,8},{4,12},{8,0},{12,4},{16,24},{20,28},{24,16},{28,20},{1,9},{5... | collective-permute-start | bytes 442376 | tf_op jit(solution)/shard_map/ppermute | solution.py:43
  33.3 11.6 %collective-permute-start.1 = (bf16[2,128,1536]{2,1,0:T(8,128)(2,1)}, bf16[2,128,1536]{2,1,0:T(8,128)(2,1)S(1)}, u32[]{:S(2)}, u32[]{:S(2)}) collective-permute-start(bf16[2,128,1536]{2,1,0:T(8,128)(2,1)} %pad_maximum_fusion.1), channel_id=1, source_target_pairs={{0,1},{1,0},{2,3},{3,2},{4,5},{5,4},{6,7},{7,6},{8,9},{9,8},{10,11... | collective-permute-start | bytes 2359304 | tf_op jit(solution)/shard_map/ppermute | solution.py:37
  53.9 7.3 %collective-permute-start.11 = (bf16[2,128,768]{2,1,0:T(8,128)(2,1)S(1)}, bf16[2,128,768]{2,1,0:T(8,128)(2,1)S(1)}, u32[]{:S(2)}, u32[]{:S(2)}) collective-permute-start(bf16[2,128,768]{2,1,0:T(8,128)(2,1)S(1)} %get-tuple-element.55), channel_id=1, source_target_pairs={{0,1},{1,0},{2,3},{3,2},{4,5},{5,4},{6,7},{7,6},{8,9},{9,8},{10,11... | collective-permute-start | bytes 1179656 | tf_op jit(solution)/shard_map/ppermute | solution.py:37
  56.9 9.9 %collective-permute-start.15 = (bf16[128,768]{1,0:T(8,128)(2,1)}, bf16[128,768]{1,0:T(8,128)(2,1)S(1)}, u32[]{:S(2)}, u32[]{:S(2)}) collective-permute-start(bf16[128,768]{1,0:T(8,128)(2,1)} %get-tuple-element.162), channel_id=1, source_target_pairs={{0,24},{4,28},{8,16},{12,20},{16,8},{20,12},{24,0},{28,4},{1,25},{... | collective-permute-start | bytes 589832 | tf_op jit(solution)/shard_map/ppermute | solution.py:43
  59.5 16.6 %collective-permute-start.14 = (bf16[128,768]{1,0:T(8,128)(2,1)}, bf16[128,768]{1,0:T(8,128)(2,1)}, u32[]{:S(2)}, u32[]{:S(2)}) collective-permute-start(bf16[128,768]{1,0:T(8,128)(2,1)} %get-tuple-element.163), channel_id=1, source_target_pairs={{0,16},{4,20},{8,24},{12,28},{16,0},{20,4},{24,8},{28,12},{1,17},{... | collective-permute-start | bytes 589832 | tf_op jit(solution)/shard_map/ppermute | solution.py:43
  59.5 16.6 %collective-permute-start.13 = (bf16[128,768]{1,0:T(8,128)(2,1)S(1)}, bf16[128,768]{1,0:T(8,128)(2,1)}, u32[]{:S(2)}, u32[]{:S(2)}) collective-permute-start(bf16[128,768]{1,0:T(8,128)(2,1)S(1)} %get-tuple-element.164), channel_id=1, source_target_pairs={{0,8},{4,12},{8,0},{12,4},{16,24},{20,28},{24,16},{28,20},{1,9},{5... | collective-permute-start | bytes 589832 | tf_op jit(solution)/shard_map/ppermute | solution.py:43
  62.9 15.0 %collective-permute-start.12 = (bf16[128,768]{1,0:T(8,128)(2,1)}, bf16[128,768]{1,0:T(8,128)(2,1)}, u32[]{:S(2)}, u32[]{:S(2)}) collective-permute-start(bf16[128,768]{1,0:T(8,128)(2,1)} %fusion.46), channel_id=1, source_target_pairs={{0,2},{1,3},{2,0},{3,1},{4,6},{5,7},{6,4},{7,5},{8,10},{9,11},{10,... | collective-permute-start | bytes 589832 | tf_op jit(solution)/shard_map/ppermute | solution.py:37
  64.5 14.9 %collective-permute-start.16 = (bf16[4,96,768]{2,1,0:T(8,128)(2,1)S(1)}, bf16[4,96,768]{2,1,0:T(8,128)(2,1)S(1)}, u32[]{:S(2)}, u32[]{:S(2)}) collective-permute-start(bf16[4,96,768]{2,1,0:T(8,128)(2,1)S(1)} %pad_maximum_fusion.4.rest_0_), channel_id=1, source_target_pairs={{0,4},{4,0},{8,12},{12,8},{16,20},{20,16},{24,28},{28,24},{1,5},{5... | collective-permute-start | bytes 1769480 | tf_op jit(solution)/shard_map/ppermute | solution.py:49
  77.3 17.4 %collective-permute-start.21 = (bf16[4,96,768]{2,1,0:T(8,128)(2,1)S(1)}, bf16[4,96,768]{2,1,0:T(8,128)(2,1)S(1)}, u32[]{:S(2)}, u32[]{:S(2)}) collective-permute-start(bf16[4,96,768]{2,1,0:T(8,128)(2,1)S(1)} %slice.389.rest_2_), channel_id=1, source_target_pairs={{0,4},{4,0},{8,12},{12,8},{16,20},{20,16},{24,28},{28,24},{1,5},{5... | collective-permute-start | bytes 1769480 | tf_op jit(solution)/shard_map/ppermute | solution.py:49
  79.5 6.2 %collective-permute-start.19 = (bf16[32,768]{1,0:T(8,128)(2,1)S(1)}, bf16[32,768]{1,0:T(8,128)(2,1)S(1)}, u32[]{:S(2)}, u32[]{:S(2)}) collective-permute-start(bf16[32,768]{1,0:T(8,128)(2,1)S(1)} %get-tuple-element.191), channel_id=1, source_target_pairs={{0,24},{4,28},{8,16},{12,20},{16,8},{20,12},{24,0},{28,4},{1,25},{... | collective-permute-start | bytes 147464 | tf_op jit(solution)/shard_map/ppermute | solution.py:43
  81.8 5.5 %collective-permute-start.18 = (bf16[32,768]{1,0:T(8,128)(2,1)S(1)}, bf16[32,768]{1,0:T(8,128)(2,1)S(1)}, u32[]{:S(2)}, u32[]{:S(2)}) collective-permute-start(bf16[32,768]{1,0:T(8,128)(2,1)S(1)} %get-tuple-element.192), channel_id=1, source_target_pairs={{0,16},{4,20},{8,24},{12,28},{16,0},{20,4},{24,8},{28,12},{1,17},{... | collective-permute-start | bytes 147464 | tf_op jit(solution)/shard_map/ppermute | solution.py:43
  82.0 5.3 %collective-permute-start.17 = (bf16[32,768]{1,0:T(8,128)(2,1)S(1)}, bf16[32,768]{1,0:T(8,128)(2,1)S(1)}, u32[]{:S(2)}, u32[]{:S(2)}) collective-permute-start(bf16[32,768]{1,0:T(8,128)(2,1)S(1)} %get-tuple-element.193), channel_id=1, source_target_pairs={{0,8},{4,12},{8,0},{12,4},{16,24},{20,28},{24,16},{28,20},{1,9},{5... | collective-permute-start | bytes 147464 | tf_op jit(solution)/shard_map/ppermute | solution.py:43
  84.0 6.9 %collective-permute-start.23 = (bf16[128,768]{1,0:T(8,128)(2,1)S(1)}, bf16[128,768]{1,0:T(8,128)(2,1)S(1)}, u32[]{:S(2)}, u32[]{:S(2)}) collective-permute-start(bf16[128,768]{1,0:T(8,128)(2,1)S(1)} %bitcast.174), channel_id=1, source_target_pairs={{0,2},{1,3},{2,0},{3,1},{4,6},{5,7},{6,4},{7,5},{8,10},{9,11},{10,... | collective-permute-start | bytes 589832 | tf_op jit(solution)/shard_map/ppermute | solution.py:37
  87.4 6.6 %collective-permute-start.20 = (bf16[128,768]{1,0:T(8,128)(2,1)S(1)}, bf16[128,768]{1,0:T(8,128)(2,1)S(1)}, u32[]{:S(2)}, u32[]{:S(2)}) collective-permute-start(bf16[128,768]{1,0:T(8,128)(2,1)S(1)} %get-tuple-element.189.own_ref), channel_id=1, source_target_pairs={{0,2},{1,3},{2,0},{3,1},{4,6},{5,7},{6,4},{7,5},{8,10},{9,11},{10,... | collective-permute-start | bytes 589832 | tf_op jit(solution)/shard_map/ppermute | solution.py:37
  91.7 6.9 %collective-permute-start.24 = (bf16[2,128,768]{2,1,0:T(8,128)(2,1)}, bf16[2,128,768]{2,1,0:T(8,128)(2,1)}, u32[]{:S(2)}, u32[]{:S(2)}) collective-permute-start(bf16[2,128,768]{2,1,0:T(8,128)(2,1)} %pad_maximum_fusion.9), channel_id=1, source_target_pairs={{0,1},{1,0},{2,3},{3,2},{4,5},{5,4},{6,7},{7,6},{8,9},{9,8},{10,11... | collective-permute-start | bytes 1179656 | tf_op jit(solution)/shard_map/ppermute | solution.py:37
  95.6 3.0 %collective-permute-start.22 = (bf16[2,128,768]{2,1,0:T(8,128)(2,1)}, bf16[2,128,768]{2,1,0:T(8,128)(2,1)}, u32[]{:S(2)}, u32[]{:S(2)}) collective-permute-start(bf16[2,128,768]{2,1,0:T(8,128)(2,1)} %pad_maximum_fusion.8), channel_id=1, source_target_pairs={{0,1},{1,0},{2,3},{3,2},{4,5},{5,4},{6,7},{7,6},{8,9},{9,8},{10,11... | collective-permute-start | bytes 1179656 | tf_op jit(solution)/shard_map/ppermute | solution.py:37
  107.3 4.8 %collective-permute-start.25 = (bf16[2,128,1536]{2,1,0:T(8,128)(2,1)}, bf16[2,128,1536]{2,1,0:T(8,128)(2,1)S(1)}, u32[]{:S(2)}, u32[]{:S(2)}) collective-permute-start(bf16[2,128,1536]{2,1,0:T(8,128)(2,1)} %get-tuple-element.60), channel_id=1, source_target_pairs={{0,1},{1,0},{2,3},{3,2},{4,5},{5,4},{6,7},{7,6},{8,9},{9,8},{10,11... | collective-permute-start | bytes 2359304 | tf_op jit(solution)/shard_map/ppermute | solution.py:37
  110.8 15.3 %collective-permute-start.27 = (bf16[4,96,768]{2,1,0:T(8,128)(2,1)S(1)}, bf16[4,96,768]{2,1,0:T(8,128)(2,1)S(1)}, u32[]{:S(2)}, u32[]{:S(2)}) collective-permute-start(bf16[4,96,768]{2,1,0:T(8,128)(2,1)S(1)} %slice_bitcast_fusion), channel_id=1, source_target_pairs={{0,4},{4,0},{8,12},{12,8},{16,20},{20,16},{24,28},{28,24},{1,5},{5... | collective-permute-start | bytes 1769480 | tf_op jit(solution)/shard_map/ppermute | solution.py:49
  112.4 13.9 %collective-permute-start.26 = (bf16[128,1536]{1,0:T(8,128)(2,1)S(1)}, bf16[128,1536]{1,0:T(8,128)(2,1)S(1)}, u32[]{:S(2)}, u32[]{:S(2)}) collective-permute-start(bf16[128,1536]{1,0:T(8,128)(2,1)S(1)} %fusion.36), channel_id=1, source_target_pairs={{0,2},{1,3},{2,0},{3,1},{4,6},{5,7},{6,4},{7,5},{8,10},{9,11},{10,... | collective-permute-start | bytes 1179656 | tf_op jit(solution)/shard_map/ppermute | solution.py:37
  126.5 7.6 %collective-permute-start.30 = (bf16[32,1536]{1,0:T(8,128)(2,1)S(1)}, bf16[32,1536]{1,0:T(8,128)(2,1)S(1)}, u32[]{:S(2)}, u32[]{:S(2)}) collective-permute-start(bf16[32,1536]{1,0:T(8,128)(2,1)S(1)} %get-tuple-element.182), channel_id=1, source_target_pairs={{0,24},{4,28},{8,16},{12,20},{16,8},{20,12},{24,0},{28,4},{1,25},{... | collective-permute-start | bytes 294920 | tf_op jit(solution)/shard_map/ppermute | solution.py:43
  128.8 8.2 %collective-permute-start.29 = (bf16[32,1536]{1,0:T(8,128)(2,1)S(1)}, bf16[32,1536]{1,0:T(8,128)(2,1)S(1)}, u32[]{:S(2)}, u32[]{:S(2)}) collective-permute-start(bf16[32,1536]{1,0:T(8,128)(2,1)S(1)} %get-tuple-element.183), channel_id=1, source_target_pairs={{0,16},{4,20},{8,24},{12,28},{16,0},{20,4},{24,8},{28,12},{1,17},{... | collective-permute-start | bytes 294920 | tf_op jit(solution)/shard_map/ppermute | solution.py:43
  128.8 8.2 %collective-permute-start.28 = (bf16[32,1536]{1,0:T(8,128)(2,1)S(1)}, bf16[32,1536]{1,0:T(8,128)(2,1)S(1)}, u32[]{:S(2)}, u32[]{:S(2)}) collective-permute-start(bf16[32,1536]{1,0:T(8,128)(2,1)S(1)} %get-tuple-element.184), channel_id=1, source_target_pairs={{0,8},{4,12},{8,0},{12,4},{16,24},{20,28},{24,16},{28,20},{1,9},{5... | collective-permute-start | bytes 294920 | tf_op jit(solution)/shard_map/ppermute | solution.py:43
  131.0 13.6 %collective-permute-start.32 = (bf16[4,96,768]{2,1,0:T(8,128)(2,1)S(1)}, bf16[4,96,768]{2,1,0:T(8,128)(2,1)S(1)}, u32[]{:S(2)}, u32[]{:S(2)}) collective-permute-start(bf16[4,96,768]{2,1,0:T(8,128)(2,1)S(1)} %slice_bitcast_fusion.2), channel_id=1, source_target_pairs={{0,4},{4,0},{8,12},{12,8},{16,20},{20,16},{24,28},{28,24},{1,5},{5... | collective-permute-start | bytes 1769480 | tf_op jit(solution)/shard_map/ppermute | solution.py:49
  137.9 6.6 %collective-permute-start.31 = (bf16[128,768]{1,0:T(8,128)(2,1)S(1)}, bf16[128,768]{1,0:T(8,128)(2,1)S(1)}, u32[]{:S(2)}, u32[]{:S(2)}) collective-permute-start(bf16[128,768]{1,0:T(8,128)(2,1)S(1)} %add_convert_fusion.own_ref), channel_id=1, source_target_pairs={{0,2},{1,3},{2,0},{3,1},{4,6},{5,7},{6,4},{7,5},{8,10},{9,11},{10,... | collective-permute-start | bytes 589832 | tf_op jit(solution)/shard_map/ppermute | solution.py:37
  144.7 4.8 %collective-permute-start.33 = (bf16[2,128,768]{2,1,0:T(8,128)(2,1)S(1)}, bf16[2,128,768]{2,1,0:T(8,128)(2,1)S(1)}, u32[]{:S(2)}, u32[]{:S(2)}) collective-permute-start(bf16[2,128,768]{2,1,0:T(8,128)(2,1)S(1)} %pad_maximum_fusion.10), channel_id=1, source_target_pairs={{0,1},{1,0},{2,3},{3,2},{4,5},{5,4},{6,7},{7,6},{8,9},{9,8},{10,11... | collective-permute-start | bytes 1179656 | tf_op jit(solution)/shard_map/ppermute | solution.py:37
  145.0 16.9 %collective-permute-start.37 = (bf16[2,96,768]{2,1,0:T(8,128)(2,1)S(1)}, bf16[2,96,768]{2,1,0:T(8,128)(2,1)S(1)}, u32[]{:S(2)}, u32[]{:S(2)}) collective-permute-start(bf16[2,96,768]{2,1,0:T(8,128)(2,1)S(1)} %get-tuple-element.156), channel_id=1, source_target_pairs={{0,16},{4,20},{8,24},{12,28},{16,0},{20,4},{24,8},{28,12},{1,17},{... | collective-permute-start | bytes 884744 | tf_op jit(solution)/shard_map/ppermute | solution.py:43
  146.1 15.9 %collective-permute-start.36 = (bf16[2,96,768]{2,1,0:T(8,128)(2,1)S(1)}, bf16[2,96,768]{2,1,0:T(8,128)(2,1)S(1)}, u32[]{:S(2)}, u32[]{:S(2)}) collective-permute-start(bf16[2,96,768]{2,1,0:T(8,128)(2,1)S(1)} %get-tuple-element.157), channel_id=1, source_target_pairs={{0,8},{4,12},{8,0},{12,4},{16,24},{20,28},{24,16},{28,20},{1,9},{5... | collective-permute-start | bytes 884744 | tf_op jit(solution)/shard_map/ppermute | solution.py:43
  147.9 20.0 %collective-permute-start.38 = (bf16[2,96,768]{2,1,0:T(8,128)(2,1)S(1)}, bf16[2,96,768]{2,1,0:T(8,128)(2,1)S(1)}, u32[]{:S(2)}, u32[]{:S(2)}) collective-permute-start(bf16[2,96,768]{2,1,0:T(8,128)(2,1)S(1)} %slice_bitcast_fusion.12), channel_id=1, source_target_pairs={{0,24},{4,28},{8,16},{12,20},{16,8},{20,12},{24,0},{28,4},{1,25},{... | collective-permute-start | bytes 884744 | tf_op jit(solution)/shard_map/ppermute | solution.py:43
  149.6 18.3 %collective-permute-start.34 = (bf16[128,768]{1,0:T(8,128)(2,1)S(1)}, bf16[128,768]{1,0:T(8,128)(2,1)S(1)}, u32[]{:S(2)}, u32[]{:S(2)}) collective-permute-start(bf16[128,768]{1,0:T(8,128)(2,1)S(1)} %get-tuple-element.68), channel_id=1, source_target_pairs={{0,2},{1,3},{2,0},{3,1},{4,6},{5,7},{6,4},{7,5},{8,10},{9,11},{10,... | collective-permute-start | bytes 589832 | tf_op jit(solution)/shard_map/ppermute | solution.py:37
  169.4 22.2 %collective-permute-start.35 = (bf16[2,128,768]{2,1,0:T(8,128)(2,1)}, bf16[2,128,768]{2,1,0:T(8,128)(2,1)}, u32[]{:S(2)}, u32[]{:S(2)}) collective-permute-start(bf16[2,128,768]{2,1,0:T(8,128)(2,1)} %pad_maximum_fusion.11), channel_id=1, source_target_pairs={{0,1},{1,0},{2,3},{3,2},{4,5},{5,4},{6,7},{7,6},{8,9},{9,8},{10,11... | collective-permute-start | bytes 1179656 | tf_op jit(solution)/shard_map/ppermute | solution.py:37
  170.0 3.9 %collective-permute-start.43 = (f32[8,768]{1,0:T(8,128)S(1)}, f32[8,768]{1,0:T(8,128)S(1)}, u32[]{:S(2)}, u32[]{:S(2)}) collective-permute-start(f32[8,768]{1,0:T(8,128)S(1)} %concatenate.55), channel_id=1, source_target_pairs={{0,4},{4,0},{8,12},{12,8},{16,20},{20,16},{24,28},{28,24},{1,5},{5... | collective-permute-start | bytes 73736 | tf_op jit(solution)/shard_map/ppermute | solution.py:49
  171.4 9.2 %collective-permute-start.41 = (bf16[2,96,768]{2,1,0:T(8,128)(2,1)S(1)}, bf16[2,96,768]{2,1,0:T(8,128)(2,1)S(1)}, u32[]{:S(2)}, u32[]{:S(2)}) collective-permute-start(bf16[2,96,768]{2,1,0:T(8,128)(2,1)S(1)} %slice_bitcast_fusion.11), channel_id=1, source_target_pairs={{0,4},{4,0},{8,12},{12,8},{16,20},{20,16},{24,28},{28,24},{1,5},{5... | collective-permute-start | bytes 884744 | tf_op jit(solution)/shard_map/ppermute | solution.py:49
  172.2 18.3 %collective-permute-start.39 = (bf16[2,128,768]{2,1,0:T(8,128)(2,1)}, bf16[2,128,768]{2,1,0:T(8,128)(2,1)S(1)}, u32[]{:S(2)}, u32[]{:S(2)}) collective-permute-start(bf16[2,128,768]{2,1,0:T(8,128)(2,1)} %copy-done.7), channel_id=1, source_target_pairs={{0,1},{1,0},{2,3},{3,2},{4,5},{5,4},{6,7},{7,6},{8,9},{9,8},{10,11... | collective-permute-start | bytes 1179656 | tf_op jit(solution)/shard_map/ppermute | solution.py:37
  175.1 5.0 %collective-permute-start.45 = (f32[8,768]{1,0:T(8,128)S(1)}, f32[8,768]{1,0:T(8,128)S(1)}, u32[]{:S(2)}, u32[]{:S(2)}) collective-permute-start(f32[8,768]{1,0:T(8,128)S(1)} %add.205), channel_id=1, source_target_pairs={{0,2},{1,3},{2,0},{3,1},{4,6},{5,7},{6,4},{7,5},{8,10},{9,11},{10,... | collective-permute-start | bytes 73736 | tf_op jit(solution)/shard_map/ppermute | solution.py:37
  180.8 12.8 %collective-permute-start.47 = (bf16[104,768]{1,0:T(8,128)(2,1)S(1)}, bf16[104,768]{1,0:T(8,128)(2,1)S(1)}, u32[]{:S(2)}, u32[]{:S(2)}) collective-permute-start(bf16[104,768]{1,0:T(8,128)(2,1)S(1)} %get-tuple-element.194), channel_id=1, source_target_pairs={{0,24},{4,28},{8,16},{12,20},{16,8},{20,12},{24,0},{28,4},{1,25},{... | collective-permute-start | bytes 479240 | tf_op jit(solution)/shard_map/ppermute | solution.py:43
  183.1 16.2 %collective-permute-start.46 = (bf16[104,768]{1,0:T(8,128)(2,1)S(1)}, bf16[104,768]{1,0:T(8,128)(2,1)S(1)}, u32[]{:S(2)}, u32[]{:S(2)}) collective-permute-start(bf16[104,768]{1,0:T(8,128)(2,1)S(1)} %get-tuple-element.195), channel_id=1, source_target_pairs={{0,16},{4,20},{8,24},{12,28},{16,0},{20,4},{24,8},{28,12},{1,17},{... | collective-permute-start | bytes 479240 | tf_op jit(solution)/shard_map/ppermute | solution.py:43
  189.1 10.2 %collective-permute-start.42 = (bf16[2,96,768]{2,1,0:T(8,128)(2,1)S(1)}, bf16[2,96,768]{2,1,0:T(8,128)(2,1)S(1)}, u32[]{:S(2)}, u32[]{:S(2)}) collective-permute-start(bf16[2,96,768]{2,1,0:T(8,128)(2,1)S(1)} %get-tuple-element.167), channel_id=1, source_target_pairs={{0,4},{4,0},{8,12},{12,8},{16,20},{20,16},{24,28},{28,24},{1,5},{5... | collective-permute-start | bytes 884744 | tf_op jit(solution)/shard_map/ppermute | solution.py:49
  190.6 8.9 %collective-permute-start.40 = (bf16[128,768]{1,0:T(8,128)(2,1)S(1)}, bf16[128,768]{1,0:T(8,128)(2,1)S(1)}, u32[]{:S(2)}, u32[]{:S(2)}) collective-permute-start(bf16[128,768]{1,0:T(8,128)(2,1)S(1)} %fusion.47), channel_id=1, source_target_pairs={{0,2},{1,3},{2,0},{3,1},{4,6},{5,7},{6,4},{7,5},{8,10},{9,11},{10,... | collective-permute-start | bytes 589832 | tf_op jit(solution)/shard_map/ppermute | solution.py:37
  199.4 5.3 %collective-permute-start.48 = (bf16[104,768]{1,0:T(8,128)(2,1)S(1)}, bf16[104,768]{1,0:T(8,128)(2,1)S(1)}, u32[]{:S(2)}, u32[]{:S(2)}) collective-permute-start(bf16[104,768]{1,0:T(8,128)(2,1)S(1)} %pad_maximum_fusion.12), channel_id=1, source_target_pairs={{0,8},{4,12},{8,0},{12,4},{16,24},{20,28},{24,16},{28,20},{1,9},{5... | collective-permute-start | bytes 479240 | tf_op jit(solution)/shard_map/ppermute | solution.py:43
  (38 other events, 251.5 us)

commit v3 on v2

--- a/solution.py
+++ b/solution.py
@@ -136,11 +136,23 @@
         target[block(at, ROWS), :] = rows
 
 
-def place_weight(target, refs, at_ref, local):
-    z, r, R = at_ref[0], at_ref[1], len(refs)
+def place_weight(target, refs, at_ref):
+    pieces = []
+    for ref in refs:
+        pieces += [ref] if len(ref.shape) == 2 else [ref.at[i] for i in range(ref.shape[0])]
+    z, r, R = at_ref[0], at_ref[1], len(pieces) // E
+    local = D // len(pieces)
     for c in range(R):
         for d in range(E):
-            target[block((z ^ d) * R + (r ^ c), local), :] = refs[c][d, :local, :]
+            at = block((z ^ d) * R + (r ^ c), local)
+            target[at, :] = pieces[c * E + d][:local, :]
+
+
+def load_weight(target, refs, at_ref):
+    if refs[0].shape == target.shape:
+        target[...] = refs[0][...]
+    else:
+        place_weight(target, refs, at_ref)
 
 
 def send_rows(source, out_ref, at_ref):
@@ -165,10 +177,7 @@
     refs, rest = rest[:pieces], rest[pieces:]
     normed_ref, qkv_ref, probs_ref, heads_ref, kept_ref, sent_ref, tokens_ref, weight_ref = rest
     t, length = at_ref[2], at_ref[3]
-    if pieces == 1:
-        weight_ref[...] = refs[0][...]
-    else:
-        place_weight(weight_ref, refs, at_ref, D // (pieces * E))
+    load_weight(weight_ref, refs, at_ref)
     place_rows(tokens_ref, own_ref, far_ref, near_ref, t)
     inputs = tokens_ref[...].astype(F32)
     normed_ref[...] = (inputs * norm_scale(inputs) * gain_ref[...]).astype(BF)
@@ -283,12 +292,8 @@
 ):
     in_refs, out_refs, rest = rest[:pieces], rest[pieces : 2 * pieces], rest[2 * pieces :]
     buffer_ref, grad_ref, activation_ref, grad_pre_ref, kept_ref, sent_ref, in_ref, out_ref = rest
-    if pieces == 1:
-        in_ref[...] = in_refs[0][...]
-        out_ref[...] = out_refs[0][...]
-    else:
-        place_weight(in_ref, in_refs, at_ref, D // (pieces * E))
-        place_weight(out_ref, out_refs, at_ref, D // (pieces * E))
+    load_weight(in_ref, in_refs, at_ref)
+    load_weight(out_ref, out_refs, at_ref)
     place_rows(buffer_ref, own_ref, far_ref, near_ref, None)
     place_rows(grad_ref, own_grad_ref, far_grad_ref, near_grad_ref, None)
     logits = mm(buffer_ref[...], router_ref[...], 1, 0)
@@ -360,8 +365,12 @@
 
     def whole(parts):
         if aligned:
-            return [jnp.stack(part) if isinstance(part, list) else part for part in parts]
-        rows = [jnp.stack(natural(list(part), z)) for part in parts]
+            return parts
+        pieces = []
+        for part in parts:
+            pieces += [part] if part.ndim == 2 else list(part)
+        pieces = [piece[:local] for piece in pieces]
+        rows = [jnp.stack(natural(pieces[c * E : (c + 1) * E], z)) for c in range(R)]
         return [jnp.stack(natural(rows, r), axis=1).reshape(D, -1)]
 
     def blocks_to_send(grad):
@@ -379,11 +388,11 @@
         [jnp.concatenate([w_qkv.reshape(local, 3 * LW), w_out_attn], axis=1), line], axis=0
     )
     packed_z = [packed] + [over_z(packed, d) for d in range(1, E)]
-    packed_r = [
-        [over_r(packed, c), *over_r(jnp.stack([part[:local] for part in packed_z[1:]]), c)]
-        for c in range(1, R)
-    ]
-    packed_all = [[part[:local] for part in parts] for parts in [packed_z] + packed_r]
+    packed_own = [over_r(packed, c) for c in range(1, R)]
+    packed_rest = after(jnp.stack([part[:local] for part in packed_z[1:]]), packed_own)
+    packed_all = list(packed_z)
+    for c in range(1, R):
+        packed_all += [packed_own[c - 1], over_r(packed_rest, c)]
     lines = jnp.stack(natural([part[local] for part in packed_z], z))
     lines = [lines] + [over_r(lines, c) for c in range(1, R)]
     lines = jnp.stack(natural(lines, r), axis=1).reshape(n, -1)
@@ -422,15 +431,17 @@
 
     grad_output = mm(to_slots[:ROWS], cotangent_all, 1, 0)
     masked = jnp.where(sent_own[:, None], grad_output, 0).astype(BF).reshape(E, SUB, D)
-    in_rows = after(w_in, packed_z)
-    in_columns = jnp.stack(deliver_z(jnp.stack([pick(in_rows, z ^ d, 1) for d in range(E)])))
-    out_rows = after(w_out, in_columns)
-    out_rows = jnp.stack([pick(out_rows, z ^ d, 1) for d in range(E)])
-    out_z = jnp.stack(deliver_z(jnp.concatenate([out_rows, masked], axis=1)))
-    out_columns, cotangent_z = out_z[:, :local], out_z[:, local:].reshape(E * SUB, D)
-    in_weight = whole([in_columns] + [over_r(in_columns, c) for c in range(1, R)])
-    out_weight = whole([out_columns] + [over_r(out_columns, c) for c in range(1, R)])
-    cotangent_parts = gather_t(cotangent_z)
+    in_rows = jnp.stack([pick(w_in, z ^ d, 1) for d in range(E)])
+    out_rows = jnp.stack([pick(w_out, z ^ d, 1) for d in range(E)])
+    out_rows = jnp.concatenate([out_rows, masked], axis=1)
+    in_columns = jnp.stack(deliver_z(after(in_rows, packed_z, packed_own, both_parts[1])))
+    in_swapped = [over_r(in_columns, c) for c in range(1, R)]
+    out_z = deliver_z(after(out_rows, in_columns))
+    out_columns = jnp.stack([part[:local] for part in out_z])
+    out_swapped = [over_r(out_columns, c) for c in range(1, R)]
+    in_weight = whole([in_columns] + in_swapped)
+    out_weight = whole([out_columns] + out_swapped)
+    router = jnp.pad(router_rows.T, ((0, 0), (0, 128 - E)))
 
     table_rows = lax.dynamic_slice_in_dim(table_flat.astype(F32).reshape(H, NB), t * LH, LH, 0)
     bucket_table = (buckets[None, :] == jnp.arange(NB, dtype=jnp.int32)[:, None]).astype(F32)
@@ -459,18 +470,21 @@
         *token_parts,
         gain_one,
         reversed_rel,
-        after(to_slots, in_columns),
+        after(to_slots, in_columns, out_rows, router, chosen_own, from_slots_own, gain_two),
         *packed_refs,
     )
-    normed_all, qkv, probs, heads_all, kept, given, tokens_all, attention_weight = forward
+    normed_all, qkv, probs, heads_all, kept, given, tokens_all, attention_weight = after(
+        forward, in_swapped, out_z
+    )
+    cotangent_z = jnp.concatenate([part[local:] for part in out_z], axis=0)
+    cotangent_parts = gather_t(cotangent_z)
     attended = scatter_t(kept, given)
     inputs = mm(to_slots[:ROWS], tokens_all, 1, 0)
     middle = inputs + attended
     scale_two = norm_scale(middle)
     normed_two = (middle * scale_two * gain_two).astype(BF)
 
-    buffer_parts = gather_t(dispatch_z(after(normed_two, out_z, in_weight)), out_weight)
-    router = jnp.pad(router_rows.T, ((0, 0), (0, 128 - E)))
+    buffer_parts = gather_t(dispatch_z(normed_two), out_weight)
     buffer, grad_expert, activation, grad_pre, kept, given = call(
         functools.partial(expert_layer, pieces=len(in_weight)),
         "expert_layer",
@@ -565,10 +579,13 @@
         heads_all,
     )
     expert_sums = jnp.stack([in_sums, out_sums], axis=1)
-    delivered = deliver_z(after(expert_sums, grad_middle))
-    late_terms, kept, given, grad_gain_one, grad_rel, delivered = after(
-        (late_terms, kept, given, grad_gain_one, grad_rel, delivered), layer_parts[1]
-    )
+    expert_sums = after(expert_sums, grad_middle)
+    delivered = [expert_sums[0], over_z(expert_sums[1], 1), over_z(expert_sums[2], 2)]
+    late_terms, kept, given, grad_gain_one, grad_rel, delivered, last = after(
+        (late_terms, kept, given, grad_gain_one, grad_rel, delivered, expert_sums[3]),
+        layer_parts[1],
+    )
+    delivered = delivered + [over_z(last, 3)]
     late_terms = blocks_to_send(late_terms)
     far_sums = add(swap_r(late_terms[:, 2:])).astype(BF)
     near_terms = swap_r(after(late_terms[:, :2], far_sums))
@@ -603,7 +620,7 @@
     )
     low = small.astype(BF)
     far = [over_z(jnp.concatenate([far_sums[d - 2], low], axis=0), d) for d in (2, 3)]
-    near_sums = add(after(near_terms, far))
+    near_sums = add(after(near_terms, far, delivered))
     near = over_z(jnp.concatenate([near_sums[1].astype(BF), low], axis=0), 1)
     late = jnp.concatenate([near_sums[0], small], axis=0)
     late = late + far[0].astype(F32) + far[1].astype(F32) + near.astype(F32)

time: 209 us -> 223 us (1.067)
  local copies, waits for them, and re-layouts: 26.9 us -> 39.8 us
  waiting for transfers between devices: 69.3 us -> 72.2 us
    ppermute x21, waiting for transfers between devices: 45.8 us -> 31.6 us  [over_z(): lax.ppermute(x, 'dp', [(i, (i // r ^ d) * r + i % r) for i in range(n)])]
    unnamed x81 -> x139, local copies, waits for them, and re-layouts: 14.2 us -> 27.1 us
    ppermute x18, waiting for transfers between devices: 10.5 us -> 21.7 us  [over_t(): return lax.ppermute(x, 'tensor', [(i, i ^ k) for i in range(T)])]
    ppermute x10, waiting for transfers between devices: 13 us -> 18.8 us  [over_r(): lax.ppermute(x, 'dp', [(i, i // r * r + (i % r ^ c)) for i in range(n)])]
    ppermute x18, starting transfers between devices: 13.2 us -> 8.57 us  [over_t(): return lax.ppermute(x, 'tensor', [(i, i ^ k) for i in range(T)])]
    ppermute x21, starting transfers between devices: 35 us -> 39.1 us  [over_z(): lax.ppermute(x, 'dp', [(i, (i // r ^ d) * r + i % r) for i in range(n)])]
    dynamic_slice x0 -> x1, local copies, waits for them, and re-layouts: none -> 3.24 us  [pick(): return lax.dynamic_index_in_dim(x, index, axis, keepdims=False)]
    another operation x5 -> x3, other arithmetic: 3.59 us -> 1.35 us  [the longest x1 1.2 us: body(): jnp.stack(deliver_z(after(in_rows, packed_z, packed_own, both_parts[1])))]
  transfers between devices with their start and end apart: 49 -> 49, of which waited for: 21 -> 24; matrix products, arithmetic and copies ran while one was open for 16% -> 17% of each run, Pallas kernels for 6% -> 9%
where the time goes in v3:
time: 223 us; the launch traced here: 222 us
  waiting for transfers between devices  72.2 us (32%)
  starting transfers between devices  61.3 us (27%)
  local copies, waits for them, and re-layouts  39.8 us (18%)
  Pallas kernels  27.2 us (12%)
  other arithmetic  13.7 us (6%)
  matrix products  5.72 us (3%)
  between operations  2.44 us (1%)
    ppermute x21, starting transfers between devices, over_z(): lax.ppermute(x, 'dp', [(i, (i // r ^ d) * r + i % r) for i in range(n)])  39.1 us
    ppermute x21, waiting for transfers between devices, over_z(): lax.ppermute(x, 'dp', [(i, (i // r ^ d) * r + i % r) for i in range(n)])  31.6 us
    pallas_call x5, Pallas kernels, call(): pl.pallas_call(kernel, out_shape=[jax.ShapeDtypeStruct(shape, kind) for s...  27.2 us
    unnamed x139, local copies, waits for them, and re-layouts  27.1 us
    ppermute x18, waiting for transfers between devices, over_t(): return lax.ppermute(x, 'tensor', [(i, i ^ k) for i in range(T)])  21.7 us
    ppermute x10, waiting for transfers between devices, over_r(): lax.ppermute(x, 'dp', [(i, i // r * r + (i % r ^ c)) for i in range(n)])  18.8 us
    ppermute x10, starting transfers between devices, over_r(): lax.ppermute(x, 'dp', [(i, i // r * r + (i % r ^ c)) for i in range(n)])  13.7 us
    ppermute x18, starting transfers between devices, over_t(): return lax.ppermute(x, 'tensor', [(i, i ^ k) for i in range(T)])  8.57 us
  transfers between devices with their start and end apart: 49, of which 24 were waited for; matrix products, arithmetic and copies ran while one was open for 17% of the time, Pallas kernels for 9%

profile of v3, /device:TPU:0, one launch (start us, length us, event | category | flops | bytes accessed | tf_op | source)
XLA Modules:
  0.0 222.3 jit_solution(5300570945964895920)
XLA Ops:
  4.4 4.1 %collective-permute-start.3 = (bf16[97,768]{1,0:T(8,128)(2,1)S(1)}, bf16[97,768]{1,0:T(8,128)(2,1)S(1)}, u32[]{:S(2)}, u32[]{:S(2)}) collective-permute-start(bf16[97,768]{1,0:T(8,128)(2,1)S(1)} %pad_maximum_fusion.16.rest_0_), channel_id=1, source_target_pairs={{0,16},{4,20},{8,24},{12,28},{16,0},{20,4},{24,8},{28,12},{1,17},{... | collective-permute-start | bytes 446984 | tf_op jit(solution)/shard_map/ppermute | solution.py:43
  11.6 1.6 constant_dynamic-update-slice_fusion.1
  13.2 1.6 constant_dynamic-update-slice_fusion
  14.9 1.5 collective-permute-start
  18.9 3.2 %constant_dynamic-slice_fusion.5 = (bf16[96,1,768]{2,1,0:T(2,128)(2,1)S(1)}, bf16[96,1,768]{2,1,0:T(2,128)(2,1)}, bf16[96,1,768]{2,1,0:T(2,128)(2,1)}, bf16[96,1...) fusion(bf16[96,4,768]{2,1,0:T(4,128)(2,1)S(1)} %copy-done.26, ...), kind=kLoop, calls=%fused_computation.213 | loop fusion | bytes 2359312 | tf_op jit(solution)/shard_map/jit(dynamic_index_in_dim)/dynamic_slice | solution.py:78
  24.2 3.2 %reverse = f32[32,1024]{1,0:T(8,128)S(1)} reverse(f32[32,1024]{1,0:T(8,128)} %bitcast.210), dimensions={1} | reverse | bytes 262144
  28.2 1.6 copy.106
  33.5 1.5 collective-permute-start.10
  36.6 1.9 pad_maximum_fusion.1
  39.4 3.0 %collective-permute-start.9 = (bf16[96,768]{1,0:T(8,128)(2,1)}, bf16[96,768]{1,0:T(8,128)(2,1)S(1)}, u32[]{:S(2)}, u32[]{:S(2)}) collective-permute-start(bf16[96,768]{1,0:T(8,128)(2,1)} %get-tuple-element.191), channel_id=1, source_target_pairs={{0,24},{4,28},{8,16},{12,20},{16,8},{20,12},{24,0},{28,4},{1,25},{... | collective-permute-start | bytes 442376 | tf_op jit(solution)/shard_map/ppermute | solution.py:43
  45.7 2.5 %collective-permute-done.9 = bf16[96,768]{1,0:T(8,128)(2,1)S(1)} collective-permute-done((bf16[96,768]{1,0:T(8,128)(2,1)}, bf16[96,768]{1,0:T(8,128)(2,1)S(1)}, u32[]{:S(2)}, u32[]{:S(2)}) %collective-permute-start.9) | collective-permute-done | bytes 147488 | tf_op jit(solution)/shard_map/ppermute | solution.py:43
  48.2 8.4 %collective-permute-done.8 = bf16[96,768]{1,0:T(8,128)(2,1)S(1)} collective-permute-done((bf16[96,768]{1,0:T(8,128)(2,1)}, bf16[96,768]{1,0:T(8,128)(2,1)S(1)}, u32[]{:S(2)}, u32[]{:S(2)}) %collective-permute-start.8) | collective-permute-done | bytes 147488 | tf_op jit(solution)/shard_map/ppermute | solution.py:43
  61.4 3.0 %collective-permute-start.13 = (bf16[128,768]{1,0:T(8,128)(2,1)S(1)}, bf16[128,768]{1,0:T(8,128)(2,1)S(1)}, u32[]{:S(2)}, u32[]{:S(2)}) collective-permute-start(bf16[128,768]{1,0:T(8,128)(2,1)S(1)} %get-tuple-element.180), channel_id=1, source_target_pairs={{0,16},{4,20},{8,24},{12,28},{16,0},{20,4},{24,8},{28,12},{1,17},{... | collective-permute-start | bytes 589832 | tf_op jit(solution)/shard_map/ppermute | solution.py:43
  67.6 7.8 %attention_forward.1 = (bf16[512,768]{1,0:T(8,128)(2,1)S(1)}, bf16[512,576]{1,0:T(8,128)(2,1)S(1)}, f32[3,512,512]{2,1,0:T(8,128)}, bf16[512,192]{1,0:T(8,128)(2...) custom-call(s32[4]{0:T(128)S(1)} %pad_add_fusion.at_ref, ...), custom_call_target="tpu_custom_call" | custom-call | flops 12000000000 | bytes 2513408 | tf_op jit(solution)/shard_map/attention_forward/pallas_call | solution.py:115
  75.4 3.2 %collective-permute-done.13 = bf16[128,768]{1,0:T(8,128)(2,1)S(1)} collective-permute-done((bf16[128,768]{1,0:T(8,128)(2,1)S(1)}, bf16[128,768]{1,0:T(8,128)(2,1)S(1)}, u32[]{:S(2)}, u32[]{:S(2)}) %collective-permute-start.13) | collective-permute-done | bytes 196640 | tf_op jit(solution)/shard_map/ppermute | solution.py:43
  78.8 1.7 collective-permute-done.15
  81.3 1.6 collective-permute-start.21
  82.9 4.7 %collective-permute-done.16 = bf16[128,768]{1,0:T(8,128)(2,1)S(1)} collective-permute-done((bf16[128,768]{1,0:T(8,128)(2,1)S(1)}, bf16[128,768]{1,0:T(8,128)(2,1)S(1)}, u32[]{:S(2)}, u32[]{:S(2)}) %collective-permute-start.16) | collective-permute-done | bytes 196640 | tf_op jit(solution)/shard_map/ppermute | solution.py:37
  88.8 2.5 %collective-permute-start.19 = (bf16[32,768]{1,0:T(8,128)(2,1)S(1)}, bf16[32,768]{1,0:T(8,128)(2,1)S(1)}, u32[]{:S(2)}, u32[]{:S(2)}) collective-permute-start(bf16[32,768]{1,0:T(8,128)(2,1)S(1)} %get-tuple-element.214), channel_id=1, source_target_pairs={{0,24},{4,28},{8,16},{12,20},{16,8},{20,12},{24,0},{28,4},{1,25},{... | collective-permute-start | bytes 147464 | tf_op jit(solution)/shard_map/ppermute | solution.py:43
  91.3 2.2 collective-permute-start.18
  94.8 1.8 collective-permute-done.18
  98.2 2.2 %collective-permute-done.23.far_grad_ref = bf16[128,768]{1,0:T(8,128)(2,1)S(1)} collective-permute-done((bf16[128,768]{1,0:T(8,128)(2,1)S(1)}, bf16[128,768]{1,0:T(8,128)(2,1)S(1)}, u32[]{:S(2)}, u32[]{:S(2)}) %collective-permute-start.23) | collective-permute-done | bytes 196640 | tf_op jit(solution)/shard_map/ppermute | solution.py:37
  101.2 2.3 %collective-permute-done.20.far_ref = bf16[128,768]{1,0:T(8,128)(2,1)S(1)} collective-permute-done((bf16[128,768]{1,0:T(8,128)(2,1)S(1)}, bf16[128,768]{1,0:T(8,128)(2,1)S(1)}, u32[]{:S(2)}, u32[]{:S(2)}) %collective-permute-start.20) | collective-permute-done | bytes 196640 | tf_op jit(solution)/shard_map/ppermute | solution.py:37
  105.4 1.9 collective-permute-done.22.near_ref
  110.3 6.4 %expert_layer.1 = (bf16[512,768]{1,0:T(8,128)(2,1)S(1)}, bf16[512,768]{1,0:T(8,128)(2,1)S(1)}, bf16[512,768]{1,0:T(8,128)(2,1)}, bf16[512,768]{1,0:T(8,128)(2,1)...) custom-call(s32[4]{0:T(128)S(1)} %pad_add_fusion.at_ref, ...), custom_call_target="tpu_custom_call" | custom-call | flops 8000000000 | bytes 4128768 | tf_op jit(solution)/shard_map/expert_layer/pallas_call | solution.py:115
  119.9 1.6 collective-permute-start.27
  123.8 11.7 %collective-permute-done.27 = bf16[4,96,768]{2,1,0:T(8,128)(2,1)S(1)} collective-permute-done((bf16[4,96,768]{2,1,0:T(8,128)(2,1)S(1)}, bf16[4,96,768]{2,1,0:T(8,128)(2,1)S(1)}, u32[]{:S(2)}, u32[]{:S(2)}) %collective-permute-start.27) | collective-permute-done | bytes 589856 | tf_op jit(solution)/shard_map/ppermute | solution.py:49
  135.9 2.4 %collective-permute-start.30 = (bf16[32,1536]{1,0:T(8,128)(2,1)S(1)}, bf16[32,1536]{1,0:T(8,128)(2,1)S(1)}, u32[]{:S(2)}, u32[]{:S(2)}) collective-permute-start(bf16[32,1536]{1,0:T(8,128)(2,1)S(1)} %get-tuple-element.203), channel_id=1, source_target_pairs={{0,24},{4,28},{8,16},{12,20},{16,8},{20,12},{24,0},{28,4},{1,25},{... | collective-permute-start | bytes 294920 | tf_op jit(solution)/shard_map/ppermute | solution.py:43
  140.4 1.6 collective-permute-start.32
  143.4 4.6 %collective-permute-done.29 = bf16[32,1536]{1,0:T(8,128)(2,1)S(1)} collective-permute-done((bf16[32,1536]{1,0:T(8,128)(2,1)S(1)}, bf16[32,1536]{1,0:T(8,128)(2,1)S(1)}, u32[]{:S(2)}, u32[]{:S(2)}) %collective-permute-start.29) | collective-permute-done | bytes 98336 | tf_op jit(solution)/shard_map/ppermute | solution.py:43
  149.6 5.7 %collective-permute-done.31.far_ref = bf16[128,768]{1,0:T(8,128)(2,1)S(1)} collective-permute-done((bf16[128,768]{1,0:T(8,128)(2,1)S(1)}, bf16[128,768]{1,0:T(8,128)(2,1)S(1)}, u32[]{:S(2)}, u32[]{:S(2)}) %collective-permute-start.31) | collective-permute-done | bytes 196640 | tf_op jit(solution)/shard_map/ppermute | solution.py:37
  156.6 2.5 %collective-permute-start.37 = (bf16[2,96,768]{2,1,0:T(8,128)(2,1)S(1)}, bf16[2,96,768]{2,1,0:T(8,128)(2,1)S(1)}, u32[]{:S(2)}, u32[]{:S(2)}) collective-permute-start(bf16[2,96,768]{2,1,0:T(8,128)(2,1)S(1)} %get-tuple-element.174), channel_id=1, source_target_pairs={{0,16},{4,20},{8,24},{12,28},{16,0},{20,4},{24,8},{28,12},{1,17},{... | collective-permute-start | bytes 884744 | tf_op jit(solution)/shard_map/ppermute | solution.py:43
  160.4 10.0 %attention_backward.1 = (bf16[2,4,96,768]{3,2,1,0:T(8,128)(2,1)S(1)}, bf16[2,128,768]{2,1,0:T(8,128)(2,1)S(1)}, bf16[2,128,768]{2,1,0:T(8,128)(2,1)S(1)}, f32[1,768]{1,0:T(1,128)S(1)}, f32[3,1024]{1,0:T(4,128)S(1)}) custom-call(s32[4]{0:T(128)S(1)} %pad_add_fusion.at_ref, bf16[128,768]{1,0:T(8,128)(2,1)S(1)} %add_convert_fusion.own_ref, ...), custom_call_target="tpu_custom_call" | custom-call | flops 12000000000 | bytes 7995392 | tf_op jit(solution)/shard_map/attention_backward/pallas_call | solution.py:115
  174.4 1.6 collective-permute-start.42
  176.1 2.3 %collective-permute-done.42 = f32[8,768]{1,0:T(8,128)S(1)} collective-permute-done((f32[8,768]{1,0:T(8,128)S(1)}, f32[8,768]{1,0:T(8,128)S(1)}, u32[]{:S(2)}, u32[]{:S(2)}) %collective-permute-start.42) | collective-permute-done | bytes 24608 | tf_op jit(solution)/shard_map/ppermute | solution.py:49
  178.4 1.6 collective-permute-start.40
  181.2 2.0 collective-permute-start.47
  183.9 4.0 %collective-permute-done.40 = bf16[2,96,768]{2,1,0:T(8,128)(2,1)S(1)} collective-permute-done((bf16[2,96,768]{2,1,0:T(8,128)(2,1)S(1)}, bf16[2,96,768]{2,1,0:T(8,128)(2,1)S(1)}, u32[]{:S(2)}, u32[]{:S(2)}) %collective-permute-start.40) | collective-permute-done | bytes 294944 | tf_op jit(solution)/shard_map/ppermute | solution.py:49
  188.0 1.6 collective-permute-start.41
  190.0 2.1 collective-permute-done.47
  192.1 2.2 collective-permute-start.46
  194.6 1.8 copy.86
  196.5 1.8 copy.87
  198.4 2.3 %collective-permute-start.39 = (bf16[128,768]{1,0:T(8,128)(2,1)S(1)}, bf16[128,768]{1,0:T(8,128)(2,1)S(1)}, u32[]{:S(2)}, u32[]{:S(2)}) collective-permute-start(bf16[128,768]{1,0:T(8,128)(2,1)S(1)} %fusion.47), channel_id=1, source_target_pairs={{0,2},{1,3},{2,0},{3,1},{4,6},{5,7},{6,4},{7,5},{8,10},{9,11},{10,... | collective-permute-start | bytes 589832 | tf_op jit(solution)/shard_map/ppermute | solution.py:37
  201.7 2.6 %collective-permute-done.39 = bf16[128,768]{1,0:T(8,128)(2,1)S(1)} collective-permute-done((bf16[128,768]{1,0:T(8,128)(2,1)S(1)}, bf16[128,768]{1,0:T(8,128)(2,1)S(1)}, u32[]{:S(2)}, u32[]{:S(2)}) %collective-permute-start.39) | collective-permute-done | bytes 196640 | tf_op jit(solution)/shard_map/ppermute | solution.py:37
  204.5 2.6 %collective-permute-done.45 = bf16[104,768]{1,0:T(8,128)(2,1)S(1)} collective-permute-done((bf16[104,768]{1,0:T(8,128)(2,1)S(1)}, bf16[104,768]{1,0:T(8,128)(2,1)S(1)}, u32[]{:S(2)}, u32[]{:S(2)}) %collective-permute-start.45) | collective-permute-done | bytes 159776 | tf_op jit(solution)/shard_map/ppermute | solution.py:43
  207.3 8.1 %collective-permute-start.48 = (bf16[104,768]{1,0:T(8,128)(2,1)S(1)}, bf16[104,768]{1,0:T(8,128)(2,1)S(1)}, u32[]{:S(2)}, u32[]{:S(2)}) collective-permute-start(bf16[104,768]{1,0:T(8,128)(2,1)S(1)} %pad_maximum_fusion.11), channel_id=1, source_target_pairs={{0,8},{4,12},{8,0},{12,4},{16,24},{20,28},{24,16},{28,20},{1,9},{5... | collective-permute-start | bytes 479240 | tf_op jit(solution)/shard_map/ppermute | solution.py:43
  216.5 2.2 collective-permute-done.48
  (339 shorter events, 65.5 us)
Async XLA Ops:
  4.4 27.4 %collective-permute-start.3 = (bf16[97,768]{1,0:T(8,128)(2,1)S(1)}, bf16[97,768]{1,0:T(8,128)(2,1)S(1)}, u32[]{:S(2)}, u32[]{:S(2)}) collective-permute-start(bf16[97,768]{1,0:T(8,128)(2,1)S(1)} %pad_maximum_fusion.16.rest_0_), channel_id=1, source_target_pairs={{0,16},{4,20},{8,24},{12,28},{16,0},{20,4},{24,8},{28,12},{1,17},{... | collective-permute-start | bytes 446984 | tf_op jit(solution)/shard_map/ppermute | solution.py:43
  8.6 23.3 %collective-permute-start.2 = (bf16[97,768]{1,0:T(8,128)(2,1)S(1)}, bf16[97,768]{1,0:T(8,128)(2,1)S(1)}, u32[]{:S(2)}, u32[]{:S(2)}) collective-permute-start(bf16[97,768]{1,0:T(8,128)(2,1)S(1)} %pad_maximum_fusion.16.rest_0_), channel_id=1, source_target_pairs={{0,24},{4,28},{8,16},{12,20},{16,8},{20,12},{24,0},{28,4},{1,25},{... | collective-permute-start | bytes 446984 | tf_op jit(solution)/shard_map/ppermute | solution.py:43
  9.9 22.0 %collective-permute-start.4 = (bf16[97,768]{1,0:T(8,128)(2,1)S(1)}, bf16[97,768]{1,0:T(8,128)(2,1)S(1)}, u32[]{:S(2)}, u32[]{:S(2)}) collective-permute-start(bf16[97,768]{1,0:T(8,128)(2,1)S(1)} %pad_maximum_fusion.16.rest_0_), channel_id=1, source_target_pairs={{0,8},{4,12},{8,0},{12,4},{16,24},{20,28},{24,16},{28,20},{1,9},{5... | collective-permute-start | bytes 446984 | tf_op jit(solution)/shard_map/ppermute | solution.py:43
  10.1 23.4 %collective-permute-start.6 = (bf16[97,768]{1,0:T(8,128)(2,1)S(1)}, bf16[97,768]{1,0:T(8,128)(2,1)S(1)}, u32[]{:S(2)}, u32[]{:S(2)}) collective-permute-start(bf16[97,768]{1,0:T(8,128)(2,1)S(1)} %pad_maximum_fusion.16.rest_0_), channel_id=1, source_target_pairs={{0,4},{4,0},{8,12},{12,8},{16,20},{20,16},{24,28},{28,24},{1,5},{5... | collective-permute-start | bytes 446984 | tf_op jit(solution)/shard_map/ppermute | solution.py:49
  14.9 21.0 %collective-permute-start = (bf16[128,1536]{1,0:T(8,128)(2,1)}, bf16[128,1536]{1,0:T(8,128)(2,1)S(1)}, u32[]{:S(2)}, u32[]{:S(2)}) collective-permute-start(bf16[128,1536]{1,0:T(8,128)(2,1)} %constant_dynamic-update-slice_fusion), channel_id=1, source_target_pairs={{0,2},{1,3},{2,0},{3,1},{4,6},{5,7},{6,4},{7,5},{8,10},{9,11},{10,... | collective-permute-start | bytes 1179656 | tf_op jit(solution)/shard_map/ppermute | solution.py:37
  32.0 3.7 %collective-permute-start.5 = (bf16[4,768]{1,0:T(4,128)(2,1)S(1)}, bf16[4,768]{1,0:T(4,128)(2,1)S(1)}, u32[]{:S(2)}, u32[]{:S(2)}) collective-permute-start(bf16[4,768]{1,0:T(4,128)(2,1)S(1)} %pad_maximum_fusion.18), channel_id=1, source_target_pairs={{0,4},{4,0},{8,12},{12,8},{16,20},{20,16},{24,28},{28,24},{1,5},{5... | collective-permute-start | bytes 18440 | tf_op jit(solution)/shard_map/ppermute | solution.py:49
  33.5 32.3 %collective-permute-start.10 = (bf16[3,96,768]{2,1,0:T(8,128)(2,1)}, bf16[3,96,768]{2,1,0:T(8,128)(2,1)S(1)}, u32[]{:S(2)}, u32[]{:S(2)}) collective-permute-start(bf16[3,96,768]{2,1,0:T(8,128)(2,1)} %pad_maximum_fusion.6), channel_id=1, source_target_pairs={{0,4},{4,0},{8,12},{12,8},{16,20},{20,16},{24,28},{28,24},{1,5},{5... | collective-permute-start | bytes 1327112 | tf_op jit(solution)/shard_map/ppermute | solution.py:49
  38.5 20.5 %collective-permute-start.1 = (bf16[2,128,1536]{2,1,0:T(8,128)(2,1)}, bf16[2,128,1536]{2,1,0:T(8,128)(2,1)S(1)}, u32[]{:S(2)}, u32[]{:S(2)}) collective-permute-start(bf16[2,128,1536]{2,1,0:T(8,128)(2,1)} %pad_maximum_fusion.1), channel_id=1, source_target_pairs={{0,1},{1,0},{2,3},{3,2},{4,5},{5,4},{6,7},{7,6},{8,9},{9,8},{10,11... | collective-permute-start | bytes 2359304 | tf_op jit(solution)/shard_map/ppermute | solution.py:37
  39.4 8.8 %collective-permute-start.9 = (bf16[96,768]{1,0:T(8,128)(2,1)}, bf16[96,768]{1,0:T(8,128)(2,1)S(1)}, u32[]{:S(2)}, u32[]{:S(2)}) collective-permute-start(bf16[96,768]{1,0:T(8,128)(2,1)} %get-tuple-element.191), channel_id=1, source_target_pairs={{0,24},{4,28},{8,16},{12,20},{16,8},{20,12},{24,0},{28,4},{1,25},{... | collective-permute-start | bytes 442376 | tf_op jit(solution)/shard_map/ppermute | solution.py:43
  42.3 14.3 %collective-permute-start.8 = (bf16[96,768]{1,0:T(8,128)(2,1)}, bf16[96,768]{1,0:T(8,128)(2,1)S(1)}, u32[]{:S(2)}, u32[]{:S(2)}) collective-permute-start(bf16[96,768]{1,0:T(8,128)(2,1)} %get-tuple-element.192), channel_id=1, source_target_pairs={{0,16},{4,20},{8,24},{12,28},{16,0},{20,4},{24,8},{28,12},{1,17},{... | collective-permute-start | bytes 442376 | tf_op jit(solution)/shard_map/ppermute | solution.py:43
  42.7 13.9 %collective-permute-start.7 = (bf16[96,768]{1,0:T(8,128)(2,1)}, bf16[96,768]{1,0:T(8,128)(2,1)}, u32[]{:S(2)}, u32[]{:S(2)}) collective-permute-start(bf16[96,768]{1,0:T(8,128)(2,1)} %get-tuple-element.193), channel_id=1, source_target_pairs={{0,8},{4,12},{8,0},{12,4},{16,24},{20,28},{24,16},{28,20},{1,9},{5... | collective-permute-start | bytes 442376 | tf_op jit(solution)/shard_map/ppermute | solution.py:43
  58.5 16.9 %collective-permute-start.11 = (bf16[4,96,768]{2,1,0:T(8,128)(2,1)S(1)}, bf16[4,96,768]{2,1,0:T(8,128)(2,1)S(1)}, u32[]{:S(2)}, u32[]{:S(2)}) collective-permute-start(bf16[4,96,768]{2,1,0:T(8,128)(2,1)S(1)} %pad_maximum_fusion.4.rest_0_), channel_id=1, source_target_pairs={{0,4},{4,0},{8,12},{12,8},{16,20},{20,16},{24,28},{28,24},{1,5},{5... | collective-permute-start | bytes 1769480 | tf_op jit(solution)/shard_map/ppermute | solution.py:49
  61.3 14.1 %collective-permute-start.12 = (bf16[128,768]{1,0:T(8,128)(2,1)S(1)}, bf16[128,768]{1,0:T(8,128)(2,1)S(1)}, u32[]{:S(2)}, u32[]{:S(2)}) collective-permute-start(bf16[128,768]{1,0:T(8,128)(2,1)S(1)} %get-tuple-element.181), channel_id=1, source_target_pairs={{0,8},{4,12},{8,0},{12,4},{16,24},{20,28},{24,16},{28,20},{1,9},{5... | collective-permute-start | bytes 589832 | tf_op jit(solution)/shard_map/ppermute | solution.py:43
  61.4 17.3 %collective-permute-start.13 = (bf16[128,768]{1,0:T(8,128)(2,1)S(1)}, bf16[128,768]{1,0:T(8,128)(2,1)S(1)}, u32[]{:S(2)}, u32[]{:S(2)}) collective-permute-start(bf16[128,768]{1,0:T(8,128)(2,1)S(1)} %get-tuple-element.180), channel_id=1, source_target_pairs={{0,16},{4,20},{8,24},{12,28},{16,0},{20,4},{24,8},{28,12},{1,17},{... | collective-permute-start | bytes 589832 | tf_op jit(solution)/shard_map/ppermute | solution.py:43
  64.4 14.2 %collective-permute-start.14 = (bf16[128,768]{1,0:T(8,128)(2,1)S(1)}, bf16[128,768]{1,0:T(8,128)(2,1)S(1)}, u32[]{:S(2)}, u32[]{:S(2)}) collective-permute-start(bf16[128,768]{1,0:T(8,128)(2,1)S(1)} %get-tuple-element.179), channel_id=1, source_target_pairs={{0,24},{4,28},{8,16},{12,20},{16,8},{20,12},{24,0},{28,4},{1,25},{... | collective-permute-start | bytes 589832 | tf_op jit(solution)/shard_map/ppermute | solution.py:43
  78.7 1.8 collective-permute-start.15
  80.5 7.0 %collective-permute-start.16 = (bf16[128,768]{1,0:T(8,128)(2,1)S(1)}, bf16[128,768]{1,0:T(8,128)(2,1)S(1)}, u32[]{:S(2)}, u32[]{:S(2)}) collective-permute-start(bf16[128,768]{1,0:T(8,128)(2,1)S(1)} %fusion.46), channel_id=1, source_target_pairs={{0,2},{1,3},{2,0},{3,1},{4,6},{5,7},{6,4},{7,5},{8,10},{9,11},{10,... | collective-permute-start | bytes 589832 | tf_op jit(solution)/shard_map/ppermute | solution.py:37
  81.3 23.1 %collective-permute-start.21 = (bf16[4,96,768]{2,1,0:T(8,128)(2,1)S(1)}, bf16[4,96,768]{2,1,0:T(8,128)(2,1)S(1)}, u32[]{:S(2)}, u32[]{:S(2)}) collective-permute-start(bf16[4,96,768]{2,1,0:T(8,128)(2,1)S(1)} %pad_maximum_fusion.5.rest_2_), channel_id=1, source_target_pairs={{0,4},{4,0},{8,12},{12,8},{16,20},{20,16},{24,28},{28,24},{1,5},{5... | collective-permute-start | bytes 1769480 | tf_op jit(solution)/shard_map/ppermute | solution.py:49
  88.8 6.1 %collective-permute-start.19 = (bf16[32,768]{1,0:T(8,128)(2,1)S(1)}, bf16[32,768]{1,0:T(8,128)(2,1)S(1)}, u32[]{:S(2)}, u32[]{:S(2)}) collective-permute-start(bf16[32,768]{1,0:T(8,128)(2,1)S(1)} %get-tuple-element.214), channel_id=1, source_target_pairs={{0,24},{4,28},{8,16},{12,20},{16,8},{20,12},{24,0},{28,4},{1,25},{... | collective-permute-start | bytes 147464 | tf_op jit(solution)/shard_map/ppermute | solution.py:43
  91.3 5.3 %collective-permute-start.18 = (bf16[32,768]{1,0:T(8,128)(2,1)S(1)}, bf16[32,768]{1,0:T(8,128)(2,1)S(1)}, u32[]{:S(2)}, u32[]{:S(2)}) collective-permute-start(bf16[32,768]{1,0:T(8,128)(2,1)S(1)} %get-tuple-element.215), channel_id=1, source_target_pairs={{0,16},{4,20},{8,24},{12,28},{16,0},{20,4},{24,8},{28,12},{1,17},{... | collective-permute-start | bytes 147464 | tf_op jit(solution)/shard_map/ppermute | solution.py:43
  93.5 4.1 %collective-permute-start.17 = (bf16[32,768]{1,0:T(8,128)(2,1)S(1)}, bf16[32,768]{1,0:T(8,128)(2,1)S(1)}, u32[]{:S(2)}, u32[]{:S(2)}) collective-permute-start(bf16[32,768]{1,0:T(8,128)(2,1)S(1)} %get-tuple-element.216), channel_id=1, source_target_pairs={{0,8},{4,12},{8,0},{12,4},{16,24},{20,28},{24,16},{28,20},{1,9},{5... | collective-permute-start | bytes 147464 | tf_op jit(solution)/shard_map/ppermute | solution.py:43
  93.6 6.8 %collective-permute-start.23 = (bf16[128,768]{1,0:T(8,128)(2,1)S(1)}, bf16[128,768]{1,0:T(8,128)(2,1)S(1)}, u32[]{:S(2)}, u32[]{:S(2)}) collective-permute-start(bf16[128,768]{1,0:T(8,128)(2,1)S(1)} %get-tuple-element.210.own_grad_ref), channel_id=1, source_target_pairs={{0,2},{1,3},{2,0},{3,1},{4,6},{5,7},{6,4},{7,5},{8,10},{9,11},{10,... | collective-permute-start | bytes 589832 | tf_op jit(solution)/shard_map/ppermute | solution.py:37
  97.6 6.0 %collective-permute-start.20 = (bf16[128,768]{1,0:T(8,128)(2,1)S(1)}, bf16[128,768]{1,0:T(8,128)(2,1)S(1)}, u32[]{:S(2)}, u32[]{:S(2)}) collective-permute-start(bf16[128,768]{1,0:T(8,128)(2,1)S(1)} %get-tuple-element.212.own_ref), channel_id=1, source_target_pairs={{0,2},{1,3},{2,0},{3,1},{4,6},{5,7},{6,4},{7,5},{8,10},{9,11},{10,... | collective-permute-start | bytes 589832 | tf_op jit(solution)/shard_map/ppermute | solution.py:37
  101.2 4.1 %collective-permute-start.24 = (bf16[2,128,768]{2,1,0:T(8,128)(2,1)}, bf16[2,128,768]{2,1,0:T(8,128)(2,1)}, u32[]{:S(2)}, u32[]{:S(2)}) collective-permute-start(bf16[2,128,768]{2,1,0:T(8,128)(2,1)} %pad_maximum_fusion.8), channel_id=1, source_target_pairs={{0,1},{1,0},{2,3},{3,2},{4,5},{5,4},{6,7},{7,6},{8,9},{9,8},{10,11... | collective-permute-start | bytes 1179656 | tf_op jit(solution)/shard_map/ppermute | solution.py:37
  105.2 2.1 collective-permute-start.22
  116.8 4.7 %collective-permute-start.25 = (bf16[2,128,1536]{2,1,0:T(8,128)(2,1)}, bf16[2,128,1536]{2,1,0:T(8,128)(2,1)S(1)}, u32[]{:S(2)}, u32[]{:S(2)}) collective-permute-start(bf16[2,128,1536]{2,1,0:T(8,128)(2,1)} %get-tuple-element.76), channel_id=1, source_target_pairs={{0,1},{1,0},{2,3},{3,2},{4,5},{5,4},{6,7},{7,6},{8,9},{9,8},{10,11... | collective-permute-start | bytes 2359304 | tf_op jit(solution)/shard_map/ppermute | solution.py:37
  119.9 15.7 %collective-permute-start.27 = (bf16[4,96,768]{2,1,0:T(8,128)(2,1)S(1)}, bf16[4,96,768]{2,1,0:T(8,128)(2,1)S(1)}, u32[]{:S(2)}, u32[]{:S(2)}) collective-permute-start(bf16[4,96,768]{2,1,0:T(8,128)(2,1)S(1)} %slice_bitcast_fusion), channel_id=1, source_target_pairs={{0,4},{4,0},{8,12},{12,8},{16,20},{20,16},{24,28},{28,24},{1,5},{5... | collective-permute-start | bytes 1769480 | tf_op jit(solution)/shard_map/ppermute | solution.py:49
  121.7 14.0 %collective-permute-start.26 = (bf16[128,1536]{1,0:T(8,128)(2,1)S(1)}, bf16[128,1536]{1,0:T(8,128)(2,1)S(1)}, u32[]{:S(2)}, u32[]{:S(2)}) collective-permute-start(bf16[128,1536]{1,0:T(8,128)(2,1)S(1)} %fusion.36), channel_id=1, source_target_pairs={{0,2},{1,3},{2,0},{3,1},{4,6},{5,7},{6,4},{7,5},{8,10},{9,11},{10,... | collective-permute-start | bytes 1179656 | tf_op jit(solution)/shard_map/ppermute | solution.py:37
  135.9 7.5 %collective-permute-start.30 = (bf16[32,1536]{1,0:T(8,128)(2,1)S(1)}, bf16[32,1536]{1,0:T(8,128)(2,1)S(1)}, u32[]{:S(2)}, u32[]{:S(2)}) collective-permute-start(bf16[32,1536]{1,0:T(8,128)(2,1)S(1)} %get-tuple-element.203), channel_id=1, source_target_pairs={{0,24},{4,28},{8,16},{12,20},{16,8},{20,12},{24,0},{28,4},{1,25},{... | collective-permute-start | bytes 294920 | tf_op jit(solution)/shard_map/ppermute | solution.py:43
  138.3 9.6 %collective-permute-start.29 = (bf16[32,1536]{1,0:T(8,128)(2,1)S(1)}, bf16[32,1536]{1,0:T(8,128)(2,1)S(1)}, u32[]{:S(2)}, u32[]{:S(2)}) collective-permute-start(bf16[32,1536]{1,0:T(8,128)(2,1)S(1)} %get-tuple-element.204), channel_id=1, source_target_pairs={{0,16},{4,20},{8,24},{12,28},{16,0},{20,4},{24,8},{28,12},{1,17},{... | collective-permute-start | bytes 294920 | tf_op jit(solution)/shard_map/ppermute | solution.py:43
  139.4 8.6 %collective-permute-start.28 = (bf16[32,1536]{1,0:T(8,128)(2,1)S(1)}, bf16[32,1536]{1,0:T(8,128)(2,1)S(1)}, u32[]{:S(2)}, u32[]{:S(2)}) collective-permute-start(bf16[32,1536]{1,0:T(8,128)(2,1)S(1)} %get-tuple-element.205), channel_id=1, source_target_pairs={{0,8},{4,12},{8,0},{12,4},{16,24},{20,28},{24,16},{28,20},{1,9},{5... | collective-permute-start | bytes 294920 | tf_op jit(solution)/shard_map/ppermute | solution.py:43
  140.4 14.9 %collective-permute-start.32 = (bf16[4,96,768]{2,1,0:T(8,128)(2,1)S(1)}, bf16[4,96,768]{2,1,0:T(8,128)(2,1)S(1)}, u32[]{:S(2)}, u32[]{:S(2)}) collective-permute-start(bf16[4,96,768]{2,1,0:T(8,128)(2,1)S(1)} %slice_bitcast_fusion.2), channel_id=1, source_target_pairs={{0,4},{4,0},{8,12},{12,8},{16,20},{20,16},{24,28},{28,24},{1,5},{5... | collective-permute-start | bytes 1769480 | tf_op jit(solution)/shard_map/ppermute | solution.py:49
  148.9 6.4 %collective-permute-start.31 = (bf16[128,768]{1,0:T(8,128)(2,1)S(1)}, bf16[128,768]{1,0:T(8,128)(2,1)S(1)}, u32[]{:S(2)}, u32[]{:S(2)}) collective-permute-start(bf16[128,768]{1,0:T(8,128)(2,1)S(1)} %add_convert_fusion.own_ref), channel_id=1, source_target_pairs={{0,2},{1,3},{2,0},{3,1},{4,6},{5,7},{6,4},{7,5},{8,10},{9,11},{10,... | collective-permute-start | bytes 589832 | tf_op jit(solution)/shard_map/ppermute | solution.py:37
  155.5 4.3 %collective-permute-start.33 = (bf16[2,128,768]{2,1,0:T(8,128)(2,1)S(1)}, bf16[2,128,768]{2,1,0:T(8,128)(2,1)S(1)}, u32[]{:S(2)}, u32[]{:S(2)}) collective-permute-start(bf16[2,128,768]{2,1,0:T(8,128)(2,1)S(1)} %pad_maximum_fusion.9), channel_id=1, source_target_pairs={{0,1},{1,0},{2,3},{3,2},{4,5},{5,4},{6,7},{7,6},{8,9},{9,8},{10,11... | collective-permute-start | bytes 1179656 | tf_op jit(solution)/shard_map/ppermute | solution.py:37
  156.5 15.4 %collective-permute-start.36 = (bf16[2,96,768]{2,1,0:T(8,128)(2,1)S(1)}, bf16[2,96,768]{2,1,0:T(8,128)(2,1)S(1)}, u32[]{:S(2)}, u32[]{:S(2)}) collective-permute-start(bf16[2,96,768]{2,1,0:T(8,128)(2,1)S(1)} %get-tuple-element.175), channel_id=1, source_target_pairs={{0,8},{4,12},{8,0},{12,4},{16,24},{20,28},{24,16},{28,20},{1,9},{5... | collective-permute-start | bytes 884744 | tf_op jit(solution)/shard_map/ppermute | solution.py:43
  156.6 16.6 %collective-permute-start.37 = (bf16[2,96,768]{2,1,0:T(8,128)(2,1)S(1)}, bf16[2,96,768]{2,1,0:T(8,128)(2,1)S(1)}, u32[]{:S(2)}, u32[]{:S(2)}) collective-permute-start(bf16[2,96,768]{2,1,0:T(8,128)(2,1)S(1)} %get-tuple-element.174), channel_id=1, source_target_pairs={{0,16},{4,20},{8,24},{12,28},{16,0},{20,4},{24,8},{28,12},{1,17},{... | collective-permute-start | bytes 884744 | tf_op jit(solution)/shard_map/ppermute | solution.py:43
  159.9 13.3 %collective-permute-start.34 = (bf16[128,768]{1,0:T(8,128)(2,1)S(1)}, bf16[128,768]{1,0:T(8,128)(2,1)S(1)}, u32[]{:S(2)}, u32[]{:S(2)}) collective-permute-start(bf16[128,768]{1,0:T(8,128)(2,1)S(1)} %get-tuple-element.84), channel_id=1, source_target_pairs={{0,2},{1,3},{2,0},{3,1},{4,6},{5,7},{6,4},{7,5},{8,10},{9,11},{10,... | collective-permute-start | bytes 589832 | tf_op jit(solution)/shard_map/ppermute | solution.py:37
  174.4 3.9 %collective-permute-start.42 = (f32[8,768]{1,0:T(8,128)S(1)}, f32[8,768]{1,0:T(8,128)S(1)}, u32[]{:S(2)}, u32[]{:S(2)}) collective-permute-start(f32[8,768]{1,0:T(8,128)S(1)} %concatenate.59), channel_id=1, source_target_pairs={{0,4},{4,0},{8,12},{12,8},{16,20},{20,16},{24,28},{28,24},{1,5},{5... | collective-permute-start | bytes 73736 | tf_op jit(solution)/shard_map/ppermute | solution.py:49
  178.4 9.5 %collective-permute-start.40 = (bf16[2,96,768]{2,1,0:T(8,128)(2,1)S(1)}, bf16[2,96,768]{2,1,0:T(8,128)(2,1)S(1)}, u32[]{:S(2)}, u32[]{:S(2)}) collective-permute-start(bf16[2,96,768]{2,1,0:T(8,128)(2,1)S(1)} %slice_bitcast_fusion.11), channel_id=1, source_target_pairs={{0,4},{4,0},{8,12},{12,8},{16,20},{20,16},{24,28},{28,24},{1,5},{5... | collective-permute-start | bytes 884744 | tf_op jit(solution)/shard_map/ppermute | solution.py:49
  180.0 3.9 %collective-permute-start.44 = (f32[8,768]{1,0:T(8,128)S(1)}, f32[8,768]{1,0:T(8,128)S(1)}, u32[]{:S(2)}, u32[]{:S(2)}) collective-permute-start(f32[8,768]{1,0:T(8,128)S(1)} %add.205), channel_id=1, source_target_pairs={{0,2},{1,3},{2,0},{3,1},{4,6},{5,7},{6,4},{7,5},{8,10},{9,11},{10,... | collective-permute-start | bytes 73736 | tf_op jit(solution)/shard_map/ppermute | solution.py:37
  180.6 20.0 %collective-permute-start.35 = (bf16[2,128,768]{2,1,0:T(8,128)(2,1)S(1)}, bf16[2,128,768]{2,1,0:T(8,128)(2,1)S(1)}, u32[]{:S(2)}, u32[]{:S(2)}) collective-permute-start(bf16[2,128,768]{2,1,0:T(8,128)(2,1)S(1)} %pad_maximum_fusion.10), channel_id=1, source_target_pairs={{0,1},{1,0},{2,3},{3,2},{4,5},{5,4},{6,7},{7,6},{8,9},{9,8},{10,11... | collective-permute-start | bytes 1179656 | tf_op jit(solution)/shard_map/ppermute | solution.py:37
  180.7 17.6 %collective-permute-start.38 = (bf16[2,128,768]{2,1,0:T(8,128)(2,1)S(1)}, bf16[2,128,768]{2,1,0:T(8,128)(2,1)S(1)}, u32[]{:S(2)}, u32[]{:S(2)}) collective-permute-start(bf16[2,128,768]{2,1,0:T(8,128)(2,1)S(1)} %copy-done.12), channel_id=1, source_target_pairs={{0,1},{1,0},{2,3},{3,2},{4,5},{5,4},{6,7},{7,6},{8,9},{9,8},{10,11... | collective-permute-start | bytes 1179656 | tf_op jit(solution)/shard_map/ppermute | solution.py:37
  181.2 10.9 %collective-permute-start.47 = (bf16[2,96,768]{2,1,0:T(8,128)(2,1)S(1)}, bf16[2,96,768]{2,1,0:T(8,128)(2,1)S(1)}, u32[]{:S(2)}, u32[]{:S(2)}) collective-permute-start(bf16[2,96,768]{2,1,0:T(8,128)(2,1)S(1)} %copy-done.50), channel_id=1, source_target_pairs={{0,24},{4,28},{8,16},{12,20},{16,8},{20,12},{24,0},{28,4},{1,25},{... | collective-permute-start | bytes 884744 | tf_op jit(solution)/shard_map/ppermute | solution.py:43
  188.0 19.2 %collective-permute-start.41 = (bf16[2,96,768]{2,1,0:T(8,128)(2,1)S(1)}, bf16[2,96,768]{2,1,0:T(8,128)(2,1)S(1)}, u32[]{:S(2)}, u32[]{:S(2)}) collective-permute-start(bf16[2,96,768]{2,1,0:T(8,128)(2,1)S(1)} %get-tuple-element.184), channel_id=1, source_target_pairs={{0,4},{4,0},{8,12},{12,8},{16,20},{20,16},{24,28},{28,24},{1,5},{5... | collective-permute-start | bytes 884744 | tf_op jit(solution)/shard_map/ppermute | solution.py:49
  189.6 17.6 %collective-permute-start.45 = (bf16[104,768]{1,0:T(8,128)(2,1)S(1)}, bf16[104,768]{1,0:T(8,128)(2,1)S(1)}, u32[]{:S(2)}, u32[]{:S(2)}) collective-permute-start(bf16[104,768]{1,0:T(8,128)(2,1)S(1)} %get-tuple-element.218), channel_id=1, source_target_pairs={{0,16},{4,20},{8,24},{12,28},{16,0},{20,4},{24,8},{28,12},{1,17},{... | collective-permute-start | bytes 479240 | tf_op jit(solution)/shard_map/ppermute | solution.py:43
  192.1 15.1 %collective-permute-start.46 = (bf16[104,768]{1,0:T(8,128)(2,1)S(1)}, bf16[104,768]{1,0:T(8,128)(2,1)S(1)}, u32[]{:S(2)}, u32[]{:S(2)}) collective-permute-start(bf16[104,768]{1,0:T(8,128)(2,1)S(1)} %get-tuple-element.217), channel_id=1, source_target_pairs={{0,24},{4,28},{8,16},{12,20},{16,8},{20,12},{24,0},{28,4},{1,25},{... | collective-permute-start | bytes 479240 | tf_op jit(solution)/shard_map/ppermute | solution.py:43
  198.4 5.9 %collective-permute-start.39 = (bf16[128,768]{1,0:T(8,128)(2,1)S(1)}, bf16[128,768]{1,0:T(8,128)(2,1)S(1)}, u32[]{:S(2)}, u32[]{:S(2)}) collective-permute-start(bf16[128,768]{1,0:T(8,128)(2,1)S(1)} %fusion.47), channel_id=1, source_target_pairs={{0,2},{1,3},{2,0},{3,1},{4,6},{5,7},{6,4},{7,5},{8,10},{9,11},{10,... | collective-permute-start | bytes 589832 | tf_op jit(solution)/shard_map/ppermute | solution.py:37
  207.3 11.3 %collective-permute-start.48 = (bf16[104,768]{1,0:T(8,128)(2,1)S(1)}, bf16[104,768]{1,0:T(8,128)(2,1)S(1)}, u32[]{:S(2)}, u32[]{:S(2)}) collective-permute-start(bf16[104,768]{1,0:T(8,128)(2,1)S(1)} %pad_maximum_fusion.11), channel_id=1, source_target_pairs={{0,8},{4,12},{8,0},{12,4},{16,24},{20,28},{24,16},{28,20},{1,9},{5... | collective-permute-start | bytes 479240 | tf_op jit(solution)/shard_map/ppermute | solution.py:43
  (66 other events, 394.2 us)

commit v4 on v3

--- a/solution.py
+++ b/solution.py
@@ -94,15 +94,15 @@
     return [x[0]] + [over_z(x[d], d) for d in range(1, E)]
 
 
-def sum_but_z(x):
+def sum_but_z(x, *earlier):
     R = lax.axis_size("dp") // E
+    x = x + over_t(x, 2)
     c = 1
     while c < R:
         x = x + over_r(x, c)
         c *= 2
-    for k in (1, 2):
-        x = x + over_t(x, k)
-    return x
+    x = after(x, *earlier)
+    return x + over_t(x, 1)
 
 
 VMEM = pl.BlockSpec(memory_space=pltpu.VMEM)
@@ -431,12 +431,13 @@
 
     grad_output = mm(to_slots[:ROWS], cotangent_all, 1, 0)
     masked = jnp.where(sent_own[:, None], grad_output, 0).astype(BF).reshape(E, SUB, D)
-    in_rows = jnp.stack([pick(w_in, z ^ d, 1) for d in range(E)])
-    out_rows = jnp.stack([pick(w_out, z ^ d, 1) for d in range(E)])
-    out_rows = jnp.concatenate([out_rows, masked], axis=1)
-    in_columns = jnp.stack(deliver_z(after(in_rows, packed_z, packed_own, both_parts[1])))
+    in_rows = after(w_in, packed_z, packed_own, both_parts[1])
+    in_z = deliver_z(jnp.stack([pick(in_rows, z ^ d, 1) for d in range(E)]))
+    in_columns = jnp.stack(after(in_z, packed_all))
     in_swapped = [over_r(in_columns, c) for c in range(1, R)]
-    out_z = deliver_z(after(out_rows, in_columns))
+    out_rows = after(w_out, in_z)
+    out_rows = jnp.stack([pick(out_rows, z ^ d, 1) for d in range(E)])
+    out_z = deliver_z(jnp.concatenate([out_rows, masked], axis=1))
     out_columns = jnp.stack([part[:local] for part in out_z])
     out_swapped = [over_r(out_columns, c) for c in range(1, R)]
     in_weight = whole([in_columns] + in_swapped)
@@ -470,11 +471,11 @@
         *token_parts,
         gain_one,
         reversed_rel,
-        after(to_slots, in_columns, out_rows, router, chosen_own, from_slots_own, gain_two),
+        after(to_slots, in_z, masked, router, chosen_own, from_slots_own, gain_two),
         *packed_refs,
     )
     normed_all, qkv, probs, heads_all, kept, given, tokens_all, attention_weight = after(
-        forward, in_swapped, out_z
+        forward, in_swapped
     )
     cotangent_z = jnp.concatenate([part[local:] for part in out_z], axis=0)
     cotangent_parts = gather_t(cotangent_z)
@@ -484,7 +485,7 @@
     scale_two = norm_scale(middle)
     normed_two = (middle * scale_two * gain_two).astype(BF)
 
-    buffer_parts = gather_t(dispatch_z(normed_two), out_weight)
+    buffer_parts = gather_t(dispatch_z(after(normed_two, out_z)), out_weight)
     buffer, grad_expert, activation, grad_pre, kept, given = call(
         functools.partial(expert_layer, pieces=len(in_weight)),
         "expert_layer",
@@ -587,7 +588,8 @@
     )
     delivered = delivered + [over_z(last, 3)]
     late_terms = blocks_to_send(late_terms)
-    far_sums = add(swap_r(late_terms[:, 2:])).astype(BF)
+    far_terms = swap_r(late_terms[:, 2:])
+    far_sums = add(far_terms).astype(BF)
     near_terms = swap_r(after(late_terms[:, :2], far_sums))
     grad_normed_one = scatter_t(kept, given)
     own_inputs = tokens.astype(F32)
@@ -616,7 +618,8 @@
                 jnp.zeros((1, D), F32),
             ],
             axis=0,
-        )
+        ),
+        far_terms,
     )
     low = small.astype(BF)
     far = [over_z(jnp.concatenate([far_sums[d - 2], low], axis=0), d) for d in (2, 3)]

time: 223 us -> 211 us (0.946)
  local copies, waits for them, and re-layouts: 39.8 us -> 28.4 us
  starting transfers between devices: 61.3 us -> 66 us
  other arithmetic: 13.7 us -> 9.5 us
    unnamed x139 -> x123, local copies, waits for them, and re-layouts: 27.1 us -> 16.3 us
    ppermute x21, waiting for transfers between devices: 31.6 us -> 38.1 us  [over_z(): lax.ppermute(x, 'dp', [(i, (i // r ^ d) * r + i % r) for i in range(n)])]
    ppermute x18, starting transfers between devices: 8.57 us -> 14.6 us  [over_t(): return lax.ppermute(x, 'tensor', [(i, i ^ k) for i in range(T)])]
    ppermute x10, starting transfers between devices: 13.7 us -> 8.67 us  [over_r(): lax.ppermute(x, 'dp', [(i, i // r * r + (i % r ^ c)) for i in range(n)])]
    ppermute x10, waiting for transfers between devices: 18.8 us -> 14.7 us  [over_r(): lax.ppermute(x, 'dp', [(i, i // r * r + (i % r ^ c)) for i in range(n)])]
    ppermute x21, starting transfers between devices: 39.1 us -> 42.7 us  [over_z(): lax.ppermute(x, 'dp', [(i, (i // r ^ d) * r + i % r) for i in range(n)])]
    dynamic_slice x1 -> x0, local copies, waits for them, and re-layouts: 3.24 us -> none  [pick(): return lax.dynamic_index_in_dim(x, index, axis, keepdims=False)]
    ppermute x18, waiting for transfers between devices: 21.7 us -> 18.8 us  [over_t(): return lax.ppermute(x, 'tensor', [(i, i ^ k) for i in range(T)])]
  transfers between devices with their start and end apart: 49 -> 49, of which waited for: 24 -> 24; matrix products, arithmetic and copies ran while one was open for 17% -> 12% of each run, Pallas kernels for 9% -> 10%
where the time goes in v4:
time: 211 us; the launch traced here: 210 us
  waiting for transfers between devices  71.5 us (34%)
  starting transfers between devices  66 us (31%)
  local copies, waits for them, and re-layouts  28.4 us (13%)
  Pallas kernels  27.2 us (13%)
  other arithmetic  9.5 us (5%)
  matrix products  5.45 us (3%)
  between operations  2.48 us (1%)
    ppermute x21, starting transfers between devices, over_z(): lax.ppermute(x, 'dp', [(i, (i // r ^ d) * r + i % r) for i in range(n)])  42.7 us
    ppermute x21, waiting for transfers between devices, over_z(): lax.ppermute(x, 'dp', [(i, (i // r ^ d) * r + i % r) for i in range(n)])  38.1 us
    pallas_call x5, Pallas kernels, call(): pl.pallas_call(kernel, out_shape=[jax.ShapeDtypeStruct(shape, kind) for s...  27.2 us
    ppermute x18, waiting for transfers between devices, over_t(): return lax.ppermute(x, 'tensor', [(i, i ^ k) for i in range(T)])  18.8 us
    unnamed x123, local copies, waits for them, and re-layouts  16.3 us
    ppermute x10, waiting for transfers between devices, over_r(): lax.ppermute(x, 'dp', [(i, i // r * r + (i % r ^ c)) for i in range(n)])  14.7 us
    ppermute x18, starting transfers between devices, over_t(): return lax.ppermute(x, 'tensor', [(i, i ^ k) for i in range(T)])  14.6 us
    ppermute x10, starting transfers between devices, over_r(): lax.ppermute(x, 'dp', [(i, i // r * r + (i % r ^ c)) for i in range(n)])  8.67 us
  transfers between devices with their start and end apart: 49, of which 24 were waited for; matrix products, arithmetic and copies ran while one was open for 12% of the time, Pallas kernels for 10%

profile of v4, /device:TPU:0, one launch (start us, length us, event | category | flops | bytes accessed | tf_op | source)
XLA Modules:
  0.0 210.5 jit_solution(16807325615206340159)
XLA Ops:
  4.4 4.1 %collective-permute-start.3 = (bf16[97,768]{1,0:T(8,128)(2,1)S(1)}, bf16[97,768]{1,0:T(8,128)(2,1)S(1)}, u32[]{:S(2)}, u32[]{:S(2)}) collective-permute-start(bf16[97,768]{1,0:T(8,128)(2,1)S(1)} %pad_maximum_fusion.18.rest_0_), channel_id=1, source_target_pairs={{0,16},{4,20},{8,24},{12,28},{16,0},{20,4},{24,8},{28,12},{1,17},{... | collective-permute-start | bytes 446984 | tf_op jit(solution)/shard_map/ppermute | solution.py:43
  10.1 1.5 collective-permute-start.6
  12.5 1.6 collective-permute-start
  17.0 3.8 %collective-permute-done.4.rest_1_ = bf16[97,768]{1,0:T(8,128)(2,1)S(1)} collective-permute-done((bf16[97,768]{1,0:T(8,128)(2,1)S(1)}, bf16[97,768]{1,0:T(8,128)(2,1)S(1)}, u32[]{:S(2)}, u32[]{:S(2)}) %collective-permute-start.4) | collective-permute-done | bytes 149024 | tf_op jit(solution)/shard_map/ppermute | solution.py:43
  21.0 1.6 collective-permute-start.5
  27.8 2.7 %collective-permute-start.7 = (bf16[96,768]{1,0:T(8,128)(2,1)}, bf16[96,768]{1,0:T(8,128)(2,1)S(1)}, u32[]{:S(2)}, u32[]{:S(2)}) collective-permute-start(bf16[96,768]{1,0:T(8,128)(2,1)} %get-tuple-element.202), channel_id=1, source_target_pairs={{0,8},{4,12},{8,0},{12,4},{16,24},{20,28},{24,16},{28,20},{1,9},{5... | collective-permute-start | bytes 442376 | tf_op jit(solution)/shard_map/ppermute | solution.py:43
  30.5 1.9 collective-permute-start.8
  34.7 3.5 %collective-permute-done.7 = bf16[96,768]{1,0:T(8,128)(2,1)S(1)} collective-permute-done((bf16[96,768]{1,0:T(8,128)(2,1)}, bf16[96,768]{1,0:T(8,128)(2,1)S(1)}, u32[]{:S(2)}, u32[]{:S(2)}) %collective-permute-start.7) | collective-permute-done | bytes 147488 | tf_op jit(solution)/shard_map/ppermute | solution.py:43
  38.7 6.0 %collective-permute-done.9 = bf16[96,768]{1,0:T(8,128)(2,1)S(1)} collective-permute-done((bf16[96,768]{1,0:T(8,128)(2,1)S(1)}, bf16[96,768]{1,0:T(8,128)(2,1)S(1)}, u32[]{:S(2)}, u32[]{:S(2)}) %collective-permute-start.9) | collective-permute-done | bytes 147488 | tf_op jit(solution)/shard_map/ppermute | solution.py:43
  47.5 1.6 collective-permute-start.11
  51.5 3.0 %collective-permute-start.14 = (bf16[128,768]{1,0:T(8,128)(2,1)S(1)}, bf16[128,768]{1,0:T(8,128)(2,1)S(1)}, u32[]{:S(2)}, u32[]{:S(2)}) collective-permute-start(bf16[128,768]{1,0:T(8,128)(2,1)S(1)} %get-tuple-element.191), channel_id=1, source_target_pairs={{0,8},{4,12},{8,0},{12,4},{16,24},{20,28},{24,16},{28,20},{1,9},{5... | collective-permute-start | bytes 589832 | tf_op jit(solution)/shard_map/ppermute | solution.py:43
  54.5 2.0 collective-permute-start.15
  58.8 7.8 %attention_forward.1 = (bf16[512,768]{1,0:T(8,128)(2,1)S(1)}, bf16[512,576]{1,0:T(8,128)(2,1)S(1)}, f32[3,512,512]{2,1,0:T(8,128)}, bf16[512,192]{1,0:T(8,128)(2...) custom-call(s32[4]{0:T(128)S(1)} %pad_add_fusion.at_ref, ...), custom_call_target="tpu_custom_call" | custom-call | flops 12000000000 | bytes 2513408 | tf_op jit(solution)/shard_map/attention_forward/pallas_call | solution.py:115
  66.7 3.6 %collective-permute-done.16 = bf16[128,768]{1,0:T(8,128)(2,1)S(1)} collective-permute-done((bf16[128,768]{1,0:T(8,128)(2,1)S(1)}, bf16[128,768]{1,0:T(8,128)(2,1)S(1)}, u32[]{:S(2)}, u32[]{:S(2)}) %collective-permute-start.16) | collective-permute-done | bytes 196640 | tf_op jit(solution)/shard_map/ppermute | solution.py:43
  71.8 1.6 collective-permute-start.13
  74.1 3.4 %collective-permute-done.13 = bf16[128,768]{1,0:T(8,128)(2,1)S(1)} collective-permute-done((bf16[128,768]{1,0:T(8,128)(2,1)S(1)}, bf16[128,768]{1,0:T(8,128)(2,1)S(1)}, u32[]{:S(2)}, u32[]{:S(2)}) %collective-permute-start.13) | collective-permute-done | bytes 196640 | tf_op jit(solution)/shard_map/ppermute | solution.py:37
  78.9 2.5 %collective-permute-start.19 = (bf16[32,768]{1,0:T(8,128)(2,1)S(1)}, bf16[32,768]{1,0:T(8,128)(2,1)S(1)}, u32[]{:S(2)}, u32[]{:S(2)}) collective-permute-start(bf16[32,768]{1,0:T(8,128)(2,1)S(1)} %get-tuple-element.220), channel_id=1, source_target_pairs={{0,24},{4,28},{8,16},{12,20},{16,8},{20,12},{24,0},{28,4},{1,25},{... | collective-permute-start | bytes 147464 | tf_op jit(solution)/shard_map/ppermute | solution.py:43
  81.4 2.4 %collective-permute-start.18 = (bf16[32,768]{1,0:T(8,128)(2,1)S(1)}, bf16[32,768]{1,0:T(8,128)(2,1)S(1)}, u32[]{:S(2)}, u32[]{:S(2)}) collective-permute-start(bf16[32,768]{1,0:T(8,128)(2,1)S(1)} %get-tuple-element.221), channel_id=1, source_target_pairs={{0,16},{4,20},{8,24},{12,28},{16,0},{20,4},{24,8},{28,12},{1,17},{... | collective-permute-start | bytes 147464 | tf_op jit(solution)/shard_map/ppermute | solution.py:43
  84.3 1.6 collective-permute-start.23
  87.9 1.6 collective-permute-start.20
  89.5 2.6 %collective-permute-done.23.far_grad_ref = bf16[128,768]{1,0:T(8,128)(2,1)S(1)} collective-permute-done((bf16[128,768]{1,0:T(8,128)(2,1)S(1)}, bf16[128,768]{1,0:T(8,128)(2,1)S(1)}, u32[]{:S(2)}, u32[]{:S(2)}) %collective-permute-start.23) | collective-permute-done | bytes 196640 | tf_op jit(solution)/shard_map/ppermute | solution.py:37
  96.1 1.9 collective-permute-done.22.near_ref
  101.1 6.4 %expert_layer.1 = (bf16[512,768]{1,0:T(8,128)(2,1)S(1)}, bf16[512,768]{1,0:T(8,128)(2,1)S(1)}, bf16[512,768]{1,0:T(8,128)(2,1)}, bf16[512,768]{1,0:T(8,128)(2,1)...) custom-call(s32[4]{0:T(128)S(1)} %pad_add_fusion.at_ref, ...), custom_call_target="tpu_custom_call" | custom-call | flops 8000000000 | bytes 4128768 | tf_op jit(solution)/shard_map/expert_layer/pallas_call | solution.py:115
  109.1 1.5 grad_w_out.1
  113.2 1.5 grad_w_in.1
  114.6 11.6 %collective-permute-done.27 = bf16[4,96,768]{2,1,0:T(8,128)(2,1)S(1)} collective-permute-done((bf16[4,96,768]{2,1,0:T(8,128)(2,1)S(1)}, bf16[4,96,768]{2,1,0:T(8,128)(2,1)S(1)}, u32[]{:S(2)}, u32[]{:S(2)}) %collective-permute-start.27) | collective-permute-done | bytes 589856 | tf_op jit(solution)/shard_map/ppermute | solution.py:49
  126.6 2.4 %collective-permute-start.30 = (bf16[32,1536]{1,0:T(8,128)(2,1)S(1)}, bf16[32,1536]{1,0:T(8,128)(2,1)S(1)}, u32[]{:S(2)}, u32[]{:S(2)}) collective-permute-start(bf16[32,1536]{1,0:T(8,128)(2,1)S(1)} %get-tuple-element.209), channel_id=1, source_target_pairs={{0,24},{4,28},{8,16},{12,20},{16,8},{20,12},{24,0},{28,4},{1,25},{... | collective-permute-start | bytes 294920 | tf_op jit(solution)/shard_map/ppermute | solution.py:43
  129.1 2.0 collective-permute-start.28
  131.7 2.5 %collective-permute-done.30 = bf16[32,1536]{1,0:T(8,128)(2,1)S(1)} collective-permute-done((bf16[32,1536]{1,0:T(8,128)(2,1)S(1)}, bf16[32,1536]{1,0:T(8,128)(2,1)S(1)}, u32[]{:S(2)}, u32[]{:S(2)}) %collective-permute-start.30) | collective-permute-done | bytes 98336 | tf_op jit(solution)/shard_map/ppermute | solution.py:43
  134.2 3.7 %collective-permute-done.29 = bf16[32,1536]{1,0:T(8,128)(2,1)S(1)} collective-permute-done((bf16[32,1536]{1,0:T(8,128)(2,1)S(1)}, bf16[32,1536]{1,0:T(8,128)(2,1)S(1)}, u32[]{:S(2)}, u32[]{:S(2)}) %collective-permute-start.29) | collective-permute-done | bytes 98336 | tf_op jit(solution)/shard_map/ppermute | solution.py:43
  140.5 4.5 %collective-permute-done.31.far_ref = bf16[128,768]{1,0:T(8,128)(2,1)S(1)} collective-permute-done((bf16[128,768]{1,0:T(8,128)(2,1)S(1)}, bf16[128,768]{1,0:T(8,128)(2,1)S(1)}, u32[]{:S(2)}, u32[]{:S(2)}) %collective-permute-start.31) | collective-permute-done | bytes 196640 | tf_op jit(solution)/shard_map/ppermute | solution.py:37
  146.6 2.6 %collective-permute-start.37 = (bf16[2,96,768]{2,1,0:T(8,128)(2,1)S(1)}, bf16[2,96,768]{2,1,0:T(8,128)(2,1)S(1)}, u32[]{:S(2)}, u32[]{:S(2)}) collective-permute-start(bf16[2,96,768]{2,1,0:T(8,128)(2,1)S(1)} %get-tuple-element.184), channel_id=1, source_target_pairs={{0,16},{4,20},{8,24},{12,28},{16,0},{20,4},{24,8},{28,12},{1,17},{... | collective-permute-start | bytes 884744 | tf_op jit(solution)/shard_map/ppermute | solution.py:43
  150.0 1.5 collective-permute-start.34
  151.5 10.0 %attention_backward.1 = (bf16[2,4,96,768]{3,2,1,0:T(8,128)(2,1)S(1)}, bf16[2,128,768]{2,1,0:T(8,128)(2,1)S(1)}, bf16[2,128,768]{2,1,0:T(8,128)(2,1)S(1)}, f32[1,768]{1,0:T(1,128)S(1)}, f32[3,1024]{1,0:T(4,128)S(1)}) custom-call(s32[4]{0:T(128)S(1)} %pad_add_fusion.at_ref, bf16[128,768]{1,0:T(8,128)(2,1)S(1)} %add_convert_fusion.1.own_ref, ...), custom_call_target="tpu_custom_call" | custom-call | flops 12000000000 | bytes 7995392 | tf_op jit(solution)/shard_map/attention_backward/pallas_call | solution.py:115
  164.3 1.5 collective-permute-start.42
  166.5 1.7 collective-permute-done.42
  169.4 2.2 %collective-permute-start.47 = (bf16[2,96,768]{2,1,0:T(8,128)(2,1)S(1)}, bf16[2,96,768]{2,1,0:T(8,128)(2,1)S(1)}, u32[]{:S(2)}, u32[]{:S(2)}) collective-permute-start(bf16[2,96,768]{2,1,0:T(8,128)(2,1)S(1)} %copy-done.42), channel_id=1, source_target_pairs={{0,24},{4,28},{8,16},{12,20},{16,8},{20,12},{24,0},{28,4},{1,25},{... | collective-permute-start | bytes 884744 | tf_op jit(solution)/shard_map/ppermute | solution.py:43
  171.7 2.1 collective-permute-done.43
  174.6 5.7 %collective-permute-done.47 = bf16[2,96,768]{2,1,0:T(8,128)(2,1)S(1)} collective-permute-done((bf16[2,96,768]{2,1,0:T(8,128)(2,1)S(1)}, bf16[2,96,768]{2,1,0:T(8,128)(2,1)S(1)}, u32[]{:S(2)}, u32[]{:S(2)}) %collective-permute-start.47) | collective-permute-done | bytes 294944 | tf_op jit(solution)/shard_map/ppermute | solution.py:43
  180.7 1.8 copy.86
  182.5 1.8 copy.87
  184.3 4.8 %collective-permute-start.45 = (bf16[104,768]{1,0:T(8,128)(2,1)S(1)}, bf16[104,768]{1,0:T(8,128)(2,1)S(1)}, u32[]{:S(2)}, u32[]{:S(2)}) collective-permute-start(bf16[104,768]{1,0:T(8,128)(2,1)S(1)} %get-tuple-element.224), channel_id=1, source_target_pairs={{0,16},{4,20},{8,24},{12,28},{16,0},{20,4},{24,8},{28,12},{1,17},{... | collective-permute-start | bytes 479240 | tf_op jit(solution)/shard_map/ppermute | solution.py:43
  189.1 2.4 %collective-permute-start.46 = (bf16[104,768]{1,0:T(8,128)(2,1)S(1)}, bf16[104,768]{1,0:T(8,128)(2,1)S(1)}, u32[]{:S(2)}, u32[]{:S(2)}) collective-permute-start(bf16[104,768]{1,0:T(8,128)(2,1)S(1)} %get-tuple-element.223), channel_id=1, source_target_pairs={{0,24},{4,28},{8,16},{12,20},{16,8},{20,12},{24,0},{28,4},{1,25},{... | collective-permute-start | bytes 479240 | tf_op jit(solution)/shard_map/ppermute | solution.py:43
  191.5 1.5 collective-permute-start.39
  194.1 3.2 %collective-permute-done.39 = bf16[128,768]{1,0:T(8,128)(2,1)S(1)} collective-permute-done((bf16[128,768]{1,0:T(8,128)(2,1)S(1)}, bf16[128,768]{1,0:T(8,128)(2,1)S(1)}, u32[]{:S(2)}, u32[]{:S(2)}) %collective-permute-start.39) | collective-permute-done | bytes 196640 | tf_op jit(solution)/shard_map/ppermute | solution.py:37
  197.5 3.4 %collective-permute-done.45 = bf16[104,768]{1,0:T(8,128)(2,1)S(1)} collective-permute-done((bf16[104,768]{1,0:T(8,128)(2,1)S(1)}, bf16[104,768]{1,0:T(8,128)(2,1)S(1)}, u32[]{:S(2)}, u32[]{:S(2)}) %collective-permute-start.45) | collective-permute-done | bytes 159776 | tf_op jit(solution)/shard_map/ppermute | solution.py:43
  201.0 2.5 %collective-permute-start.48 = (bf16[104,768]{1,0:T(8,128)(2,1)S(1)}, bf16[104,768]{1,0:T(8,128)(2,1)S(1)}, u32[]{:S(2)}, u32[]{:S(2)}) collective-permute-start(bf16[104,768]{1,0:T(8,128)(2,1)S(1)} %pad_maximum_fusion.9), channel_id=1, source_target_pairs={{0,8},{4,12},{8,0},{12,4},{16,24},{20,28},{24,16},{28,20},{1,9},{5... | collective-permute-start | bytes 479240 | tf_op jit(solution)/shard_map/ppermute | solution.py:43
  204.7 2.2 %collective-permute-done.48 = bf16[104,768]{1,0:T(8,128)(2,1)S(1)} collective-permute-done((bf16[104,768]{1,0:T(8,128)(2,1)S(1)}, bf16[104,768]{1,0:T(8,128)(2,1)S(1)}, u32[]{:S(2)}, u32[]{:S(2)}) %collective-permute-start.48) | collective-permute-done | bytes 159776 | tf_op jit(solution)/shard_map/ppermute | solution.py:43
  (323 shorter events, 58.8 us)
Async XLA Ops:
  4.4 16.5 %collective-permute-start.3 = (bf16[97,768]{1,0:T(8,128)(2,1)S(1)}, bf16[97,768]{1,0:T(8,128)(2,1)S(1)}, u32[]{:S(2)}, u32[]{:S(2)}) collective-permute-start(bf16[97,768]{1,0:T(8,128)(2,1)S(1)} %pad_maximum_fusion.18.rest_0_), channel_id=1, source_target_pairs={{0,16},{4,20},{8,24},{12,28},{16,0},{20,4},{24,8},{28,12},{1,17},{... | collective-permute-start | bytes 446984 | tf_op jit(solution)/shard_map/ppermute | solution.py:43
  8.5 12.4 %collective-permute-start.2 = (bf16[97,768]{1,0:T(8,128)(2,1)S(1)}, bf16[97,768]{1,0:T(8,128)(2,1)S(1)}, u32[]{:S(2)}, u32[]{:S(2)}) collective-permute-start(bf16[97,768]{1,0:T(8,128)(2,1)S(1)} %pad_maximum_fusion.18.rest_0_), channel_id=1, source_target_pairs={{0,24},{4,28},{8,16},{12,20},{16,8},{20,12},{24,0},{28,4},{1,25},{... | collective-permute-start | bytes 446984 | tf_op jit(solution)/shard_map/ppermute | solution.py:43
  9.8 11.0 %collective-permute-start.4 = (bf16[97,768]{1,0:T(8,128)(2,1)S(1)}, bf16[97,768]{1,0:T(8,128)(2,1)S(1)}, u32[]{:S(2)}, u32[]{:S(2)}) collective-permute-start(bf16[97,768]{1,0:T(8,128)(2,1)S(1)} %pad_maximum_fusion.18.rest_0_), channel_id=1, source_target_pairs={{0,8},{4,12},{8,0},{12,4},{16,24},{20,28},{24,16},{28,20},{1,9},{5... | collective-permute-start | bytes 446984 | tf_op jit(solution)/shard_map/ppermute | solution.py:43
  10.1 13.4 %collective-permute-start.6 = (bf16[97,768]{1,0:T(8,128)(2,1)S(1)}, bf16[97,768]{1,0:T(8,128)(2,1)S(1)}, u32[]{:S(2)}, u32[]{:S(2)}) collective-permute-start(bf16[97,768]{1,0:T(8,128)(2,1)S(1)} %pad_maximum_fusion.18.rest_0_), channel_id=1, source_target_pairs={{0,4},{4,0},{8,12},{12,8},{16,20},{20,16},{24,28},{28,24},{1,5},{5... | collective-permute-start | bytes 446984 | tf_op jit(solution)/shard_map/ppermute | solution.py:49
  12.5 12.3 %collective-permute-start = (bf16[128,1536]{1,0:T(8,128)(2,1)S(1)}, bf16[128,1536]{1,0:T(8,128)(2,1)S(1)}, u32[]{:S(2)}, u32[]{:S(2)}) collective-permute-start(bf16[128,1536]{1,0:T(8,128)(2,1)S(1)} %constant_dynamic-update-slice_fusion), channel_id=1, source_target_pairs={{0,2},{1,3},{2,0},{3,1},{4,6},{5,7},{6,4},{7,5},{8,10},{9,11},{10,... | collective-permute-start | bytes 1179656 | tf_op jit(solution)/shard_map/ppermute | solution.py:37
  21.0 3.8 %collective-permute-start.5 = (bf16[4,768]{1,0:T(4,128)(2,1)S(1)}, bf16[4,768]{1,0:T(4,128)(2,1)S(1)}, u32[]{:S(2)}, u32[]{:S(2)}) collective-permute-start(bf16[4,768]{1,0:T(4,128)(2,1)S(1)} %pad_maximum_fusion.20), channel_id=1, source_target_pairs={{0,4},{4,0},{8,12},{12,8},{16,20},{20,16},{24,28},{28,24},{1,5},{5... | collective-permute-start | bytes 18440 | tf_op jit(solution)/shard_map/ppermute | solution.py:49
  23.5 23.2 %collective-permute-start.10 = (bf16[3,96,768]{2,1,0:T(8,128)(2,1)}, bf16[3,96,768]{2,1,0:T(8,128)(2,1)S(1)}, u32[]{:S(2)}, u32[]{:S(2)}) collective-permute-start(bf16[3,96,768]{2,1,0:T(8,128)(2,1)} %pad_maximum_fusion.4), channel_id=1, source_target_pairs={{0,4},{4,0},{8,12},{12,8},{16,20},{20,16},{24,28},{28,24},{1,5},{5... | collective-permute-start | bytes 1327112 | tf_op jit(solution)/shard_map/ppermute | solution.py:49
  25.8 23.3 %collective-permute-start.1 = (bf16[2,128,1536]{2,1,0:T(8,128)(2,1)}, bf16[2,128,1536]{2,1,0:T(8,128)(2,1)}, u32[]{:S(2)}, u32[]{:S(2)}) collective-permute-start(bf16[2,128,1536]{2,1,0:T(8,128)(2,1)} %pad_maximum_fusion.1), channel_id=1, source_target_pairs={{0,1},{1,0},{2,3},{3,2},{4,5},{5,4},{6,7},{7,6},{8,9},{9,8},{10,11... | collective-permute-start | bytes 2359304 | tf_op jit(solution)/shard_map/ppermute | solution.py:37
  27.8 10.5 %collective-permute-start.7 = (bf16[96,768]{1,0:T(8,128)(2,1)}, bf16[96,768]{1,0:T(8,128)(2,1)S(1)}, u32[]{:S(2)}, u32[]{:S(2)}) collective-permute-start(bf16[96,768]{1,0:T(8,128)(2,1)} %get-tuple-element.202), channel_id=1, source_target_pairs={{0,8},{4,12},{8,0},{12,4},{16,24},{20,28},{24,16},{28,20},{1,9},{5... | collective-permute-start | bytes 442376 | tf_op jit(solution)/shard_map/ppermute | solution.py:43
  30.5 8.2 %collective-permute-start.8 = (bf16[96,768]{1,0:T(8,128)(2,1)}, bf16[96,768]{1,0:T(8,128)(2,1)S(1)}, u32[]{:S(2)}, u32[]{:S(2)}) collective-permute-start(bf16[96,768]{1,0:T(8,128)(2,1)} %get-tuple-element.201), channel_id=1, source_target_pairs={{0,16},{4,20},{8,24},{12,28},{16,0},{20,4},{24,8},{28,12},{1,17},{... | collective-permute-start | bytes 442376 | tf_op jit(solution)/shard_map/ppermute | solution.py:43
  32.4 12.3 %collective-permute-start.9 = (bf16[96,768]{1,0:T(8,128)(2,1)S(1)}, bf16[96,768]{1,0:T(8,128)(2,1)S(1)}, u32[]{:S(2)}, u32[]{:S(2)}) collective-permute-start(bf16[96,768]{1,0:T(8,128)(2,1)S(1)} %get-tuple-element.200), channel_id=1, source_target_pairs={{0,24},{4,28},{8,16},{12,20},{16,8},{20,12},{24,0},{28,4},{1,25},{... | collective-permute-start | bytes 442376 | tf_op jit(solution)/shard_map/ppermute | solution.py:43
  47.5 19.1 %collective-permute-start.11 = (bf16[4,96,768]{2,1,0:T(8,128)(2,1)S(1)}, bf16[4,96,768]{2,1,0:T(8,128)(2,1)S(1)}, u32[]{:S(2)}, u32[]{:S(2)}) collective-permute-start(bf16[4,96,768]{2,1,0:T(8,128)(2,1)S(1)} %pad_maximum_fusion.2.rest_0_), channel_id=1, source_target_pairs={{0,4},{4,0},{8,12},{12,8},{16,20},{20,16},{24,28},{28,24},{1,5},{5... | collective-permute-start | bytes 1769480 | tf_op jit(solution)/shard_map/ppermute | solution.py:49
  51.5 21.9 %collective-permute-start.14 = (bf16[128,768]{1,0:T(8,128)(2,1)S(1)}, bf16[128,768]{1,0:T(8,128)(2,1)S(1)}, u32[]{:S(2)}, u32[]{:S(2)}) collective-permute-start(bf16[128,768]{1,0:T(8,128)(2,1)S(1)} %get-tuple-element.191), channel_id=1, source_target_pairs={{0,8},{4,12},{8,0},{12,4},{16,24},{20,28},{24,16},{28,20},{1,9},{5... | collective-permute-start | bytes 589832 | tf_op jit(solution)/shard_map/ppermute | solution.py:43
  54.5 17.1 %collective-permute-start.15 = (bf16[128,768]{1,0:T(8,128)(2,1)S(1)}, bf16[128,768]{1,0:T(8,128)(2,1)S(1)}, u32[]{:S(2)}, u32[]{:S(2)}) collective-permute-start(bf16[128,768]{1,0:T(8,128)(2,1)S(1)} %get-tuple-element.190), channel_id=1, source_target_pairs={{0,16},{4,20},{8,24},{12,28},{16,0},{20,4},{24,8},{28,12},{1,17},{... | collective-permute-start | bytes 589832 | tf_op jit(solution)/shard_map/ppermute | solution.py:43
  56.4 13.9 %collective-permute-start.16 = (bf16[128,768]{1,0:T(8,128)(2,1)S(1)}, bf16[128,768]{1,0:T(8,128)(2,1)S(1)}, u32[]{:S(2)}, u32[]{:S(2)}) collective-permute-start(bf16[128,768]{1,0:T(8,128)(2,1)S(1)} %get-tuple-element.189), channel_id=1, source_target_pairs={{0,24},{4,28},{8,16},{12,20},{16,8},{20,12},{24,0},{28,4},{1,25},{... | collective-permute-start | bytes 589832 | tf_op jit(solution)/shard_map/ppermute | solution.py:43
  66.7 4.9 %collective-permute-start.12 = (bf16[2,128,768]{2,1,0:T(8,128)(2,1)S(1)}, bf16[2,128,768]{2,1,0:T(8,128)(2,1)S(1)}, u32[]{:S(2)}, u32[]{:S(2)}) collective-permute-start(bf16[2,128,768]{2,1,0:T(8,128)(2,1)S(1)} %get-tuple-element.82), channel_id=1, source_target_pairs={{0,1},{1,0},{2,3},{3,2},{4,5},{5,4},{6,7},{7,6},{8,9},{9,8},{10,11... | collective-permute-start | bytes 1179656 | tf_op jit(solution)/shard_map/ppermute | solution.py:37
  71.8 5.7 %collective-permute-start.13 = (bf16[128,768]{1,0:T(8,128)(2,1)S(1)}, bf16[128,768]{1,0:T(8,128)(2,1)S(1)}, u32[]{:S(2)}, u32[]{:S(2)}) collective-permute-start(bf16[128,768]{1,0:T(8,128)(2,1)S(1)} %fusion.45), channel_id=1, source_target_pairs={{0,2},{1,3},{2,0},{3,1},{4,6},{5,7},{6,4},{7,5},{8,10},{9,11},{10,... | collective-permute-start | bytes 589832 | tf_op jit(solution)/shard_map/ppermute | solution.py:37
  73.4 21.7 %collective-permute-start.21 = (bf16[4,96,768]{2,1,0:T(8,128)(2,1)S(1)}, bf16[4,96,768]{2,1,0:T(8,128)(2,1)S(1)}, u32[]{:S(2)}, u32[]{:S(2)}) collective-permute-start(bf16[4,96,768]{2,1,0:T(8,128)(2,1)S(1)} %pad_maximum_fusion.3.rest_2_), channel_id=1, source_target_pairs={{0,4},{4,0},{8,12},{12,8},{16,20},{20,16},{24,28},{28,24},{1,5},{5... | collective-permute-start | bytes 1769480 | tf_op jit(solution)/shard_map/ppermute | solution.py:49
  78.9 7.0 %collective-permute-start.19 = (bf16[32,768]{1,0:T(8,128)(2,1)S(1)}, bf16[32,768]{1,0:T(8,128)(2,1)S(1)}, u32[]{:S(2)}, u32[]{:S(2)}) collective-permute-start(bf16[32,768]{1,0:T(8,128)(2,1)S(1)} %get-tuple-element.220), channel_id=1, source_target_pairs={{0,24},{4,28},{8,16},{12,20},{16,8},{20,12},{24,0},{28,4},{1,25},{... | collective-permute-start | bytes 147464 | tf_op jit(solution)/shard_map/ppermute | solution.py:43
  81.4 5.1 %collective-permute-start.18 = (bf16[32,768]{1,0:T(8,128)(2,1)S(1)}, bf16[32,768]{1,0:T(8,128)(2,1)S(1)}, u32[]{:S(2)}, u32[]{:S(2)}) collective-permute-start(bf16[32,768]{1,0:T(8,128)(2,1)S(1)} %get-tuple-element.221), channel_id=1, source_target_pairs={{0,16},{4,20},{8,24},{12,28},{16,0},{20,4},{24,8},{28,12},{1,17},{... | collective-permute-start | bytes 147464 | tf_op jit(solution)/shard_map/ppermute | solution.py:43
  83.8 4.1 %collective-permute-start.17 = (bf16[32,768]{1,0:T(8,128)(2,1)S(1)}, bf16[32,768]{1,0:T(8,128)(2,1)S(1)}, u32[]{:S(2)}, u32[]{:S(2)}) collective-permute-start(bf16[32,768]{1,0:T(8,128)(2,1)S(1)} %get-tuple-element.222), channel_id=1, source_target_pairs={{0,8},{4,12},{8,0},{12,4},{16,24},{20,28},{24,16},{28,20},{1,9},{5... | collective-permute-start | bytes 147464 | tf_op jit(solution)/shard_map/ppermute | solution.py:43
  84.3 7.8 %collective-permute-start.23 = (bf16[128,768]{1,0:T(8,128)(2,1)S(1)}, bf16[128,768]{1,0:T(8,128)(2,1)S(1)}, u32[]{:S(2)}, u32[]{:S(2)}) collective-permute-start(bf16[128,768]{1,0:T(8,128)(2,1)S(1)} %get-tuple-element.216.own_grad_ref), channel_id=1, source_target_pairs={{0,2},{1,3},{2,0},{3,1},{4,6},{5,7},{6,4},{7,5},{8,10},{9,11},{10,... | collective-permute-start | bytes 589832 | tf_op jit(solution)/shard_map/ppermute | solution.py:37
  87.9 6.4 %collective-permute-start.20 = (bf16[128,768]{1,0:T(8,128)(2,1)S(1)}, bf16[128,768]{1,0:T(8,128)(2,1)S(1)}, u32[]{:S(2)}, u32[]{:S(2)}) collective-permute-start(bf16[128,768]{1,0:T(8,128)(2,1)S(1)} %get-tuple-element.218.own_ref), channel_id=1, source_target_pairs={{0,2},{1,3},{2,0},{3,1},{4,6},{5,7},{6,4},{7,5},{8,10},{9,11},{10,... | collective-permute-start | bytes 589832 | tf_op jit(solution)/shard_map/ppermute | solution.py:37
  92.9 3.2 %collective-permute-start.24 = (bf16[2,128,768]{2,1,0:T(8,128)(2,1)}, bf16[2,128,768]{2,1,0:T(8,128)(2,1)}, u32[]{:S(2)}, u32[]{:S(2)}) collective-permute-start(bf16[2,128,768]{2,1,0:T(8,128)(2,1)} %pad_maximum_fusion.6), channel_id=1, source_target_pairs={{0,1},{1,0},{2,3},{3,2},{4,5},{5,4},{6,7},{7,6},{8,9},{9,8},{10,11... | collective-permute-start | bytes 1179656 | tf_op jit(solution)/shard_map/ppermute | solution.py:37
  107.5 3.7 %collective-permute-start.25 = (bf16[2,128,1536]{2,1,0:T(8,128)(2,1)}, bf16[2,128,1536]{2,1,0:T(8,128)(2,1)S(1)}, u32[]{:S(2)}, u32[]{:S(2)}) collective-permute-start(bf16[2,128,1536]{2,1,0:T(8,128)(2,1)} %get-tuple-element.87), channel_id=1, source_target_pairs={{0,1},{1,0},{2,3},{3,2},{4,5},{5,4},{6,7},{7,6},{8,9},{9,8},{10,11... | collective-permute-start | bytes 2359304 | tf_op jit(solution)/shard_map/ppermute | solution.py:37
  110.6 15.7 %collective-permute-start.27 = (bf16[4,96,768]{2,1,0:T(8,128)(2,1)S(1)}, bf16[4,96,768]{2,1,0:T(8,128)(2,1)S(1)}, u32[]{:S(2)}, u32[]{:S(2)}) collective-permute-start(bf16[4,96,768]{2,1,0:T(8,128)(2,1)S(1)} %slice_bitcast_fusion), channel_id=1, source_target_pairs={{0,4},{4,0},{8,12},{12,8},{16,20},{20,16},{24,28},{28,24},{1,5},{5... | collective-permute-start | bytes 1769480 | tf_op jit(solution)/shard_map/ppermute | solution.py:49
  111.8 14.6 %collective-permute-start.26 = (bf16[128,1536]{1,0:T(8,128)(2,1)S(1)}, bf16[128,1536]{1,0:T(8,128)(2,1)S(1)}, u32[]{:S(2)}, u32[]{:S(2)}) collective-permute-start(bf16[128,1536]{1,0:T(8,128)(2,1)S(1)} %fusion.35), channel_id=1, source_target_pairs={{0,2},{1,3},{2,0},{3,1},{4,6},{5,7},{6,4},{7,5},{8,10},{9,11},{10,... | collective-permute-start | bytes 1179656 | tf_op jit(solution)/shard_map/ppermute | solution.py:37
  126.6 7.6 %collective-permute-start.30 = (bf16[32,1536]{1,0:T(8,128)(2,1)S(1)}, bf16[32,1536]{1,0:T(8,128)(2,1)S(1)}, u32[]{:S(2)}, u32[]{:S(2)}) collective-permute-start(bf16[32,1536]{1,0:T(8,128)(2,1)S(1)} %get-tuple-element.209), channel_id=1, source_target_pairs={{0,24},{4,28},{8,16},{12,20},{16,8},{20,12},{24,0},{28,4},{1,25},{... | collective-permute-start | bytes 294920 | tf_op jit(solution)/shard_map/ppermute | solution.py:43
  129.1 8.8 %collective-permute-start.29 = (bf16[32,1536]{1,0:T(8,128)(2,1)S(1)}, bf16[32,1536]{1,0:T(8,128)(2,1)S(1)}, u32[]{:S(2)}, u32[]{:S(2)}) collective-permute-start(bf16[32,1536]{1,0:T(8,128)(2,1)S(1)} %get-tuple-element.210), channel_id=1, source_target_pairs={{0,16},{4,20},{8,24},{12,28},{16,0},{20,4},{24,8},{28,12},{1,17},{... | collective-permute-start | bytes 294920 | tf_op jit(solution)/shard_map/ppermute | solution.py:43
  129.1 8.8 %collective-permute-start.28 = (bf16[32,1536]{1,0:T(8,128)(2,1)S(1)}, bf16[32,1536]{1,0:T(8,128)(2,1)S(1)}, u32[]{:S(2)}, u32[]{:S(2)}) collective-permute-start(bf16[32,1536]{1,0:T(8,128)(2,1)S(1)} %get-tuple-element.211), channel_id=1, source_target_pairs={{0,8},{4,12},{8,0},{12,4},{16,24},{20,28},{24,16},{28,20},{1,9},{5... | collective-permute-start | bytes 294920 | tf_op jit(solution)/shard_map/ppermute | solution.py:43
  131.1 14.0 %collective-permute-start.32 = (bf16[4,96,768]{2,1,0:T(8,128)(2,1)S(1)}, bf16[4,96,768]{2,1,0:T(8,128)(2,1)S(1)}, u32[]{:S(2)}, u32[]{:S(2)}) collective-permute-start(bf16[4,96,768]{2,1,0:T(8,128)(2,1)S(1)} %slice_bitcast_fusion.2), channel_id=1, source_target_pairs={{0,4},{4,0},{8,12},{12,8},{16,20},{20,16},{24,28},{28,24},{1,5},{5... | collective-permute-start | bytes 1769480 | tf_op jit(solution)/shard_map/ppermute | solution.py:49
  138.9 6.1 %collective-permute-start.31 = (bf16[128,768]{1,0:T(8,128)(2,1)S(1)}, bf16[128,768]{1,0:T(8,128)(2,1)S(1)}, u32[]{:S(2)}, u32[]{:S(2)}) collective-permute-start(bf16[128,768]{1,0:T(8,128)(2,1)S(1)} %add_convert_fusion.1.own_ref), channel_id=1, source_target_pairs={{0,2},{1,3},{2,0},{3,1},{4,6},{5,7},{6,4},{7,5},{8,10},{9,11},{10,... | collective-permute-start | bytes 589832 | tf_op jit(solution)/shard_map/ppermute | solution.py:37
  145.3 4.7 %collective-permute-start.33 = (bf16[2,128,768]{2,1,0:T(8,128)(2,1)S(1)}, bf16[2,128,768]{2,1,0:T(8,128)(2,1)S(1)}, u32[]{:S(2)}, u32[]{:S(2)}) collective-permute-start(bf16[2,128,768]{2,1,0:T(8,128)(2,1)S(1)} %pad_maximum_fusion.7), channel_id=1, source_target_pairs={{0,1},{1,0},{2,3},{3,2},{4,5},{5,4},{6,7},{7,6},{8,9},{9,8},{10,11... | collective-permute-start | bytes 1179656 | tf_op jit(solution)/shard_map/ppermute | solution.py:37
  146.3 16.7 %collective-permute-start.36 = (bf16[2,96,768]{2,1,0:T(8,128)(2,1)S(1)}, bf16[2,96,768]{2,1,0:T(8,128)(2,1)S(1)}, u32[]{:S(2)}, u32[]{:S(2)}) collective-permute-start(bf16[2,96,768]{2,1,0:T(8,128)(2,1)S(1)} %get-tuple-element.185), channel_id=1, source_target_pairs={{0,8},{4,12},{8,0},{12,4},{16,24},{20,28},{24,16},{28,20},{1,9},{5... | collective-permute-start | bytes 884744 | tf_op jit(solution)/shard_map/ppermute | solution.py:43
  146.6 16.4 %collective-permute-start.37 = (bf16[2,96,768]{2,1,0:T(8,128)(2,1)S(1)}, bf16[2,96,768]{2,1,0:T(8,128)(2,1)S(1)}, u32[]{:S(2)}, u32[]{:S(2)}) collective-permute-start(bf16[2,96,768]{2,1,0:T(8,128)(2,1)S(1)} %get-tuple-element.184), channel_id=1, source_target_pairs={{0,16},{4,20},{8,24},{12,28},{16,0},{20,4},{24,8},{28,12},{1,17},{... | collective-permute-start | bytes 884744 | tf_op jit(solution)/shard_map/ppermute | solution.py:43
  150.0 13.0 %collective-permute-start.34 = (bf16[128,768]{1,0:T(8,128)(2,1)S(1)}, bf16[128,768]{1,0:T(8,128)(2,1)S(1)}, u32[]{:S(2)}, u32[]{:S(2)}) collective-permute-start(bf16[128,768]{1,0:T(8,128)(2,1)S(1)} %get-tuple-element.95), channel_id=1, source_target_pairs={{0,2},{1,3},{2,0},{3,1},{4,6},{5,7},{6,4},{7,5},{8,10},{9,11},{10,... | collective-permute-start | bytes 589832 | tf_op jit(solution)/shard_map/ppermute | solution.py:37
  164.3 3.9 %collective-permute-start.42 = (f32[8,768]{1,0:T(8,128)S(1)}, f32[8,768]{1,0:T(8,128)S(1)}, u32[]{:S(2)}, u32[]{:S(2)}) collective-permute-start(f32[8,768]{1,0:T(8,128)S(1)} %concatenate.59), channel_id=1, source_target_pairs={{0,2},{1,3},{2,0},{3,1},{4,6},{5,7},{6,4},{7,5},{8,10},{9,11},{10,... | collective-permute-start | bytes 73736 | tf_op jit(solution)/shard_map/ppermute | solution.py:37
  165.8 8.0 %collective-permute-start.40 = (bf16[2,96,768]{2,1,0:T(8,128)(2,1)S(1)}, bf16[2,96,768]{2,1,0:T(8,128)(2,1)S(1)}, u32[]{:S(2)}, u32[]{:S(2)}) collective-permute-start(bf16[2,96,768]{2,1,0:T(8,128)(2,1)S(1)} %slice_bitcast_fusion.11), channel_id=1, source_target_pairs={{0,4},{4,0},{8,12},{12,8},{16,20},{20,16},{24,28},{28,24},{1,5},{5... | collective-permute-start | bytes 884744 | tf_op jit(solution)/shard_map/ppermute | solution.py:49
  168.2 5.6 %collective-permute-start.43 = (f32[8,768]{1,0:T(8,128)S(1)}, f32[8,768]{1,0:T(8,128)S(1)}, u32[]{:S(2)}, u32[]{:S(2)}) collective-permute-start(f32[8,768]{1,0:T(8,128)S(1)} %add.204), channel_id=1, source_target_pairs={{0,4},{4,0},{8,12},{12,8},{16,20},{20,16},{24,28},{28,24},{1,5},{5... | collective-permute-start | bytes 73736 | tf_op jit(solution)/shard_map/ppermute | solution.py:49
  168.8 24.2 %collective-permute-start.35 = (bf16[2,128,768]{2,1,0:T(8,128)(2,1)S(1)}, bf16[2,128,768]{2,1,0:T(8,128)(2,1)S(1)}, u32[]{:S(2)}, u32[]{:S(2)}) collective-permute-start(bf16[2,128,768]{2,1,0:T(8,128)(2,1)S(1)} %pad_maximum_fusion.8), channel_id=1, source_target_pairs={{0,1},{1,0},{2,3},{3,2},{4,5},{5,4},{6,7},{7,6},{8,9},{9,8},{10,11... | collective-permute-start | bytes 1179656 | tf_op jit(solution)/shard_map/ppermute | solution.py:37
  168.9 22.5 %collective-permute-start.38 = (bf16[2,128,768]{2,1,0:T(8,128)(2,1)S(1)}, bf16[2,128,768]{2,1,0:T(8,128)(2,1)S(1)}, u32[]{:S(2)}, u32[]{:S(2)}) collective-permute-start(bf16[2,128,768]{2,1,0:T(8,128)(2,1)S(1)} %copy-done.12), channel_id=1, source_target_pairs={{0,1},{1,0},{2,3},{3,2},{4,5},{5,4},{6,7},{7,6},{8,9},{9,8},{10,11... | collective-permute-start | bytes 1179656 | tf_op jit(solution)/shard_map/ppermute | solution.py:37
  169.4 10.9 %collective-permute-start.47 = (bf16[2,96,768]{2,1,0:T(8,128)(2,1)S(1)}, bf16[2,96,768]{2,1,0:T(8,128)(2,1)S(1)}, u32[]{:S(2)}, u32[]{:S(2)}) collective-permute-start(bf16[2,96,768]{2,1,0:T(8,128)(2,1)S(1)} %copy-done.42), channel_id=1, source_target_pairs={{0,24},{4,28},{8,16},{12,20},{16,8},{20,12},{24,0},{28,4},{1,25},{... | collective-permute-start | bytes 884744 | tf_op jit(solution)/shard_map/ppermute | solution.py:43
  173.8 10.5 %collective-permute-start.44 = (f32[8,768]{1,0:T(8,128)S(1)}, f32[8,768]{1,0:T(8,128)S(1)}, u32[]{:S(2)}, u32[]{:S(2)}) collective-permute-start(f32[8,768]{1,0:T(8,128)S(1)} %add.205), channel_id=1, source_target_pairs={{0,1},{1,0},{2,3},{3,2},{4,5},{5,4},{6,7},{7,6},{8,9},{9,8},{10,11... | collective-permute-start | bytes 73736 | tf_op jit(solution)/shard_map/ppermute | solution.py:37
  174.0 26.9 %collective-permute-start.41 = (bf16[2,96,768]{2,1,0:T(8,128)(2,1)S(1)}, bf16[2,96,768]{2,1,0:T(8,128)(2,1)S(1)}, u32[]{:S(2)}, u32[]{:S(2)}) collective-permute-start(bf16[2,96,768]{2,1,0:T(8,128)(2,1)S(1)} %get-tuple-element.194), channel_id=1, source_target_pairs={{0,4},{4,0},{8,12},{12,8},{16,20},{20,16},{24,28},{28,24},{1,5},{5... | collective-permute-start | bytes 884744 | tf_op jit(solution)/shard_map/ppermute | solution.py:49
  184.3 16.6 %collective-permute-start.45 = (bf16[104,768]{1,0:T(8,128)(2,1)S(1)}, bf16[104,768]{1,0:T(8,128)(2,1)S(1)}, u32[]{:S(2)}, u32[]{:S(2)}) collective-permute-start(bf16[104,768]{1,0:T(8,128)(2,1)S(1)} %get-tuple-element.224), channel_id=1, source_target_pairs={{0,16},{4,20},{8,24},{12,28},{16,0},{20,4},{24,8},{28,12},{1,17},{... | collective-permute-start | bytes 479240 | tf_op jit(solution)/shard_map/ppermute | solution.py:43
  189.1 11.9 %collective-permute-start.46 = (bf16[104,768]{1,0:T(8,128)(2,1)S(1)}, bf16[104,768]{1,0:T(8,128)(2,1)S(1)}, u32[]{:S(2)}, u32[]{:S(2)}) collective-permute-start(bf16[104,768]{1,0:T(8,128)(2,1)S(1)} %get-tuple-element.223), channel_id=1, source_target_pairs={{0,24},{4,28},{8,16},{12,20},{16,8},{20,12},{24,0},{28,4},{1,25},{... | collective-permute-start | bytes 479240 | tf_op jit(solution)/shard_map/ppermute | solution.py:43
  191.5 5.7 %collective-permute-start.39 = (bf16[128,768]{1,0:T(8,128)(2,1)S(1)}, bf16[128,768]{1,0:T(8,128)(2,1)S(1)}, u32[]{:S(2)}, u32[]{:S(2)}) collective-permute-start(bf16[128,768]{1,0:T(8,128)(2,1)S(1)} %fusion.46), channel_id=1, source_target_pairs={{0,2},{1,3},{2,0},{3,1},{4,6},{5,7},{6,4},{7,5},{8,10},{9,11},{10,... | collective-permute-start | bytes 589832 | tf_op jit(solution)/shard_map/ppermute | solution.py:37
  201.0 5.8 %collective-permute-start.48 = (bf16[104,768]{1,0:T(8,128)(2,1)S(1)}, bf16[104,768]{1,0:T(8,128)(2,1)S(1)}, u32[]{:S(2)}, u32[]{:S(2)}) collective-permute-start(bf16[104,768]{1,0:T(8,128)(2,1)S(1)} %pad_maximum_fusion.9), channel_id=1, source_target_pairs={{0,8},{4,12},{8,0},{12,4},{16,24},{20,28},{24,16},{28,20},{1,9},{5... | collective-permute-start | bytes 479240 | tf_op jit(solution)/shard_map/ppermute | solution.py:43
  (62 other events, 325.6 us)

commit v5 on v4

--- a/solution.py
+++ b/solution.py
@@ -68,9 +68,13 @@
     return [own, near[0], far, near[1]]
 
 
-def scatter_t(kept, sent, *earlier):
-    first = over_t(sent, 1).astype(F32)
-    away = after((kept[1].astype(F32) + first[1]).astype(BF), *earlier)
+def scatter_t(kept, sent):
+    return finish_scatter(kept, over_t(sent, 1))
+
+
+def finish_scatter(kept, first):
+    first = first.astype(F32)
+    away = (kept[1].astype(F32) + first[1]).astype(BF)
     return kept[0].astype(F32) + first[0] + over_t(away, 2).astype(F32)
 
 
@@ -433,15 +437,9 @@
     masked = jnp.where(sent_own[:, None], grad_output, 0).astype(BF).reshape(E, SUB, D)
     in_rows = after(w_in, packed_z, packed_own, both_parts[1])
     in_z = deliver_z(jnp.stack([pick(in_rows, z ^ d, 1) for d in range(E)]))
-    in_columns = jnp.stack(after(in_z, packed_all))
-    in_swapped = [over_r(in_columns, c) for c in range(1, R)]
-    out_rows = after(w_out, in_z)
+    out_rows = after(w_out, in_z[1:3])
     out_rows = jnp.stack([pick(out_rows, z ^ d, 1) for d in range(E)])
-    out_z = deliver_z(jnp.concatenate([out_rows, masked], axis=1))
-    out_columns = jnp.stack([part[:local] for part in out_z])
-    out_swapped = [over_r(out_columns, c) for c in range(1, R)]
-    in_weight = whole([in_columns] + in_swapped)
-    out_weight = whole([out_columns] + out_swapped)
+    out_rows = jnp.concatenate([out_rows, masked], axis=1)
     router = jnp.pad(router_rows.T, ((0, 0), (0, 128 - E)))
 
     table_rows = lax.dynamic_slice_in_dim(table_flat.astype(F32).reshape(H, NB), t * LH, LH, 0)
@@ -471,12 +469,20 @@
         *token_parts,
         gain_one,
         reversed_rel,
-        after(to_slots, in_z, masked, router, chosen_own, from_slots_own, gain_two),
+        after(to_slots, in_z[1:3], out_rows, router, chosen_own, from_slots_own, gain_two),
         *packed_refs,
     )
     normed_all, qkv, probs, heads_all, kept, given, tokens_all, attention_weight = after(
-        forward, in_swapped
-    )
+        forward, in_z
+    )
+    in_z, out_rows = after((in_z, out_rows), kept)
+    in_columns = jnp.stack(in_z)
+    in_swapped = [over_r(in_columns, c) for c in range(1, R)]
+    in_weight = whole([in_columns] + in_swapped)
+    out_z = deliver_z(out_rows)
+    out_columns = jnp.stack([part[:local] for part in out_z])
+    out_swapped = [over_r(out_columns, c) for c in range(1, R)]
+    out_weight = whole([out_columns] + out_swapped)
     cotangent_z = jnp.concatenate([part[local:] for part in out_z], axis=0)
     cotangent_parts = gather_t(cotangent_z)
     attended = scatter_t(kept, given)
@@ -485,7 +491,8 @@
     scale_two = norm_scale(middle)
     normed_two = (middle * scale_two * gain_two).astype(BF)
 
-    buffer_parts = gather_t(dispatch_z(after(normed_two, out_z)), out_weight)
+    buffer_z = dispatch_z(after(normed_two, out_z))
+    buffer_parts = gather_t(after(buffer_z, in_swapped), out_weight)
     buffer, grad_expert, activation, grad_pre, kept, given = call(
         functools.partial(expert_layer, pieces=len(in_weight)),
         "expert_layer",
@@ -581,17 +588,17 @@
     )
     expert_sums = jnp.stack([in_sums, out_sums], axis=1)
     expert_sums = after(expert_sums, grad_middle)
-    delivered = [expert_sums[0], over_z(expert_sums[1], 1), over_z(expert_sums[2], 2)]
-    late_terms, kept, given, grad_gain_one, grad_rel, delivered, last = after(
-        (late_terms, kept, given, grad_gain_one, grad_rel, delivered, expert_sums[3]),
-        layer_parts[1],
-    )
-    delivered = delivered + [over_z(last, 3)]
+    delivered = deliver_z(expert_sums)
+    late_terms, kept, given, grad_gain_one, grad_rel = after(
+        (late_terms, kept, given, grad_gain_one, grad_rel), layer_parts[1]
+    )
     late_terms = blocks_to_send(late_terms)
     far_terms = swap_r(late_terms[:, 2:])
+    delivered = after(delivered, far_terms)
     far_sums = add(far_terms).astype(BF)
     near_terms = swap_r(after(late_terms[:, :2], far_sums))
-    grad_normed_one = scatter_t(kept, given)
+    given = over_t(given, 1)
+    grad_normed_one = finish_scatter(kept, given)
     own_inputs = tokens.astype(F32)
     grad_slots = jnp.concatenate(in_order(grad_parts), axis=0)
     grad_tokens = mm(from_slots_own, grad_slots, 1, 0) + norm_back(
@@ -620,10 +627,12 @@
             axis=0,
         ),
         far_terms,
-    )
-    low = small.astype(BF)
+        given,
+        layer_parts[2],
+    )
+    low = after(small, delivered).astype(BF)
     far = [over_z(jnp.concatenate([far_sums[d - 2], low], axis=0), d) for d in (2, 3)]
-    near_sums = add(after(near_terms, far, delivered))
+    near_sums = add(after(near_terms, far))
     near = over_z(jnp.concatenate([near_sums[1].astype(BF), low], axis=0), 1)
     late = jnp.concatenate([near_sums[0], small], axis=0)
     late = late + far[0].astype(F32) + far[1].astype(F32) + near.astype(F32)

time: 211 us -> 217 us (1.028)
  starting transfers between devices: 66 us -> 72.2 us
  other arithmetic: 9.5 us -> 12.9 us
  waiting for transfers between devices: 71.5 us -> 68.3 us
    ppermute x10, starting transfers between devices: 8.67 us -> 14.4 us  [over_r(): lax.ppermute(x, 'dp', [(i, i // r * r + (i % r ^ c)) for i in range(n)])]
    ppermute x18, waiting for transfers between devices: 18.8 us -> 14.7 us  [over_t(): return lax.ppermute(x, 'tensor', [(i, i ^ k) for i in range(T)])]
    select_n x5, other arithmetic: 0.27 us -> 2.77 us  [natural(): jnp.where(flip, parts[j ^ bit], parts[j])]
    unnamed x123 -> x95, local copies, waits for them, and re-layouts: 16.3 us -> 15.7 us
  transfers between devices with their start and end apart: 49 -> 49, of which waited for: 24 -> 20; matrix products, arithmetic and copies ran while one was open for 12% -> 14% of each run, Pallas kernels for 10% -> 10%
where the time goes in v5:
time: 217 us
  starting transfers between devices  72.2 us (33%)
  waiting for transfers between devices  68.3 us (31%)
  local copies, waits for them, and re-layouts  29 us (13%)
  Pallas kernels  27.2 us (13%)
  other arithmetic  12.9 us (6%)
  matrix products  4.7 us (2%)
  between operations  2.41 us (1%)
    ppermute x21, starting transfers between devices, over_z(): lax.ppermute(x, 'dp', [(i, (i // r ^ d) * r + i % r) for i in range(n)])  43.8 us
    ppermute x21, waiting for transfers between devices, over_z(): lax.ppermute(x, 'dp', [(i, (i // r ^ d) * r + i % r) for i in range(n)])  39 us
    pallas_call x5, Pallas kernels, call(): pl.pallas_call(kernel, out_shape=[jax.ShapeDtypeStruct(shape, kind) for s...  27.2 us
    unnamed x95, local copies, waits for them, and re-layouts  15.7 us
    ppermute x18, waiting for transfers between devices, over_t(): return lax.ppermute(x, 'tensor', [(i, i ^ k) for i in range(T)])  14.7 us
    ppermute x10, waiting for transfers between devices, over_r(): lax.ppermute(x, 'dp', [(i, i // r * r + (i % r ^ c)) for i in range(n)])  14.5 us
    ppermute x10, starting transfers between devices, over_r(): lax.ppermute(x, 'dp', [(i, i // r * r + (i % r ^ c)) for i in range(n)])  14.4 us
    ppermute x18, starting transfers between devices, over_t(): return lax.ppermute(x, 'tensor', [(i, i ^ k) for i in range(T)])  14.1 us
  transfers between devices with their start and end apart: 49, of which 20 were waited for; matrix products, arithmetic and copies ran while one was open for 14% of the time, Pallas kernels for 10%

profile of v5, /device:TPU:0, one launch (start us, length us, event | category | flops | bytes accessed | tf_op | source)
XLA Modules:
  0.0 216.7 jit_solution(5583779379429594160)
XLA Ops:
  4.3 4.1 %collective-permute-start.3 = (bf16[97,768]{1,0:T(8,128)(2,1)S(1)}, bf16[97,768]{1,0:T(8,128)(2,1)S(1)}, u32[]{:S(2)}, u32[]{:S(2)}) collective-permute-start(bf16[97,768]{1,0:T(8,128)(2,1)S(1)} %pad_maximum_fusion.15.rest_0_), channel_id=1, source_target_pairs={{0,16},{4,20},{8,24},{12,28},{16,0},{20,4},{24,8},{28,12},{1,17},{... | collective-permute-start | bytes 446984 | tf_op jit(solution)/shard_map/ppermute | solution.py:43
  10.0 1.5 collective-permute-start.6
  13.4 1.6 collective-permute-start
  18.5 2.3 %collective-permute-done.4.rest_1_ = bf16[97,768]{1,0:T(8,128)(2,1)S(1)} collective-permute-done((bf16[97,768]{1,0:T(8,128)(2,1)S(1)}, bf16[97,768]{1,0:T(8,128)(2,1)S(1)}, u32[]{:S(2)}, u32[]{:S(2)}) %collective-permute-start.4) | collective-permute-done | bytes 149024 | tf_op jit(solution)/shard_map/ppermute | solution.py:43
  21.0 1.6 collective-permute-start.5
  27.0 2.8 %collective-permute-start.7 = (bf16[96,768]{1,0:T(8,128)(2,1)}, bf16[96,768]{1,0:T(8,128)(2,1)S(1)}, u32[]{:S(2)}, u32[]{:S(2)}) collective-permute-start(bf16[96,768]{1,0:T(8,128)(2,1)} %get-tuple-element.205), channel_id=1, source_target_pairs={{0,8},{4,12},{8,0},{12,4},{16,24},{20,28},{24,16},{28,20},{1,9},{5... | collective-permute-start | bytes 442376 | tf_op jit(solution)/shard_map/ppermute | solution.py:43
  29.7 1.9 collective-permute-start.8
  32.5 1.5 collective-permute-start.10
  34.0 3.5 %collective-permute-done.7 = bf16[96,768]{1,0:T(8,128)(2,1)S(1)} collective-permute-done((bf16[96,768]{1,0:T(8,128)(2,1)}, bf16[96,768]{1,0:T(8,128)(2,1)S(1)}, u32[]{:S(2)}, u32[]{:S(2)}) %collective-permute-start.7) | collective-permute-done | bytes 147488 | tf_op jit(solution)/shard_map/ppermute | solution.py:43
  43.0 7.8 %attention_forward.1 = (bf16[512,768]{1,0:T(8,128)(2,1)S(1)}, bf16[512,576]{1,0:T(8,128)(2,1)S(1)}, f32[3,512,512]{2,1,0:T(8,128)}, bf16[512,192]{1,0:T(8,128)(2...) custom-call(s32[4]{0:T(128)S(1)} %pad_add_fusion.at_ref, ...), custom_call_target="tpu_custom_call" | custom-call | flops 12000000000 | bytes 2513408 | tf_op jit(solution)/shard_map/attention_forward/pallas_call | solution.py:119
  51.0 6.2 %collective-permute-start.13 = (bf16[128,768]{1,0:T(8,128)(2,1)S(1)}, bf16[128,768]{1,0:T(8,128)(2,1)S(1)}, u32[]{:S(2)}, u32[]{:S(2)}) collective-permute-start(bf16[128,768]{1,0:T(8,128)(2,1)S(1)} %get-tuple-element.197), channel_id=1, source_target_pairs={{0,8},{4,12},{8,0},{12,4},{16,24},{20,28},{24,16},{28,20},{1,9},{5... | collective-permute-start | bytes 589832 | tf_op jit(solution)/shard_map/ppermute | solution.py:43
  57.2 3.4 %collective-permute-start.14 = (bf16[128,768]{1,0:T(8,128)(2,1)S(1)}, bf16[128,768]{1,0:T(8,128)(2,1)S(1)}, u32[]{:S(2)}, u32[]{:S(2)}) collective-permute-start(bf16[128,768]{1,0:T(8,128)(2,1)S(1)} %get-tuple-element.196), channel_id=1, source_target_pairs={{0,16},{4,20},{8,24},{12,28},{16,0},{20,4},{24,8},{28,12},{1,17},{... | collective-permute-start | bytes 589832 | tf_op jit(solution)/shard_map/ppermute | solution.py:43
  61.6 1.6 collective-permute-start.19
  63.1 10.9 %collective-permute-done.15 = bf16[128,768]{1,0:T(8,128)(2,1)S(1)} collective-permute-done((bf16[128,768]{1,0:T(8,128)(2,1)S(1)}, bf16[128,768]{1,0:T(8,128)(2,1)S(1)}, u32[]{:S(2)}, u32[]{:S(2)}) %collective-permute-start.15) | collective-permute-done | bytes 196640 | tf_op jit(solution)/shard_map/ppermute | solution.py:43
  74.9 1.6 collective-permute-start.12
  76.6 1.5 collective-permute-start.21
  78.2 2.7 %collective-permute-done.12 = bf16[128,768]{1,0:T(8,128)(2,1)S(1)} collective-permute-done((bf16[128,768]{1,0:T(8,128)(2,1)S(1)}, bf16[128,768]{1,0:T(8,128)(2,1)S(1)}, u32[]{:S(2)}, u32[]{:S(2)}) %collective-permute-start.12) | collective-permute-done | bytes 196640 | tf_op jit(solution)/shard_map/ppermute | solution.py:37
  81.5 2.4 %collective-permute-start.18 = (bf16[32,768]{1,0:T(8,128)(2,1)S(1)}, bf16[32,768]{1,0:T(8,128)(2,1)S(1)}, u32[]{:S(2)}, u32[]{:S(2)}) collective-permute-start(bf16[32,768]{1,0:T(8,128)(2,1)S(1)} %get-tuple-element.224), channel_id=1, source_target_pairs={{0,24},{4,28},{8,16},{12,20},{16,8},{20,12},{24,0},{28,4},{1,25},{... | collective-permute-start | bytes 147464 | tf_op jit(solution)/shard_map/ppermute | solution.py:43
  83.9 4.0 %collective-permute-start.17 = (bf16[32,768]{1,0:T(8,128)(2,1)S(1)}, bf16[32,768]{1,0:T(8,128)(2,1)S(1)}, u32[]{:S(2)}, u32[]{:S(2)}) collective-permute-start(bf16[32,768]{1,0:T(8,128)(2,1)S(1)} %get-tuple-element.225), channel_id=1, source_target_pairs={{0,16},{4,20},{8,24},{12,28},{16,0},{20,4},{24,8},{28,12},{1,17},{... | collective-permute-start | bytes 147464 | tf_op jit(solution)/shard_map/ppermute | solution.py:43
  88.0 1.6 collective-permute-start.23
  92.1 1.6 collective-permute-start.20
  93.7 1.8 collective-permute-done.23.far_grad_ref
  96.3 1.7 collective-permute-done.20.far_ref
  99.8 1.9 collective-permute-done.22.near_ref
  104.8 6.4 %expert_layer.1 = (bf16[512,768]{1,0:T(8,128)(2,1)S(1)}, bf16[512,768]{1,0:T(8,128)(2,1)S(1)}, bf16[512,768]{1,0:T(8,128)(2,1)}, bf16[512,768]{1,0:T(8,128)(2,1)...) custom-call(s32[4]{0:T(128)S(1)} %pad_add_fusion.at_ref, ...), custom_call_target="tpu_custom_call" | custom-call | flops 8000000000 | bytes 4128768 | tf_op jit(solution)/shard_map/expert_layer/pallas_call | solution.py:119
  114.3 1.6 collective-permute-start.27
  116.2 1.6 collective-permute-start.26
  119.2 10.8 %collective-permute-done.27 = bf16[4,96,768]{2,1,0:T(8,128)(2,1)S(1)} collective-permute-done((bf16[4,96,768]{2,1,0:T(8,128)(2,1)S(1)}, bf16[4,96,768]{2,1,0:T(8,128)(2,1)S(1)}, u32[]{:S(2)}, u32[]{:S(2)}) %collective-permute-start.27) | collective-permute-done | bytes 589856 | tf_op jit(solution)/shard_map/ppermute | solution.py:49
  130.4 2.3 %collective-permute-start.30 = (bf16[32,1536]{1,0:T(8,128)(2,1)S(1)}, bf16[32,1536]{1,0:T(8,128)(2,1)S(1)}, u32[]{:S(2)}, u32[]{:S(2)}) collective-permute-start(bf16[32,1536]{1,0:T(8,128)(2,1)S(1)} %get-tuple-element.215), channel_id=1, source_target_pairs={{0,24},{4,28},{8,16},{12,20},{16,8},{20,12},{24,0},{28,4},{1,25},{... | collective-permute-start | bytes 294920 | tf_op jit(solution)/shard_map/ppermute | solution.py:43
  134.8 1.6 collective-permute-start.32
  136.4 1.5 collective-permute-done.30
  137.9 4.2 %collective-permute-done.29 = bf16[32,1536]{1,0:T(8,128)(2,1)S(1)} collective-permute-done((bf16[32,1536]{1,0:T(8,128)(2,1)S(1)}, bf16[32,1536]{1,0:T(8,128)(2,1)S(1)}, u32[]{:S(2)}, u32[]{:S(2)}) %collective-permute-start.29) | collective-permute-done | bytes 98336 | tf_op jit(solution)/shard_map/ppermute | solution.py:43
  143.1 1.6 collective-permute-start.31
  144.9 4.4 %collective-permute-done.31.far_ref = bf16[128,768]{1,0:T(8,128)(2,1)S(1)} collective-permute-done((bf16[128,768]{1,0:T(8,128)(2,1)S(1)}, bf16[128,768]{1,0:T(8,128)(2,1)S(1)}, u32[]{:S(2)}, u32[]{:S(2)}) %collective-permute-start.31) | collective-permute-done | bytes 196640 | tf_op jit(solution)/shard_map/ppermute | solution.py:37
  151.0 2.6 %collective-permute-start.44 = (bf16[2,96,768]{2,1,0:T(8,128)(2,1)}, bf16[2,96,768]{2,1,0:T(8,128)(2,1)}, u32[]{:S(2)}, u32[]{:S(2)}) collective-permute-start(bf16[2,96,768]{2,1,0:T(8,128)(2,1)} %get-tuple-element.188), channel_id=1, source_target_pairs={{0,16},{4,20},{8,24},{12,28},{16,0},{20,4},{24,8},{28,12},{1,17},{... | collective-permute-start | bytes 884744 | tf_op jit(solution)/shard_map/ppermute | solution.py:43
  155.9 1.5 collective-permute-start.34
  157.4 10.0 %attention_backward.1 = (bf16[2,4,96,768]{3,2,1,0:T(8,128)(2,1)S(1)}, bf16[2,128,768]{2,1,0:T(8,128)(2,1)S(1)}, bf16[2,128,768]{2,1,0:T(8,128)(2,1)S(1)}, f32[1,768]{1,0:T(1,128)S(1)}, f32[3,1024]{1,0:T(4,128)S(1)}) custom-call(s32[4]{0:T(128)S(1)} %pad_add_fusion.at_ref, bf16[128,768]{1,0:T(8,128)(2,1)S(1)} %add_convert_fusion.1.own_ref, ...), custom_call_target="tpu_custom_call" | custom-call | flops 12000000000 | bytes 7995392 | tf_op jit(solution)/shard_map/attention_backward/pallas_call | solution.py:119
  170.6 1.6 collective-permute-start.38
  172.2 1.7 collective-permute-done.40
  175.5 3.7 %collective-permute-done.41 = f32[8,768]{1,0:T(8,128)S(1)} collective-permute-done((f32[8,768]{1,0:T(8,128)S(1)}, f32[8,768]{1,0:T(8,128)S(1)}, u32[]{:S(2)}, u32[]{:S(2)}) %collective-permute-start.41) | collective-permute-done | bytes 24608 | tf_op jit(solution)/shard_map/ppermute | solution.py:49
  182.6 1.6 collective-permute-start.39
  184.3 1.8 copy.86
  186.2 1.8 copy.87
  188.1 1.6 collective-permute-start.37
  190.9 2.1 collective-permute-start.46
  194.9 10.7 %collective-permute-done.46 = bf16[104,768]{1,0:T(8,128)(2,1)S(1)} collective-permute-done((bf16[104,768]{1,0:T(8,128)(2,1)S(1)}, bf16[104,768]{1,0:T(8,128)(2,1)S(1)}, u32[]{:S(2)}, u32[]{:S(2)}) %collective-permute-start.46) | collective-permute-done | bytes 159776 | tf_op jit(solution)/shard_map/ppermute | solution.py:43
  205.8 3.5 %collective-permute-start.48 = (bf16[104,768]{1,0:T(8,128)(2,1)S(1)}, bf16[104,768]{1,0:T(8,128)(2,1)S(1)}, u32[]{:S(2)}, u32[]{:S(2)}) collective-permute-start(bf16[104,768]{1,0:T(8,128)(2,1)S(1)} %pad_maximum_fusion.10), channel_id=1, source_target_pairs={{0,8},{4,12},{8,0},{12,4},{16,24},{20,28},{24,16},{28,20},{1,9},{5... | collective-permute-start | bytes 479240 | tf_op jit(solution)/shard_map/ppermute | solution.py:43
  210.4 2.7 %collective-permute-done.48 = bf16[104,768]{1,0:T(8,128)(2,1)S(1)} collective-permute-done((bf16[104,768]{1,0:T(8,128)(2,1)S(1)}, bf16[104,768]{1,0:T(8,128)(2,1)S(1)}, u32[]{:S(2)}, u32[]{:S(2)}) %collective-permute-start.48) | collective-permute-done | bytes 159776 | tf_op jit(solution)/shard_map/ppermute | solution.py:43
  (297 shorter events, 60.0 us)
Async XLA Ops:
  4.3 16.5 %collective-permute-start.3 = (bf16[97,768]{1,0:T(8,128)(2,1)S(1)}, bf16[97,768]{1,0:T(8,128)(2,1)S(1)}, u32[]{:S(2)}, u32[]{:S(2)}) collective-permute-start(bf16[97,768]{1,0:T(8,128)(2,1)S(1)} %pad_maximum_fusion.15.rest_0_), channel_id=1, source_target_pairs={{0,16},{4,20},{8,24},{12,28},{16,0},{20,4},{24,8},{28,12},{1,17},{... | collective-permute-start | bytes 446984 | tf_op jit(solution)/shard_map/ppermute | solution.py:43
  8.5 12.4 %collective-permute-start.2 = (bf16[97,768]{1,0:T(8,128)(2,1)S(1)}, bf16[97,768]{1,0:T(8,128)(2,1)S(1)}, u32[]{:S(2)}, u32[]{:S(2)}) collective-permute-start(bf16[97,768]{1,0:T(8,128)(2,1)S(1)} %pad_maximum_fusion.15.rest_0_), channel_id=1, source_target_pairs={{0,24},{4,28},{8,16},{12,20},{16,8},{20,12},{24,0},{28,4},{1,25},{... | collective-permute-start | bytes 446984 | tf_op jit(solution)/shard_map/ppermute | solution.py:43
  9.8 11.0 %collective-permute-start.4 = (bf16[97,768]{1,0:T(8,128)(2,1)S(1)}, bf16[97,768]{1,0:T(8,128)(2,1)S(1)}, u32[]{:S(2)}, u32[]{:S(2)}) collective-permute-start(bf16[97,768]{1,0:T(8,128)(2,1)S(1)} %pad_maximum_fusion.15.rest_0_), channel_id=1, source_target_pairs={{0,8},{4,12},{8,0},{12,4},{16,24},{20,28},{24,16},{28,20},{1,9},{5... | collective-permute-start | bytes 446984 | tf_op jit(solution)/shard_map/ppermute | solution.py:43
  10.0 13.4 %collective-permute-start.6 = (bf16[97,768]{1,0:T(8,128)(2,1)S(1)}, bf16[97,768]{1,0:T(8,128)(2,1)S(1)}, u32[]{:S(2)}, u32[]{:S(2)}) collective-permute-start(bf16[97,768]{1,0:T(8,128)(2,1)S(1)} %pad_maximum_fusion.15.rest_0_), channel_id=1, source_target_pairs={{0,4},{4,0},{8,12},{12,8},{16,20},{20,16},{24,28},{28,24},{1,5},{5... | collective-permute-start | bytes 446984 | tf_op jit(solution)/shard_map/ppermute | solution.py:49
  13.4 10.5 %collective-permute-start = (bf16[128,1536]{1,0:T(8,128)(2,1)S(1)}, bf16[128,1536]{1,0:T(8,128)(2,1)S(1)}, u32[]{:S(2)}, u32[]{:S(2)}) collective-permute-start(bf16[128,1536]{1,0:T(8,128)(2,1)S(1)} %constant_dynamic-update-slice_fusion), channel_id=1, source_target_pairs={{0,2},{1,3},{2,0},{3,1},{4,6},{5,7},{6,4},{7,5},{8,10},{9,11},{10,... | collective-permute-start | bytes 1179656 | tf_op jit(solution)/shard_map/ppermute | solution.py:37
  21.0 3.9 %collective-permute-start.5 = (bf16[4,768]{1,0:T(4,128)(2,1)S(1)}, bf16[4,768]{1,0:T(4,128)(2,1)S(1)}, u32[]{:S(2)}, u32[]{:S(2)}) collective-permute-start(bf16[4,768]{1,0:T(4,128)(2,1)S(1)} %pad_maximum_fusion.17), channel_id=1, source_target_pairs={{0,4},{4,0},{8,12},{12,8},{16,20},{20,16},{24,28},{28,24},{1,5},{5... | collective-permute-start | bytes 18440 | tf_op jit(solution)/shard_map/ppermute | solution.py:49
  23.4 19.5 %collective-permute-start.9 = (bf16[3,96,768]{2,1,0:T(8,128)(2,1)}, bf16[3,96,768]{2,1,0:T(8,128)(2,1)S(1)}, u32[]{:S(2)}, u32[]{:S(2)}) collective-permute-start(bf16[3,96,768]{2,1,0:T(8,128)(2,1)} %pad_maximum_fusion.5), channel_id=1, source_target_pairs={{0,4},{4,0},{8,12},{12,8},{16,20},{20,16},{24,28},{28,24},{1,5},{5... | collective-permute-start | bytes 1327112 | tf_op jit(solution)/shard_map/ppermute | solution.py:49
  24.9 14.6 %collective-permute-start.1 = (bf16[2,128,1536]{2,1,0:T(8,128)(2,1)}, bf16[2,128,1536]{2,1,0:T(8,128)(2,1)}, u32[]{:S(2)}, u32[]{:S(2)}) collective-permute-start(bf16[2,128,1536]{2,1,0:T(8,128)(2,1)} %pad_maximum_fusion.1), channel_id=1, source_target_pairs={{0,1},{1,0},{2,3},{3,2},{4,5},{5,4},{6,7},{7,6},{8,9},{9,8},{10,11... | collective-permute-start | bytes 2359304 | tf_op jit(solution)/shard_map/ppermute | solution.py:37
  27.0 10.6 %collective-permute-start.7 = (bf16[96,768]{1,0:T(8,128)(2,1)}, bf16[96,768]{1,0:T(8,128)(2,1)S(1)}, u32[]{:S(2)}, u32[]{:S(2)}) collective-permute-start(bf16[96,768]{1,0:T(8,128)(2,1)} %get-tuple-element.205), channel_id=1, source_target_pairs={{0,8},{4,12},{8,0},{12,4},{16,24},{20,28},{24,16},{28,20},{1,9},{5... | collective-permute-start | bytes 442376 | tf_op jit(solution)/shard_map/ppermute | solution.py:43
  29.7 8.5 %collective-permute-start.8 = (bf16[96,768]{1,0:T(8,128)(2,1)}, bf16[96,768]{1,0:T(8,128)(2,1)}, u32[]{:S(2)}, u32[]{:S(2)}) collective-permute-start(bf16[96,768]{1,0:T(8,128)(2,1)} %get-tuple-element.204), channel_id=1, source_target_pairs={{0,16},{4,20},{8,24},{12,28},{16,0},{20,4},{24,8},{28,12},{1,17},{... | collective-permute-start | bytes 442376 | tf_op jit(solution)/shard_map/ppermute | solution.py:43
  32.5 18.3 %collective-permute-start.10 = (bf16[96,768]{1,0:T(8,128)(2,1)}, bf16[96,768]{1,0:T(8,128)(2,1)S(1)}, u32[]{:S(2)}, u32[]{:S(2)}) collective-permute-start(bf16[96,768]{1,0:T(8,128)(2,1)} %get-tuple-element.202), channel_id=1, source_target_pairs={{0,24},{4,28},{8,16},{12,20},{16,8},{20,12},{24,0},{28,4},{1,25},{... | collective-permute-start | bytes 442376 | tf_op jit(solution)/shard_map/ppermute | solution.py:43
  50.9 23.9 %collective-permute-start.11 = (bf16[2,128,768]{2,1,0:T(8,128)(2,1)S(1)}, bf16[2,128,768]{2,1,0:T(8,128)(2,1)S(1)}, u32[]{:S(2)}, u32[]{:S(2)}) collective-permute-start(bf16[2,128,768]{2,1,0:T(8,128)(2,1)S(1)} %get-tuple-element.82), channel_id=1, source_target_pairs={{0,1},{1,0},{2,3},{3,2},{4,5},{5,4},{6,7},{7,6},{8,9},{9,8},{10,11... | collective-permute-start | bytes 1179656 | tf_op jit(solution)/shard_map/ppermute | solution.py:37
  51.0 25.5 %collective-permute-start.13 = (bf16[128,768]{1,0:T(8,128)(2,1)S(1)}, bf16[128,768]{1,0:T(8,128)(2,1)S(1)}, u32[]{:S(2)}, u32[]{:S(2)}) collective-permute-start(bf16[128,768]{1,0:T(8,128)(2,1)S(1)} %get-tuple-element.197), channel_id=1, source_target_pairs={{0,8},{4,12},{8,0},{12,4},{16,24},{20,28},{24,16},{28,20},{1,9},{5... | collective-permute-start | bytes 589832 | tf_op jit(solution)/shard_map/ppermute | solution.py:43
  57.2 17.5 %collective-permute-start.14 = (bf16[128,768]{1,0:T(8,128)(2,1)S(1)}, bf16[128,768]{1,0:T(8,128)(2,1)S(1)}, u32[]{:S(2)}, u32[]{:S(2)}) collective-permute-start(bf16[128,768]{1,0:T(8,128)(2,1)S(1)} %get-tuple-element.196), channel_id=1, source_target_pairs={{0,16},{4,20},{8,24},{12,28},{16,0},{20,4},{24,8},{28,12},{1,17},{... | collective-permute-start | bytes 589832 | tf_op jit(solution)/shard_map/ppermute | solution.py:43
  60.6 13.5 %collective-permute-start.15 = (bf16[128,768]{1,0:T(8,128)(2,1)S(1)}, bf16[128,768]{1,0:T(8,128)(2,1)S(1)}, u32[]{:S(2)}, u32[]{:S(2)}) collective-permute-start(bf16[128,768]{1,0:T(8,128)(2,1)S(1)} %get-tuple-element.195), channel_id=1, source_target_pairs={{0,24},{4,28},{8,16},{12,20},{16,8},{20,12},{24,0},{28,4},{1,25},{... | collective-permute-start | bytes 589832 | tf_op jit(solution)/shard_map/ppermute | solution.py:43
  61.6 30.5 %collective-permute-start.19 = (bf16[4,96,768]{2,1,0:T(8,128)(2,1)S(1)}, bf16[4,96,768]{2,1,0:T(8,128)(2,1)S(1)}, u32[]{:S(2)}, u32[]{:S(2)}) collective-permute-start(bf16[4,96,768]{2,1,0:T(8,128)(2,1)S(1)} %pad_maximum_fusion.3.rest_0_), channel_id=1, source_target_pairs={{0,4},{4,0},{8,12},{12,8},{16,20},{20,16},{24,28},{28,24},{1,5},{5... | collective-permute-start | bytes 1769480 | tf_op jit(solution)/shard_map/ppermute | solution.py:49
  74.9 6.0 %collective-permute-start.12 = (bf16[128,768]{1,0:T(8,128)(2,1)S(1)}, bf16[128,768]{1,0:T(8,128)(2,1)S(1)}, u32[]{:S(2)}, u32[]{:S(2)}) collective-permute-start(bf16[128,768]{1,0:T(8,128)(2,1)S(1)} %fusion.45), channel_id=1, source_target_pairs={{0,2},{1,3},{2,0},{3,1},{4,6},{5,7},{6,4},{7,5},{8,10},{9,11},{10,... | collective-permute-start | bytes 589832 | tf_op jit(solution)/shard_map/ppermute | solution.py:37
  76.6 22.2 %collective-permute-start.21 = (bf16[4,96,768]{2,1,0:T(8,128)(2,1)S(1)}, bf16[4,96,768]{2,1,0:T(8,128)(2,1)S(1)}, u32[]{:S(2)}, u32[]{:S(2)}) collective-permute-start(bf16[4,96,768]{2,1,0:T(8,128)(2,1)S(1)} %pad_maximum_fusion.4.rest_2_), channel_id=1, source_target_pairs={{0,4},{4,0},{8,12},{12,8},{16,20},{20,16},{24,28},{28,24},{1,5},{5... | collective-permute-start | bytes 1769480 | tf_op jit(solution)/shard_map/ppermute | solution.py:49
  81.5 6.5 %collective-permute-start.18 = (bf16[32,768]{1,0:T(8,128)(2,1)S(1)}, bf16[32,768]{1,0:T(8,128)(2,1)S(1)}, u32[]{:S(2)}, u32[]{:S(2)}) collective-permute-start(bf16[32,768]{1,0:T(8,128)(2,1)S(1)} %get-tuple-element.224), channel_id=1, source_target_pairs={{0,24},{4,28},{8,16},{12,20},{16,8},{20,12},{24,0},{28,4},{1,25},{... | collective-permute-start | bytes 147464 | tf_op jit(solution)/shard_map/ppermute | solution.py:43
  83.9 6.8 %collective-permute-start.17 = (bf16[32,768]{1,0:T(8,128)(2,1)S(1)}, bf16[32,768]{1,0:T(8,128)(2,1)S(1)}, u32[]{:S(2)}, u32[]{:S(2)}) collective-permute-start(bf16[32,768]{1,0:T(8,128)(2,1)S(1)} %get-tuple-element.225), channel_id=1, source_target_pairs={{0,16},{4,20},{8,24},{12,28},{16,0},{20,4},{24,8},{28,12},{1,17},{... | collective-permute-start | bytes 147464 | tf_op jit(solution)/shard_map/ppermute | solution.py:43
  88.0 4.1 %collective-permute-start.16 = (bf16[32,768]{1,0:T(8,128)(2,1)S(1)}, bf16[32,768]{1,0:T(8,128)(2,1)S(1)}, u32[]{:S(2)}, u32[]{:S(2)}) collective-permute-start(bf16[32,768]{1,0:T(8,128)(2,1)S(1)} %get-tuple-element.226), channel_id=1, source_target_pairs={{0,8},{4,12},{8,0},{12,4},{16,24},{20,28},{24,16},{28,20},{1,9},{5... | collective-permute-start | bytes 147464 | tf_op jit(solution)/shard_map/ppermute | solution.py:43
  88.0 7.5 %collective-permute-start.23 = (bf16[128,768]{1,0:T(8,128)(2,1)S(1)}, bf16[128,768]{1,0:T(8,128)(2,1)S(1)}, u32[]{:S(2)}, u32[]{:S(2)}) collective-permute-start(bf16[128,768]{1,0:T(8,128)(2,1)S(1)} %get-tuple-element.222.own_grad_ref), channel_id=1, source_target_pairs={{0,2},{1,3},{2,0},{3,1},{4,6},{5,7},{6,4},{7,5},{8,10},{9,11},{10,... | collective-permute-start | bytes 589832 | tf_op jit(solution)/shard_map/ppermute | solution.py:37
  92.1 5.9 %collective-permute-start.20 = (bf16[128,768]{1,0:T(8,128)(2,1)S(1)}, bf16[128,768]{1,0:T(8,128)(2,1)S(1)}, u32[]{:S(2)}, u32[]{:S(2)}) collective-permute-start(bf16[128,768]{1,0:T(8,128)(2,1)S(1)} %pad_maximum_fusion.13.own_ref), channel_id=1, source_target_pairs={{0,2},{1,3},{2,0},{3,1},{4,6},{5,7},{6,4},{7,5},{8,10},{9,11},{10,... | collective-permute-start | bytes 589832 | tf_op jit(solution)/shard_map/ppermute | solution.py:37
  96.3 3.5 %collective-permute-start.24 = (bf16[2,128,768]{2,1,0:T(8,128)(2,1)}, bf16[2,128,768]{2,1,0:T(8,128)(2,1)}, u32[]{:S(2)}, u32[]{:S(2)}) collective-permute-start(bf16[2,128,768]{2,1,0:T(8,128)(2,1)} %pad_maximum_fusion.7), channel_id=1, source_target_pairs={{0,1},{1,0},{2,3},{3,2},{4,5},{5,4},{6,7},{7,6},{8,9},{9,8},{10,11... | collective-permute-start | bytes 1179656 | tf_op jit(solution)/shard_map/ppermute | solution.py:37
  99.6 2.1 collective-permute-start.22
  111.2 4.7 %collective-permute-start.25 = (bf16[2,128,1536]{2,1,0:T(8,128)(2,1)}, bf16[2,128,1536]{2,1,0:T(8,128)(2,1)S(1)}, u32[]{:S(2)}, u32[]{:S(2)}) collective-permute-start(bf16[2,128,1536]{2,1,0:T(8,128)(2,1)} %get-tuple-element.92), channel_id=1, source_target_pairs={{0,1},{1,0},{2,3},{3,2},{4,5},{5,4},{6,7},{7,6},{8,9},{9,8},{10,11... | collective-permute-start | bytes 2359304 | tf_op jit(solution)/shard_map/ppermute | solution.py:37
  114.3 15.7 %collective-permute-start.27 = (bf16[4,96,768]{2,1,0:T(8,128)(2,1)S(1)}, bf16[4,96,768]{2,1,0:T(8,128)(2,1)S(1)}, u32[]{:S(2)}, u32[]{:S(2)}) collective-permute-start(bf16[4,96,768]{2,1,0:T(8,128)(2,1)S(1)} %slice_bitcast_fusion), channel_id=1, source_target_pairs={{0,4},{4,0},{8,12},{12,8},{16,20},{20,16},{24,28},{28,24},{1,5},{5... | collective-permute-start | bytes 1769480 | tf_op jit(solution)/shard_map/ppermute | solution.py:49
  116.2 14.0 %collective-permute-start.26 = (bf16[128,1536]{1,0:T(8,128)(2,1)S(1)}, bf16[128,1536]{1,0:T(8,128)(2,1)S(1)}, u32[]{:S(2)}, u32[]{:S(2)}) collective-permute-start(bf16[128,1536]{1,0:T(8,128)(2,1)S(1)} %fusion.35), channel_id=1, source_target_pairs={{0,2},{1,3},{2,0},{3,1},{4,6},{5,7},{6,4},{7,5},{8,10},{9,11},{10,... | collective-permute-start | bytes 1179656 | tf_op jit(solution)/shard_map/ppermute | solution.py:37
  130.4 7.6 %collective-permute-start.30 = (bf16[32,1536]{1,0:T(8,128)(2,1)S(1)}, bf16[32,1536]{1,0:T(8,128)(2,1)S(1)}, u32[]{:S(2)}, u32[]{:S(2)}) collective-permute-start(bf16[32,1536]{1,0:T(8,128)(2,1)S(1)} %get-tuple-element.215), channel_id=1, source_target_pairs={{0,24},{4,28},{8,16},{12,20},{16,8},{20,12},{24,0},{28,4},{1,25},{... | collective-permute-start | bytes 294920 | tf_op jit(solution)/shard_map/ppermute | solution.py:43
  132.7 9.5 %collective-permute-start.29 = (bf16[32,1536]{1,0:T(8,128)(2,1)S(1)}, bf16[32,1536]{1,0:T(8,128)(2,1)S(1)}, u32[]{:S(2)}, u32[]{:S(2)}) collective-permute-start(bf16[32,1536]{1,0:T(8,128)(2,1)S(1)} %get-tuple-element.216), channel_id=1, source_target_pairs={{0,16},{4,20},{8,24},{12,28},{16,0},{20,4},{24,8},{28,12},{1,17},{... | collective-permute-start | bytes 294920 | tf_op jit(solution)/shard_map/ppermute | solution.py:43
  133.6 8.6 %collective-permute-start.28 = (bf16[32,1536]{1,0:T(8,128)(2,1)S(1)}, bf16[32,1536]{1,0:T(8,128)(2,1)S(1)}, u32[]{:S(2)}, u32[]{:S(2)}) collective-permute-start(bf16[32,1536]{1,0:T(8,128)(2,1)S(1)} %get-tuple-element.217), channel_id=1, source_target_pairs={{0,8},{4,12},{8,0},{12,4},{16,24},{20,28},{24,16},{28,20},{1,9},{5... | collective-permute-start | bytes 294920 | tf_op jit(solution)/shard_map/ppermute | solution.py:43
  134.8 14.6 %collective-permute-start.32 = (bf16[4,96,768]{2,1,0:T(8,128)(2,1)S(1)}, bf16[4,96,768]{2,1,0:T(8,128)(2,1)S(1)}, u32[]{:S(2)}, u32[]{:S(2)}) collective-permute-start(bf16[4,96,768]{2,1,0:T(8,128)(2,1)S(1)} %slice_bitcast_fusion.2), channel_id=1, source_target_pairs={{0,4},{4,0},{8,12},{12,8},{16,20},{20,16},{24,28},{28,24},{1,5},{5... | collective-permute-start | bytes 1769480 | tf_op jit(solution)/shard_map/ppermute | solution.py:49
  143.1 6.2 %collective-permute-start.31 = (bf16[128,768]{1,0:T(8,128)(2,1)S(1)}, bf16[128,768]{1,0:T(8,128)(2,1)S(1)}, u32[]{:S(2)}, u32[]{:S(2)}) collective-permute-start(bf16[128,768]{1,0:T(8,128)(2,1)S(1)} %add_convert_fusion.1.own_ref), channel_id=1, source_target_pairs={{0,2},{1,3},{2,0},{3,1},{4,6},{5,7},{6,4},{7,5},{8,10},{9,11},{10,... | collective-permute-start | bytes 589832 | tf_op jit(solution)/shard_map/ppermute | solution.py:37
  149.6 6.3 %collective-permute-start.33 = (bf16[2,128,768]{2,1,0:T(8,128)(2,1)S(1)}, bf16[2,128,768]{2,1,0:T(8,128)(2,1)S(1)}, u32[]{:S(2)}, u32[]{:S(2)}) collective-permute-start(bf16[2,128,768]{2,1,0:T(8,128)(2,1)S(1)} %pad_maximum_fusion.8), channel_id=1, source_target_pairs={{0,1},{1,0},{2,3},{3,2},{4,5},{5,4},{6,7},{7,6},{8,9},{9,8},{10,11... | collective-permute-start | bytes 1179656 | tf_op jit(solution)/shard_map/ppermute | solution.py:37
  150.7 28.5 %collective-permute-start.43 = (bf16[2,96,768]{2,1,0:T(8,128)(2,1)}, bf16[2,96,768]{2,1,0:T(8,128)(2,1)}, u32[]{:S(2)}, u32[]{:S(2)}) collective-permute-start(bf16[2,96,768]{2,1,0:T(8,128)(2,1)} %get-tuple-element.189), channel_id=1, source_target_pairs={{0,8},{4,12},{8,0},{12,4},{16,24},{20,28},{24,16},{28,20},{1,9},{5... | collective-permute-start | bytes 884744 | tf_op jit(solution)/shard_map/ppermute | solution.py:43
  151.0 28.8 %collective-permute-start.44 = (bf16[2,96,768]{2,1,0:T(8,128)(2,1)}, bf16[2,96,768]{2,1,0:T(8,128)(2,1)}, u32[]{:S(2)}, u32[]{:S(2)}) collective-permute-start(bf16[2,96,768]{2,1,0:T(8,128)(2,1)} %get-tuple-element.188), channel_id=1, source_target_pairs={{0,16},{4,20},{8,24},{12,28},{16,0},{20,4},{24,8},{28,12},{1,17},{... | collective-permute-start | bytes 884744 | tf_op jit(solution)/shard_map/ppermute | solution.py:43
  154.4 25.4 %collective-permute-start.45 = (bf16[2,96,768]{2,1,0:T(8,128)(2,1)}, bf16[2,96,768]{2,1,0:T(8,128)(2,1)}, u32[]{:S(2)}, u32[]{:S(2)}) collective-permute-start(bf16[2,96,768]{2,1,0:T(8,128)(2,1)} %slice_bitcast_fusion.9), channel_id=1, source_target_pairs={{0,24},{4,28},{8,16},{12,20},{16,8},{20,12},{24,0},{28,4},{1,25},{... | collective-permute-start | bytes 884744 | tf_op jit(solution)/shard_map/ppermute | solution.py:43
  155.9 13.0 %collective-permute-start.34 = (bf16[128,768]{1,0:T(8,128)(2,1)S(1)}, bf16[128,768]{1,0:T(8,128)(2,1)S(1)}, u32[]{:S(2)}, u32[]{:S(2)}) collective-permute-start(bf16[128,768]{1,0:T(8,128)(2,1)S(1)} %get-tuple-element.100), channel_id=1, source_target_pairs={{0,2},{1,3},{2,0},{3,1},{4,6},{5,7},{6,4},{7,5},{8,10},{9,11},{10,... | collective-permute-start | bytes 589832 | tf_op jit(solution)/shard_map/ppermute | solution.py:37
  170.0 3.9 %collective-permute-start.40 = (f32[8,768]{1,0:T(8,128)S(1)}, f32[8,768]{1,0:T(8,128)S(1)}, u32[]{:S(2)}, u32[]{:S(2)}) collective-permute-start(f32[8,768]{1,0:T(8,128)S(1)} %concatenate.59), channel_id=1, source_target_pairs={{0,2},{1,3},{2,0},{3,1},{4,6},{5,7},{6,4},{7,5},{8,10},{9,11},{10,... | collective-permute-start | bytes 73736 | tf_op jit(solution)/shard_map/ppermute | solution.py:37
  170.6 9.2 %collective-permute-start.38 = (bf16[2,96,768]{2,1,0:T(8,128)(2,1)S(1)}, bf16[2,96,768]{2,1,0:T(8,128)(2,1)S(1)}, u32[]{:S(2)}, u32[]{:S(2)}) collective-permute-start(bf16[2,96,768]{2,1,0:T(8,128)(2,1)S(1)} %slice_bitcast_fusion.12), channel_id=1, source_target_pairs={{0,4},{4,0},{8,12},{12,8},{16,20},{20,16},{24,28},{28,24},{1,5},{5... | collective-permute-start | bytes 884744 | tf_op jit(solution)/shard_map/ppermute | solution.py:49
  173.9 5.3 %collective-permute-start.41 = (f32[8,768]{1,0:T(8,128)S(1)}, f32[8,768]{1,0:T(8,128)S(1)}, u32[]{:S(2)}, u32[]{:S(2)}) collective-permute-start(f32[8,768]{1,0:T(8,128)S(1)} %add.204), channel_id=1, source_target_pairs={{0,4},{4,0},{8,12},{12,8},{16,20},{20,16},{24,28},{28,24},{1,5},{5... | collective-permute-start | bytes 73736 | tf_op jit(solution)/shard_map/ppermute | solution.py:49
  179.2 10.5 %collective-permute-start.35 = (bf16[2,128,768]{2,1,0:T(8,128)(2,1)S(1)}, bf16[2,128,768]{2,1,0:T(8,128)(2,1)S(1)}, u32[]{:S(2)}, u32[]{:S(2)}) collective-permute-start(bf16[2,128,768]{2,1,0:T(8,128)(2,1)S(1)} %pad_maximum_fusion.9), channel_id=1, source_target_pairs={{0,1},{1,0},{2,3},{3,2},{4,5},{5,4},{6,7},{7,6},{8,9},{9,8},{10,11... | collective-permute-start | bytes 1179656 | tf_op jit(solution)/shard_map/ppermute | solution.py:37
  179.2 8.7 %collective-permute-start.36 = (bf16[2,128,768]{2,1,0:T(8,128)(2,1)S(1)}, bf16[2,128,768]{2,1,0:T(8,128)(2,1)S(1)}, u32[]{:S(2)}, u32[]{:S(2)}) collective-permute-start(bf16[2,128,768]{2,1,0:T(8,128)(2,1)S(1)} %copy-done.10), channel_id=1, source_target_pairs={{0,1},{1,0},{2,3},{3,2},{4,5},{5,4},{6,7},{7,6},{8,9},{9,8},{10,11... | collective-permute-start | bytes 1179656 | tf_op jit(solution)/shard_map/ppermute | solution.py:37
  182.6 23.0 %collective-permute-start.39 = (bf16[2,96,768]{2,1,0:T(8,128)(2,1)S(1)}, bf16[2,96,768]{2,1,0:T(8,128)(2,1)S(1)}, u32[]{:S(2)}, u32[]{:S(2)}) collective-permute-start(bf16[2,96,768]{2,1,0:T(8,128)(2,1)S(1)} %get-tuple-element.200), channel_id=1, source_target_pairs={{0,4},{4,0},{8,12},{12,8},{16,20},{20,16},{24,28},{28,24},{1,5},{5... | collective-permute-start | bytes 884744 | tf_op jit(solution)/shard_map/ppermute | solution.py:49
  188.1 6.6 %collective-permute-start.37 = (bf16[128,768]{1,0:T(8,128)(2,1)S(1)}, bf16[128,768]{1,0:T(8,128)(2,1)S(1)}, u32[]{:S(2)}, u32[]{:S(2)}) collective-permute-start(bf16[128,768]{1,0:T(8,128)(2,1)S(1)} %fusion.46), channel_id=1, source_target_pairs={{0,2},{1,3},{2,0},{3,1},{4,6},{5,7},{6,4},{7,5},{8,10},{9,11},{10,... | collective-permute-start | bytes 589832 | tf_op jit(solution)/shard_map/ppermute | solution.py:37
  190.9 14.7 %collective-permute-start.46 = (bf16[104,768]{1,0:T(8,128)(2,1)S(1)}, bf16[104,768]{1,0:T(8,128)(2,1)S(1)}, u32[]{:S(2)}, u32[]{:S(2)}) collective-permute-start(bf16[104,768]{1,0:T(8,128)(2,1)S(1)} %get-tuple-element.228), channel_id=1, source_target_pairs={{0,16},{4,20},{8,24},{12,28},{16,0},{20,4},{24,8},{28,12},{1,17},{... | collective-permute-start | bytes 479240 | tf_op jit(solution)/shard_map/ppermute | solution.py:43
  193.0 12.7 %collective-permute-start.47 = (bf16[104,768]{1,0:T(8,128)(2,1)S(1)}, bf16[104,768]{1,0:T(8,128)(2,1)S(1)}, u32[]{:S(2)}, u32[]{:S(2)}) collective-permute-start(bf16[104,768]{1,0:T(8,128)(2,1)S(1)} %get-tuple-element.227), channel_id=1, source_target_pairs={{0,24},{4,28},{8,16},{12,20},{16,8},{20,12},{24,0},{28,4},{1,25},{... | collective-permute-start | bytes 479240 | tf_op jit(solution)/shard_map/ppermute | solution.py:43
  205.8 7.3 %collective-permute-start.48 = (bf16[104,768]{1,0:T(8,128)(2,1)S(1)}, bf16[104,768]{1,0:T(8,128)(2,1)S(1)}, u32[]{:S(2)}, u32[]{:S(2)}) collective-permute-start(bf16[104,768]{1,0:T(8,128)(2,1)S(1)} %pad_maximum_fusion.10), channel_id=1, source_target_pairs={{0,8},{4,12},{8,0},{12,4},{16,24},{20,28},{24,16},{28,20},{1,9},{5... | collective-permute-start | bytes 479240 | tf_op jit(solution)/shard_map/ppermute | solution.py:43
  (47 other events, 339.7 us)

commit v6 on v5

--- a/solution.py
+++ b/solution.py
@@ -100,11 +100,11 @@
 
 def sum_but_z(x, *earlier):
     R = lax.axis_size("dp") // E
-    x = x + over_t(x, 2)
     c = 1
     while c < R:
         x = x + over_r(x, c)
         c *= 2
+    x = x + over_t(x, 2)
     x = after(x, *earlier)
     return x + over_t(x, 1)
 
@@ -475,8 +475,9 @@
     normed_all, qkv, probs, heads_all, kept, given, tokens_all, attention_weight = after(
         forward, in_z
     )
-    in_z, out_rows = after((in_z, out_rows), kept)
-    in_columns = jnp.stack(in_z)
+    given = over_t(given, 1)
+    out_rows = after(out_rows, given)
+    in_columns = jnp.stack(after(in_z, given))
     in_swapped = [over_r(in_columns, c) for c in range(1, R)]
     in_weight = whole([in_columns] + in_swapped)
     out_z = deliver_z(out_rows)
@@ -485,7 +486,7 @@
     out_weight = whole([out_columns] + out_swapped)
     cotangent_z = jnp.concatenate([part[local:] for part in out_z], axis=0)
     cotangent_parts = gather_t(cotangent_z)
-    attended = scatter_t(kept, given)
+    attended = finish_scatter(kept, given)
     inputs = mm(to_slots[:ROWS], tokens_all, 1, 0)
     middle = inputs + attended
     scale_two = norm_scale(middle)
@@ -632,7 +633,8 @@
     )
     low = after(small, delivered).astype(BF)
     far = [over_z(jnp.concatenate([far_sums[d - 2], low], axis=0), d) for d in (2, 3)]
-    near_sums = add(after(near_terms, far))
+    near_terms, delivered = after((near_terms, delivered), far)
+    near_sums = add(near_terms)
     near = over_z(jnp.concatenate([near_sums[1].astype(BF), low], axis=0), 1)
     late = jnp.concatenate([near_sums[0], small], axis=0)
     late = late + far[0].astype(F32) + far[1].astype(F32) + near.astype(F32)

time: 217 us -> 217 us (level)
  starting transfers between devices: 72.2 us -> 63.5 us
  local copies, waits for them, and re-layouts: 29 us -> 34.4 us
    ppermute x18, starting transfers between devices: 14.1 us -> 9.22 us  [over_t(): return lax.ppermute(x, 'tensor', [(i, i ^ k) for i in range(T)])]
    ppermute x21, waiting for transfers between devices: 39 us -> 36 us  [over_z(): lax.ppermute(x, 'dp', [(i, (i // r ^ d) * r + i % r) for i in range(n)])]
    ppermute x10, starting transfers between devices: 14.4 us -> 11.6 us  [over_r(): lax.ppermute(x, 'dp', [(i, i // r * r + (i % r ^ c)) for i in range(n)])]
    unnamed x95 -> x93, local copies, waits for them, and re-layouts: 15.7 us -> 18.3 us
    ppermute x18, waiting for transfers between devices: 14.7 us -> 17 us  [over_t(): return lax.ppermute(x, 'tensor', [(i, i ^ k) for i in range(T)])]
  transfers between devices with their start and end apart: 49 -> 49, of which waited for: 20 -> 21; matrix products, arithmetic and copies ran while one was open for 14% -> 15% of each run, Pallas kernels for 10% -> 10%
where the time goes in v6:
time: 217 us; the launch traced here: 216 us
  waiting for transfers between devices  68.5 us (32%)
  starting transfers between devices  63.5 us (29%)
  local copies, waits for them, and re-layouts  34.4 us (16%)
  Pallas kernels  27.4 us (13%)
  other arithmetic  13.8 us (6%)
  matrix products  6.23 us (3%)
  between operations  2.33 us (1%)
    ppermute x21, starting transfers between devices, over_z(): lax.ppermute(x, 'dp', [(i, (i // r ^ d) * r + i % r) for i in range(n)])  42.7 us
    ppermute x21, waiting for transfers between devices, over_z(): lax.ppermute(x, 'dp', [(i, (i // r ^ d) * r + i % r) for i in range(n)])  36 us
    pallas_call x5, Pallas kernels, call(): pl.pallas_call(kernel, out_shape=[jax.ShapeDtypeStruct(shape, kind) for s...  27.4 us
    unnamed x93, local copies, waits for them, and re-layouts  18.3 us
    ppermute x18, waiting for transfers between devices, over_t(): return lax.ppermute(x, 'tensor', [(i, i ^ k) for i in range(T)])  17 us
    ppermute x10, waiting for transfers between devices, over_r(): lax.ppermute(x, 'dp', [(i, i // r * r + (i % r ^ c)) for i in range(n)])  15.5 us
    ppermute x10, starting transfers between devices, over_r(): lax.ppermute(x, 'dp', [(i, i // r * r + (i % r ^ c)) for i in range(n)])  11.6 us
    ppermute x18, starting transfers between devices, over_t(): return lax.ppermute(x, 'tensor', [(i, i ^ k) for i in range(T)])  9.22 us
  transfers between devices with their start and end apart: 49, of which 21 were waited for; matrix products, arithmetic and copies ran while one was open for 15% of the time, Pallas kernels for 10%

profile of v6, /device:TPU:0, one launch (start us, length us, event | category | flops | bytes accessed | tf_op | source)
XLA Modules:
  0.0 216.2 jit_solution(3975062187271341147)
XLA Ops:
  4.3 4.1 %collective-permute-start.3 = (bf16[97,768]{1,0:T(8,128)(2,1)S(1)}, bf16[97,768]{1,0:T(8,128)(2,1)S(1)}, u32[]{:S(2)}, u32[]{:S(2)}) collective-permute-start(bf16[97,768]{1,0:T(8,128)(2,1)S(1)} %pad_maximum_fusion.15.rest_0_), channel_id=1, source_target_pairs={{0,16},{4,20},{8,24},{12,28},{16,0},{20,4},{24,8},{28,12},{1,17},{... | collective-permute-start | bytes 446984 | tf_op jit(solution)/shard_map/ppermute | solution.py:43
  8.5 1.3 collective-permute-start.2
  10.0 1.5 collective-permute-start.6
  13.4 1.6 collective-permute-start
  17.9 2.9 %collective-permute-done.4.rest_1_ = bf16[97,768]{1,0:T(8,128)(2,1)S(1)} collective-permute-done((bf16[97,768]{1,0:T(8,128)(2,1)S(1)}, bf16[97,768]{1,0:T(8,128)(2,1)S(1)}, u32[]{:S(2)}, u32[]{:S(2)}) %collective-permute-start.4) | collective-permute-done | bytes 149024 | tf_op jit(solution)/shard_map/ppermute | solution.py:43
  21.0 1.6 collective-permute-start.5
  27.0 2.8 %collective-permute-start.7 = (bf16[96,768]{1,0:T(8,128)(2,1)}, bf16[96,768]{1,0:T(8,128)(2,1)S(1)}, u32[]{:S(2)}, u32[]{:S(2)}) collective-permute-start(bf16[96,768]{1,0:T(8,128)(2,1)} %get-tuple-element.213), channel_id=1, source_target_pairs={{0,8},{4,12},{8,0},{12,4},{16,24},{20,28},{24,16},{28,20},{1,9},{5... | collective-permute-start | bytes 442376 | tf_op jit(solution)/shard_map/ppermute | solution.py:43
  29.7 1.9 collective-permute-start.8
  32.5 1.5 collective-permute-start.10
  34.0 3.6 %collective-permute-done.7 = bf16[96,768]{1,0:T(8,128)(2,1)S(1)} collective-permute-done((bf16[96,768]{1,0:T(8,128)(2,1)}, bf16[96,768]{1,0:T(8,128)(2,1)S(1)}, u32[]{:S(2)}, u32[]{:S(2)}) %collective-permute-start.7) | collective-permute-done | bytes 147488 | tf_op jit(solution)/shard_map/ppermute | solution.py:43
  40.8 1.8 select_convert_fusion
  44.6 8.1 %attention_forward.1 = (bf16[512,768]{1,0:T(8,128)(2,1)S(1)}, bf16[512,576]{1,0:T(8,128)(2,1)S(1)}, f32[3,512,512]{2,1,0:T(8,128)}, bf16[512,192]{1,0:T(8,128)(2...) custom-call(s32[4]{0:T(128)S(1)} %pad_add_fusion.at_ref, ...), custom_call_target="tpu_custom_call" | custom-call | flops 12000000000 | bytes 2513408 | tf_op jit(solution)/shard_map/attention_forward/pallas_call | solution.py:119
  55.8 1.8 collective-permute-done.11
  59.8 1.6 collective-permute-start.12
  61.4 6.2 %collective-permute-start.13 = (bf16[128,768]{1,0:T(8,128)(2,1)S(1)}, bf16[128,768]{1,0:T(8,128)(2,1)S(1)}, u32[]{:S(2)}, u32[]{:S(2)}) collective-permute-start(bf16[128,768]{1,0:T(8,128)(2,1)S(1)} %get-tuple-element.205), channel_id=1, source_target_pairs={{0,8},{4,12},{8,0},{12,4},{16,24},{20,28},{24,16},{28,20},{1,9},{5... | collective-permute-start | bytes 589832 | tf_op jit(solution)/shard_map/ppermute | solution.py:43
  67.6 3.4 %collective-permute-start.14 = (bf16[128,768]{1,0:T(8,128)(2,1)S(1)}, bf16[128,768]{1,0:T(8,128)(2,1)S(1)}, u32[]{:S(2)}, u32[]{:S(2)}) collective-permute-start(bf16[128,768]{1,0:T(8,128)(2,1)S(1)} %get-tuple-element.204), channel_id=1, source_target_pairs={{0,16},{4,20},{8,24},{12,28},{16,0},{20,4},{24,8},{28,12},{1,17},{... | collective-permute-start | bytes 589832 | tf_op jit(solution)/shard_map/ppermute | solution.py:43
  72.0 1.6 collective-permute-start.19
  76.0 9.2 %collective-permute-done.14 = bf16[128,768]{1,0:T(8,128)(2,1)S(1)} collective-permute-done((bf16[128,768]{1,0:T(8,128)(2,1)S(1)}, bf16[128,768]{1,0:T(8,128)(2,1)S(1)}, u32[]{:S(2)}, u32[]{:S(2)}) %collective-permute-start.14) | collective-permute-done | bytes 196640 | tf_op jit(solution)/shard_map/ppermute | solution.py:43
  85.3 1.6 collective-permute-start.21
  87.0 2.4 %collective-permute-start.18 = (bf16[32,768]{1,0:T(8,128)(2,1)S(1)}, bf16[32,768]{1,0:T(8,128)(2,1)S(1)}, u32[]{:S(2)}, u32[]{:S(2)}) collective-permute-start(bf16[32,768]{1,0:T(8,128)(2,1)S(1)} %get-tuple-element.232), channel_id=1, source_target_pairs={{0,24},{4,28},{8,16},{12,20},{16,8},{20,12},{24,0},{28,4},{1,25},{... | collective-permute-start | bytes 147464 | tf_op jit(solution)/shard_map/ppermute | solution.py:43
  89.4 3.3 %collective-permute-start.17 = (bf16[32,768]{1,0:T(8,128)(2,1)S(1)}, bf16[32,768]{1,0:T(8,128)(2,1)S(1)}, u32[]{:S(2)}, u32[]{:S(2)}) collective-permute-start(bf16[32,768]{1,0:T(8,128)(2,1)S(1)} %get-tuple-element.233), channel_id=1, source_target_pairs={{0,16},{4,20},{8,24},{12,28},{16,0},{20,4},{24,8},{28,12},{1,17},{... | collective-permute-start | bytes 147464 | tf_op jit(solution)/shard_map/ppermute | solution.py:43
  93.5 1.8 collective-permute-done.17
  95.3 1.5 collective-permute-done.16
  97.4 3.2 %collective-permute-done.23.far_grad_ref = bf16[128,768]{1,0:T(8,128)(2,1)S(1)} collective-permute-done((bf16[128,768]{1,0:T(8,128)(2,1)S(1)}, bf16[128,768]{1,0:T(8,128)(2,1)S(1)}, u32[]{:S(2)}, u32[]{:S(2)}) %collective-permute-start.23) | collective-permute-done | bytes 196640 | tf_op jit(solution)/shard_map/ppermute | solution.py:37
  104.6 1.9 collective-permute-done.22.near_ref
  109.6 6.4 %expert_layer.1 = (bf16[512,768]{1,0:T(8,128)(2,1)S(1)}, bf16[512,768]{1,0:T(8,128)(2,1)S(1)}, bf16[512,768]{1,0:T(8,128)(2,1)}, bf16[512,768]{1,0:T(8,128)(2,1)...) custom-call(s32[4]{0:T(128)S(1)} %pad_add_fusion.at_ref, ...), custom_call_target="tpu_custom_call" | custom-call | flops 8000000000 | bytes 4128768 | tf_op jit(solution)/shard_map/expert_layer/pallas_call | solution.py:119
  117.6 1.5 grad_w_out.1
  120.9 1.5 grad_w_in.1
  122.4 12.5 %collective-permute-done.27 = bf16[4,96,768]{2,1,0:T(8,128)(2,1)S(1)} collective-permute-done((bf16[4,96,768]{2,1,0:T(8,128)(2,1)S(1)}, bf16[4,96,768]{2,1,0:T(8,128)(2,1)S(1)}, u32[]{:S(2)}, u32[]{:S(2)}) %collective-permute-start.27) | collective-permute-done | bytes 589856 | tf_op jit(solution)/shard_map/ppermute | solution.py:49
  135.2 2.5 %collective-permute-start.30 = (bf16[32,1536]{1,0:T(8,128)(2,1)S(1)}, bf16[32,1536]{1,0:T(8,128)(2,1)S(1)}, u32[]{:S(2)}, u32[]{:S(2)}) collective-permute-start(bf16[32,1536]{1,0:T(8,128)(2,1)S(1)} %get-tuple-element.223), channel_id=1, source_target_pairs={{0,24},{4,28},{8,16},{12,20},{16,8},{20,12},{24,0},{28,4},{1,25},{... | collective-permute-start | bytes 294920 | tf_op jit(solution)/shard_map/ppermute | solution.py:43
  137.7 2.0 collective-permute-start.28
  140.3 2.5 %collective-permute-done.30 = bf16[32,1536]{1,0:T(8,128)(2,1)S(1)} collective-permute-done((bf16[32,1536]{1,0:T(8,128)(2,1)S(1)}, bf16[32,1536]{1,0:T(8,128)(2,1)S(1)}, u32[]{:S(2)}, u32[]{:S(2)}) %collective-permute-start.30) | collective-permute-done | bytes 98336 | tf_op jit(solution)/shard_map/ppermute | solution.py:43
  142.8 3.8 %collective-permute-done.29 = bf16[32,1536]{1,0:T(8,128)(2,1)S(1)} collective-permute-done((bf16[32,1536]{1,0:T(8,128)(2,1)S(1)}, bf16[32,1536]{1,0:T(8,128)(2,1)S(1)}, u32[]{:S(2)}, u32[]{:S(2)}) %collective-permute-start.29) | collective-permute-done | bytes 98336 | tf_op jit(solution)/shard_map/ppermute | solution.py:43
  148.3 5.3 %collective-permute-done.31.far_ref = bf16[128,768]{1,0:T(8,128)(2,1)S(1)} collective-permute-done((bf16[128,768]{1,0:T(8,128)(2,1)S(1)}, bf16[128,768]{1,0:T(8,128)(2,1)S(1)}, u32[]{:S(2)}, u32[]{:S(2)}) %collective-permute-start.31) | collective-permute-done | bytes 196640 | tf_op jit(solution)/shard_map/ppermute | solution.py:37
  155.3 2.6 %collective-permute-start.41 = (bf16[2,96,768]{2,1,0:T(8,128)(2,1)}, bf16[2,96,768]{2,1,0:T(8,128)(2,1)}, u32[]{:S(2)}, u32[]{:S(2)}) collective-permute-start(bf16[2,96,768]{2,1,0:T(8,128)(2,1)} %get-tuple-element.196), channel_id=1, source_target_pairs={{0,16},{4,20},{8,24},{12,28},{16,0},{20,4},{24,8},{28,12},{1,17},{... | collective-permute-start | bytes 884744 | tf_op jit(solution)/shard_map/ppermute | solution.py:43
  158.7 1.4 collective-permute-start.42
  160.6 10.0 %attention_backward.1 = (bf16[2,4,96,768]{3,2,1,0:T(8,128)(2,1)S(1)}, bf16[2,128,768]{2,1,0:T(8,128)(2,1)S(1)}, bf16[2,128,768]{2,1,0:T(8,128)(2,1)S(1)}, f32[1,768]{1,0:T(1,128)S(1)}, f32[3,1024]{1,0:T(4,128)S(1)}) custom-call(s32[4]{0:T(128)S(1)} %pad_add_fusion.at_ref, bf16[128,768]{1,0:T(8,128)(2,1)S(1)} %add_convert_fusion.1.own_ref, ...), custom_call_target="tpu_custom_call" | custom-call | flops 12000000000 | bytes 7995392 | tf_op jit(solution)/shard_map/attention_backward/pallas_call | solution.py:119
  173.8 1.6 collective-permute-start.38
  175.4 2.0 collective-permute-done.43
  177.4 1.5 collective-permute-start.44
  179.0 2.2 %collective-permute-done.44 = f32[8,768]{1,0:T(8,128)S(1)} collective-permute-done((f32[8,768]{1,0:T(8,128)S(1)}, f32[8,768]{1,0:T(8,128)S(1)}, u32[]{:S(2)}, u32[]{:S(2)}) %collective-permute-start.44) | collective-permute-done | bytes 24608 | tf_op jit(solution)/shard_map/ppermute | solution.py:37
  182.3 1.6 collective-permute-start.39
  184.1 1.6 collective-permute-start.37
  188.1 1.5 collective-permute-start.47
  190.6 10.1 %collective-permute-done.46 = bf16[104,768]{1,0:T(8,128)(2,1)S(1)} collective-permute-done((bf16[104,768]{1,0:T(8,128)(2,1)S(1)}, bf16[104,768]{1,0:T(8,128)(2,1)S(1)}, u32[]{:S(2)}, u32[]{:S(2)}) %collective-permute-start.46) | collective-permute-done | bytes 159776 | tf_op jit(solution)/shard_map/ppermute | solution.py:43
  203.7 4.0 %collective-permute-start.48 = (bf16[104,768]{1,0:T(8,128)(2,1)S(1)}, bf16[104,768]{1,0:T(8,128)(2,1)S(1)}, u32[]{:S(2)}, u32[]{:S(2)}) collective-permute-start(bf16[104,768]{1,0:T(8,128)(2,1)S(1)} %pad_maximum_fusion.10), channel_id=1, source_target_pairs={{0,8},{4,12},{8,0},{12,4},{16,24},{20,28},{24,16},{28,20},{1,9},{5... | collective-permute-start | bytes 479240 | tf_op jit(solution)/shard_map/ppermute | solution.py:43
  207.8 1.8 copy.86
  209.7 1.8 copy.87
  (293 shorter events, 60.3 us)
Async XLA Ops:
  4.3 16.5 %collective-permute-start.3 = (bf16[97,768]{1,0:T(8,128)(2,1)S(1)}, bf16[97,768]{1,0:T(8,128)(2,1)S(1)}, u32[]{:S(2)}, u32[]{:S(2)}) collective-permute-start(bf16[97,768]{1,0:T(8,128)(2,1)S(1)} %pad_maximum_fusion.15.rest_0_), channel_id=1, source_target_pairs={{0,16},{4,20},{8,24},{12,28},{16,0},{20,4},{24,8},{28,12},{1,17},{... | collective-permute-start | bytes 446984 | tf_op jit(solution)/shard_map/ppermute | solution.py:43
  8.5 12.4 %collective-permute-start.2 = (bf16[97,768]{1,0:T(8,128)(2,1)S(1)}, bf16[97,768]{1,0:T(8,128)(2,1)S(1)}, u32[]{:S(2)}, u32[]{:S(2)}) collective-permute-start(bf16[97,768]{1,0:T(8,128)(2,1)S(1)} %pad_maximum_fusion.15.rest_0_), channel_id=1, source_target_pairs={{0,24},{4,28},{8,16},{12,20},{16,8},{20,12},{24,0},{28,4},{1,25},{... | collective-permute-start | bytes 446984 | tf_op jit(solution)/shard_map/ppermute | solution.py:43
  9.8 11.0 %collective-permute-start.4 = (bf16[97,768]{1,0:T(8,128)(2,1)S(1)}, bf16[97,768]{1,0:T(8,128)(2,1)S(1)}, u32[]{:S(2)}, u32[]{:S(2)}) collective-permute-start(bf16[97,768]{1,0:T(8,128)(2,1)S(1)} %pad_maximum_fusion.15.rest_0_), channel_id=1, source_target_pairs={{0,8},{4,12},{8,0},{12,4},{16,24},{20,28},{24,16},{28,20},{1,9},{5... | collective-permute-start | bytes 446984 | tf_op jit(solution)/shard_map/ppermute | solution.py:43
  10.0 13.4 %collective-permute-start.6 = (bf16[97,768]{1,0:T(8,128)(2,1)S(1)}, bf16[97,768]{1,0:T(8,128)(2,1)S(1)}, u32[]{:S(2)}, u32[]{:S(2)}) collective-permute-start(bf16[97,768]{1,0:T(8,128)(2,1)S(1)} %pad_maximum_fusion.15.rest_0_), channel_id=1, source_target_pairs={{0,4},{4,0},{8,12},{12,8},{16,20},{20,16},{24,28},{28,24},{1,5},{5... | collective-permute-start | bytes 446984 | tf_op jit(solution)/shard_map/ppermute | solution.py:49
  13.4 10.6 %collective-permute-start = (bf16[128,1536]{1,0:T(8,128)(2,1)S(1)}, bf16[128,1536]{1,0:T(8,128)(2,1)S(1)}, u32[]{:S(2)}, u32[]{:S(2)}) collective-permute-start(bf16[128,1536]{1,0:T(8,128)(2,1)S(1)} %constant_dynamic-update-slice_fusion), channel_id=1, source_target_pairs={{0,2},{1,3},{2,0},{3,1},{4,6},{5,7},{6,4},{7,5},{8,10},{9,11},{10,... | collective-permute-start | bytes 1179656 | tf_op jit(solution)/shard_map/ppermute | solution.py:37
  21.0 4.0 %collective-permute-start.5 = (bf16[4,768]{1,0:T(4,128)(2,1)S(1)}, bf16[4,768]{1,0:T(4,128)(2,1)S(1)}, u32[]{:S(2)}, u32[]{:S(2)}) collective-permute-start(bf16[4,768]{1,0:T(4,128)(2,1)S(1)} %pad_maximum_fusion.17), channel_id=1, source_target_pairs={{0,4},{4,0},{8,12},{12,8},{16,20},{20,16},{24,28},{28,24},{1,5},{5... | collective-permute-start | bytes 18440 | tf_op jit(solution)/shard_map/ppermute | solution.py:49
  23.5 21.1 %collective-permute-start.9 = (bf16[3,96,768]{2,1,0:T(8,128)(2,1)}, bf16[3,96,768]{2,1,0:T(8,128)(2,1)S(1)}, u32[]{:S(2)}, u32[]{:S(2)}) collective-permute-start(bf16[3,96,768]{2,1,0:T(8,128)(2,1)} %pad_maximum_fusion.5), channel_id=1, source_target_pairs={{0,4},{4,0},{8,12},{12,8},{16,20},{20,16},{24,28},{28,24},{1,5},{5... | collective-permute-start | bytes 1327112 | tf_op jit(solution)/shard_map/ppermute | solution.py:49
  24.9 14.5 %collective-permute-start.1 = (bf16[2,128,1536]{2,1,0:T(8,128)(2,1)}, bf16[2,128,1536]{2,1,0:T(8,128)(2,1)}, u32[]{:S(2)}, u32[]{:S(2)}) collective-permute-start(bf16[2,128,1536]{2,1,0:T(8,128)(2,1)} %pad_maximum_fusion.1), channel_id=1, source_target_pairs={{0,1},{1,0},{2,3},{3,2},{4,5},{5,4},{6,7},{7,6},{8,9},{9,8},{10,11... | collective-permute-start | bytes 2359304 | tf_op jit(solution)/shard_map/ppermute | solution.py:37
  27.0 10.6 %collective-permute-start.7 = (bf16[96,768]{1,0:T(8,128)(2,1)}, bf16[96,768]{1,0:T(8,128)(2,1)S(1)}, u32[]{:S(2)}, u32[]{:S(2)}) collective-permute-start(bf16[96,768]{1,0:T(8,128)(2,1)} %get-tuple-element.213), channel_id=1, source_target_pairs={{0,8},{4,12},{8,0},{12,4},{16,24},{20,28},{24,16},{28,20},{1,9},{5... | collective-permute-start | bytes 442376 | tf_op jit(solution)/shard_map/ppermute | solution.py:43
  29.7 7.9 %collective-permute-start.8 = (bf16[96,768]{1,0:T(8,128)(2,1)}, bf16[96,768]{1,0:T(8,128)(2,1)}, u32[]{:S(2)}, u32[]{:S(2)}) collective-permute-start(bf16[96,768]{1,0:T(8,128)(2,1)} %get-tuple-element.212), channel_id=1, source_target_pairs={{0,16},{4,20},{8,24},{12,28},{16,0},{20,4},{24,8},{28,12},{1,17},{... | collective-permute-start | bytes 442376 | tf_op jit(solution)/shard_map/ppermute | solution.py:43
  32.5 22.6 %collective-permute-start.10 = (bf16[96,768]{1,0:T(8,128)(2,1)}, bf16[96,768]{1,0:T(8,128)(2,1)S(1)}, u32[]{:S(2)}, u32[]{:S(2)}) collective-permute-start(bf16[96,768]{1,0:T(8,128)(2,1)} %get-tuple-element.210), channel_id=1, source_target_pairs={{0,24},{4,28},{8,16},{12,20},{16,8},{20,12},{24,0},{28,4},{1,25},{... | collective-permute-start | bytes 442376 | tf_op jit(solution)/shard_map/ppermute | solution.py:43
  55.7 1.9 collective-permute-start.11
  59.8 14.5 %collective-permute-start.12 = (bf16[128,768]{1,0:T(8,128)(2,1)S(1)}, bf16[128,768]{1,0:T(8,128)(2,1)S(1)}, u32[]{:S(2)}, u32[]{:S(2)}) collective-permute-start(bf16[128,768]{1,0:T(8,128)(2,1)S(1)} %fusion.45), channel_id=1, source_target_pairs={{0,2},{1,3},{2,0},{3,1},{4,6},{5,7},{6,4},{7,5},{8,10},{9,11},{10,... | collective-permute-start | bytes 589832 | tf_op jit(solution)/shard_map/ppermute | solution.py:37
  61.4 14.6 %collective-permute-start.13 = (bf16[128,768]{1,0:T(8,128)(2,1)S(1)}, bf16[128,768]{1,0:T(8,128)(2,1)S(1)}, u32[]{:S(2)}, u32[]{:S(2)}) collective-permute-start(bf16[128,768]{1,0:T(8,128)(2,1)S(1)} %get-tuple-element.205), channel_id=1, source_target_pairs={{0,8},{4,12},{8,0},{12,4},{16,24},{20,28},{24,16},{28,20},{1,9},{5... | collective-permute-start | bytes 589832 | tf_op jit(solution)/shard_map/ppermute | solution.py:43
  67.6 17.6 %collective-permute-start.14 = (bf16[128,768]{1,0:T(8,128)(2,1)S(1)}, bf16[128,768]{1,0:T(8,128)(2,1)S(1)}, u32[]{:S(2)}, u32[]{:S(2)}) collective-permute-start(bf16[128,768]{1,0:T(8,128)(2,1)S(1)} %get-tuple-element.204), channel_id=1, source_target_pairs={{0,16},{4,20},{8,24},{12,28},{16,0},{20,4},{24,8},{28,12},{1,17},{... | collective-permute-start | bytes 589832 | tf_op jit(solution)/shard_map/ppermute | solution.py:43
  71.0 14.2 %collective-permute-start.15 = (bf16[128,768]{1,0:T(8,128)(2,1)S(1)}, bf16[128,768]{1,0:T(8,128)(2,1)S(1)}, u32[]{:S(2)}, u32[]{:S(2)}) collective-permute-start(bf16[128,768]{1,0:T(8,128)(2,1)S(1)} %get-tuple-element.203), channel_id=1, source_target_pairs={{0,24},{4,28},{8,16},{12,20},{16,8},{20,12},{24,0},{28,4},{1,25},{... | collective-permute-start | bytes 589832 | tf_op jit(solution)/shard_map/ppermute | solution.py:43
  72.0 24.9 %collective-permute-start.19 = (bf16[4,96,768]{2,1,0:T(8,128)(2,1)S(1)}, bf16[4,96,768]{2,1,0:T(8,128)(2,1)S(1)}, u32[]{:S(2)}, u32[]{:S(2)}) collective-permute-start(bf16[4,96,768]{2,1,0:T(8,128)(2,1)S(1)} %pad_maximum_fusion.3.rest_0_), channel_id=1, source_target_pairs={{0,4},{4,0},{8,12},{12,8},{16,20},{20,16},{24,28},{28,24},{1,5},{5... | collective-permute-start | bytes 1769480 | tf_op jit(solution)/shard_map/ppermute | solution.py:49
  85.3 18.3 %collective-permute-start.21 = (bf16[4,96,768]{2,1,0:T(8,128)(2,1)S(1)}, bf16[4,96,768]{2,1,0:T(8,128)(2,1)S(1)}, u32[]{:S(2)}, u32[]{:S(2)}) collective-permute-start(bf16[4,96,768]{2,1,0:T(8,128)(2,1)S(1)} %pad_maximum_fusion.4.rest_2_), channel_id=1, source_target_pairs={{0,4},{4,0},{8,12},{12,8},{16,20},{20,16},{24,28},{28,24},{1,5},{5... | collective-permute-start | bytes 1769480 | tf_op jit(solution)/shard_map/ppermute | solution.py:49
  87.0 6.1 %collective-permute-start.18 = (bf16[32,768]{1,0:T(8,128)(2,1)S(1)}, bf16[32,768]{1,0:T(8,128)(2,1)S(1)}, u32[]{:S(2)}, u32[]{:S(2)}) collective-permute-start(bf16[32,768]{1,0:T(8,128)(2,1)S(1)} %get-tuple-element.232), channel_id=1, source_target_pairs={{0,24},{4,28},{8,16},{12,20},{16,8},{20,12},{24,0},{28,4},{1,25},{... | collective-permute-start | bytes 147464 | tf_op jit(solution)/shard_map/ppermute | solution.py:43
  89.4 5.9 %collective-permute-start.17 = (bf16[32,768]{1,0:T(8,128)(2,1)S(1)}, bf16[32,768]{1,0:T(8,128)(2,1)S(1)}, u32[]{:S(2)}, u32[]{:S(2)}) collective-permute-start(bf16[32,768]{1,0:T(8,128)(2,1)S(1)} %get-tuple-element.233), channel_id=1, source_target_pairs={{0,16},{4,20},{8,24},{12,28},{16,0},{20,4},{24,8},{28,12},{1,17},{... | collective-permute-start | bytes 147464 | tf_op jit(solution)/shard_map/ppermute | solution.py:43
  92.7 4.1 %collective-permute-start.16 = (bf16[32,768]{1,0:T(8,128)(2,1)S(1)}, bf16[32,768]{1,0:T(8,128)(2,1)S(1)}, u32[]{:S(2)}, u32[]{:S(2)}) collective-permute-start(bf16[32,768]{1,0:T(8,128)(2,1)S(1)} %get-tuple-element.234), channel_id=1, source_target_pairs={{0,8},{4,12},{8,0},{12,4},{16,24},{20,28},{24,16},{28,20},{1,9},{5... | collective-permute-start | bytes 147464 | tf_op jit(solution)/shard_map/ppermute | solution.py:43
  93.0 7.6 %collective-permute-start.23 = (bf16[128,768]{1,0:T(8,128)(2,1)S(1)}, bf16[128,768]{1,0:T(8,128)(2,1)S(1)}, u32[]{:S(2)}, u32[]{:S(2)}) collective-permute-start(bf16[128,768]{1,0:T(8,128)(2,1)S(1)} %get-tuple-element.230.own_grad_ref), channel_id=1, source_target_pairs={{0,2},{1,3},{2,0},{3,1},{4,6},{5,7},{6,4},{7,5},{8,10},{9,11},{10,... | collective-permute-start | bytes 589832 | tf_op jit(solution)/shard_map/ppermute | solution.py:37
  96.9 5.9 %collective-permute-start.20 = (bf16[128,768]{1,0:T(8,128)(2,1)S(1)}, bf16[128,768]{1,0:T(8,128)(2,1)S(1)}, u32[]{:S(2)}, u32[]{:S(2)}) collective-permute-start(bf16[128,768]{1,0:T(8,128)(2,1)S(1)} %pad_maximum_fusion.13.own_ref), channel_id=1, source_target_pairs={{0,2},{1,3},{2,0},{3,1},{4,6},{5,7},{6,4},{7,5},{8,10},{9,11},{10,... | collective-permute-start | bytes 589832 | tf_op jit(solution)/shard_map/ppermute | solution.py:37
  101.5 3.2 %collective-permute-start.24 = (bf16[2,128,768]{2,1,0:T(8,128)(2,1)}, bf16[2,128,768]{2,1,0:T(8,128)(2,1)}, u32[]{:S(2)}, u32[]{:S(2)}) collective-permute-start(bf16[2,128,768]{2,1,0:T(8,128)(2,1)} %pad_maximum_fusion.7), channel_id=1, source_target_pairs={{0,1},{1,0},{2,3},{3,2},{4,5},{5,4},{6,7},{7,6},{8,9},{9,8},{10,11... | collective-permute-start | bytes 1179656 | tf_op jit(solution)/shard_map/ppermute | solution.py:37
  104.5 2.1 collective-permute-start.22
  116.0 3.7 %collective-permute-start.25 = (bf16[2,128,1536]{2,1,0:T(8,128)(2,1)}, bf16[2,128,1536]{2,1,0:T(8,128)(2,1)S(1)}, u32[]{:S(2)}, u32[]{:S(2)}) collective-permute-start(bf16[2,128,1536]{2,1,0:T(8,128)(2,1)} %get-tuple-element.96), channel_id=1, source_target_pairs={{0,1},{1,0},{2,3},{3,2},{4,5},{5,4},{6,7},{7,6},{8,9},{9,8},{10,11... | collective-permute-start | bytes 2359304 | tf_op jit(solution)/shard_map/ppermute | solution.py:37
  119.1 15.7 %collective-permute-start.27 = (bf16[4,96,768]{2,1,0:T(8,128)(2,1)S(1)}, bf16[4,96,768]{2,1,0:T(8,128)(2,1)S(1)}, u32[]{:S(2)}, u32[]{:S(2)}) collective-permute-start(bf16[4,96,768]{2,1,0:T(8,128)(2,1)S(1)} %slice_bitcast_fusion), channel_id=1, source_target_pairs={{0,4},{4,0},{8,12},{12,8},{16,20},{20,16},{24,28},{28,24},{1,5},{5... | collective-permute-start | bytes 1769480 | tf_op jit(solution)/shard_map/ppermute | solution.py:49
  120.3 14.7 %collective-permute-start.26 = (bf16[128,1536]{1,0:T(8,128)(2,1)S(1)}, bf16[128,1536]{1,0:T(8,128)(2,1)S(1)}, u32[]{:S(2)}, u32[]{:S(2)}) collective-permute-start(bf16[128,1536]{1,0:T(8,128)(2,1)S(1)} %fusion.35), channel_id=1, source_target_pairs={{0,2},{1,3},{2,0},{3,1},{4,6},{5,7},{6,4},{7,5},{8,10},{9,11},{10,... | collective-permute-start | bytes 1179656 | tf_op jit(solution)/shard_map/ppermute | solution.py:37
  135.2 7.6 %collective-permute-start.30 = (bf16[32,1536]{1,0:T(8,128)(2,1)S(1)}, bf16[32,1536]{1,0:T(8,128)(2,1)S(1)}, u32[]{:S(2)}, u32[]{:S(2)}) collective-permute-start(bf16[32,1536]{1,0:T(8,128)(2,1)S(1)} %get-tuple-element.223), channel_id=1, source_target_pairs={{0,24},{4,28},{8,16},{12,20},{16,8},{20,12},{24,0},{28,4},{1,25},{... | collective-permute-start | bytes 294920 | tf_op jit(solution)/shard_map/ppermute | solution.py:43
  137.6 8.9 %collective-permute-start.29 = (bf16[32,1536]{1,0:T(8,128)(2,1)S(1)}, bf16[32,1536]{1,0:T(8,128)(2,1)S(1)}, u32[]{:S(2)}, u32[]{:S(2)}) collective-permute-start(bf16[32,1536]{1,0:T(8,128)(2,1)S(1)} %get-tuple-element.224), channel_id=1, source_target_pairs={{0,16},{4,20},{8,24},{12,28},{16,0},{20,4},{24,8},{28,12},{1,17},{... | collective-permute-start | bytes 294920 | tf_op jit(solution)/shard_map/ppermute | solution.py:43
  137.7 8.9 %collective-permute-start.28 = (bf16[32,1536]{1,0:T(8,128)(2,1)S(1)}, bf16[32,1536]{1,0:T(8,128)(2,1)S(1)}, u32[]{:S(2)}, u32[]{:S(2)}) collective-permute-start(bf16[32,1536]{1,0:T(8,128)(2,1)S(1)} %get-tuple-element.225), channel_id=1, source_target_pairs={{0,8},{4,12},{8,0},{12,4},{16,24},{20,28},{24,16},{28,20},{1,9},{5... | collective-permute-start | bytes 294920 | tf_op jit(solution)/shard_map/ppermute | solution.py:43
  139.7 14.0 %collective-permute-start.32 = (bf16[4,96,768]{2,1,0:T(8,128)(2,1)S(1)}, bf16[4,96,768]{2,1,0:T(8,128)(2,1)S(1)}, u32[]{:S(2)}, u32[]{:S(2)}) collective-permute-start(bf16[4,96,768]{2,1,0:T(8,128)(2,1)S(1)} %slice_bitcast_fusion.2), channel_id=1, source_target_pairs={{0,4},{4,0},{8,12},{12,8},{16,20},{20,16},{24,28},{28,24},{1,5},{5... | collective-permute-start | bytes 1769480 | tf_op jit(solution)/shard_map/ppermute | solution.py:49
  147.5 6.0 %collective-permute-start.31 = (bf16[128,768]{1,0:T(8,128)(2,1)S(1)}, bf16[128,768]{1,0:T(8,128)(2,1)S(1)}, u32[]{:S(2)}, u32[]{:S(2)}) collective-permute-start(bf16[128,768]{1,0:T(8,128)(2,1)S(1)} %add_convert_fusion.1.own_ref), channel_id=1, source_target_pairs={{0,2},{1,3},{2,0},{3,1},{4,6},{5,7},{6,4},{7,5},{8,10},{9,11},{10,... | collective-permute-start | bytes 589832 | tf_op jit(solution)/shard_map/ppermute | solution.py:37
  153.8 6.3 %collective-permute-start.33 = (bf16[2,128,768]{2,1,0:T(8,128)(2,1)S(1)}, bf16[2,128,768]{2,1,0:T(8,128)(2,1)S(1)}, u32[]{:S(2)}, u32[]{:S(2)}) collective-permute-start(bf16[2,128,768]{2,1,0:T(8,128)(2,1)S(1)} %pad_maximum_fusion.8), channel_id=1, source_target_pairs={{0,1},{1,0},{2,3},{3,2},{4,5},{5,4},{6,7},{7,6},{8,9},{9,8},{10,11... | collective-permute-start | bytes 1179656 | tf_op jit(solution)/shard_map/ppermute | solution.py:37
  155.0 27.3 %collective-permute-start.40 = (bf16[2,96,768]{2,1,0:T(8,128)(2,1)}, bf16[2,96,768]{2,1,0:T(8,128)(2,1)}, u32[]{:S(2)}, u32[]{:S(2)}) collective-permute-start(bf16[2,96,768]{2,1,0:T(8,128)(2,1)} %get-tuple-element.197), channel_id=1, source_target_pairs={{0,8},{4,12},{8,0},{12,4},{16,24},{20,28},{24,16},{28,20},{1,9},{5... | collective-permute-start | bytes 884744 | tf_op jit(solution)/shard_map/ppermute | solution.py:43
  155.3 28.6 %collective-permute-start.41 = (bf16[2,96,768]{2,1,0:T(8,128)(2,1)}, bf16[2,96,768]{2,1,0:T(8,128)(2,1)}, u32[]{:S(2)}, u32[]{:S(2)}) collective-permute-start(bf16[2,96,768]{2,1,0:T(8,128)(2,1)} %get-tuple-element.196), channel_id=1, source_target_pairs={{0,16},{4,20},{8,24},{12,28},{16,0},{20,4},{24,8},{28,12},{1,17},{... | collective-permute-start | bytes 884744 | tf_op jit(solution)/shard_map/ppermute | solution.py:43
  158.7 25.2 %collective-permute-start.42 = (bf16[2,96,768]{2,1,0:T(8,128)(2,1)}, bf16[2,96,768]{2,1,0:T(8,128)(2,1)}, u32[]{:S(2)}, u32[]{:S(2)}) collective-permute-start(bf16[2,96,768]{2,1,0:T(8,128)(2,1)} %slice_bitcast_fusion.9), channel_id=1, source_target_pairs={{0,24},{4,28},{8,16},{12,20},{16,8},{20,12},{24,0},{28,4},{1,25},{... | collective-permute-start | bytes 884744 | tf_op jit(solution)/shard_map/ppermute | solution.py:43
  160.1 12.0 %collective-permute-start.34 = (bf16[128,768]{1,0:T(8,128)(2,1)S(1)}, bf16[128,768]{1,0:T(8,128)(2,1)S(1)}, u32[]{:S(2)}, u32[]{:S(2)}) collective-permute-start(bf16[128,768]{1,0:T(8,128)(2,1)S(1)} %get-tuple-element.104), channel_id=1, source_target_pairs={{0,2},{1,3},{2,0},{3,1},{4,6},{5,7},{6,4},{7,5},{8,10},{9,11},{10,... | collective-permute-start | bytes 589832 | tf_op jit(solution)/shard_map/ppermute | solution.py:37
  173.2 4.2 %collective-permute-start.43 = (f32[8,768]{1,0:T(8,128)S(1)}, f32[8,768]{1,0:T(8,128)S(1)}, u32[]{:S(2)}, u32[]{:S(2)}) collective-permute-start(f32[8,768]{1,0:T(8,128)S(1)} %concatenate.59), channel_id=1, source_target_pairs={{0,4},{4,0},{8,12},{12,8},{16,20},{20,16},{24,28},{28,24},{1,5},{5... | collective-permute-start | bytes 73736 | tf_op jit(solution)/shard_map/ppermute | solution.py:49
  173.8 8.3 %collective-permute-start.38 = (bf16[2,96,768]{2,1,0:T(8,128)(2,1)S(1)}, bf16[2,96,768]{2,1,0:T(8,128)(2,1)S(1)}, u32[]{:S(2)}, u32[]{:S(2)}) collective-permute-start(bf16[2,96,768]{2,1,0:T(8,128)(2,1)S(1)} %slice_bitcast_fusion.12), channel_id=1, source_target_pairs={{0,4},{4,0},{8,12},{12,8},{16,20},{20,16},{24,28},{28,24},{1,5},{5... | collective-permute-start | bytes 884744 | tf_op jit(solution)/shard_map/ppermute | solution.py:49
  177.4 3.8 %collective-permute-start.44 = (f32[8,768]{1,0:T(8,128)S(1)}, f32[8,768]{1,0:T(8,128)S(1)}, u32[]{:S(2)}, u32[]{:S(2)}) collective-permute-start(f32[8,768]{1,0:T(8,128)S(1)} %add.204), channel_id=1, source_target_pairs={{0,2},{1,3},{2,0},{3,1},{4,6},{5,7},{6,4},{7,5},{8,10},{9,11},{10,... | collective-permute-start | bytes 73736 | tf_op jit(solution)/shard_map/ppermute | solution.py:37
  181.2 4.4 %collective-permute-start.35 = (bf16[2,128,768]{2,1,0:T(8,128)(2,1)S(1)}, bf16[2,128,768]{2,1,0:T(8,128)(2,1)S(1)}, u32[]{:S(2)}, u32[]{:S(2)}) collective-permute-start(bf16[2,128,768]{2,1,0:T(8,128)(2,1)S(1)} %pad_maximum_fusion.9), channel_id=1, source_target_pairs={{0,1},{1,0},{2,3},{3,2},{4,5},{5,4},{6,7},{7,6},{8,9},{9,8},{10,11... | collective-permute-start | bytes 1179656 | tf_op jit(solution)/shard_map/ppermute | solution.py:37
  182.2 1.7 collective-permute-start.36
  182.3 18.4 %collective-permute-start.39 = (bf16[2,96,768]{2,1,0:T(8,128)(2,1)S(1)}, bf16[2,96,768]{2,1,0:T(8,128)(2,1)S(1)}, u32[]{:S(2)}, u32[]{:S(2)}) collective-permute-start(bf16[2,96,768]{2,1,0:T(8,128)(2,1)S(1)} %get-tuple-element.208), channel_id=1, source_target_pairs={{0,4},{4,0},{8,12},{12,8},{16,20},{20,16},{24,28},{28,24},{1,5},{5... | collective-permute-start | bytes 884744 | tf_op jit(solution)/shard_map/ppermute | solution.py:49
  184.1 19.3 %collective-permute-start.37 = (bf16[128,768]{1,0:T(8,128)(2,1)S(1)}, bf16[128,768]{1,0:T(8,128)(2,1)S(1)}, u32[]{:S(2)}, u32[]{:S(2)}) collective-permute-start(bf16[128,768]{1,0:T(8,128)(2,1)S(1)} %fusion.46), channel_id=1, source_target_pairs={{0,2},{1,3},{2,0},{3,1},{4,6},{5,7},{6,4},{7,5},{8,10},{9,11},{10,... | collective-permute-start | bytes 589832 | tf_op jit(solution)/shard_map/ppermute | solution.py:37
  186.9 13.8 %collective-permute-start.46 = (bf16[104,768]{1,0:T(8,128)(2,1)S(1)}, bf16[104,768]{1,0:T(8,128)(2,1)S(1)}, u32[]{:S(2)}, u32[]{:S(2)}) collective-permute-start(bf16[104,768]{1,0:T(8,128)(2,1)S(1)} %get-tuple-element.236), channel_id=1, source_target_pairs={{0,16},{4,20},{8,24},{12,28},{16,0},{20,4},{24,8},{28,12},{1,17},{... | collective-permute-start | bytes 479240 | tf_op jit(solution)/shard_map/ppermute | solution.py:43
  188.1 12.6 %collective-permute-start.47 = (bf16[104,768]{1,0:T(8,128)(2,1)S(1)}, bf16[104,768]{1,0:T(8,128)(2,1)S(1)}, u32[]{:S(2)}, u32[]{:S(2)}) collective-permute-start(bf16[104,768]{1,0:T(8,128)(2,1)S(1)} %get-tuple-element.235), channel_id=1, source_target_pairs={{0,24},{4,28},{8,16},{12,20},{16,8},{20,12},{24,0},{28,4},{1,25},{... | collective-permute-start | bytes 479240 | tf_op jit(solution)/shard_map/ppermute | solution.py:43
  203.7 8.8 %collective-permute-start.48 = (bf16[104,768]{1,0:T(8,128)(2,1)S(1)}, bf16[104,768]{1,0:T(8,128)(2,1)S(1)}, u32[]{:S(2)}, u32[]{:S(2)}) collective-permute-start(bf16[104,768]{1,0:T(8,128)(2,1)S(1)} %pad_maximum_fusion.10), channel_id=1, source_target_pairs={{0,8},{4,12},{8,0},{12,4},{16,24},{20,28},{24,16},{28,20},{1,9},{5... | collective-permute-start | bytes 479240 | tf_op jit(solution)/shard_map/ppermute | solution.py:43
  (44 other events, 271.5 us)

commit v7 on v5

--- a/solution.py
+++ b/solution.py
@@ -100,13 +100,13 @@
 
 def sum_but_z(x, *earlier):
     R = lax.axis_size("dp") // E
-    x = x + over_t(x, 2)
     c = 1
     while c < R:
         x = x + over_r(x, c)
         c *= 2
     x = after(x, *earlier)
-    return x + over_t(x, 1)
+    x = x + over_t(x, 1)
+    return x + over_t(x, 2)
 
 
 VMEM = pl.BlockSpec(memory_space=pltpu.VMEM)
@@ -436,11 +436,14 @@
     grad_output = mm(to_slots[:ROWS], cotangent_all, 1, 0)
     masked = jnp.where(sent_own[:, None], grad_output, 0).astype(BF).reshape(E, SUB, D)
     in_rows = after(w_in, packed_z, packed_own, both_parts[1])
-    in_z = deliver_z(jnp.stack([pick(in_rows, z ^ d, 1) for d in range(E)]))
-    out_rows = after(w_out, in_z[1:3])
+    in_columns = jnp.stack(deliver_z(jnp.stack([pick(in_rows, z ^ d, 1) for d in range(E)])))
+    out_rows = after(w_out, in_columns)
     out_rows = jnp.stack([pick(out_rows, z ^ d, 1) for d in range(E)])
-    out_rows = jnp.concatenate([out_rows, masked], axis=1)
-    router = jnp.pad(router_rows.T, ((0, 0), (0, 128 - E)))
+    out_z = jnp.stack(deliver_z(jnp.concatenate([out_rows, masked], axis=1)))
+    out_columns, cotangent_z = out_z[:, :local], out_z[:, local:].reshape(E * SUB, D)
+    in_weight = whole([in_columns] + [over_r(in_columns, c) for c in range(1, R)])
+    out_weight = whole([out_columns] + [over_r(out_columns, c) for c in range(1, R)])
+    cotangent_parts = gather_t(cotangent_z)
 
     table_rows = lax.dynamic_slice_in_dim(table_flat.astype(F32).reshape(H, NB), t * LH, LH, 0)
     bucket_table = (buckets[None, :] == jnp.arange(NB, dtype=jnp.int32)[:, None]).astype(F32)
@@ -469,30 +472,18 @@
         *token_parts,
         gain_one,
         reversed_rel,
-        after(to_slots, in_z[1:3], out_rows, router, chosen_own, from_slots_own, gain_two),
+        after(to_slots, in_columns),
         *packed_refs,
     )
-    normed_all, qkv, probs, heads_all, kept, given, tokens_all, attention_weight = after(
-        forward, in_z
-    )
-    in_z, out_rows = after((in_z, out_rows), kept)
-    in_columns = jnp.stack(in_z)
-    in_swapped = [over_r(in_columns, c) for c in range(1, R)]
-    in_weight = whole([in_columns] + in_swapped)
-    out_z = deliver_z(out_rows)
-    out_columns = jnp.stack([part[:local] for part in out_z])
-    out_swapped = [over_r(out_columns, c) for c in range(1, R)]
-    out_weight = whole([out_columns] + out_swapped)
-    cotangent_z = jnp.concatenate([part[local:] for part in out_z], axis=0)
-    cotangent_parts = gather_t(cotangent_z)
+    normed_all, qkv, probs, heads_all, kept, given, tokens_all, attention_weight = forward
     attended = scatter_t(kept, given)
     inputs = mm(to_slots[:ROWS], tokens_all, 1, 0)
     middle = inputs + attended
     scale_two = norm_scale(middle)
     normed_two = (middle * scale_two * gain_two).astype(BF)
 
-    buffer_z = dispatch_z(after(normed_two, out_z))
-    buffer_parts = gather_t(after(buffer_z, in_swapped), out_weight)
+    buffer_parts = gather_t(dispatch_z(after(normed_two, out_z, in_weight)), out_weight)
+    router = jnp.pad(router_rows.T, ((0, 0), (0, 128 - E)))
     buffer, grad_expert, activation, grad_pre, kept, given = call(
         functools.partial(expert_layer, pieces=len(in_weight)),
         "expert_layer",
@@ -556,7 +547,6 @@
     grad_gain_two = jnp.sum(grad_normed_two * middle * scale_two, axis=0, keepdims=True)
     grad_middle = (grad_output + norm_back(grad_normed_two, middle, scale_two, gain_two)).astype(BF)
     grad_parts = gather_t(grad_middle, in_sums)
-    layer_parts = gather_t(after(layer_rows, grad_parts))
 
     late_terms, kept, given, grad_gain_one, grad_rel = call(
         attention_backward,
@@ -587,17 +577,12 @@
         heads_all,
     )
     expert_sums = jnp.stack([in_sums, out_sums], axis=1)
-    expert_sums = after(expert_sums, grad_middle)
-    delivered = deliver_z(expert_sums)
-    late_terms, kept, given, grad_gain_one, grad_rel = after(
-        (late_terms, kept, given, grad_gain_one, grad_rel), layer_parts[1]
-    )
-    late_terms = blocks_to_send(late_terms)
-    far_terms = swap_r(late_terms[:, 2:])
-    delivered = after(delivered, far_terms)
-    far_sums = add(far_terms).astype(BF)
-    near_terms = swap_r(after(late_terms[:, :2], far_sums))
-    given = over_t(given, 1)
+    delivered = deliver_z(after(expert_sums, grad_middle))
+    late_terms = swap_r(blocks_to_send(late_terms))
+    delivered = after(delivered, late_terms)
+    late_sums = add(late_terms)
+    given = over_t(after(given, late_terms), 1)
+    layer_parts = gather_t(after(layer_rows, given))
     grad_normed_one = finish_scatter(kept, given)
     own_inputs = tokens.astype(F32)
     grad_slots = jnp.concatenate(in_order(grad_parts), axis=0)
@@ -626,16 +611,12 @@
             ],
             axis=0,
         ),
-        far_terms,
-        given,
-        layer_parts[2],
-    )
-    low = after(small, delivered).astype(BF)
-    far = [over_z(jnp.concatenate([far_sums[d - 2], low], axis=0), d) for d in (2, 3)]
-    near_sums = add(after(near_terms, far))
-    near = over_z(jnp.concatenate([near_sums[1].astype(BF), low], axis=0), 1)
-    late = jnp.concatenate([near_sums[0], small], axis=0)
-    late = late + far[0].astype(F32) + far[1].astype(F32) + near.astype(F32)
+        late_terms,
+    )
+    low = after(small, given, layer_parts[1]).astype(BF)
+    late = [over_z(jnp.concatenate([late_sums[d].astype(BF), low], axis=0), d) for d in (3, 2, 1)]
+    late, grad_tokens = after((late, grad_tokens), layer_out)
+    late = jnp.concatenate([late_sums[0], small], axis=0) + add(late)
     late, small = late[:local], late[local:]
     small_own = lax.dynamic_slice_in_dim(small[: E + 2], at_dp * local, local, 1)
     table_own = lax.dynamic_slice_in_dim(small[E + 2], at_dp * (H * NB // n), H * NB // n, 0)

time: 217 us -> 224 us (1.032)
  starting transfers between devices: 72.2 us -> 55.4 us
  waiting for transfers between devices: 68.3 us -> 83.2 us
  other arithmetic: 12.9 us -> 16.9 us
  local copies, waits for them, and re-layouts: 29 us -> 31.3 us
    ppermute x21, starting transfers between devices: 43.8 us -> 30.7 us  [over_z(): lax.ppermute(x, 'dp', [(i, (i // r ^ d) * r + i % r) for i in range(n)])]
    ppermute x10 -> x9, waiting for transfers between devices: 14.5 us -> 22.4 us  [over_r(): lax.ppermute(x, 'dp', [(i, i // r * r + (i % r ^ c)) for i in range(n)])]
    ppermute x21, waiting for transfers between devices: 39 us -> 45.7 us  [over_z(): lax.ppermute(x, 'dp', [(i, (i // r ^ d) * r + i % r) for i in range(n)])]
    ppermute x10 -> x9, starting transfers between devices: 14.4 us -> 11.1 us  [over_r(): lax.ppermute(x, 'dp', [(i, i // r * r + (i % r ^ c)) for i in range(n)])]
    unnamed x95 -> x87, local copies, waits for them, and re-layouts: 15.7 us -> 16.5 us
  transfers between devices with their start and end apart: 49 -> 48, of which waited for: 20 -> 18; matrix products, arithmetic and copies ran while one was open for 14% -> 16% of each run, Pallas kernels for 10% -> 6%
where the time goes in v7:
time: 224 us; the launch traced here: 223 us
  waiting for transfers between devices  83.2 us (37%)
  starting transfers between devices  55.4 us (25%)
  local copies, waits for them, and re-layouts  31.3 us (14%)
  Pallas kernels  27.2 us (12%)
  other arithmetic  16.9 us (8%)
  matrix products  6.58 us (3%)
  between operations  2.36 us (1%)
    ppermute x21, waiting for transfers between devices, over_z(): lax.ppermute(x, 'dp', [(i, (i // r ^ d) * r + i % r) for i in range(n)])  45.7 us
    ppermute x21, starting transfers between devices, over_z(): lax.ppermute(x, 'dp', [(i, (i // r ^ d) * r + i % r) for i in range(n)])  30.7 us
    pallas_call x5, Pallas kernels, call(): pl.pallas_call(kernel, out_shape=[jax.ShapeDtypeStruct(shape, kind) for s...  27.2 us
    ppermute x9, waiting for transfers between devices, over_r(): lax.ppermute(x, 'dp', [(i, i // r * r + (i % r ^ c)) for i in range(n)])  22.4 us
    unnamed x87, local copies, waits for them, and re-layouts  16.5 us
    ppermute x18, waiting for transfers between devices, over_t(): return lax.ppermute(x, 'tensor', [(i, i ^ k) for i in range(T)])  15.1 us
    ppermute x18, starting transfers between devices, over_t(): return lax.ppermute(x, 'tensor', [(i, i ^ k) for i in range(T)])  13.6 us
    ppermute x9, starting transfers between devices, over_r(): lax.ppermute(x, 'dp', [(i, i // r * r + (i % r ^ c)) for i in range(n)])  11.1 us
  transfers between devices with their start and end apart: 48, of which 18 were waited for; matrix products, arithmetic and copies ran while one was open for 16% of the time, Pallas kernels for 6%

profile of v7, /device:TPU:0, one launch (start us, length us, event | category | flops | bytes accessed | tf_op | source)
XLA Modules:
  0.0 223.0 jit_solution(14545950600019979243)
XLA Ops:
  4.4 3.0 %collective-permute-start.6 = (bf16[97,768]{1,0:T(8,128)(2,1)S(1)}, bf16[97,768]{1,0:T(8,128)(2,1)S(1)}, u32[]{:S(2)}, u32[]{:S(2)}) collective-permute-start(bf16[97,768]{1,0:T(8,128)(2,1)S(1)} %pad_maximum_fusion.14.rest_0_), channel_id=1, source_target_pairs={{0,4},{4,0},{8,12},{12,8},{16,20},{20,16},{24,28},{28,24},{1,5},{5... | collective-permute-start | bytes 446984 | tf_op jit(solution)/shard_map/ppermute | solution.py:49
  7.4 1.6 collective-permute-start.4
  9.0 2.6 %collective-permute-start.3 = (bf16[97,768]{1,0:T(8,128)(2,1)S(1)}, bf16[97,768]{1,0:T(8,128)(2,1)S(1)}, u32[]{:S(2)}, u32[]{:S(2)}) collective-permute-start(bf16[97,768]{1,0:T(8,128)(2,1)S(1)} %pad_maximum_fusion.14.rest_0_), channel_id=1, source_target_pairs={{0,16},{4,20},{8,24},{12,28},{16,0},{20,4},{24,8},{28,12},{1,17},{... | collective-permute-start | bytes 446984 | tf_op jit(solution)/shard_map/ppermute | solution.py:43
  12.8 1.6 collective-permute-start
  17.2 6.6 %collective-permute-done.3.rest_2_ = bf16[97,768]{1,0:T(8,128)(2,1)S(1)} collective-permute-done((bf16[97,768]{1,0:T(8,128)(2,1)S(1)}, bf16[97,768]{1,0:T(8,128)(2,1)S(1)}, u32[]{:S(2)}, u32[]{:S(2)}) %collective-permute-start.3) | collective-permute-done | bytes 149024 | tf_op jit(solution)/shard_map/ppermute | solution.py:43
  25.4 1.5 collective-permute-start.10
  30.8 2.1 collective-permute-start.9
  32.9 1.6 collective-permute-start.8
  35.6 3.9 %collective-permute-done.9 = bf16[96,768]{1,0:T(8,128)(2,1)S(1)} collective-permute-done((bf16[96,768]{1,0:T(8,128)(2,1)}, bf16[96,768]{1,0:T(8,128)(2,1)S(1)}, u32[]{:S(2)}, u32[]{:S(2)}) %collective-permute-start.9) | collective-permute-done | bytes 147488 | tf_op jit(solution)/shard_map/ppermute | solution.py:43
  39.6 8.9 %collective-permute-done.8 = bf16[96,768]{1,0:T(8,128)(2,1)S(1)} collective-permute-done((bf16[96,768]{1,0:T(8,128)(2,1)}, bf16[96,768]{1,0:T(8,128)(2,1)S(1)}, u32[]{:S(2)}, u32[]{:S(2)}) %collective-permute-start.8) | collective-permute-done | bytes 147488 | tf_op jit(solution)/shard_map/ppermute | solution.py:43
  55.6 7.8 %attention_forward.1 = (bf16[512,768]{1,0:T(8,128)(2,1)S(1)}, bf16[512,576]{1,0:T(8,128)(2,1)S(1)}, f32[3,512,512]{2,1,0:T(8,128)}, bf16[512,192]{1,0:T(8,128)(2...) custom-call(s32[4]{0:T(128)S(1)} %pad_add_fusion.at_ref, ...), custom_call_target="tpu_custom_call" | custom-call | flops 12000000000 | bytes 2513408 | tf_op jit(solution)/shard_map/attention_forward/pallas_call | solution.py:119
  63.5 1.9 select_convert_fusion
  66.3 2.3 %collective-permute-start.15 = (bf16[128,768]{1,0:T(8,128)(2,1)}, bf16[128,768]{1,0:T(8,128)(2,1)S(1)}, u32[]{:S(2)}, u32[]{:S(2)}) collective-permute-start(bf16[128,768]{1,0:T(8,128)(2,1)} %get-tuple-element.164), channel_id=1, source_target_pairs={{0,24},{4,28},{8,16},{12,20},{16,8},{20,12},{24,0},{28,4},{1,25},{... | collective-permute-start | bytes 589832 | tf_op jit(solution)/shard_map/ppermute | solution.py:43
  68.6 2.1 collective-permute-start.13
  72.3 1.5 collective-permute-start.12
  74.3 1.8 collective-permute-done.15
  76.2 9.1 %collective-permute-done.14 = bf16[128,768]{1,0:T(8,128)(2,1)S(1)} collective-permute-done((bf16[128,768]{1,0:T(8,128)(2,1)S(1)}, bf16[128,768]{1,0:T(8,128)(2,1)S(1)}, u32[]{:S(2)}, u32[]{:S(2)}) %collective-permute-start.14) | collective-permute-done | bytes 196640 | tf_op jit(solution)/shard_map/ppermute | solution.py:43
  87.1 1.4 multiply_reduce_fusion.3
  88.7 2.5 %collective-permute-start.19 = (bf16[32,768]{1,0:T(8,128)(2,1)S(1)}, bf16[32,768]{1,0:T(8,128)(2,1)S(1)}, u32[]{:S(2)}, u32[]{:S(2)}) collective-permute-start(bf16[32,768]{1,0:T(8,128)(2,1)S(1)} %get-tuple-element.192), channel_id=1, source_target_pairs={{0,24},{4,28},{8,16},{12,20},{16,8},{20,12},{24,0},{28,4},{1,25},{... | collective-permute-start | bytes 147464 | tf_op jit(solution)/shard_map/ppermute | solution.py:43
  91.2 1.9 collective-permute-start.17
  93.2 1.6 collective-permute-start.23
  95.1 1.3 collective-permute-done.18
  97.6 2.5 %collective-permute-done.23.far_grad_ref = bf16[128,768]{1,0:T(8,128)(2,1)S(1)} collective-permute-done((bf16[128,768]{1,0:T(8,128)(2,1)S(1)}, bf16[128,768]{1,0:T(8,128)(2,1)S(1)}, u32[]{:S(2)}, u32[]{:S(2)}) %collective-permute-start.23) | collective-permute-done | bytes 196640 | tf_op jit(solution)/shard_map/ppermute | solution.py:37
  100.9 2.2 collective-permute-done.20.far_ref
  109.9 6.5 %expert_layer.1 = (bf16[512,768]{1,0:T(8,128)(2,1)S(1)}, bf16[512,768]{1,0:T(8,128)(2,1)S(1)}, bf16[512,768]{1,0:T(8,128)(2,1)}, bf16[512,768]{1,0:T(8,128)(2,1)...) custom-call(s32[4]{0:T(128)S(1)} %pad_add_fusion.at_ref, ...), custom_call_target="tpu_custom_call" | custom-call | flops 8000000000 | bytes 4128768 | tf_op jit(solution)/shard_map/expert_layer/pallas_call | solution.py:119
  118.3 1.5 grad_w_out.1
  121.5 1.6 collective-permute-start.26
  123.0 1.5 grad_w_in.1
  124.5 10.7 %collective-permute-done.27 = bf16[4,96,768]{2,1,0:T(8,128)(2,1)S(1)} collective-permute-done((bf16[4,96,768]{2,1,0:T(8,128)(2,1)S(1)}, bf16[4,96,768]{2,1,0:T(8,128)(2,1)S(1)}, u32[]{:S(2)}, u32[]{:S(2)}) %collective-permute-start.27) | collective-permute-done | bytes 589856 | tf_op jit(solution)/shard_map/ppermute | solution.py:49
  135.5 1.7 collective-permute-start.30
  137.2 2.8 %collective-permute-start.28 = (bf16[32,1536]{1,0:T(8,128)(2,1)S(1)}, bf16[32,1536]{1,0:T(8,128)(2,1)S(1)}, u32[]{:S(2)}, u32[]{:S(2)}) collective-permute-start(bf16[32,1536]{1,0:T(8,128)(2,1)S(1)} %get-tuple-element.187), channel_id=1, source_target_pairs={{0,8},{4,12},{8,0},{12,4},{16,24},{20,28},{24,16},{28,20},{1,9},{5... | collective-permute-start | bytes 294920 | tf_op jit(solution)/shard_map/ppermute | solution.py:43
  141.3 1.8 collective-permute-done.30
  143.1 2.9 %collective-permute-done.29 = bf16[32,1536]{1,0:T(8,128)(2,1)S(1)} collective-permute-done((bf16[32,1536]{1,0:T(8,128)(2,1)S(1)}, bf16[32,1536]{1,0:T(8,128)(2,1)S(1)}, u32[]{:S(2)}, u32[]{:S(2)}) %collective-permute-start.29) | collective-permute-done | bytes 98336 | tf_op jit(solution)/shard_map/ppermute | solution.py:43
  147.7 1.5 collective-permute-start.31
  149.3 4.8 %collective-permute-done.31.far_ref = bf16[128,768]{1,0:T(8,128)(2,1)S(1)} collective-permute-done((bf16[128,768]{1,0:T(8,128)(2,1)S(1)}, bf16[128,768]{1,0:T(8,128)(2,1)S(1)}, u32[]{:S(2)}, u32[]{:S(2)}) %collective-permute-start.31) | collective-permute-done | bytes 196640 | tf_op jit(solution)/shard_map/ppermute | solution.py:37
  155.5 2.1 collective-permute-start.45
  157.7 10.0 %attention_backward.1 = (bf16[2,4,96,768]{3,2,1,0:T(8,128)(2,1)S(1)}, bf16[2,128,768]{2,1,0:T(8,128)(2,1)S(1)}, bf16[2,128,768]{2,1,0:T(8,128)(2,1)S(1)}, f32[1,768]{1,0:T(1,128)S(1)}, f32[3,1024]{1,0:T(4,128)S(1)}) custom-call(s32[4]{0:T(128)S(1)} %pad_add_fusion.at_ref, bf16[128,768]{1,0:T(8,128)(2,1)S(1)} %add_convert_fusion.own_ref, ...), custom_call_target="tpu_custom_call" | custom-call | flops 12000000000 | bytes 7995392 | tf_op jit(solution)/shard_map/attention_backward/pallas_call | solution.py:119
  170.0 1.5 collective-permute-start.34
  171.5 2.0 collective-permute-start.47
  175.1 10.8 %collective-permute-done.38 = f32[8,768]{1,0:T(8,128)S(1)} collective-permute-done((f32[8,768]{1,0:T(8,128)S(1)}, f32[8,768]{1,0:T(8,128)S(1)}, u32[]{:S(2)}, u32[]{:S(2)}) %collective-permute-start.38) | collective-permute-done | bytes 24608 | tf_op jit(solution)/shard_map/ppermute | solution.py:49
  190.4 1.5 collective-permute-start.40
  192.0 1.8 copy.87
  193.8 1.8 copy.86
  197.9 5.6 %collective-permute-done.36 = bf16[128,768]{1,0:T(8,128)(2,1)S(1)} collective-permute-done((bf16[128,768]{1,0:T(8,128)(2,1)S(1)}, bf16[128,768]{1,0:T(8,128)(2,1)S(1)}, u32[]{:S(2)}, u32[]{:S(2)}) %collective-permute-start.36) | collective-permute-done | bytes 196640 | tf_op jit(solution)/shard_map/ppermute | solution.py:37
  204.6 1.7 collective-permute-start.42
  206.3 1.8 collective-permute-start.41
  210.4 2.5 %collective-permute-done.43 = bf16[104,768]{1,0:T(8,128)(2,1)S(1)} collective-permute-done((bf16[104,768]{1,0:T(8,128)(2,1)S(1)}, bf16[104,768]{1,0:T(8,128)(2,1)S(1)}, u32[]{:S(2)}, u32[]{:S(2)}) %collective-permute-start.43) | collective-permute-done | bytes 159776 | tf_op jit(solution)/shard_map/ppermute | solution.py:43
  213.0 6.4 %collective-permute-done.42 = bf16[104,768]{1,0:T(8,128)(2,1)S(1)} collective-permute-done((bf16[104,768]{1,0:T(8,128)(2,1)S(1)}, bf16[104,768]{1,0:T(8,128)(2,1)S(1)}, u32[]{:S(2)}, u32[]{:S(2)}) %collective-permute-start.42) | collective-permute-done | bytes 159776 | tf_op jit(solution)/shard_map/ppermute | solution.py:43
  (273 shorter events, 60.5 us)
Async XLA Ops:
  4.4 21.0 %collective-permute-start.6 = (bf16[97,768]{1,0:T(8,128)(2,1)S(1)}, bf16[97,768]{1,0:T(8,128)(2,1)S(1)}, u32[]{:S(2)}, u32[]{:S(2)}) collective-permute-start(bf16[97,768]{1,0:T(8,128)(2,1)S(1)} %pad_maximum_fusion.14.rest_0_), channel_id=1, source_target_pairs={{0,4},{4,0},{8,12},{12,8},{16,20},{20,16},{24,28},{28,24},{1,5},{5... | collective-permute-start | bytes 446984 | tf_op jit(solution)/shard_map/ppermute | solution.py:49
  7.4 9.7 %collective-permute-start.4 = (bf16[97,768]{1,0:T(8,128)(2,1)S(1)}, bf16[97,768]{1,0:T(8,128)(2,1)S(1)}, u32[]{:S(2)}, u32[]{:S(2)}) collective-permute-start(bf16[97,768]{1,0:T(8,128)(2,1)S(1)} %pad_maximum_fusion.14.rest_0_), channel_id=1, source_target_pairs={{0,8},{4,12},{8,0},{12,4},{16,24},{20,28},{24,16},{28,20},{1,9},{5... | collective-permute-start | bytes 446984 | tf_op jit(solution)/shard_map/ppermute | solution.py:43
  9.0 14.8 %collective-permute-start.3 = (bf16[97,768]{1,0:T(8,128)(2,1)S(1)}, bf16[97,768]{1,0:T(8,128)(2,1)S(1)}, u32[]{:S(2)}, u32[]{:S(2)}) collective-permute-start(bf16[97,768]{1,0:T(8,128)(2,1)S(1)} %pad_maximum_fusion.14.rest_0_), channel_id=1, source_target_pairs={{0,16},{4,20},{8,24},{12,28},{16,0},{20,4},{24,8},{28,12},{1,17},{... | collective-permute-start | bytes 446984 | tf_op jit(solution)/shard_map/ppermute | solution.py:43
  11.6 12.2 %collective-permute-start.2 = (bf16[97,768]{1,0:T(8,128)(2,1)S(1)}, bf16[97,768]{1,0:T(8,128)(2,1)S(1)}, u32[]{:S(2)}, u32[]{:S(2)}) collective-permute-start(bf16[97,768]{1,0:T(8,128)(2,1)S(1)} %pad_maximum_fusion.14.rest_0_), channel_id=1, source_target_pairs={{0,24},{4,28},{8,16},{12,20},{16,8},{20,12},{24,0},{28,4},{1,25},{... | collective-permute-start | bytes 446984 | tf_op jit(solution)/shard_map/ppermute | solution.py:43
  12.8 15.0 %collective-permute-start = (bf16[128,1536]{1,0:T(8,128)(2,1)S(1)}, bf16[128,1536]{1,0:T(8,128)(2,1)S(1)}, u32[]{:S(2)}, u32[]{:S(2)}) collective-permute-start(bf16[128,1536]{1,0:T(8,128)(2,1)S(1)} %constant_dynamic-update-slice_fusion), channel_id=1, source_target_pairs={{0,2},{1,3},{2,0},{3,1},{4,6},{5,7},{6,4},{7,5},{8,10},{9,11},{10,... | collective-permute-start | bytes 1179656 | tf_op jit(solution)/shard_map/ppermute | solution.py:37
  23.9 3.8 %collective-permute-start.5 = (bf16[4,768]{1,0:T(4,128)(2,1)S(1)}, bf16[4,768]{1,0:T(4,128)(2,1)S(1)}, u32[]{:S(2)}, u32[]{:S(2)}) collective-permute-start(bf16[4,768]{1,0:T(4,128)(2,1)S(1)} %pad_maximum_fusion.16), channel_id=1, source_target_pairs={{0,4},{4,0},{8,12},{12,8},{16,20},{20,16},{24,28},{28,24},{1,5},{5... | collective-permute-start | bytes 18440 | tf_op jit(solution)/shard_map/ppermute | solution.py:49
  25.4 28.4 %collective-permute-start.10 = (bf16[3,96,768]{2,1,0:T(8,128)(2,1)}, bf16[3,96,768]{2,1,0:T(8,128)(2,1)S(1)}, u32[]{:S(2)}, u32[]{:S(2)}) collective-permute-start(bf16[3,96,768]{2,1,0:T(8,128)(2,1)} %pad_maximum_fusion.5), channel_id=1, source_target_pairs={{0,4},{4,0},{8,12},{12,8},{16,20},{20,16},{24,28},{28,24},{1,5},{5... | collective-permute-start | bytes 1327112 | tf_op jit(solution)/shard_map/ppermute | solution.py:49
  28.8 22.6 %collective-permute-start.1 = (bf16[2,128,1536]{2,1,0:T(8,128)(2,1)}, bf16[2,128,1536]{2,1,0:T(8,128)(2,1)}, u32[]{:S(2)}, u32[]{:S(2)}) collective-permute-start(bf16[2,128,1536]{2,1,0:T(8,128)(2,1)} %pad_maximum_fusion.1), channel_id=1, source_target_pairs={{0,1},{1,0},{2,3},{3,2},{4,5},{5,4},{6,7},{7,6},{8,9},{9,8},{10,11... | collective-permute-start | bytes 2359304 | tf_op jit(solution)/shard_map/ppermute | solution.py:37
  30.8 8.8 %collective-permute-start.9 = (bf16[96,768]{1,0:T(8,128)(2,1)}, bf16[96,768]{1,0:T(8,128)(2,1)S(1)}, u32[]{:S(2)}, u32[]{:S(2)}) collective-permute-start(bf16[96,768]{1,0:T(8,128)(2,1)} %get-tuple-element.177), channel_id=1, source_target_pairs={{0,24},{4,28},{8,16},{12,20},{16,8},{20,12},{24,0},{28,4},{1,25},{... | collective-permute-start | bytes 442376 | tf_op jit(solution)/shard_map/ppermute | solution.py:43
  32.9 15.5 %collective-permute-start.8 = (bf16[96,768]{1,0:T(8,128)(2,1)}, bf16[96,768]{1,0:T(8,128)(2,1)S(1)}, u32[]{:S(2)}, u32[]{:S(2)}) collective-permute-start(bf16[96,768]{1,0:T(8,128)(2,1)} %get-tuple-element.178), channel_id=1, source_target_pairs={{0,16},{4,20},{8,24},{12,28},{16,0},{20,4},{24,8},{28,12},{1,17},{... | collective-permute-start | bytes 442376 | tf_op jit(solution)/shard_map/ppermute | solution.py:43
  34.5 13.9 %collective-permute-start.7 = (bf16[96,768]{1,0:T(8,128)(2,1)S(1)}, bf16[96,768]{1,0:T(8,128)(2,1)S(1)}, u32[]{:S(2)}, u32[]{:S(2)}) collective-permute-start(bf16[96,768]{1,0:T(8,128)(2,1)S(1)} %get-tuple-element.179), channel_id=1, source_target_pairs={{0,8},{4,12},{8,0},{12,4},{16,24},{20,28},{24,16},{28,20},{1,9},{5... | collective-permute-start | bytes 442376 | tf_op jit(solution)/shard_map/ppermute | solution.py:43
  63.4 7.2 %collective-permute-start.11 = (bf16[2,128,768]{2,1,0:T(8,128)(2,1)S(1)}, bf16[2,128,768]{2,1,0:T(8,128)(2,1)S(1)}, u32[]{:S(2)}, u32[]{:S(2)}) collective-permute-start(bf16[2,128,768]{2,1,0:T(8,128)(2,1)S(1)} %get-tuple-element.56), channel_id=1, source_target_pairs={{0,1},{1,0},{2,3},{3,2},{4,5},{5,4},{6,7},{7,6},{8,9},{9,8},{10,11... | collective-permute-start | bytes 1179656 | tf_op jit(solution)/shard_map/ppermute | solution.py:37
  66.3 9.9 %collective-permute-start.15 = (bf16[128,768]{1,0:T(8,128)(2,1)}, bf16[128,768]{1,0:T(8,128)(2,1)S(1)}, u32[]{:S(2)}, u32[]{:S(2)}) collective-permute-start(bf16[128,768]{1,0:T(8,128)(2,1)} %get-tuple-element.164), channel_id=1, source_target_pairs={{0,24},{4,28},{8,16},{12,20},{16,8},{20,12},{24,0},{28,4},{1,25},{... | collective-permute-start | bytes 589832 | tf_op jit(solution)/shard_map/ppermute | solution.py:43
  68.6 16.7 %collective-permute-start.14 = (bf16[128,768]{1,0:T(8,128)(2,1)S(1)}, bf16[128,768]{1,0:T(8,128)(2,1)S(1)}, u32[]{:S(2)}, u32[]{:S(2)}) collective-permute-start(bf16[128,768]{1,0:T(8,128)(2,1)S(1)} %get-tuple-element.165), channel_id=1, source_target_pairs={{0,16},{4,20},{8,24},{12,28},{16,0},{20,4},{24,8},{28,12},{1,17},{... | collective-permute-start | bytes 589832 | tf_op jit(solution)/shard_map/ppermute | solution.py:43
  68.6 16.7 %collective-permute-start.13 = (bf16[128,768]{1,0:T(8,128)(2,1)S(1)}, bf16[128,768]{1,0:T(8,128)(2,1)}, u32[]{:S(2)}, u32[]{:S(2)}) collective-permute-start(bf16[128,768]{1,0:T(8,128)(2,1)S(1)} %get-tuple-element.166), channel_id=1, source_target_pairs={{0,8},{4,12},{8,0},{12,4},{16,24},{20,28},{24,16},{28,20},{1,9},{5... | collective-permute-start | bytes 589832 | tf_op jit(solution)/shard_map/ppermute | solution.py:43
  72.3 14.7 %collective-permute-start.12 = (bf16[128,768]{1,0:T(8,128)(2,1)}, bf16[128,768]{1,0:T(8,128)(2,1)}, u32[]{:S(2)}, u32[]{:S(2)}) collective-permute-start(bf16[128,768]{1,0:T(8,128)(2,1)} %fusion.43), channel_id=1, source_target_pairs={{0,2},{1,3},{2,0},{3,1},{4,6},{5,7},{6,4},{7,5},{8,10},{9,11},{10,... | collective-permute-start | bytes 589832 | tf_op jit(solution)/shard_map/ppermute | solution.py:37
  73.9 14.6 %collective-permute-start.16 = (bf16[4,96,768]{2,1,0:T(8,128)(2,1)S(1)}, bf16[4,96,768]{2,1,0:T(8,128)(2,1)S(1)}, u32[]{:S(2)}, u32[]{:S(2)}) collective-permute-start(bf16[4,96,768]{2,1,0:T(8,128)(2,1)S(1)} %pad_maximum_fusion.4.rest_0_), channel_id=1, source_target_pairs={{0,4},{4,0},{8,12},{12,8},{16,20},{20,16},{24,28},{28,24},{1,5},{5... | collective-permute-start | bytes 1769480 | tf_op jit(solution)/shard_map/ppermute | solution.py:49
  86.5 17.5 %collective-permute-start.21 = (bf16[4,96,768]{2,1,0:T(8,128)(2,1)S(1)}, bf16[4,96,768]{2,1,0:T(8,128)(2,1)S(1)}, u32[]{:S(2)}, u32[]{:S(2)}) collective-permute-start(bf16[4,96,768]{2,1,0:T(8,128)(2,1)S(1)} %slice.367.rest_2_), channel_id=1, source_target_pairs={{0,4},{4,0},{8,12},{12,8},{16,20},{20,16},{24,28},{28,24},{1,5},{5... | collective-permute-start | bytes 1769480 | tf_op jit(solution)/shard_map/ppermute | solution.py:49
  88.7 6.4 %collective-permute-start.19 = (bf16[32,768]{1,0:T(8,128)(2,1)S(1)}, bf16[32,768]{1,0:T(8,128)(2,1)S(1)}, u32[]{:S(2)}, u32[]{:S(2)}) collective-permute-start(bf16[32,768]{1,0:T(8,128)(2,1)S(1)} %get-tuple-element.192), channel_id=1, source_target_pairs={{0,24},{4,28},{8,16},{12,20},{16,8},{20,12},{24,0},{28,4},{1,25},{... | collective-permute-start | bytes 147464 | tf_op jit(solution)/shard_map/ppermute | solution.py:43
  91.2 5.2 %collective-permute-start.18 = (bf16[32,768]{1,0:T(8,128)(2,1)S(1)}, bf16[32,768]{1,0:T(8,128)(2,1)S(1)}, u32[]{:S(2)}, u32[]{:S(2)}) collective-permute-start(bf16[32,768]{1,0:T(8,128)(2,1)S(1)} %get-tuple-element.193), channel_id=1, source_target_pairs={{0,16},{4,20},{8,24},{12,28},{16,0},{20,4},{24,8},{28,12},{1,17},{... | collective-permute-start | bytes 147464 | tf_op jit(solution)/shard_map/ppermute | solution.py:43
  91.2 5.2 %collective-permute-start.17 = (bf16[32,768]{1,0:T(8,128)(2,1)S(1)}, bf16[32,768]{1,0:T(8,128)(2,1)S(1)}, u32[]{:S(2)}, u32[]{:S(2)}) collective-permute-start(bf16[32,768]{1,0:T(8,128)(2,1)S(1)} %get-tuple-element.194), channel_id=1, source_target_pairs={{0,8},{4,12},{8,0},{12,4},{16,24},{20,28},{24,16},{28,20},{1,9},{5... | collective-permute-start | bytes 147464 | tf_op jit(solution)/shard_map/ppermute | solution.py:43
  93.2 6.9 %collective-permute-start.23 = (bf16[128,768]{1,0:T(8,128)(2,1)S(1)}, bf16[128,768]{1,0:T(8,128)(2,1)S(1)}, u32[]{:S(2)}, u32[]{:S(2)}) collective-permute-start(bf16[128,768]{1,0:T(8,128)(2,1)S(1)} %bitcast.169), channel_id=1, source_target_pairs={{0,2},{1,3},{2,0},{3,1},{4,6},{5,7},{6,4},{7,5},{8,10},{9,11},{10,... | collective-permute-start | bytes 589832 | tf_op jit(solution)/shard_map/ppermute | solution.py:37
  96.4 6.7 %collective-permute-start.20 = (bf16[128,768]{1,0:T(8,128)(2,1)S(1)}, bf16[128,768]{1,0:T(8,128)(2,1)S(1)}, u32[]{:S(2)}, u32[]{:S(2)}) collective-permute-start(bf16[128,768]{1,0:T(8,128)(2,1)S(1)} %get-tuple-element.190.own_ref), channel_id=1, source_target_pairs={{0,2},{1,3},{2,0},{3,1},{4,6},{5,7},{6,4},{7,5},{8,10},{9,11},{10,... | collective-permute-start | bytes 589832 | tf_op jit(solution)/shard_map/ppermute | solution.py:37
  100.9 6.9 %collective-permute-start.24 = (bf16[2,128,768]{2,1,0:T(8,128)(2,1)}, bf16[2,128,768]{2,1,0:T(8,128)(2,1)}, u32[]{:S(2)}, u32[]{:S(2)}) collective-permute-start(bf16[2,128,768]{2,1,0:T(8,128)(2,1)} %pad_maximum_fusion.7), channel_id=1, source_target_pairs={{0,1},{1,0},{2,3},{3,2},{4,5},{5,4},{6,7},{7,6},{8,9},{9,8},{10,11... | collective-permute-start | bytes 1179656 | tf_op jit(solution)/shard_map/ppermute | solution.py:37
  104.7 3.0 %collective-permute-start.22 = (bf16[2,128,768]{2,1,0:T(8,128)(2,1)}, bf16[2,128,768]{2,1,0:T(8,128)(2,1)}, u32[]{:S(2)}, u32[]{:S(2)}) collective-permute-start(bf16[2,128,768]{2,1,0:T(8,128)(2,1)} %pad_maximum_fusion.6), channel_id=1, source_target_pairs={{0,1},{1,0},{2,3},{3,2},{4,5},{5,4},{6,7},{7,6},{8,9},{9,8},{10,11... | collective-permute-start | bytes 1179656 | tf_op jit(solution)/shard_map/ppermute | solution.py:37
  116.4 4.8 %collective-permute-start.25 = (bf16[2,128,1536]{2,1,0:T(8,128)(2,1)}, bf16[2,128,1536]{2,1,0:T(8,128)(2,1)S(1)}, u32[]{:S(2)}, u32[]{:S(2)}) collective-permute-start(bf16[2,128,1536]{2,1,0:T(8,128)(2,1)} %get-tuple-element.61), channel_id=1, source_target_pairs={{0,1},{1,0},{2,3},{3,2},{4,5},{5,4},{6,7},{7,6},{8,9},{9,8},{10,11... | collective-permute-start | bytes 2359304 | tf_op jit(solution)/shard_map/ppermute | solution.py:37
  119.9 15.3 %collective-permute-start.27 = (bf16[4,96,768]{2,1,0:T(8,128)(2,1)S(1)}, bf16[4,96,768]{2,1,0:T(8,128)(2,1)S(1)}, u32[]{:S(2)}, u32[]{:S(2)}) collective-permute-start(bf16[4,96,768]{2,1,0:T(8,128)(2,1)S(1)} %slice_bitcast_fusion), channel_id=1, source_target_pairs={{0,4},{4,0},{8,12},{12,8},{16,20},{20,16},{24,28},{28,24},{1,5},{5... | collective-permute-start | bytes 1769480 | tf_op jit(solution)/shard_map/ppermute | solution.py:49
  121.5 13.9 %collective-permute-start.26 = (bf16[128,1536]{1,0:T(8,128)(2,1)S(1)}, bf16[128,1536]{1,0:T(8,128)(2,1)S(1)}, u32[]{:S(2)}, u32[]{:S(2)}) collective-permute-start(bf16[128,1536]{1,0:T(8,128)(2,1)S(1)} %fusion.35), channel_id=1, source_target_pairs={{0,2},{1,3},{2,0},{3,1},{4,6},{5,7},{6,4},{7,5},{8,10},{9,11},{10,... | collective-permute-start | bytes 1179656 | tf_op jit(solution)/shard_map/ppermute | solution.py:37
  135.5 7.6 %collective-permute-start.30 = (bf16[32,1536]{1,0:T(8,128)(2,1)S(1)}, bf16[32,1536]{1,0:T(8,128)(2,1)S(1)}, u32[]{:S(2)}, u32[]{:S(2)}) collective-permute-start(bf16[32,1536]{1,0:T(8,128)(2,1)S(1)} %get-tuple-element.185), channel_id=1, source_target_pairs={{0,24},{4,28},{8,16},{12,20},{16,8},{20,12},{24,0},{28,4},{1,25},{... | collective-permute-start | bytes 294920 | tf_op jit(solution)/shard_map/ppermute | solution.py:43
  137.2 8.9 %collective-permute-start.29 = (bf16[32,1536]{1,0:T(8,128)(2,1)S(1)}, bf16[32,1536]{1,0:T(8,128)(2,1)S(1)}, u32[]{:S(2)}, u32[]{:S(2)}) collective-permute-start(bf16[32,1536]{1,0:T(8,128)(2,1)S(1)} %get-tuple-element.186), channel_id=1, source_target_pairs={{0,16},{4,20},{8,24},{12,28},{16,0},{20,4},{24,8},{28,12},{1,17},{... | collective-permute-start | bytes 294920 | tf_op jit(solution)/shard_map/ppermute | solution.py:43
  137.2 8.9 %collective-permute-start.28 = (bf16[32,1536]{1,0:T(8,128)(2,1)S(1)}, bf16[32,1536]{1,0:T(8,128)(2,1)S(1)}, u32[]{:S(2)}, u32[]{:S(2)}) collective-permute-start(bf16[32,1536]{1,0:T(8,128)(2,1)S(1)} %get-tuple-element.187), channel_id=1, source_target_pairs={{0,8},{4,12},{8,0},{12,4},{16,24},{20,28},{24,16},{28,20},{1,9},{5... | collective-permute-start | bytes 294920 | tf_op jit(solution)/shard_map/ppermute | solution.py:43
  140.0 14.2 %collective-permute-start.32 = (bf16[4,96,768]{2,1,0:T(8,128)(2,1)S(1)}, bf16[4,96,768]{2,1,0:T(8,128)(2,1)S(1)}, u32[]{:S(2)}, u32[]{:S(2)}) collective-permute-start(bf16[4,96,768]{2,1,0:T(8,128)(2,1)S(1)} %slice_bitcast_fusion.4), channel_id=1, source_target_pairs={{0,4},{4,0},{8,12},{12,8},{16,20},{20,16},{24,28},{28,24},{1,5},{5... | collective-permute-start | bytes 1769480 | tf_op jit(solution)/shard_map/ppermute | solution.py:49
  147.7 6.5 %collective-permute-start.31 = (bf16[128,768]{1,0:T(8,128)(2,1)S(1)}, bf16[128,768]{1,0:T(8,128)(2,1)S(1)}, u32[]{:S(2)}, u32[]{:S(2)}) collective-permute-start(bf16[128,768]{1,0:T(8,128)(2,1)S(1)} %add_convert_fusion.own_ref), channel_id=1, source_target_pairs={{0,2},{1,3},{2,0},{3,1},{4,6},{5,7},{6,4},{7,5},{8,10},{9,11},{10,... | collective-permute-start | bytes 589832 | tf_op jit(solution)/shard_map/ppermute | solution.py:37
  154.4 3.3 %collective-permute-start.33 = (bf16[2,128,768]{2,1,0:T(8,128)(2,1)S(1)}, bf16[2,128,768]{2,1,0:T(8,128)(2,1)S(1)}, u32[]{:S(2)}, u32[]{:S(2)}) collective-permute-start(bf16[2,128,768]{2,1,0:T(8,128)(2,1)S(1)} %pad_maximum_fusion.8), channel_id=1, source_target_pairs={{0,1},{1,0},{2,3},{3,2},{4,5},{5,4},{6,7},{7,6},{8,9},{9,8},{10,11... | collective-permute-start | bytes 1179656 | tf_op jit(solution)/shard_map/ppermute | solution.py:37
  155.5 30.4 %collective-permute-start.46 = (bf16[2,96,768]{2,1,0:T(8,128)(2,1)}, bf16[2,96,768]{2,1,0:T(8,128)(2,1)}, u32[]{:S(2)}, u32[]{:S(2)}) collective-permute-start(bf16[2,96,768]{2,1,0:T(8,128)(2,1)} %get-tuple-element.156), channel_id=1, source_target_pairs={{0,16},{4,20},{8,24},{12,28},{16,0},{20,4},{24,8},{28,12},{1,17},{... | collective-permute-start | bytes 884744 | tf_op jit(solution)/shard_map/ppermute | solution.py:43
  155.5 30.4 %collective-permute-start.45 = (bf16[2,96,768]{2,1,0:T(8,128)(2,1)}, bf16[2,96,768]{2,1,0:T(8,128)(2,1)}, u32[]{:S(2)}, u32[]{:S(2)}) collective-permute-start(bf16[2,96,768]{2,1,0:T(8,128)(2,1)} %get-tuple-element.157), channel_id=1, source_target_pairs={{0,8},{4,12},{8,0},{12,4},{16,24},{20,28},{24,16},{28,20},{1,9},{5... | collective-permute-start | bytes 884744 | tf_op jit(solution)/shard_map/ppermute | solution.py:43
  170.0 15.9 %collective-permute-start.34 = (bf16[4,96,768]{2,1,0:T(8,128)(2,1)}, bf16[4,96,768]{2,1,0:T(8,128)(2,1)}, u32[]{:S(2)}, u32[]{:S(2)}) collective-permute-start(bf16[4,96,768]{2,1,0:T(8,128)(2,1)} %slice_bitcast_fusion.2), channel_id=1, source_target_pairs={{0,4},{4,0},{8,12},{12,8},{16,20},{20,16},{24,28},{28,24},{1,5},{5... | collective-permute-start | bytes 1769480 | tf_op jit(solution)/shard_map/ppermute | solution.py:49
  171.5 14.4 %collective-permute-start.47 = (bf16[2,96,768]{2,1,0:T(8,128)(2,1)S(1)}, bf16[2,96,768]{2,1,0:T(8,128)(2,1)S(1)}, u32[]{:S(2)}, u32[]{:S(2)}) collective-permute-start(bf16[2,96,768]{2,1,0:T(8,128)(2,1)S(1)} %slice_bitcast_fusion.11), channel_id=1, source_target_pairs={{0,24},{4,28},{8,16},{12,20},{16,8},{20,12},{24,0},{28,4},{1,25},{... | collective-permute-start | bytes 884744 | tf_op jit(solution)/shard_map/ppermute | solution.py:43
  174.2 11.7 %collective-permute-start.38 = (f32[8,768]{1,0:T(8,128)S(1)}, f32[8,768]{1,0:T(8,128)S(1)}, u32[]{:S(2)}, u32[]{:S(2)}) collective-permute-start(f32[8,768]{1,0:T(8,128)S(1)} %concatenate.54), channel_id=1, source_target_pairs={{0,4},{4,0},{8,12},{12,8},{16,20},{20,16},{24,28},{28,24},{1,5},{5... | collective-permute-start | bytes 73736 | tf_op jit(solution)/shard_map/ppermute | solution.py:49
  188.4 2.0 collective-permute-start.39
  188.5 7.1 %collective-permute-start.35 = (bf16[2,128,768]{2,1,0:T(8,128)(2,1)S(1)}, bf16[2,128,768]{2,1,0:T(8,128)(2,1)S(1)}, u32[]{:S(2)}, u32[]{:S(2)}) collective-permute-start(bf16[2,128,768]{2,1,0:T(8,128)(2,1)S(1)} %copy-done.10), channel_id=1, source_target_pairs={{0,1},{1,0},{2,3},{3,2},{4,5},{5,4},{6,7},{7,6},{8,9},{9,8},{10,11... | collective-permute-start | bytes 1179656 | tf_op jit(solution)/shard_map/ppermute | solution.py:37
  190.4 5.2 %collective-permute-start.40 = (f32[8,768]{1,0:T(8,128)S(1)}, f32[8,768]{1,0:T(8,128)S(1)}, u32[]{:S(2)}, u32[]{:S(2)}) collective-permute-start(f32[8,768]{1,0:T(8,128)S(1)} %add.196), channel_id=1, source_target_pairs={{0,2},{1,3},{2,0},{3,1},{4,6},{5,7},{6,4},{7,5},{8,10},{9,11},{10,... | collective-permute-start | bytes 73736 | tf_op jit(solution)/shard_map/ppermute | solution.py:37
  195.6 7.9 %collective-permute-start.36 = (bf16[128,768]{1,0:T(8,128)(2,1)S(1)}, bf16[128,768]{1,0:T(8,128)(2,1)S(1)}, u32[]{:S(2)}, u32[]{:S(2)}) collective-permute-start(bf16[128,768]{1,0:T(8,128)(2,1)S(1)} %copy-done.33), channel_id=1, source_target_pairs={{0,2},{1,3},{2,0},{3,1},{4,6},{5,7},{6,4},{7,5},{8,10},{9,11},{10,... | collective-permute-start | bytes 589832 | tf_op jit(solution)/shard_map/ppermute | solution.py:37
  196.6 11.5 %collective-permute-start.44 = (bf16[128,768]{1,0:T(8,128)(2,1)S(1)}, bf16[128,768]{1,0:T(8,128)(2,1)S(1)}, u32[]{:S(2)}, u32[]{:S(2)}) collective-permute-start(bf16[128,768]{1,0:T(8,128)(2,1)S(1)} %fusion.44), channel_id=1, source_target_pairs={{0,2},{1,3},{2,0},{3,1},{4,6},{5,7},{6,4},{7,5},{8,10},{9,11},{10,... | collective-permute-start | bytes 589832 | tf_op jit(solution)/shard_map/ppermute | solution.py:37
  203.5 5.9 %collective-permute-start.37 = (bf16[2,128,768]{2,1,0:T(8,128)(2,1)S(1)}, bf16[2,128,768]{2,1,0:T(8,128)(2,1)S(1)}, u32[]{:S(2)}, u32[]{:S(2)}) collective-permute-start(bf16[2,128,768]{2,1,0:T(8,128)(2,1)S(1)} %pad_maximum_fusion.9), channel_id=1, source_target_pairs={{0,1},{1,0},{2,3},{3,2},{4,5},{5,4},{6,7},{7,6},{8,9},{9,8},{10,11... | collective-permute-start | bytes 1179656 | tf_op jit(solution)/shard_map/ppermute | solution.py:37
  203.6 9.3 %collective-permute-start.43 = (bf16[104,768]{1,0:T(8,128)(2,1)S(1)}, bf16[104,768]{1,0:T(8,128)(2,1)S(1)}, u32[]{:S(2)}, u32[]{:S(2)}) collective-permute-start(bf16[104,768]{1,0:T(8,128)(2,1)S(1)} %get-tuple-element.195), channel_id=1, source_target_pairs={{0,8},{4,12},{8,0},{12,4},{16,24},{20,28},{24,16},{28,20},{1,9},{5... | collective-permute-start | bytes 479240 | tf_op jit(solution)/shard_map/ppermute | solution.py:43
  204.6 14.7 %collective-permute-start.42 = (bf16[104,768]{1,0:T(8,128)(2,1)S(1)}, bf16[104,768]{1,0:T(8,128)(2,1)S(1)}, u32[]{:S(2)}, u32[]{:S(2)}) collective-permute-start(bf16[104,768]{1,0:T(8,128)(2,1)S(1)} %get-tuple-element.196), channel_id=1, source_target_pairs={{0,16},{4,20},{8,24},{12,28},{16,0},{20,4},{24,8},{28,12},{1,17},{... | collective-permute-start | bytes 479240 | tf_op jit(solution)/shard_map/ppermute | solution.py:43
  206.3 13.0 %collective-permute-start.41 = (bf16[104,768]{1,0:T(8,128)(2,1)S(1)}, bf16[104,768]{1,0:T(8,128)(2,1)S(1)}, u32[]{:S(2)}, u32[]{:S(2)}) collective-permute-start(bf16[104,768]{1,0:T(8,128)(2,1)S(1)} %get-tuple-element.197), channel_id=1, source_target_pairs={{0,24},{4,28},{8,16},{12,20},{16,8},{20,12},{24,0},{28,4},{1,25},{... | collective-permute-start | bytes 479240 | tf_op jit(solution)/shard_map/ppermute | solution.py:43
  (40 other events, 211.1 us)

commit v8 on v2

--- a/solution.py
+++ b/solution.py
@@ -68,9 +68,13 @@
     return [own, near[0], far, near[1]]
 
 
-def scatter_t(kept, sent, *earlier):
-    first = over_t(sent, 1).astype(F32)
-    away = after((kept[1].astype(F32) + first[1]).astype(BF), *earlier)
+def scatter_t(kept, sent):
+    return finish_scatter(kept, over_t(sent, 1))
+
+
+def finish_scatter(kept, first):
+    first = first.astype(F32)
+    away = (kept[1].astype(F32) + first[1]).astype(BF)
     return kept[0].astype(F32) + first[0] + over_t(away, 2).astype(F32)
 
 
@@ -94,15 +98,15 @@
     return [x[0]] + [over_z(x[d], d) for d in range(1, E)]
 
 
-def sum_but_z(x):
+def sum_but_z(x, *earlier):
     R = lax.axis_size("dp") // E
     c = 1
     while c < R:
         x = x + over_r(x, c)
         c *= 2
-    for k in (1, 2):
-        x = x + over_t(x, k)
-    return x
+    x = x + over_t(x, 2)
+    x = after(x, *earlier)
+    return x + over_t(x, 1)
 
 
 VMEM = pl.BlockSpec(memory_space=pltpu.VMEM)
@@ -566,13 +570,16 @@
     )
     expert_sums = jnp.stack([in_sums, out_sums], axis=1)
     delivered = deliver_z(after(expert_sums, grad_middle))
-    late_terms, kept, given, grad_gain_one, grad_rel, delivered = after(
-        (late_terms, kept, given, grad_gain_one, grad_rel, delivered), layer_parts[1]
+    late_terms, kept, given, grad_gain_one, grad_rel = after(
+        (late_terms, kept, given, grad_gain_one, grad_rel), layer_parts[1]
     )
     late_terms = blocks_to_send(late_terms)
-    far_sums = add(swap_r(late_terms[:, 2:])).astype(BF)
+    far_terms = swap_r(late_terms[:, 2:])
+    delivered = after(delivered, far_terms)
+    far_sums = add(far_terms).astype(BF)
     near_terms = swap_r(after(late_terms[:, :2], far_sums))
-    grad_normed_one = scatter_t(kept, given)
+    given = over_t(given, 1)
+    grad_normed_one = finish_scatter(kept, given)
     own_inputs = tokens.astype(F32)
     grad_slots = jnp.concatenate(in_order(grad_parts), axis=0)
     grad_tokens = mm(from_slots_own, grad_slots, 1, 0) + norm_back(
@@ -599,12 +606,17 @@
                 jnp.zeros((1, D), F32),
             ],
             axis=0,
-        )
-    )
-    low = small.astype(BF)
+        ),
+        far_terms,
+        given,
+        layer_parts[2],
+    )
+    low = after(small, delivered).astype(BF)
     far = [over_z(jnp.concatenate([far_sums[d - 2], low], axis=0), d) for d in (2, 3)]
     near_sums = add(after(near_terms, far))
-    near = over_z(jnp.concatenate([near_sums[1].astype(BF), low], axis=0), 1)
+    near = jnp.concatenate([near_sums[1].astype(BF), low], axis=0)
+    delivered = after(delivered, near)
+    near = over_z(near, 1)
     late = jnp.concatenate([near_sums[0], small], axis=0)
     late = late + far[0].astype(F32) + far[1].astype(F32) + near.astype(F32)
     late, small = late[:local], late[local:]

time: 209 us -> 208 us (level)
  starting transfers between devices: 60.6 us -> 53.3 us
  waiting for transfers between devices: 69.3 us -> 71.8 us
    ppermute x21, starting transfers between devices: 35 us -> 29.3 us  [over_z(): lax.ppermute(x, 'dp', [(i, (i // r ^ d) * r + i % r) for i in range(n)])]
    ppermute x18, waiting for transfers between devices: 10.5 us -> 13.7 us  [over_t(): return lax.ppermute(x, 'tensor', [(i, i ^ k) for i in range(T)])]
    select_n x5, other arithmetic: 0.25 us -> 2.82 us  [natural(): jnp.where(flip, parts[j ^ bit], parts[j])]
    ppermute x21, waiting for transfers between devices: 45.8 us -> 43.5 us  [over_z(): lax.ppermute(x, 'dp', [(i, (i // r ^ d) * r + i % r) for i in range(n)])]
    unnamed x81 -> x89, local copies, waits for them, and re-layouts: 14.2 us -> 15.7 us
  transfers between devices with their start and end apart: 49 -> 49, of which waited for: 21 -> 20; matrix products, arithmetic and copies ran while one was open for 16% -> 17% of each run, Pallas kernels for 6% -> 6%
where the time goes in v8:
time: 208 us; the launch traced here: 207 us
  waiting for transfers between devices  71.8 us (35%)
  starting transfers between devices  53.3 us (26%)
  local copies, waits for them, and re-layouts  28.2 us (14%)
  Pallas kernels  27.6 us (13%)
  other arithmetic  16.8 us (8%)
  matrix products  6.58 us (3%)
  between operations  2.37 us (1%)
    ppermute x21, waiting for transfers between devices, over_z(): lax.ppermute(x, 'dp', [(i, (i // r ^ d) * r + i % r) for i in range(n)])  43.5 us
    ppermute x21, starting transfers between devices, over_z(): lax.ppermute(x, 'dp', [(i, (i // r ^ d) * r + i % r) for i in range(n)])  29.3 us
    pallas_call x5, Pallas kernels, call(): pl.pallas_call(kernel, out_shape=[jax.ShapeDtypeStruct(shape, kind) for s...  27.6 us
    unnamed x89, local copies, waits for them, and re-layouts  15.7 us
    ppermute x10, waiting for transfers between devices, over_r(): lax.ppermute(x, 'dp', [(i, i // r * r + (i % r ^ c)) for i in range(n)])  14.6 us
    ppermute x18, waiting for transfers between devices, over_t(): return lax.ppermute(x, 'tensor', [(i, i ^ k) for i in range(T)])  13.7 us
    ppermute x18, starting transfers between devices, over_t(): return lax.ppermute(x, 'tensor', [(i, i ^ k) for i in range(T)])  12.4 us
    ppermute x10, starting transfers between devices, over_r(): lax.ppermute(x, 'dp', [(i, i // r * r + (i % r ^ c)) for i in range(n)])  11.6 us
  transfers between devices with their start and end apart: 49, of which 20 were waited for; matrix products, arithmetic and copies ran while one was open for 17% of the time, Pallas kernels for 6%

profile of v8, /device:TPU:0, one launch (start us, length us, event | category | flops | bytes accessed | tf_op | source)
XLA Modules:
  0.0 206.7 jit_solution(5802209525458397794)
XLA Ops:
  4.4 3.0 %collective-permute-start.9 = (bf16[97,768]{1,0:T(8,128)(2,1)S(1)}, bf16[97,768]{1,0:T(8,128)(2,1)S(1)}, u32[]{:S(2)}, u32[]{:S(2)}) collective-permute-start(bf16[97,768]{1,0:T(8,128)(2,1)S(1)} %pad_maximum_fusion.16), channel_id=1, source_target_pairs={{0,4},{4,0},{8,12},{12,8},{16,20},{20,16},{24,28},{28,24},{1,5},{5... | collective-permute-start | bytes 446984 | tf_op jit(solution)/shard_map/ppermute | solution.py:49
  7.4 1.6 collective-permute-start.4
  9.0 2.6 %collective-permute-start.3 = (bf16[97,768]{1,0:T(8,128)(2,1)S(1)}, bf16[97,768]{1,0:T(8,128)(2,1)S(1)}, u32[]{:S(2)}, u32[]{:S(2)}) collective-permute-start(bf16[97,768]{1,0:T(8,128)(2,1)S(1)} %pad_maximum_fusion.16), channel_id=1, source_target_pairs={{0,16},{4,20},{8,24},{12,28},{16,0},{20,4},{24,8},{28,12},{1,17},{... | collective-permute-start | bytes 446984 | tf_op jit(solution)/shard_map/ppermute | solution.py:43
  13.7 1.6 collective-permute-start
  18.8 5.0 %collective-permute-done.3 = bf16[97,768]{1,0:T(8,128)(2,1)S(1)} collective-permute-done((bf16[97,768]{1,0:T(8,128)(2,1)S(1)}, bf16[97,768]{1,0:T(8,128)(2,1)S(1)}, u32[]{:S(2)}, u32[]{:S(2)}) %collective-permute-start.3) | collective-permute-done | bytes 149024 | tf_op jit(solution)/shard_map/ppermute | solution.py:43
  25.4 1.5 collective-permute-start.10
  27.7 2.1 %collective-permute-start.8 = (bf16[96,768]{1,0:T(8,128)(2,1)}, bf16[96,768]{1,0:T(8,128)(2,1)S(1)}, u32[]{:S(2)}, u32[]{:S(2)}) collective-permute-start(bf16[96,768]{1,0:T(8,128)(2,1)} %get-tuple-element.186), channel_id=1, source_target_pairs={{0,24},{4,28},{8,16},{12,20},{16,8},{20,12},{24,0},{28,4},{1,25},{... | collective-permute-start | bytes 442376 | tf_op jit(solution)/shard_map/ppermute | solution.py:43
  29.9 1.7 collective-permute-start.7
  33.9 2.6 %collective-permute-done.8 = bf16[96,768]{1,0:T(8,128)(2,1)S(1)} collective-permute-done((bf16[96,768]{1,0:T(8,128)(2,1)}, bf16[96,768]{1,0:T(8,128)(2,1)S(1)}, u32[]{:S(2)}, u32[]{:S(2)}) %collective-permute-start.8) | collective-permute-done | bytes 147488 | tf_op jit(solution)/shard_map/ppermute | solution.py:43
  36.4 5.0 %collective-permute-done.7 = bf16[96,768]{1,0:T(8,128)(2,1)} collective-permute-done((bf16[96,768]{1,0:T(8,128)(2,1)S(1)}, bf16[96,768]{1,0:T(8,128)(2,1)}, u32[]{:S(2)}, u32[]{:S(2)}) %collective-permute-start.7) | collective-permute-done | bytes 147488 | tf_op jit(solution)/shard_map/ppermute | solution.py:43
  45.9 8.0 %attention_forward.1 = (bf16[512,768]{1,0:T(8,128)(2,1)S(1)}, bf16[512,576]{1,0:T(8,128)(2,1)S(1)}, f32[3,512,512]{2,1,0:T(8,128)}, bf16[512,192]{1,0:T(8,128)(2...) custom-call(s32[4]{0:T(128)S(1)} %pad_add_fusion.at_ref, ...), custom_call_target="tpu_custom_call" | custom-call | flops 12000000000 | bytes 2505728 | tf_op jit(solution)/shard_map/attention_forward/pallas_call | solution.py:119
  54.0 1.9 select_convert_fusion
  56.9 2.6 %collective-permute-start.15 = (bf16[128,768]{1,0:T(8,128)(2,1)}, bf16[128,768]{1,0:T(8,128)(2,1)S(1)}, u32[]{:S(2)}, u32[]{:S(2)}) collective-permute-start(bf16[128,768]{1,0:T(8,128)(2,1)} %get-tuple-element.174), channel_id=1, source_target_pairs={{0,24},{4,28},{8,16},{12,20},{16,8},{20,12},{24,0},{28,4},{1,25},{... | collective-permute-start | bytes 589832 | tf_op jit(solution)/shard_map/ppermute | solution.py:43
  59.5 1.7 collective-permute-start.13
  62.9 1.5 collective-permute-start.12
  65.1 1.7 collective-permute-done.15
  66.7 9.4 %collective-permute-done.14 = bf16[128,768]{1,0:T(8,128)(2,1)} collective-permute-done((bf16[128,768]{1,0:T(8,128)(2,1)}, bf16[128,768]{1,0:T(8,128)(2,1)}, u32[]{:S(2)}, u32[]{:S(2)}) %collective-permute-start.14) | collective-permute-done | bytes 196640 | tf_op jit(solution)/shard_map/ppermute | solution.py:43
  79.5 2.3 %collective-permute-start.19 = (bf16[32,768]{1,0:T(8,128)(2,1)S(1)}, bf16[32,768]{1,0:T(8,128)(2,1)S(1)}, u32[]{:S(2)}, u32[]{:S(2)}) collective-permute-start(bf16[32,768]{1,0:T(8,128)(2,1)S(1)} %get-tuple-element.203), channel_id=1, source_target_pairs={{0,24},{4,28},{8,16},{12,20},{16,8},{20,12},{24,0},{28,4},{1,25},{... | collective-permute-start | bytes 147464 | tf_op jit(solution)/shard_map/ppermute | solution.py:43
  82.0 2.0 collective-permute-start.17
  84.0 1.6 collective-permute-start.23
  85.8 1.6 collective-permute-done.18
  88.6 2.3 %collective-permute-done.23.far_grad_ref = bf16[128,768]{1,0:T(8,128)(2,1)S(1)} collective-permute-done((bf16[128,768]{1,0:T(8,128)(2,1)S(1)}, bf16[128,768]{1,0:T(8,128)(2,1)S(1)}, u32[]{:S(2)}, u32[]{:S(2)}) %collective-permute-start.23) | collective-permute-done | bytes 196640 | tf_op jit(solution)/shard_map/ppermute | solution.py:37
  91.7 2.2 %collective-permute-done.20.far_ref = bf16[128,768]{1,0:T(8,128)(2,1)S(1)} collective-permute-done((bf16[128,768]{1,0:T(8,128)(2,1)S(1)}, bf16[128,768]{1,0:T(8,128)(2,1)S(1)}, u32[]{:S(2)}, u32[]{:S(2)}) %collective-permute-start.20) | collective-permute-done | bytes 196640 | tf_op jit(solution)/shard_map/ppermute | solution.py:37
  100.7 6.6 %expert_layer.1 = (bf16[512,768]{1,0:T(8,128)(2,1)S(1)}, bf16[512,768]{1,0:T(8,128)(2,1)S(1)}, bf16[512,768]{1,0:T(8,128)(2,1)}, bf16[512,768]{1,0:T(8,128)(2,1)...) custom-call(s32[4]{0:T(128)S(1)} %pad_add_fusion.at_ref, ...), custom_call_target="tpu_custom_call" | custom-call | flops 8000000000 | bytes 4128768 | tf_op jit(solution)/shard_map/expert_layer/pallas_call | solution.py:119
  109.2 1.5 grad_w_out.1
  112.4 1.6 collective-permute-start.26
  113.9 1.5 grad_w_in.1
  115.4 10.7 %collective-permute-done.27 = bf16[4,96,768]{2,1,0:T(8,128)(2,1)S(1)} collective-permute-done((bf16[4,96,768]{2,1,0:T(8,128)(2,1)S(1)}, bf16[4,96,768]{2,1,0:T(8,128)(2,1)S(1)}, u32[]{:S(2)}, u32[]{:S(2)}) %collective-permute-start.27) | collective-permute-done | bytes 589856 | tf_op jit(solution)/shard_map/ppermute | solution.py:49
  126.4 2.3 %collective-permute-start.30 = (bf16[32,1536]{1,0:T(8,128)(2,1)S(1)}, bf16[32,1536]{1,0:T(8,128)(2,1)S(1)}, u32[]{:S(2)}, u32[]{:S(2)}) collective-permute-start(bf16[32,1536]{1,0:T(8,128)(2,1)S(1)} %get-tuple-element.194), channel_id=1, source_target_pairs={{0,24},{4,28},{8,16},{12,20},{16,8},{20,12},{24,0},{28,4},{1,25},{... | collective-permute-start | bytes 294920 | tf_op jit(solution)/shard_map/ppermute | solution.py:43
  128.7 2.2 %collective-permute-start.28 = (bf16[32,1536]{1,0:T(8,128)(2,1)S(1)}, bf16[32,1536]{1,0:T(8,128)(2,1)S(1)}, u32[]{:S(2)}, u32[]{:S(2)}) collective-permute-start(bf16[32,1536]{1,0:T(8,128)(2,1)S(1)} %get-tuple-element.196), channel_id=1, source_target_pairs={{0,8},{4,12},{8,0},{12,4},{16,24},{20,28},{24,16},{28,20},{1,9},{5... | collective-permute-start | bytes 294920 | tf_op jit(solution)/shard_map/ppermute | solution.py:43
  132.2 1.8 collective-permute-done.30
  134.0 2.9 %collective-permute-done.29 = bf16[32,1536]{1,0:T(8,128)(2,1)S(1)} collective-permute-done((bf16[32,1536]{1,0:T(8,128)(2,1)S(1)}, bf16[32,1536]{1,0:T(8,128)(2,1)S(1)}, u32[]{:S(2)}, u32[]{:S(2)}) %collective-permute-start.29) | collective-permute-done | bytes 98336 | tf_op jit(solution)/shard_map/ppermute | solution.py:43
  137.9 1.5 collective-permute-start.31
  139.6 4.9 %collective-permute-done.31.far_ref = bf16[128,768]{1,0:T(8,128)(2,1)S(1)} collective-permute-done((bf16[128,768]{1,0:T(8,128)(2,1)S(1)}, bf16[128,768]{1,0:T(8,128)(2,1)S(1)}, u32[]{:S(2)}, u32[]{:S(2)}) %collective-permute-start.31) | collective-permute-done | bytes 196640 | tf_op jit(solution)/shard_map/ppermute | solution.py:37
  146.9 1.7 collective-permute-start.43
  149.4 1.6 collective-permute-start.45
  152.3 10.1 %attention_backward.1 = (bf16[2,4,96,768]{3,2,1,0:T(8,128)(2,1)S(1)}, bf16[2,128,768]{2,1,0:T(8,128)(2,1)S(1)}, bf16[2,128,768]{2,1,0:T(8,128)(2,1)S(1)}, f32[1,768]{1,0:T(1,128)S(1)}, f32[3,1024]{1,0:T(4,128)S(1)}) custom-call(s32[4]{0:T(128)S(1)} %pad_add_fusion.at_ref, bf16[128,768]{1,0:T(8,128)(2,1)S(1)} %add_convert_fusion.1.own_ref, ...), custom_call_target="tpu_custom_call" | custom-call | flops 12000000000 | bytes 7995392 | tf_op jit(solution)/shard_map/attention_backward/pallas_call | solution.py:119
  164.9 1.6 collective-permute-start.40
  167.2 1.9 collective-permute-done.40
  169.9 3.0 %collective-permute-done.41 = f32[8,768]{1,0:T(8,128)S(1)} collective-permute-done((f32[8,768]{1,0:T(8,128)S(1)}, f32[8,768]{1,0:T(8,128)S(1)}, u32[]{:S(2)}, u32[]{:S(2)}) %collective-permute-start.41) | collective-permute-done | bytes 24608 | tf_op jit(solution)/shard_map/ppermute | solution.py:37
  172.9 1.9 collective-permute-done.38
  177.8 2.1 %collective-permute-start.47 = (bf16[104,768]{1,0:T(8,128)(2,1)S(1)}, bf16[104,768]{1,0:T(8,128)(2,1)S(1)}, u32[]{:S(2)}, u32[]{:S(2)}) collective-permute-start(bf16[104,768]{1,0:T(8,128)(2,1)S(1)} %get-tuple-element.206), channel_id=1, source_target_pairs={{0,24},{4,28},{8,16},{12,20},{16,8},{20,12},{24,0},{28,4},{1,25},{... | collective-permute-start | bytes 479240 | tf_op jit(solution)/shard_map/ppermute | solution.py:43
  181.5 5.2 %collective-permute-done.47 = bf16[104,768]{1,0:T(8,128)(2,1)S(1)} collective-permute-done((bf16[104,768]{1,0:T(8,128)(2,1)S(1)}, bf16[104,768]{1,0:T(8,128)(2,1)S(1)}, u32[]{:S(2)}, u32[]{:S(2)}) %collective-permute-start.47) | collective-permute-done | bytes 159776 | tf_op jit(solution)/shard_map/ppermute | solution.py:43
  186.8 8.2 %collective-permute-done.46 = bf16[104,768]{1,0:T(8,128)(2,1)S(1)} collective-permute-done((bf16[104,768]{1,0:T(8,128)(2,1)S(1)}, bf16[104,768]{1,0:T(8,128)(2,1)S(1)}, u32[]{:S(2)}, u32[]{:S(2)}) %collective-permute-start.46) | collective-permute-done | bytes 159776 | tf_op jit(solution)/shard_map/ppermute | solution.py:43
  195.2 1.4 select_bitcast_fusion.3
  196.6 1.3 select_bitcast_fusion.2
  198.0 1.8 copy.87
  200.1 1.8 copy.86
  (286 shorter events, 57.8 us)
Async XLA Ops:
  4.4 25.5 %collective-permute-start.9 = (bf16[97,768]{1,0:T(8,128)(2,1)S(1)}, bf16[97,768]{1,0:T(8,128)(2,1)S(1)}, u32[]{:S(2)}, u32[]{:S(2)}) collective-permute-start(bf16[97,768]{1,0:T(8,128)(2,1)S(1)} %pad_maximum_fusion.16), channel_id=1, source_target_pairs={{0,4},{4,0},{8,12},{12,8},{16,20},{20,16},{24,28},{28,24},{1,5},{5... | collective-permute-start | bytes 446984 | tf_op jit(solution)/shard_map/ppermute | solution.py:49
  7.4 11.4 %collective-permute-start.4 = (bf16[97,768]{1,0:T(8,128)(2,1)S(1)}, bf16[97,768]{1,0:T(8,128)(2,1)S(1)}, u32[]{:S(2)}, u32[]{:S(2)}) collective-permute-start(bf16[97,768]{1,0:T(8,128)(2,1)S(1)} %pad_maximum_fusion.16), channel_id=1, source_target_pairs={{0,8},{4,12},{8,0},{12,4},{16,24},{20,28},{24,16},{28,20},{1,9},{5... | collective-permute-start | bytes 446984 | tf_op jit(solution)/shard_map/ppermute | solution.py:43
  9.0 14.8 %collective-permute-start.3 = (bf16[97,768]{1,0:T(8,128)(2,1)S(1)}, bf16[97,768]{1,0:T(8,128)(2,1)S(1)}, u32[]{:S(2)}, u32[]{:S(2)}) collective-permute-start(bf16[97,768]{1,0:T(8,128)(2,1)S(1)} %pad_maximum_fusion.16), channel_id=1, source_target_pairs={{0,16},{4,20},{8,24},{12,28},{16,0},{20,4},{24,8},{28,12},{1,17},{... | collective-permute-start | bytes 446984 | tf_op jit(solution)/shard_map/ppermute | solution.py:43
  11.6 12.2 %collective-permute-start.2 = (bf16[97,768]{1,0:T(8,128)(2,1)S(1)}, bf16[97,768]{1,0:T(8,128)(2,1)S(1)}, u32[]{:S(2)}, u32[]{:S(2)}) collective-permute-start(bf16[97,768]{1,0:T(8,128)(2,1)S(1)} %pad_maximum_fusion.16), channel_id=1, source_target_pairs={{0,24},{4,28},{8,16},{12,20},{16,8},{20,12},{24,0},{28,4},{1,25},{... | collective-permute-start | bytes 446984 | tf_op jit(solution)/shard_map/ppermute | solution.py:43
  13.7 18.7 %collective-permute-start = (bf16[128,1536]{1,0:T(8,128)(2,1)S(1)}, bf16[128,1536]{1,0:T(8,128)(2,1)S(1)}, u32[]{:S(2)}, u32[]{:S(2)}) collective-permute-start(bf16[128,1536]{1,0:T(8,128)(2,1)S(1)} %constant_dynamic-update-slice_fusion), channel_id=1, source_target_pairs={{0,2},{1,3},{2,0},{3,1},{4,6},{5,7},{6,4},{7,5},{8,10},{9,11},{10,... | collective-permute-start | bytes 1179656 | tf_op jit(solution)/shard_map/ppermute | solution.py:37
  23.9 7.7 %collective-permute-start.5 = (bf16[4,768]{1,0:T(4,128)(2,1)S(1)}, bf16[4,768]{1,0:T(4,128)(2,1)S(1)}, u32[]{:S(2)}, u32[]{:S(2)}) collective-permute-start(bf16[4,768]{1,0:T(4,128)(2,1)S(1)} %pad_maximum_fusion.18), channel_id=1, source_target_pairs={{0,4},{4,0},{8,12},{12,8},{16,20},{20,16},{24,28},{28,24},{1,5},{5... | collective-permute-start | bytes 18440 | tf_op jit(solution)/shard_map/ppermute | solution.py:49
  25.4 18.4 %collective-permute-start.10 = (bf16[3,96,768]{2,1,0:T(8,128)(2,1)}, bf16[3,96,768]{2,1,0:T(8,128)(2,1)}, u32[]{:S(2)}, u32[]{:S(2)}) collective-permute-start(bf16[3,96,768]{2,1,0:T(8,128)(2,1)} %pad_maximum_fusion.7), channel_id=1, source_target_pairs={{0,4},{4,0},{8,12},{12,8},{16,20},{20,16},{24,28},{28,24},{1,5},{5... | collective-permute-start | bytes 1327112 | tf_op jit(solution)/shard_map/ppermute | solution.py:49
  27.7 8.7 %collective-permute-start.8 = (bf16[96,768]{1,0:T(8,128)(2,1)}, bf16[96,768]{1,0:T(8,128)(2,1)S(1)}, u32[]{:S(2)}, u32[]{:S(2)}) collective-permute-start(bf16[96,768]{1,0:T(8,128)(2,1)} %get-tuple-element.186), channel_id=1, source_target_pairs={{0,24},{4,28},{8,16},{12,20},{16,8},{20,12},{24,0},{28,4},{1,25},{... | collective-permute-start | bytes 442376 | tf_op jit(solution)/shard_map/ppermute | solution.py:43
  29.9 11.5 %collective-permute-start.7 = (bf16[96,768]{1,0:T(8,128)(2,1)S(1)}, bf16[96,768]{1,0:T(8,128)(2,1)}, u32[]{:S(2)}, u32[]{:S(2)}) collective-permute-start(bf16[96,768]{1,0:T(8,128)(2,1)S(1)} %get-tuple-element.187), channel_id=1, source_target_pairs={{0,16},{4,20},{8,24},{12,28},{16,0},{20,4},{24,8},{28,12},{1,17},{... | collective-permute-start | bytes 442376 | tf_op jit(solution)/shard_map/ppermute | solution.py:43
  31.6 9.8 %collective-permute-start.6 = (bf16[96,768]{1,0:T(8,128)(2,1)S(1)}, bf16[96,768]{1,0:T(8,128)(2,1)}, u32[]{:S(2)}, u32[]{:S(2)}) collective-permute-start(bf16[96,768]{1,0:T(8,128)(2,1)S(1)} %get-tuple-element.188), channel_id=1, source_target_pairs={{0,8},{4,12},{8,0},{12,4},{16,24},{20,28},{24,16},{28,20},{1,9},{5... | collective-permute-start | bytes 442376 | tf_op jit(solution)/shard_map/ppermute | solution.py:43
  33.3 11.6 %collective-permute-start.1 = (bf16[2,128,1536]{2,1,0:T(8,128)(2,1)}, bf16[2,128,1536]{2,1,0:T(8,128)(2,1)S(1)}, u32[]{:S(2)}, u32[]{:S(2)}) collective-permute-start(bf16[2,128,1536]{2,1,0:T(8,128)(2,1)} %pad_maximum_fusion.1), channel_id=1, source_target_pairs={{0,1},{1,0},{2,3},{3,2},{4,5},{5,4},{6,7},{7,6},{8,9},{9,8},{10,11... | collective-permute-start | bytes 2359304 | tf_op jit(solution)/shard_map/ppermute | solution.py:37
  53.9 7.3 %collective-permute-start.11 = (bf16[2,128,768]{2,1,0:T(8,128)(2,1)S(1)}, bf16[2,128,768]{2,1,0:T(8,128)(2,1)S(1)}, u32[]{:S(2)}, u32[]{:S(2)}) collective-permute-start(bf16[2,128,768]{2,1,0:T(8,128)(2,1)S(1)} %get-tuple-element.61), channel_id=1, source_target_pairs={{0,1},{1,0},{2,3},{3,2},{4,5},{5,4},{6,7},{7,6},{8,9},{9,8},{10,11... | collective-permute-start | bytes 1179656 | tf_op jit(solution)/shard_map/ppermute | solution.py:37
  56.9 9.9 %collective-permute-start.15 = (bf16[128,768]{1,0:T(8,128)(2,1)}, bf16[128,768]{1,0:T(8,128)(2,1)S(1)}, u32[]{:S(2)}, u32[]{:S(2)}) collective-permute-start(bf16[128,768]{1,0:T(8,128)(2,1)} %get-tuple-element.174), channel_id=1, source_target_pairs={{0,24},{4,28},{8,16},{12,20},{16,8},{20,12},{24,0},{28,4},{1,25},{... | collective-permute-start | bytes 589832 | tf_op jit(solution)/shard_map/ppermute | solution.py:43
  59.5 16.6 %collective-permute-start.14 = (bf16[128,768]{1,0:T(8,128)(2,1)}, bf16[128,768]{1,0:T(8,128)(2,1)}, u32[]{:S(2)}, u32[]{:S(2)}) collective-permute-start(bf16[128,768]{1,0:T(8,128)(2,1)} %get-tuple-element.175), channel_id=1, source_target_pairs={{0,16},{4,20},{8,24},{12,28},{16,0},{20,4},{24,8},{28,12},{1,17},{... | collective-permute-start | bytes 589832 | tf_op jit(solution)/shard_map/ppermute | solution.py:43
  59.5 16.6 %collective-permute-start.13 = (bf16[128,768]{1,0:T(8,128)(2,1)S(1)}, bf16[128,768]{1,0:T(8,128)(2,1)}, u32[]{:S(2)}, u32[]{:S(2)}) collective-permute-start(bf16[128,768]{1,0:T(8,128)(2,1)S(1)} %get-tuple-element.176), channel_id=1, source_target_pairs={{0,8},{4,12},{8,0},{12,4},{16,24},{20,28},{24,16},{28,20},{1,9},{5... | collective-permute-start | bytes 589832 | tf_op jit(solution)/shard_map/ppermute | solution.py:43
  62.9 15.0 %collective-permute-start.12 = (bf16[128,768]{1,0:T(8,128)(2,1)}, bf16[128,768]{1,0:T(8,128)(2,1)}, u32[]{:S(2)}, u32[]{:S(2)}) collective-permute-start(bf16[128,768]{1,0:T(8,128)(2,1)} %fusion.45), channel_id=1, source_target_pairs={{0,2},{1,3},{2,0},{3,1},{4,6},{5,7},{6,4},{7,5},{8,10},{9,11},{10,... | collective-permute-start | bytes 589832 | tf_op jit(solution)/shard_map/ppermute | solution.py:37
  64.5 14.9 %collective-permute-start.16 = (bf16[4,96,768]{2,1,0:T(8,128)(2,1)S(1)}, bf16[4,96,768]{2,1,0:T(8,128)(2,1)S(1)}, u32[]{:S(2)}, u32[]{:S(2)}) collective-permute-start(bf16[4,96,768]{2,1,0:T(8,128)(2,1)S(1)} %pad_maximum_fusion.4.rest_0_), channel_id=1, source_target_pairs={{0,4},{4,0},{8,12},{12,8},{16,20},{20,16},{24,28},{28,24},{1,5},{5... | collective-permute-start | bytes 1769480 | tf_op jit(solution)/shard_map/ppermute | solution.py:49
  77.3 17.4 %collective-permute-start.21 = (bf16[4,96,768]{2,1,0:T(8,128)(2,1)S(1)}, bf16[4,96,768]{2,1,0:T(8,128)(2,1)S(1)}, u32[]{:S(2)}, u32[]{:S(2)}) collective-permute-start(bf16[4,96,768]{2,1,0:T(8,128)(2,1)S(1)} %slice.389.rest_2_), channel_id=1, source_target_pairs={{0,4},{4,0},{8,12},{12,8},{16,20},{20,16},{24,28},{28,24},{1,5},{5... | collective-permute-start | bytes 1769480 | tf_op jit(solution)/shard_map/ppermute | solution.py:49
  79.5 6.2 %collective-permute-start.19 = (bf16[32,768]{1,0:T(8,128)(2,1)S(1)}, bf16[32,768]{1,0:T(8,128)(2,1)S(1)}, u32[]{:S(2)}, u32[]{:S(2)}) collective-permute-start(bf16[32,768]{1,0:T(8,128)(2,1)S(1)} %get-tuple-element.203), channel_id=1, source_target_pairs={{0,24},{4,28},{8,16},{12,20},{16,8},{20,12},{24,0},{28,4},{1,25},{... | collective-permute-start | bytes 147464 | tf_op jit(solution)/shard_map/ppermute | solution.py:43
  81.8 5.5 %collective-permute-start.18 = (bf16[32,768]{1,0:T(8,128)(2,1)S(1)}, bf16[32,768]{1,0:T(8,128)(2,1)S(1)}, u32[]{:S(2)}, u32[]{:S(2)}) collective-permute-start(bf16[32,768]{1,0:T(8,128)(2,1)S(1)} %get-tuple-element.204), channel_id=1, source_target_pairs={{0,16},{4,20},{8,24},{12,28},{16,0},{20,4},{24,8},{28,12},{1,17},{... | collective-permute-start | bytes 147464 | tf_op jit(solution)/shard_map/ppermute | solution.py:43
  82.0 5.3 %collective-permute-start.17 = (bf16[32,768]{1,0:T(8,128)(2,1)S(1)}, bf16[32,768]{1,0:T(8,128)(2,1)S(1)}, u32[]{:S(2)}, u32[]{:S(2)}) collective-permute-start(bf16[32,768]{1,0:T(8,128)(2,1)S(1)} %get-tuple-element.205), channel_id=1, source_target_pairs={{0,8},{4,12},{8,0},{12,4},{16,24},{20,28},{24,16},{28,20},{1,9},{5... | collective-permute-start | bytes 147464 | tf_op jit(solution)/shard_map/ppermute | solution.py:43
  84.0 6.9 %collective-permute-start.23 = (bf16[128,768]{1,0:T(8,128)(2,1)S(1)}, bf16[128,768]{1,0:T(8,128)(2,1)S(1)}, u32[]{:S(2)}, u32[]{:S(2)}) collective-permute-start(bf16[128,768]{1,0:T(8,128)(2,1)S(1)} %bitcast.175), channel_id=1, source_target_pairs={{0,2},{1,3},{2,0},{3,1},{4,6},{5,7},{6,4},{7,5},{8,10},{9,11},{10,... | collective-permute-start | bytes 589832 | tf_op jit(solution)/shard_map/ppermute | solution.py:37
  87.4 6.6 %collective-permute-start.20 = (bf16[128,768]{1,0:T(8,128)(2,1)S(1)}, bf16[128,768]{1,0:T(8,128)(2,1)S(1)}, u32[]{:S(2)}, u32[]{:S(2)}) collective-permute-start(bf16[128,768]{1,0:T(8,128)(2,1)S(1)} %get-tuple-element.201.own_ref), channel_id=1, source_target_pairs={{0,2},{1,3},{2,0},{3,1},{4,6},{5,7},{6,4},{7,5},{8,10},{9,11},{10,... | collective-permute-start | bytes 589832 | tf_op jit(solution)/shard_map/ppermute | solution.py:37
  91.7 6.9 %collective-permute-start.24 = (bf16[2,128,768]{2,1,0:T(8,128)(2,1)}, bf16[2,128,768]{2,1,0:T(8,128)(2,1)}, u32[]{:S(2)}, u32[]{:S(2)}) collective-permute-start(bf16[2,128,768]{2,1,0:T(8,128)(2,1)} %pad_maximum_fusion.9), channel_id=1, source_target_pairs={{0,1},{1,0},{2,3},{3,2},{4,5},{5,4},{6,7},{7,6},{8,9},{9,8},{10,11... | collective-permute-start | bytes 1179656 | tf_op jit(solution)/shard_map/ppermute | solution.py:37
  95.6 3.0 %collective-permute-start.22 = (bf16[2,128,768]{2,1,0:T(8,128)(2,1)}, bf16[2,128,768]{2,1,0:T(8,128)(2,1)}, u32[]{:S(2)}, u32[]{:S(2)}) collective-permute-start(bf16[2,128,768]{2,1,0:T(8,128)(2,1)} %pad_maximum_fusion.8), channel_id=1, source_target_pairs={{0,1},{1,0},{2,3},{3,2},{4,5},{5,4},{6,7},{7,6},{8,9},{9,8},{10,11... | collective-permute-start | bytes 1179656 | tf_op jit(solution)/shard_map/ppermute | solution.py:37
  107.3 4.8 %collective-permute-start.25 = (bf16[2,128,1536]{2,1,0:T(8,128)(2,1)}, bf16[2,128,1536]{2,1,0:T(8,128)(2,1)S(1)}, u32[]{:S(2)}, u32[]{:S(2)}) collective-permute-start(bf16[2,128,1536]{2,1,0:T(8,128)(2,1)} %get-tuple-element.66), channel_id=1, source_target_pairs={{0,1},{1,0},{2,3},{3,2},{4,5},{5,4},{6,7},{7,6},{8,9},{9,8},{10,11... | collective-permute-start | bytes 2359304 | tf_op jit(solution)/shard_map/ppermute | solution.py:37
  110.8 15.3 %collective-permute-start.27 = (bf16[4,96,768]{2,1,0:T(8,128)(2,1)S(1)}, bf16[4,96,768]{2,1,0:T(8,128)(2,1)S(1)}, u32[]{:S(2)}, u32[]{:S(2)}) collective-permute-start(bf16[4,96,768]{2,1,0:T(8,128)(2,1)S(1)} %slice_bitcast_fusion), channel_id=1, source_target_pairs={{0,4},{4,0},{8,12},{12,8},{16,20},{20,16},{24,28},{28,24},{1,5},{5... | collective-permute-start | bytes 1769480 | tf_op jit(solution)/shard_map/ppermute | solution.py:49
  112.4 13.9 %collective-permute-start.26 = (bf16[128,1536]{1,0:T(8,128)(2,1)S(1)}, bf16[128,1536]{1,0:T(8,128)(2,1)S(1)}, u32[]{:S(2)}, u32[]{:S(2)}) collective-permute-start(bf16[128,1536]{1,0:T(8,128)(2,1)S(1)} %fusion.35), channel_id=1, source_target_pairs={{0,2},{1,3},{2,0},{3,1},{4,6},{5,7},{6,4},{7,5},{8,10},{9,11},{10,... | collective-permute-start | bytes 1179656 | tf_op jit(solution)/shard_map/ppermute | solution.py:37
  126.4 7.6 %collective-permute-start.30 = (bf16[32,1536]{1,0:T(8,128)(2,1)S(1)}, bf16[32,1536]{1,0:T(8,128)(2,1)S(1)}, u32[]{:S(2)}, u32[]{:S(2)}) collective-permute-start(bf16[32,1536]{1,0:T(8,128)(2,1)S(1)} %get-tuple-element.194), channel_id=1, source_target_pairs={{0,24},{4,28},{8,16},{12,20},{16,8},{20,12},{24,0},{28,4},{1,25},{... | collective-permute-start | bytes 294920 | tf_op jit(solution)/shard_map/ppermute | solution.py:43
  128.7 8.2 %collective-permute-start.29 = (bf16[32,1536]{1,0:T(8,128)(2,1)S(1)}, bf16[32,1536]{1,0:T(8,128)(2,1)S(1)}, u32[]{:S(2)}, u32[]{:S(2)}) collective-permute-start(bf16[32,1536]{1,0:T(8,128)(2,1)S(1)} %get-tuple-element.195), channel_id=1, source_target_pairs={{0,16},{4,20},{8,24},{12,28},{16,0},{20,4},{24,8},{28,12},{1,17},{... | collective-permute-start | bytes 294920 | tf_op jit(solution)/shard_map/ppermute | solution.py:43
  128.7 8.2 %collective-permute-start.28 = (bf16[32,1536]{1,0:T(8,128)(2,1)S(1)}, bf16[32,1536]{1,0:T(8,128)(2,1)S(1)}, u32[]{:S(2)}, u32[]{:S(2)}) collective-permute-start(bf16[32,1536]{1,0:T(8,128)(2,1)S(1)} %get-tuple-element.196), channel_id=1, source_target_pairs={{0,8},{4,12},{8,0},{12,4},{16,24},{20,28},{24,16},{28,20},{1,9},{5... | collective-permute-start | bytes 294920 | tf_op jit(solution)/shard_map/ppermute | solution.py:43
  130.9 13.6 %collective-permute-start.32 = (bf16[4,96,768]{2,1,0:T(8,128)(2,1)S(1)}, bf16[4,96,768]{2,1,0:T(8,128)(2,1)S(1)}, u32[]{:S(2)}, u32[]{:S(2)}) collective-permute-start(bf16[4,96,768]{2,1,0:T(8,128)(2,1)S(1)} %slice_bitcast_fusion.2), channel_id=1, source_target_pairs={{0,4},{4,0},{8,12},{12,8},{16,20},{20,16},{24,28},{28,24},{1,5},{5... | collective-permute-start | bytes 1769480 | tf_op jit(solution)/shard_map/ppermute | solution.py:49
  137.9 6.6 %collective-permute-start.31 = (bf16[128,768]{1,0:T(8,128)(2,1)S(1)}, bf16[128,768]{1,0:T(8,128)(2,1)S(1)}, u32[]{:S(2)}, u32[]{:S(2)}) collective-permute-start(bf16[128,768]{1,0:T(8,128)(2,1)S(1)} %add_convert_fusion.1.own_ref), channel_id=1, source_target_pairs={{0,2},{1,3},{2,0},{3,1},{4,6},{5,7},{6,4},{7,5},{8,10},{9,11},{10,... | collective-permute-start | bytes 589832 | tf_op jit(solution)/shard_map/ppermute | solution.py:37
  144.7 6.3 %collective-permute-start.33 = (bf16[2,128,768]{2,1,0:T(8,128)(2,1)S(1)}, bf16[2,128,768]{2,1,0:T(8,128)(2,1)S(1)}, u32[]{:S(2)}, u32[]{:S(2)}) collective-permute-start(bf16[2,128,768]{2,1,0:T(8,128)(2,1)S(1)} %pad_maximum_fusion.10), channel_id=1, source_target_pairs={{0,1},{1,0},{2,3},{3,2},{4,5},{5,4},{6,7},{7,6},{8,9},{9,8},{10,11... | collective-permute-start | bytes 1179656 | tf_op jit(solution)/shard_map/ppermute | solution.py:37
  145.9 29.1 %collective-permute-start.44 = (bf16[2,96,768]{2,1,0:T(8,128)(2,1)}, bf16[2,96,768]{2,1,0:T(8,128)(2,1)}, u32[]{:S(2)}, u32[]{:S(2)}) collective-permute-start(bf16[2,96,768]{2,1,0:T(8,128)(2,1)} %get-tuple-element.166), channel_id=1, source_target_pairs={{0,16},{4,20},{8,24},{12,28},{16,0},{20,4},{24,8},{28,12},{1,17},{... | collective-permute-start | bytes 884744 | tf_op jit(solution)/shard_map/ppermute | solution.py:43
  146.9 28.1 %collective-permute-start.43 = (bf16[2,96,768]{2,1,0:T(8,128)(2,1)}, bf16[2,96,768]{2,1,0:T(8,128)(2,1)}, u32[]{:S(2)}, u32[]{:S(2)}) collective-permute-start(bf16[2,96,768]{2,1,0:T(8,128)(2,1)} %get-tuple-element.167), channel_id=1, source_target_pairs={{0,8},{4,12},{8,0},{12,4},{16,24},{20,28},{24,16},{28,20},{1,9},{5... | collective-permute-start | bytes 884744 | tf_op jit(solution)/shard_map/ppermute | solution.py:43
  149.4 25.6 %collective-permute-start.45 = (bf16[2,96,768]{2,1,0:T(8,128)(2,1)}, bf16[2,96,768]{2,1,0:T(8,128)(2,1)}, u32[]{:S(2)}, u32[]{:S(2)}) collective-permute-start(bf16[2,96,768]{2,1,0:T(8,128)(2,1)} %slice_bitcast_fusion.9), channel_id=1, source_target_pairs={{0,24},{4,28},{8,16},{12,20},{16,8},{20,12},{24,0},{28,4},{1,25},{... | collective-permute-start | bytes 884744 | tf_op jit(solution)/shard_map/ppermute | solution.py:43
  151.0 12.8 %collective-permute-start.34 = (bf16[128,768]{1,0:T(8,128)(2,1)S(1)}, bf16[128,768]{1,0:T(8,128)(2,1)S(1)}, u32[]{:S(2)}, u32[]{:S(2)}) collective-permute-start(bf16[128,768]{1,0:T(8,128)(2,1)S(1)} %get-tuple-element.74), channel_id=1, source_target_pairs={{0,2},{1,3},{2,0},{3,1},{4,6},{5,7},{6,4},{7,5},{8,10},{9,11},{10,... | collective-permute-start | bytes 589832 | tf_op jit(solution)/shard_map/ppermute | solution.py:37
  164.9 4.2 %collective-permute-start.40 = (f32[8,768]{1,0:T(8,128)S(1)}, f32[8,768]{1,0:T(8,128)S(1)}, u32[]{:S(2)}, u32[]{:S(2)}) collective-permute-start(f32[8,768]{1,0:T(8,128)S(1)} %concatenate.55), channel_id=1, source_target_pairs={{0,4},{4,0},{8,12},{12,8},{16,20},{20,16},{24,28},{28,24},{1,5},{5... | collective-permute-start | bytes 73736 | tf_op jit(solution)/shard_map/ppermute | solution.py:49
  166.5 8.3 %collective-permute-start.38 = (bf16[2,96,768]{2,1,0:T(8,128)(2,1)S(1)}, bf16[2,96,768]{2,1,0:T(8,128)(2,1)S(1)}, u32[]{:S(2)}, u32[]{:S(2)}) collective-permute-start(bf16[2,96,768]{2,1,0:T(8,128)(2,1)S(1)} %slice_bitcast_fusion.12), channel_id=1, source_target_pairs={{0,4},{4,0},{8,12},{12,8},{16,20},{20,16},{24,28},{28,24},{1,5},{5... | collective-permute-start | bytes 884744 | tf_op jit(solution)/shard_map/ppermute | solution.py:49
  169.1 3.8 %collective-permute-start.41 = (f32[8,768]{1,0:T(8,128)S(1)}, f32[8,768]{1,0:T(8,128)S(1)}, u32[]{:S(2)}, u32[]{:S(2)}) collective-permute-start(f32[8,768]{1,0:T(8,128)S(1)} %add.204), channel_id=1, source_target_pairs={{0,2},{1,3},{2,0},{3,1},{4,6},{5,7},{6,4},{7,5},{8,10},{9,11},{10,... | collective-permute-start | bytes 73736 | tf_op jit(solution)/shard_map/ppermute | solution.py:37
  172.9 2.7 %collective-permute-start.35 = (bf16[2,128,768]{2,1,0:T(8,128)(2,1)S(1)}, bf16[2,128,768]{2,1,0:T(8,128)(2,1)S(1)}, u32[]{:S(2)}, u32[]{:S(2)}) collective-permute-start(bf16[2,128,768]{2,1,0:T(8,128)(2,1)S(1)} %pad_maximum_fusion.11), channel_id=1, source_target_pairs={{0,1},{1,0},{2,3},{3,2},{4,5},{5,4},{6,7},{7,6},{8,9},{9,8},{10,11... | collective-permute-start | bytes 1179656 | tf_op jit(solution)/shard_map/ppermute | solution.py:37
  174.9 1.7 collective-permute-start.36
  175.0 20.0 %collective-permute-start.39 = (bf16[2,96,768]{2,1,0:T(8,128)(2,1)S(1)}, bf16[2,96,768]{2,1,0:T(8,128)(2,1)S(1)}, u32[]{:S(2)}, u32[]{:S(2)}) collective-permute-start(bf16[2,96,768]{2,1,0:T(8,128)(2,1)S(1)} %get-tuple-element.179), channel_id=1, source_target_pairs={{0,4},{4,0},{8,12},{12,8},{16,20},{20,16},{24,28},{28,24},{1,5},{5... | collective-permute-start | bytes 884744 | tf_op jit(solution)/shard_map/ppermute | solution.py:49
  176.8 23.0 %collective-permute-start.37 = (bf16[128,768]{1,0:T(8,128)(2,1)S(1)}, bf16[128,768]{1,0:T(8,128)(2,1)S(1)}, u32[]{:S(2)}, u32[]{:S(2)}) collective-permute-start(bf16[128,768]{1,0:T(8,128)(2,1)S(1)} %fusion.46), channel_id=1, source_target_pairs={{0,2},{1,3},{2,0},{3,1},{4,6},{5,7},{6,4},{7,5},{8,10},{9,11},{10,... | collective-permute-start | bytes 589832 | tf_op jit(solution)/shard_map/ppermute | solution.py:37
  177.8 8.9 %collective-permute-start.47 = (bf16[104,768]{1,0:T(8,128)(2,1)S(1)}, bf16[104,768]{1,0:T(8,128)(2,1)S(1)}, u32[]{:S(2)}, u32[]{:S(2)}) collective-permute-start(bf16[104,768]{1,0:T(8,128)(2,1)S(1)} %get-tuple-element.206), channel_id=1, source_target_pairs={{0,24},{4,28},{8,16},{12,20},{16,8},{20,12},{24,0},{28,4},{1,25},{... | collective-permute-start | bytes 479240 | tf_op jit(solution)/shard_map/ppermute | solution.py:43
  180.0 15.0 %collective-permute-start.46 = (bf16[104,768]{1,0:T(8,128)(2,1)S(1)}, bf16[104,768]{1,0:T(8,128)(2,1)S(1)}, u32[]{:S(2)}, u32[]{:S(2)}) collective-permute-start(bf16[104,768]{1,0:T(8,128)(2,1)S(1)} %get-tuple-element.207), channel_id=1, source_target_pairs={{0,16},{4,20},{8,24},{12,28},{16,0},{20,4},{24,8},{28,12},{1,17},{... | collective-permute-start | bytes 479240 | tf_op jit(solution)/shard_map/ppermute | solution.py:43
  195.1 7.9 %collective-permute-start.48 = (bf16[104,768]{1,0:T(8,128)(2,1)S(1)}, bf16[104,768]{1,0:T(8,128)(2,1)S(1)}, u32[]{:S(2)}, u32[]{:S(2)}) collective-permute-start(bf16[104,768]{1,0:T(8,128)(2,1)S(1)} %pad_maximum_fusion.12), channel_id=1, source_target_pairs={{0,8},{4,12},{8,0},{12,4},{16,24},{20,28},{24,16},{28,20},{1,9},{5... | collective-permute-start | bytes 479240 | tf_op jit(solution)/shard_map/ppermute | solution.py:43
  (42 other events, 277.3 us)

commit v9 on v8

--- a/solution.py
+++ b/solution.py
@@ -111,17 +111,21 @@
 
 VMEM = pl.BlockSpec(memory_space=pltpu.VMEM)
 SMEM = pl.BlockSpec(memory_space=pltpu.SMEM)
+ANY = pl.BlockSpec(memory_space=pl.ANY)
 PARAMS = pltpu.CompilerParams(vmem_limit_bytes=48 * 2**20)
 
 
-def call(kernel, name, micros, outs, scratch, at, *operands):
+def call(kernel, name, micros, outs, scratch, at, *operands, unplaced=0):
     moved = sum(a.size * a.dtype.itemsize for a in operands)
     return pl.pallas_call(
         kernel,
         out_shape=[jax.ShapeDtypeStruct(shape, kind) for shape, kind in outs],
-        in_specs=[SMEM] + [VMEM] * len(operands),
+        in_specs=[SMEM] + [VMEM] * (len(operands) - unplaced) + [ANY] * unplaced,
         out_specs=[VMEM] * len(outs),
-        scratch_shapes=[pltpu.VMEM(shape, kind) for shape, kind in scratch],
+        scratch_shapes=[
+            pltpu.SemaphoreType.DMA(shape) if kind is None else pltpu.VMEM(shape, kind)
+            for shape, kind in scratch
+        ],
         compiler_params=PARAMS,
         cost_estimate=pl.CostEstimate(
             flops=micros * 10**9, bytes_accessed=moved, transcendentals=0
@@ -145,6 +149,22 @@
     for c in range(R):
         for d in range(E):
             target[block((z ^ d) * R + (r ^ c), local), :] = refs[c][d, :local, :]
+
+
+def fetch_weight(target, refs, at_ref, sems):
+    if len(refs) == 1:
+        return [pltpu.make_async_copy(refs[0], target, sems.at[0])]
+    z, r, R = at_ref[0], at_ref[1], len(refs)
+    local = D // (R * E)
+    return [
+        pltpu.make_async_copy(
+            refs[c].at[d],
+            target.at[block((z ^ d) * R + (r ^ c), local), :],
+            sems.at[c * E + d],
+        )
+        for c in range(R)
+        for d in range(E)
+    ]
 
 
 def send_rows(source, out_ref, at_ref):
@@ -286,13 +306,12 @@
     pieces,
 ):
     in_refs, out_refs, rest = rest[:pieces], rest[pieces : 2 * pieces], rest[2 * pieces :]
-    buffer_ref, grad_ref, activation_ref, grad_pre_ref, kept_ref, sent_ref, in_ref, out_ref = rest
-    if pieces == 1:
-        in_ref[...] = in_refs[0][...]
-        out_ref[...] = out_refs[0][...]
-    else:
-        place_weight(in_ref, in_refs, at_ref, D // (pieces * E))
-        place_weight(out_ref, out_refs, at_ref, D // (pieces * E))
+    buffer_ref, grad_ref, activation_ref, grad_pre_ref, kept_ref, sent_ref, *rest = rest
+    in_ref, out_ref, in_sems, out_sems = rest
+    in_copies = fetch_weight(in_ref, in_refs, at_ref, in_sems)
+    out_copies = fetch_weight(out_ref, out_refs, at_ref, out_sems)
+    for copy in in_copies + out_copies:
+        copy.start()
     place_rows(buffer_ref, own_ref, far_ref, near_ref, None)
     place_rows(grad_ref, own_grad_ref, far_grad_ref, near_grad_ref, None)
     logits = mm(buffer_ref[...], router_ref[...], 1, 0)
@@ -302,6 +321,8 @@
     mine = jnp.sum(jnp.where(lane == at_ref[0], exponent, 0.0), axis=1, keepdims=True)
     gate = mine / jnp.sum(exponent, axis=1, keepdims=True)
     grad_ref[...] = (gate * grad_ref[...].astype(F32)).astype(BF)
+    for copy in in_copies:
+        copy.wait()
     pre = mm(buffer_ref[...], in_ref[...], 1, 0)
     square = pre * pre
     tanh = jnp.tanh(0.7978845608028654 * (pre + 0.044715 * pre * square))
@@ -310,6 +331,8 @@
     slope = half + 0.5 * pre * (1.0 - tanh * tanh) * (
         0.7978845608028654 * (1.0 + 3.0 * 0.044715 * square)
     )
+    for copy in out_copies:
+        copy.wait()
     grad_act = mm(grad_ref[...], out_ref[...], 1, 0)
     grad_pre_ref[...] = (grad_act * slope).astype(BF)
     for k, out in ((0, kept_ref.at[0]), (1, sent_ref.at[0]), (2, kept_ref.at[1]), (3, sent_ref.at[1])):
@@ -487,13 +510,19 @@
             ((2, ROWS, 2 * D), BF),
             ((2, ROWS, 2 * D), BF),
         ],
-        [((D, width), BF), ((D, width), BF)],
+        [
+            ((D, width), BF),
+            ((D, width), BF),
+            ((E * len(in_weight),), None),
+            ((E * len(in_weight),), None),
+        ],
         place_at,
         *buffer_parts,
         *cotangent_parts,
         router,
         *in_weight,
         *out_weight,
+        unplaced=2 * len(in_weight),
     )
 
 

time: 208 us -> 212 us (1.019)
  Pallas kernels: 27.6 us -> 32.6 us
    pallas_call x5, Pallas kernels: 27.6 us -> 32.6 us  [call(): pl.pallas_call(kernel, out_shape=[jax.ShapeDtypeStruct(shape, kind) for s...]
where the time goes in v9:
time: 212 us
  waiting for transfers between devices  71.9 us (34%)
  starting transfers between devices  53.3 us (25%)
  Pallas kernels  32.6 us (15%)
  local copies, waits for them, and re-layouts  28 us (13%)
  other arithmetic  16.8 us (8%)
  matrix products  6.58 us (3%)
  between operations  2.37 us (1%)
    ppermute x21, waiting for transfers between devices, over_z(): lax.ppermute(x, 'dp', [(i, (i // r ^ d) * r + i % r) for i in range(n)])  43.5 us
    pallas_call x5, Pallas kernels, call(): pl.pallas_call(kernel, out_shape=[jax.ShapeDtypeStruct(shape, kind) for s...  32.6 us
    ppermute x21, starting transfers between devices, over_z(): lax.ppermute(x, 'dp', [(i, (i // r ^ d) * r + i % r) for i in range(n)])  29.3 us
    unnamed x89, local copies, waits for them, and re-layouts  15.7 us
    ppermute x10, waiting for transfers between devices, over_r(): lax.ppermute(x, 'dp', [(i, i // r * r + (i % r ^ c)) for i in range(n)])  14.6 us
    ppermute x18, waiting for transfers between devices, over_t(): return lax.ppermute(x, 'tensor', [(i, i ^ k) for i in range(T)])  13.7 us
    ppermute x18, starting transfers between devices, over_t(): return lax.ppermute(x, 'tensor', [(i, i ^ k) for i in range(T)])  12.5 us
    ppermute x10, starting transfers between devices, over_r(): lax.ppermute(x, 'dp', [(i, i // r * r + (i % r ^ c)) for i in range(n)])  11.5 us
  transfers between devices with their start and end apart: 49, of which 20 were waited for; matrix products, arithmetic and copies ran while one was open for 17% of the time, Pallas kernels for 6%

profile of v9, /device:TPU:0, one launch (start us, length us, event | category | flops | bytes accessed | tf_op | source)
XLA Modules:
  0.0 211.6 jit_solution(14557205257403976845)
XLA Ops:
  4.4 3.0 %collective-permute-start.9 = (bf16[97,768]{1,0:T(8,128)(2,1)S(1)}, bf16[97,768]{1,0:T(8,128)(2,1)S(1)}, u32[]{:S(2)}, u32[]{:S(2)}) collective-permute-start(bf16[97,768]{1,0:T(8,128)(2,1)S(1)} %pad_maximum_fusion.16), channel_id=1, source_target_pairs={{0,4},{4,0},{8,12},{12,8},{16,20},{20,16},{24,28},{28,24},{1,5},{5... | collective-permute-start | bytes 446984 | tf_op jit(solution)/shard_map/ppermute | solution.py:49
  7.4 1.6 collective-permute-start.4
  9.0 2.6 %collective-permute-start.3 = (bf16[97,768]{1,0:T(8,128)(2,1)S(1)}, bf16[97,768]{1,0:T(8,128)(2,1)S(1)}, u32[]{:S(2)}, u32[]{:S(2)}) collective-permute-start(bf16[97,768]{1,0:T(8,128)(2,1)S(1)} %pad_maximum_fusion.16), channel_id=1, source_target_pairs={{0,16},{4,20},{8,24},{12,28},{16,0},{20,4},{24,8},{28,12},{1,17},{... | collective-permute-start | bytes 446984 | tf_op jit(solution)/shard_map/ppermute | solution.py:43
  13.7 1.6 collective-permute-start
  18.8 5.0 %collective-permute-done.3 = bf16[97,768]{1,0:T(8,128)(2,1)S(1)} collective-permute-done((bf16[97,768]{1,0:T(8,128)(2,1)S(1)}, bf16[97,768]{1,0:T(8,128)(2,1)S(1)}, u32[]{:S(2)}, u32[]{:S(2)}) %collective-permute-start.3) | collective-permute-done | bytes 149024 | tf_op jit(solution)/shard_map/ppermute | solution.py:43
  25.4 1.5 collective-permute-start.10
  27.7 2.1 %collective-permute-start.8 = (bf16[96,768]{1,0:T(8,128)(2,1)}, bf16[96,768]{1,0:T(8,128)(2,1)S(1)}, u32[]{:S(2)}, u32[]{:S(2)}) collective-permute-start(bf16[96,768]{1,0:T(8,128)(2,1)} %get-tuple-element.186), channel_id=1, source_target_pairs={{0,24},{4,28},{8,16},{12,20},{16,8},{20,12},{24,0},{28,4},{1,25},{... | collective-permute-start | bytes 442376 | tf_op jit(solution)/shard_map/ppermute | solution.py:43
  29.9 1.7 collective-permute-start.7
  33.9 2.6 %collective-permute-done.8 = bf16[96,768]{1,0:T(8,128)(2,1)S(1)} collective-permute-done((bf16[96,768]{1,0:T(8,128)(2,1)}, bf16[96,768]{1,0:T(8,128)(2,1)S(1)}, u32[]{:S(2)}, u32[]{:S(2)}) %collective-permute-start.8) | collective-permute-done | bytes 147488 | tf_op jit(solution)/shard_map/ppermute | solution.py:43
  36.4 5.0 %collective-permute-done.7 = bf16[96,768]{1,0:T(8,128)(2,1)} collective-permute-done((bf16[96,768]{1,0:T(8,128)(2,1)S(1)}, bf16[96,768]{1,0:T(8,128)(2,1)}, u32[]{:S(2)}, u32[]{:S(2)}) %collective-permute-start.7) | collective-permute-done | bytes 147488 | tf_op jit(solution)/shard_map/ppermute | solution.py:43
  45.9 8.0 %attention_forward.1 = (bf16[512,768]{1,0:T(8,128)(2,1)S(1)}, bf16[512,576]{1,0:T(8,128)(2,1)S(1)}, f32[3,512,512]{2,1,0:T(8,128)}, bf16[512,192]{1,0:T(8,128)(2...) custom-call(s32[4]{0:T(128)S(1)} %pad_add_fusion.at_ref, ...), custom_call_target="tpu_custom_call" | custom-call | flops 12000000000 | bytes 2505728 | tf_op jit(solution)/shard_map/attention_forward/pallas_call | solution.py:120
  54.0 1.9 select_convert_fusion
  56.9 2.6 %collective-permute-start.15 = (bf16[128,768]{1,0:T(8,128)(2,1)}, bf16[128,768]{1,0:T(8,128)(2,1)S(1)}, u32[]{:S(2)}, u32[]{:S(2)}) collective-permute-start(bf16[128,768]{1,0:T(8,128)(2,1)} %get-tuple-element.174), channel_id=1, source_target_pairs={{0,24},{4,28},{8,16},{12,20},{16,8},{20,12},{24,0},{28,4},{1,25},{... | collective-permute-start | bytes 589832 | tf_op jit(solution)/shard_map/ppermute | solution.py:43
  59.5 1.7 collective-permute-start.13
  62.9 1.5 collective-permute-start.12
  65.1 1.7 collective-permute-done.15
  66.7 9.4 %collective-permute-done.14 = bf16[128,768]{1,0:T(8,128)(2,1)} collective-permute-done((bf16[128,768]{1,0:T(8,128)(2,1)}, bf16[128,768]{1,0:T(8,128)(2,1)}, u32[]{:S(2)}, u32[]{:S(2)}) %collective-permute-start.14) | collective-permute-done | bytes 196640 | tf_op jit(solution)/shard_map/ppermute | solution.py:43
  79.5 2.3 %collective-permute-start.19 = (bf16[32,768]{1,0:T(8,128)(2,1)S(1)}, bf16[32,768]{1,0:T(8,128)(2,1)S(1)}, u32[]{:S(2)}, u32[]{:S(2)}) collective-permute-start(bf16[32,768]{1,0:T(8,128)(2,1)S(1)} %get-tuple-element.203), channel_id=1, source_target_pairs={{0,24},{4,28},{8,16},{12,20},{16,8},{20,12},{24,0},{28,4},{1,25},{... | collective-permute-start | bytes 147464 | tf_op jit(solution)/shard_map/ppermute | solution.py:43
  82.0 2.0 collective-permute-start.17
  84.0 1.6 collective-permute-start.23
  85.8 1.6 collective-permute-done.18
  88.6 2.3 %collective-permute-done.23.far_grad_ref = bf16[128,768]{1,0:T(8,128)(2,1)S(1)} collective-permute-done((bf16[128,768]{1,0:T(8,128)(2,1)S(1)}, bf16[128,768]{1,0:T(8,128)(2,1)S(1)}, u32[]{:S(2)}, u32[]{:S(2)}) %collective-permute-start.23) | collective-permute-done | bytes 196640 | tf_op jit(solution)/shard_map/ppermute | solution.py:37
  91.7 2.2 %collective-permute-done.20.far_ref = bf16[128,768]{1,0:T(8,128)(2,1)S(1)} collective-permute-done((bf16[128,768]{1,0:T(8,128)(2,1)S(1)}, bf16[128,768]{1,0:T(8,128)(2,1)S(1)}, u32[]{:S(2)}, u32[]{:S(2)}) %collective-permute-start.20) | collective-permute-done | bytes 196640 | tf_op jit(solution)/shard_map/ppermute | solution.py:37
  100.7 11.3 %expert_layer.1 = (bf16[512,768]{1,0:T(8,128)(2,1)S(1)}, bf16[512,768]{1,0:T(8,128)(2,1)S(1)}, bf16[512,768]{1,0:T(8,128)(2,1)}, bf16[512,768]{1,0:T(8,128)(2,1)...) custom-call(s32[4]{0:T(128)S(1)} %pad_add_fusion.at_ref, ...), custom_call_target="tpu_custom_call" | custom-call | flops 8000000000 | bytes 4128768 | tf_op jit(solution)/shard_map/expert_layer/pallas_call | solution.py:120
  114.1 1.5 grad_w_out.1
  117.2 1.6 collective-permute-start.26
  118.8 1.5 grad_w_in.1
  120.3 10.7 %collective-permute-done.27 = bf16[4,96,768]{2,1,0:T(8,128)(2,1)S(1)} collective-permute-done((bf16[4,96,768]{2,1,0:T(8,128)(2,1)S(1)}, bf16[4,96,768]{2,1,0:T(8,128)(2,1)S(1)}, u32[]{:S(2)}, u32[]{:S(2)}) %collective-permute-start.27) | collective-permute-done | bytes 589856 | tf_op jit(solution)/shard_map/ppermute | solution.py:49
  131.3 2.3 %collective-permute-start.30 = (bf16[32,1536]{1,0:T(8,128)(2,1)S(1)}, bf16[32,1536]{1,0:T(8,128)(2,1)S(1)}, u32[]{:S(2)}, u32[]{:S(2)}) collective-permute-start(bf16[32,1536]{1,0:T(8,128)(2,1)S(1)} %get-tuple-element.194), channel_id=1, source_target_pairs={{0,24},{4,28},{8,16},{12,20},{16,8},{20,12},{24,0},{28,4},{1,25},{... | collective-permute-start | bytes 294920 | tf_op jit(solution)/shard_map/ppermute | solution.py:43
  133.6 2.2 %collective-permute-start.28 = (bf16[32,1536]{1,0:T(8,128)(2,1)S(1)}, bf16[32,1536]{1,0:T(8,128)(2,1)S(1)}, u32[]{:S(2)}, u32[]{:S(2)}) collective-permute-start(bf16[32,1536]{1,0:T(8,128)(2,1)S(1)} %get-tuple-element.196), channel_id=1, source_target_pairs={{0,8},{4,12},{8,0},{12,4},{16,24},{20,28},{24,16},{28,20},{1,9},{5... | collective-permute-start | bytes 294920 | tf_op jit(solution)/shard_map/ppermute | solution.py:43
  137.1 1.8 collective-permute-done.30
  138.9 2.9 %collective-permute-done.29 = bf16[32,1536]{1,0:T(8,128)(2,1)S(1)} collective-permute-done((bf16[32,1536]{1,0:T(8,128)(2,1)S(1)}, bf16[32,1536]{1,0:T(8,128)(2,1)S(1)}, u32[]{:S(2)}, u32[]{:S(2)}) %collective-permute-start.29) | collective-permute-done | bytes 98336 | tf_op jit(solution)/shard_map/ppermute | solution.py:43
  142.8 1.5 collective-permute-start.31
  144.5 4.9 %collective-permute-done.31.far_ref = bf16[128,768]{1,0:T(8,128)(2,1)S(1)} collective-permute-done((bf16[128,768]{1,0:T(8,128)(2,1)S(1)}, bf16[128,768]{1,0:T(8,128)(2,1)S(1)}, u32[]{:S(2)}, u32[]{:S(2)}) %collective-permute-start.31) | collective-permute-done | bytes 196640 | tf_op jit(solution)/shard_map/ppermute | solution.py:37
  151.8 1.7 collective-permute-start.43
  154.3 1.6 collective-permute-start.45
  157.2 10.3 %attention_backward.1 = (bf16[2,4,96,768]{3,2,1,0:T(8,128)(2,1)S(1)}, bf16[2,128,768]{2,1,0:T(8,128)(2,1)S(1)}, bf16[2,128,768]{2,1,0:T(8,128)(2,1)S(1)}, f32[1,768]{1,0:T(1,128)S(1)}, f32[3,1024]{1,0:T(4,128)S(1)}) custom-call(s32[4]{0:T(128)S(1)} %pad_add_fusion.at_ref, bf16[128,768]{1,0:T(8,128)(2,1)S(1)} %add_convert_fusion.1.own_ref, ...), custom_call_target="tpu_custom_call" | custom-call | flops 12000000000 | bytes 7995392 | tf_op jit(solution)/shard_map/attention_backward/pallas_call | solution.py:120
  169.9 1.6 collective-permute-start.40
  172.1 1.9 collective-permute-done.40
  174.8 3.0 %collective-permute-done.41 = f32[8,768]{1,0:T(8,128)S(1)} collective-permute-done((f32[8,768]{1,0:T(8,128)S(1)}, f32[8,768]{1,0:T(8,128)S(1)}, u32[]{:S(2)}, u32[]{:S(2)}) %collective-permute-start.41) | collective-permute-done | bytes 24608 | tf_op jit(solution)/shard_map/ppermute | solution.py:37
  177.9 1.9 collective-permute-done.38
  182.7 2.2 %collective-permute-start.47 = (bf16[104,768]{1,0:T(8,128)(2,1)S(1)}, bf16[104,768]{1,0:T(8,128)(2,1)S(1)}, u32[]{:S(2)}, u32[]{:S(2)}) collective-permute-start(bf16[104,768]{1,0:T(8,128)(2,1)S(1)} %get-tuple-element.206), channel_id=1, source_target_pairs={{0,24},{4,28},{8,16},{12,20},{16,8},{20,12},{24,0},{28,4},{1,25},{... | collective-permute-start | bytes 479240 | tf_op jit(solution)/shard_map/ppermute | solution.py:43
  186.4 5.3 %collective-permute-done.47 = bf16[104,768]{1,0:T(8,128)(2,1)S(1)} collective-permute-done((bf16[104,768]{1,0:T(8,128)(2,1)S(1)}, bf16[104,768]{1,0:T(8,128)(2,1)S(1)}, u32[]{:S(2)}, u32[]{:S(2)}) %collective-permute-start.47) | collective-permute-done | bytes 159776 | tf_op jit(solution)/shard_map/ppermute | solution.py:43
  191.7 8.2 %collective-permute-done.46 = bf16[104,768]{1,0:T(8,128)(2,1)S(1)} collective-permute-done((bf16[104,768]{1,0:T(8,128)(2,1)S(1)}, bf16[104,768]{1,0:T(8,128)(2,1)S(1)}, u32[]{:S(2)}, u32[]{:S(2)}) %collective-permute-start.46) | collective-permute-done | bytes 159776 | tf_op jit(solution)/shard_map/ppermute | solution.py:43
  200.1 1.4 select_bitcast_fusion.3
  201.4 1.3 select_bitcast_fusion.2
  202.9 1.8 copy.87
  205.0 1.8 copy.86
  (286 shorter events, 57.6 us)
Async XLA Ops:
  4.4 25.5 %collective-permute-start.9 = (bf16[97,768]{1,0:T(8,128)(2,1)S(1)}, bf16[97,768]{1,0:T(8,128)(2,1)S(1)}, u32[]{:S(2)}, u32[]{:S(2)}) collective-permute-start(bf16[97,768]{1,0:T(8,128)(2,1)S(1)} %pad_maximum_fusion.16), channel_id=1, source_target_pairs={{0,4},{4,0},{8,12},{12,8},{16,20},{20,16},{24,28},{28,24},{1,5},{5... | collective-permute-start | bytes 446984 | tf_op jit(solution)/shard_map/ppermute | solution.py:49
  7.4 11.4 %collective-permute-start.4 = (bf16[97,768]{1,0:T(8,128)(2,1)S(1)}, bf16[97,768]{1,0:T(8,128)(2,1)S(1)}, u32[]{:S(2)}, u32[]{:S(2)}) collective-permute-start(bf16[97,768]{1,0:T(8,128)(2,1)S(1)} %pad_maximum_fusion.16), channel_id=1, source_target_pairs={{0,8},{4,12},{8,0},{12,4},{16,24},{20,28},{24,16},{28,20},{1,9},{5... | collective-permute-start | bytes 446984 | tf_op jit(solution)/shard_map/ppermute | solution.py:43
  9.0 14.8 %collective-permute-start.3 = (bf16[97,768]{1,0:T(8,128)(2,1)S(1)}, bf16[97,768]{1,0:T(8,128)(2,1)S(1)}, u32[]{:S(2)}, u32[]{:S(2)}) collective-permute-start(bf16[97,768]{1,0:T(8,128)(2,1)S(1)} %pad_maximum_fusion.16), channel_id=1, source_target_pairs={{0,16},{4,20},{8,24},{12,28},{16,0},{20,4},{24,8},{28,12},{1,17},{... | collective-permute-start | bytes 446984 | tf_op jit(solution)/shard_map/ppermute | solution.py:43
  11.6 12.2 %collective-permute-start.2 = (bf16[97,768]{1,0:T(8,128)(2,1)S(1)}, bf16[97,768]{1,0:T(8,128)(2,1)S(1)}, u32[]{:S(2)}, u32[]{:S(2)}) collective-permute-start(bf16[97,768]{1,0:T(8,128)(2,1)S(1)} %pad_maximum_fusion.16), channel_id=1, source_target_pairs={{0,24},{4,28},{8,16},{12,20},{16,8},{20,12},{24,0},{28,4},{1,25},{... | collective-permute-start | bytes 446984 | tf_op jit(solution)/shard_map/ppermute | solution.py:43
  13.7 18.7 %collective-permute-start = (bf16[128,1536]{1,0:T(8,128)(2,1)S(1)}, bf16[128,1536]{1,0:T(8,128)(2,1)S(1)}, u32[]{:S(2)}, u32[]{:S(2)}) collective-permute-start(bf16[128,1536]{1,0:T(8,128)(2,1)S(1)} %constant_dynamic-update-slice_fusion), channel_id=1, source_target_pairs={{0,2},{1,3},{2,0},{3,1},{4,6},{5,7},{6,4},{7,5},{8,10},{9,11},{10,... | collective-permute-start | bytes 1179656 | tf_op jit(solution)/shard_map/ppermute | solution.py:37
  23.9 7.7 %collective-permute-start.5 = (bf16[4,768]{1,0:T(4,128)(2,1)S(1)}, bf16[4,768]{1,0:T(4,128)(2,1)S(1)}, u32[]{:S(2)}, u32[]{:S(2)}) collective-permute-start(bf16[4,768]{1,0:T(4,128)(2,1)S(1)} %pad_maximum_fusion.18), channel_id=1, source_target_pairs={{0,4},{4,0},{8,12},{12,8},{16,20},{20,16},{24,28},{28,24},{1,5},{5... | collective-permute-start | bytes 18440 | tf_op jit(solution)/shard_map/ppermute | solution.py:49
  25.4 18.4 %collective-permute-start.10 = (bf16[3,96,768]{2,1,0:T(8,128)(2,1)}, bf16[3,96,768]{2,1,0:T(8,128)(2,1)}, u32[]{:S(2)}, u32[]{:S(2)}) collective-permute-start(bf16[3,96,768]{2,1,0:T(8,128)(2,1)} %pad_maximum_fusion.7), channel_id=1, source_target_pairs={{0,4},{4,0},{8,12},{12,8},{16,20},{20,16},{24,28},{28,24},{1,5},{5... | collective-permute-start | bytes 1327112 | tf_op jit(solution)/shard_map/ppermute | solution.py:49
  27.7 8.7 %collective-permute-start.8 = (bf16[96,768]{1,0:T(8,128)(2,1)}, bf16[96,768]{1,0:T(8,128)(2,1)S(1)}, u32[]{:S(2)}, u32[]{:S(2)}) collective-permute-start(bf16[96,768]{1,0:T(8,128)(2,1)} %get-tuple-element.186), channel_id=1, source_target_pairs={{0,24},{4,28},{8,16},{12,20},{16,8},{20,12},{24,0},{28,4},{1,25},{... | collective-permute-start | bytes 442376 | tf_op jit(solution)/shard_map/ppermute | solution.py:43
  29.9 11.5 %collective-permute-start.7 = (bf16[96,768]{1,0:T(8,128)(2,1)S(1)}, bf16[96,768]{1,0:T(8,128)(2,1)}, u32[]{:S(2)}, u32[]{:S(2)}) collective-permute-start(bf16[96,768]{1,0:T(8,128)(2,1)S(1)} %get-tuple-element.187), channel_id=1, source_target_pairs={{0,16},{4,20},{8,24},{12,28},{16,0},{20,4},{24,8},{28,12},{1,17},{... | collective-permute-start | bytes 442376 | tf_op jit(solution)/shard_map/ppermute | solution.py:43
  31.6 9.8 %collective-permute-start.6 = (bf16[96,768]{1,0:T(8,128)(2,1)S(1)}, bf16[96,768]{1,0:T(8,128)(2,1)}, u32[]{:S(2)}, u32[]{:S(2)}) collective-permute-start(bf16[96,768]{1,0:T(8,128)(2,1)S(1)} %get-tuple-element.188), channel_id=1, source_target_pairs={{0,8},{4,12},{8,0},{12,4},{16,24},{20,28},{24,16},{28,20},{1,9},{5... | collective-permute-start | bytes 442376 | tf_op jit(solution)/shard_map/ppermute | solution.py:43
  33.3 11.6 %collective-permute-start.1 = (bf16[2,128,1536]{2,1,0:T(8,128)(2,1)}, bf16[2,128,1536]{2,1,0:T(8,128)(2,1)S(1)}, u32[]{:S(2)}, u32[]{:S(2)}) collective-permute-start(bf16[2,128,1536]{2,1,0:T(8,128)(2,1)} %pad_maximum_fusion.1), channel_id=1, source_target_pairs={{0,1},{1,0},{2,3},{3,2},{4,5},{5,4},{6,7},{7,6},{8,9},{9,8},{10,11... | collective-permute-start | bytes 2359304 | tf_op jit(solution)/shard_map/ppermute | solution.py:37
  53.9 7.3 %collective-permute-start.11 = (bf16[2,128,768]{2,1,0:T(8,128)(2,1)S(1)}, bf16[2,128,768]{2,1,0:T(8,128)(2,1)S(1)}, u32[]{:S(2)}, u32[]{:S(2)}) collective-permute-start(bf16[2,128,768]{2,1,0:T(8,128)(2,1)S(1)} %get-tuple-element.61), channel_id=1, source_target_pairs={{0,1},{1,0},{2,3},{3,2},{4,5},{5,4},{6,7},{7,6},{8,9},{9,8},{10,11... | collective-permute-start | bytes 1179656 | tf_op jit(solution)/shard_map/ppermute | solution.py:37
  56.9 9.9 %collective-permute-start.15 = (bf16[128,768]{1,0:T(8,128)(2,1)}, bf16[128,768]{1,0:T(8,128)(2,1)S(1)}, u32[]{:S(2)}, u32[]{:S(2)}) collective-permute-start(bf16[128,768]{1,0:T(8,128)(2,1)} %get-tuple-element.174), channel_id=1, source_target_pairs={{0,24},{4,28},{8,16},{12,20},{16,8},{20,12},{24,0},{28,4},{1,25},{... | collective-permute-start | bytes 589832 | tf_op jit(solution)/shard_map/ppermute | solution.py:43
  59.5 16.6 %collective-permute-start.14 = (bf16[128,768]{1,0:T(8,128)(2,1)}, bf16[128,768]{1,0:T(8,128)(2,1)}, u32[]{:S(2)}, u32[]{:S(2)}) collective-permute-start(bf16[128,768]{1,0:T(8,128)(2,1)} %get-tuple-element.175), channel_id=1, source_target_pairs={{0,16},{4,20},{8,24},{12,28},{16,0},{20,4},{24,8},{28,12},{1,17},{... | collective-permute-start | bytes 589832 | tf_op jit(solution)/shard_map/ppermute | solution.py:43
  59.5 16.6 %collective-permute-start.13 = (bf16[128,768]{1,0:T(8,128)(2,1)S(1)}, bf16[128,768]{1,0:T(8,128)(2,1)}, u32[]{:S(2)}, u32[]{:S(2)}) collective-permute-start(bf16[128,768]{1,0:T(8,128)(2,1)S(1)} %get-tuple-element.176), channel_id=1, source_target_pairs={{0,8},{4,12},{8,0},{12,4},{16,24},{20,28},{24,16},{28,20},{1,9},{5... | collective-permute-start | bytes 589832 | tf_op jit(solution)/shard_map/ppermute | solution.py:43
  62.9 15.0 %collective-permute-start.12 = (bf16[128,768]{1,0:T(8,128)(2,1)}, bf16[128,768]{1,0:T(8,128)(2,1)}, u32[]{:S(2)}, u32[]{:S(2)}) collective-permute-start(bf16[128,768]{1,0:T(8,128)(2,1)} %fusion.45), channel_id=1, source_target_pairs={{0,2},{1,3},{2,0},{3,1},{4,6},{5,7},{6,4},{7,5},{8,10},{9,11},{10,... | collective-permute-start | bytes 589832 | tf_op jit(solution)/shard_map/ppermute | solution.py:37
  64.5 14.9 %collective-permute-start.16 = (bf16[4,96,768]{2,1,0:T(8,128)(2,1)S(1)}, bf16[4,96,768]{2,1,0:T(8,128)(2,1)S(1)}, u32[]{:S(2)}, u32[]{:S(2)}) collective-permute-start(bf16[4,96,768]{2,1,0:T(8,128)(2,1)S(1)} %pad_maximum_fusion.4.rest_0_), channel_id=1, source_target_pairs={{0,4},{4,0},{8,12},{12,8},{16,20},{20,16},{24,28},{28,24},{1,5},{5... | collective-permute-start | bytes 1769480 | tf_op jit(solution)/shard_map/ppermute | solution.py:49
  77.3 17.4 %collective-permute-start.21 = (bf16[4,96,768]{2,1,0:T(8,128)(2,1)S(1)}, bf16[4,96,768]{2,1,0:T(8,128)(2,1)S(1)}, u32[]{:S(2)}, u32[]{:S(2)}) collective-permute-start(bf16[4,96,768]{2,1,0:T(8,128)(2,1)S(1)} %slice.389.rest_2_), channel_id=1, source_target_pairs={{0,4},{4,0},{8,12},{12,8},{16,20},{20,16},{24,28},{28,24},{1,5},{5... | collective-permute-start | bytes 1769480 | tf_op jit(solution)/shard_map/ppermute | solution.py:49
  79.5 6.2 %collective-permute-start.19 = (bf16[32,768]{1,0:T(8,128)(2,1)S(1)}, bf16[32,768]{1,0:T(8,128)(2,1)S(1)}, u32[]{:S(2)}, u32[]{:S(2)}) collective-permute-start(bf16[32,768]{1,0:T(8,128)(2,1)S(1)} %get-tuple-element.203), channel_id=1, source_target_pairs={{0,24},{4,28},{8,16},{12,20},{16,8},{20,12},{24,0},{28,4},{1,25},{... | collective-permute-start | bytes 147464 | tf_op jit(solution)/shard_map/ppermute | solution.py:43
  81.8 5.5 %collective-permute-start.18 = (bf16[32,768]{1,0:T(8,128)(2,1)S(1)}, bf16[32,768]{1,0:T(8,128)(2,1)S(1)}, u32[]{:S(2)}, u32[]{:S(2)}) collective-permute-start(bf16[32,768]{1,0:T(8,128)(2,1)S(1)} %get-tuple-element.204), channel_id=1, source_target_pairs={{0,16},{4,20},{8,24},{12,28},{16,0},{20,4},{24,8},{28,12},{1,17},{... | collective-permute-start | bytes 147464 | tf_op jit(solution)/shard_map/ppermute | solution.py:43
  82.0 5.3 %collective-permute-start.17 = (bf16[32,768]{1,0:T(8,128)(2,1)S(1)}, bf16[32,768]{1,0:T(8,128)(2,1)S(1)}, u32[]{:S(2)}, u32[]{:S(2)}) collective-permute-start(bf16[32,768]{1,0:T(8,128)(2,1)S(1)} %get-tuple-element.205), channel_id=1, source_target_pairs={{0,8},{4,12},{8,0},{12,4},{16,24},{20,28},{24,16},{28,20},{1,9},{5... | collective-permute-start | bytes 147464 | tf_op jit(solution)/shard_map/ppermute | solution.py:43
  84.0 6.9 %collective-permute-start.23 = (bf16[128,768]{1,0:T(8,128)(2,1)S(1)}, bf16[128,768]{1,0:T(8,128)(2,1)S(1)}, u32[]{:S(2)}, u32[]{:S(2)}) collective-permute-start(bf16[128,768]{1,0:T(8,128)(2,1)S(1)} %bitcast.175), channel_id=1, source_target_pairs={{0,2},{1,3},{2,0},{3,1},{4,6},{5,7},{6,4},{7,5},{8,10},{9,11},{10,... | collective-permute-start | bytes 589832 | tf_op jit(solution)/shard_map/ppermute | solution.py:37
  87.4 6.6 %collective-permute-start.20 = (bf16[128,768]{1,0:T(8,128)(2,1)S(1)}, bf16[128,768]{1,0:T(8,128)(2,1)S(1)}, u32[]{:S(2)}, u32[]{:S(2)}) collective-permute-start(bf16[128,768]{1,0:T(8,128)(2,1)S(1)} %get-tuple-element.201.own_ref), channel_id=1, source_target_pairs={{0,2},{1,3},{2,0},{3,1},{4,6},{5,7},{6,4},{7,5},{8,10},{9,11},{10,... | collective-permute-start | bytes 589832 | tf_op jit(solution)/shard_map/ppermute | solution.py:37
  91.7 6.9 %collective-permute-start.24 = (bf16[2,128,768]{2,1,0:T(8,128)(2,1)}, bf16[2,128,768]{2,1,0:T(8,128)(2,1)}, u32[]{:S(2)}, u32[]{:S(2)}) collective-permute-start(bf16[2,128,768]{2,1,0:T(8,128)(2,1)} %pad_maximum_fusion.9), channel_id=1, source_target_pairs={{0,1},{1,0},{2,3},{3,2},{4,5},{5,4},{6,7},{7,6},{8,9},{9,8},{10,11... | collective-permute-start | bytes 1179656 | tf_op jit(solution)/shard_map/ppermute | solution.py:37
  95.6 3.0 %collective-permute-start.22 = (bf16[2,128,768]{2,1,0:T(8,128)(2,1)}, bf16[2,128,768]{2,1,0:T(8,128)(2,1)}, u32[]{:S(2)}, u32[]{:S(2)}) collective-permute-start(bf16[2,128,768]{2,1,0:T(8,128)(2,1)} %pad_maximum_fusion.8), channel_id=1, source_target_pairs={{0,1},{1,0},{2,3},{3,2},{4,5},{5,4},{6,7},{7,6},{8,9},{9,8},{10,11... | collective-permute-start | bytes 1179656 | tf_op jit(solution)/shard_map/ppermute | solution.py:37
  112.1 4.8 %collective-permute-start.25 = (bf16[2,128,1536]{2,1,0:T(8,128)(2,1)}, bf16[2,128,1536]{2,1,0:T(8,128)(2,1)S(1)}, u32[]{:S(2)}, u32[]{:S(2)}) collective-permute-start(bf16[2,128,1536]{2,1,0:T(8,128)(2,1)} %get-tuple-element.66), channel_id=1, source_target_pairs={{0,1},{1,0},{2,3},{3,2},{4,5},{5,4},{6,7},{7,6},{8,9},{9,8},{10,11... | collective-permute-start | bytes 2359304 | tf_op jit(solution)/shard_map/ppermute | solution.py:37
  115.7 15.3 %collective-permute-start.27 = (bf16[4,96,768]{2,1,0:T(8,128)(2,1)S(1)}, bf16[4,96,768]{2,1,0:T(8,128)(2,1)S(1)}, u32[]{:S(2)}, u32[]{:S(2)}) collective-permute-start(bf16[4,96,768]{2,1,0:T(8,128)(2,1)S(1)} %slice_bitcast_fusion), channel_id=1, source_target_pairs={{0,4},{4,0},{8,12},{12,8},{16,20},{20,16},{24,28},{28,24},{1,5},{5... | collective-permute-start | bytes 1769480 | tf_op jit(solution)/shard_map/ppermute | solution.py:49
  117.2 13.9 %collective-permute-start.26 = (bf16[128,1536]{1,0:T(8,128)(2,1)S(1)}, bf16[128,1536]{1,0:T(8,128)(2,1)S(1)}, u32[]{:S(2)}, u32[]{:S(2)}) collective-permute-start(bf16[128,1536]{1,0:T(8,128)(2,1)S(1)} %fusion.35), channel_id=1, source_target_pairs={{0,2},{1,3},{2,0},{3,1},{4,6},{5,7},{6,4},{7,5},{8,10},{9,11},{10,... | collective-permute-start | bytes 1179656 | tf_op jit(solution)/shard_map/ppermute | solution.py:37
  131.3 7.6 %collective-permute-start.30 = (bf16[32,1536]{1,0:T(8,128)(2,1)S(1)}, bf16[32,1536]{1,0:T(8,128)(2,1)S(1)}, u32[]{:S(2)}, u32[]{:S(2)}) collective-permute-start(bf16[32,1536]{1,0:T(8,128)(2,1)S(1)} %get-tuple-element.194), channel_id=1, source_target_pairs={{0,24},{4,28},{8,16},{12,20},{16,8},{20,12},{24,0},{28,4},{1,25},{... | collective-permute-start | bytes 294920 | tf_op jit(solution)/shard_map/ppermute | solution.py:43
  133.6 8.2 %collective-permute-start.29 = (bf16[32,1536]{1,0:T(8,128)(2,1)S(1)}, bf16[32,1536]{1,0:T(8,128)(2,1)S(1)}, u32[]{:S(2)}, u32[]{:S(2)}) collective-permute-start(bf16[32,1536]{1,0:T(8,128)(2,1)S(1)} %get-tuple-element.195), channel_id=1, source_target_pairs={{0,16},{4,20},{8,24},{12,28},{16,0},{20,4},{24,8},{28,12},{1,17},{... | collective-permute-start | bytes 294920 | tf_op jit(solution)/shard_map/ppermute | solution.py:43
  133.6 8.2 %collective-permute-start.28 = (bf16[32,1536]{1,0:T(8,128)(2,1)S(1)}, bf16[32,1536]{1,0:T(8,128)(2,1)S(1)}, u32[]{:S(2)}, u32[]{:S(2)}) collective-permute-start(bf16[32,1536]{1,0:T(8,128)(2,1)S(1)} %get-tuple-element.196), channel_id=1, source_target_pairs={{0,8},{4,12},{8,0},{12,4},{16,24},{20,28},{24,16},{28,20},{1,9},{5... | collective-permute-start | bytes 294920 | tf_op jit(solution)/shard_map/ppermute | solution.py:43
  135.8 13.6 %collective-permute-start.32 = (bf16[4,96,768]{2,1,0:T(8,128)(2,1)S(1)}, bf16[4,96,768]{2,1,0:T(8,128)(2,1)S(1)}, u32[]{:S(2)}, u32[]{:S(2)}) collective-permute-start(bf16[4,96,768]{2,1,0:T(8,128)(2,1)S(1)} %slice_bitcast_fusion.2), channel_id=1, source_target_pairs={{0,4},{4,0},{8,12},{12,8},{16,20},{20,16},{24,28},{28,24},{1,5},{5... | collective-permute-start | bytes 1769480 | tf_op jit(solution)/shard_map/ppermute | solution.py:49
  142.8 6.6 %collective-permute-start.31 = (bf16[128,768]{1,0:T(8,128)(2,1)S(1)}, bf16[128,768]{1,0:T(8,128)(2,1)S(1)}, u32[]{:S(2)}, u32[]{:S(2)}) collective-permute-start(bf16[128,768]{1,0:T(8,128)(2,1)S(1)} %add_convert_fusion.1.own_ref), channel_id=1, source_target_pairs={{0,2},{1,3},{2,0},{3,1},{4,6},{5,7},{6,4},{7,5},{8,10},{9,11},{10,... | collective-permute-start | bytes 589832 | tf_op jit(solution)/shard_map/ppermute | solution.py:37
  149.6 6.3 %collective-permute-start.33 = (bf16[2,128,768]{2,1,0:T(8,128)(2,1)S(1)}, bf16[2,128,768]{2,1,0:T(8,128)(2,1)S(1)}, u32[]{:S(2)}, u32[]{:S(2)}) collective-permute-start(bf16[2,128,768]{2,1,0:T(8,128)(2,1)S(1)} %pad_maximum_fusion.10), channel_id=1, source_target_pairs={{0,1},{1,0},{2,3},{3,2},{4,5},{5,4},{6,7},{7,6},{8,9},{9,8},{10,11... | collective-permute-start | bytes 1179656 | tf_op jit(solution)/shard_map/ppermute | solution.py:37
  150.8 29.1 %collective-permute-start.44 = (bf16[2,96,768]{2,1,0:T(8,128)(2,1)}, bf16[2,96,768]{2,1,0:T(8,128)(2,1)}, u32[]{:S(2)}, u32[]{:S(2)}) collective-permute-start(bf16[2,96,768]{2,1,0:T(8,128)(2,1)} %get-tuple-element.166), channel_id=1, source_target_pairs={{0,16},{4,20},{8,24},{12,28},{16,0},{20,4},{24,8},{28,12},{1,17},{... | collective-permute-start | bytes 884744 | tf_op jit(solution)/shard_map/ppermute | solution.py:43
  151.8 28.1 %collective-permute-start.43 = (bf16[2,96,768]{2,1,0:T(8,128)(2,1)}, bf16[2,96,768]{2,1,0:T(8,128)(2,1)}, u32[]{:S(2)}, u32[]{:S(2)}) collective-permute-start(bf16[2,96,768]{2,1,0:T(8,128)(2,1)} %get-tuple-element.167), channel_id=1, source_target_pairs={{0,8},{4,12},{8,0},{12,4},{16,24},{20,28},{24,16},{28,20},{1,9},{5... | collective-permute-start | bytes 884744 | tf_op jit(solution)/shard_map/ppermute | solution.py:43
  154.3 25.6 %collective-permute-start.45 = (bf16[2,96,768]{2,1,0:T(8,128)(2,1)}, bf16[2,96,768]{2,1,0:T(8,128)(2,1)}, u32[]{:S(2)}, u32[]{:S(2)}) collective-permute-start(bf16[2,96,768]{2,1,0:T(8,128)(2,1)} %slice_bitcast_fusion.9), channel_id=1, source_target_pairs={{0,24},{4,28},{8,16},{12,20},{16,8},{20,12},{24,0},{28,4},{1,25},{... | collective-permute-start | bytes 884744 | tf_op jit(solution)/shard_map/ppermute | solution.py:43
  155.9 13.1 %collective-permute-start.34 = (bf16[128,768]{1,0:T(8,128)(2,1)S(1)}, bf16[128,768]{1,0:T(8,128)(2,1)S(1)}, u32[]{:S(2)}, u32[]{:S(2)}) collective-permute-start(bf16[128,768]{1,0:T(8,128)(2,1)S(1)} %get-tuple-element.74), channel_id=1, source_target_pairs={{0,2},{1,3},{2,0},{3,1},{4,6},{5,7},{6,4},{7,5},{8,10},{9,11},{10,... | collective-permute-start | bytes 589832 | tf_op jit(solution)/shard_map/ppermute | solution.py:37
  169.9 4.2 %collective-permute-start.40 = (f32[8,768]{1,0:T(8,128)S(1)}, f32[8,768]{1,0:T(8,128)S(1)}, u32[]{:S(2)}, u32[]{:S(2)}) collective-permute-start(f32[8,768]{1,0:T(8,128)S(1)} %concatenate.55), channel_id=1, source_target_pairs={{0,4},{4,0},{8,12},{12,8},{16,20},{20,16},{24,28},{28,24},{1,5},{5... | collective-permute-start | bytes 73736 | tf_op jit(solution)/shard_map/ppermute | solution.py:49
  171.5 8.3 %collective-permute-start.38 = (bf16[2,96,768]{2,1,0:T(8,128)(2,1)S(1)}, bf16[2,96,768]{2,1,0:T(8,128)(2,1)S(1)}, u32[]{:S(2)}, u32[]{:S(2)}) collective-permute-start(bf16[2,96,768]{2,1,0:T(8,128)(2,1)S(1)} %slice_bitcast_fusion.12), channel_id=1, source_target_pairs={{0,4},{4,0},{8,12},{12,8},{16,20},{20,16},{24,28},{28,24},{1,5},{5... | collective-permute-start | bytes 884744 | tf_op jit(solution)/shard_map/ppermute | solution.py:49
  174.0 3.8 %collective-permute-start.41 = (f32[8,768]{1,0:T(8,128)S(1)}, f32[8,768]{1,0:T(8,128)S(1)}, u32[]{:S(2)}, u32[]{:S(2)}) collective-permute-start(f32[8,768]{1,0:T(8,128)S(1)} %add.204), channel_id=1, source_target_pairs={{0,2},{1,3},{2,0},{3,1},{4,6},{5,7},{6,4},{7,5},{8,10},{9,11},{10,... | collective-permute-start | bytes 73736 | tf_op jit(solution)/shard_map/ppermute | solution.py:37
  177.8 2.7 %collective-permute-start.35 = (bf16[2,128,768]{2,1,0:T(8,128)(2,1)S(1)}, bf16[2,128,768]{2,1,0:T(8,128)(2,1)S(1)}, u32[]{:S(2)}, u32[]{:S(2)}) collective-permute-start(bf16[2,128,768]{2,1,0:T(8,128)(2,1)S(1)} %pad_maximum_fusion.11), channel_id=1, source_target_pairs={{0,1},{1,0},{2,3},{3,2},{4,5},{5,4},{6,7},{7,6},{8,9},{9,8},{10,11... | collective-permute-start | bytes 1179656 | tf_op jit(solution)/shard_map/ppermute | solution.py:37
  179.8 1.7 collective-permute-start.36
  180.0 19.9 %collective-permute-start.39 = (bf16[2,96,768]{2,1,0:T(8,128)(2,1)S(1)}, bf16[2,96,768]{2,1,0:T(8,128)(2,1)S(1)}, u32[]{:S(2)}, u32[]{:S(2)}) collective-permute-start(bf16[2,96,768]{2,1,0:T(8,128)(2,1)S(1)} %get-tuple-element.179), channel_id=1, source_target_pairs={{0,4},{4,0},{8,12},{12,8},{16,20},{20,16},{24,28},{28,24},{1,5},{5... | collective-permute-start | bytes 884744 | tf_op jit(solution)/shard_map/ppermute | solution.py:49
  181.8 22.9 %collective-permute-start.37 = (bf16[128,768]{1,0:T(8,128)(2,1)S(1)}, bf16[128,768]{1,0:T(8,128)(2,1)S(1)}, u32[]{:S(2)}, u32[]{:S(2)}) collective-permute-start(bf16[128,768]{1,0:T(8,128)(2,1)S(1)} %fusion.46), channel_id=1, source_target_pairs={{0,2},{1,3},{2,0},{3,1},{4,6},{5,7},{6,4},{7,5},{8,10},{9,11},{10,... | collective-permute-start | bytes 589832 | tf_op jit(solution)/shard_map/ppermute | solution.py:37
  182.7 8.9 %collective-permute-start.47 = (bf16[104,768]{1,0:T(8,128)(2,1)S(1)}, bf16[104,768]{1,0:T(8,128)(2,1)S(1)}, u32[]{:S(2)}, u32[]{:S(2)}) collective-permute-start(bf16[104,768]{1,0:T(8,128)(2,1)S(1)} %get-tuple-element.206), channel_id=1, source_target_pairs={{0,24},{4,28},{8,16},{12,20},{16,8},{20,12},{24,0},{28,4},{1,25},{... | collective-permute-start | bytes 479240 | tf_op jit(solution)/shard_map/ppermute | solution.py:43
  184.9 15.0 %collective-permute-start.46 = (bf16[104,768]{1,0:T(8,128)(2,1)S(1)}, bf16[104,768]{1,0:T(8,128)(2,1)S(1)}, u32[]{:S(2)}, u32[]{:S(2)}) collective-permute-start(bf16[104,768]{1,0:T(8,128)(2,1)S(1)} %get-tuple-element.207), channel_id=1, source_target_pairs={{0,16},{4,20},{8,24},{12,28},{16,0},{20,4},{24,8},{28,12},{1,17},{... | collective-permute-start | bytes 479240 | tf_op jit(solution)/shard_map/ppermute | solution.py:43
  200.0 7.9 %collective-permute-start.48 = (bf16[104,768]{1,0:T(8,128)(2,1)S(1)}, bf16[104,768]{1,0:T(8,128)(2,1)S(1)}, u32[]{:S(2)}, u32[]{:S(2)}) collective-permute-start(bf16[104,768]{1,0:T(8,128)(2,1)S(1)} %pad_maximum_fusion.12), channel_id=1, source_target_pairs={{0,8},{4,12},{8,0},{12,4},{16,24},{20,28},{24,16},{28,20},{1,9},{5... | collective-permute-start | bytes 479240 | tf_op jit(solution)/shard_map/ppermute | solution.py:43
  (42 other events, 286.6 us)
